TPU v7x, 128 devices: a whole 4x4x4 slice. The times are simulated.
128 devices in a mesh: row: 16 (over x_hi, z, core), col: 8 (over y, x_lo).
Axes of the slice: x: 4 (x_hi: 2, x_lo: 2; x = x_hi * 2 + x_lo), y: 4, z: 4, core: 2. Of those that a mesh axis runs over, the one named last changes fastest.
Arguments:
- image_embed: float32 [16384, 1152], P(('row', 'col')), may hold values from -6 to 6
- text_embed: float32 [16384, 1152], P(('row', 'col')), may hold values from -6 to 6
- exponent_of_sharpness: float32 [1], replicated, may hold values from 3 to 3.7
- bias: float32 [1], replicated, may hold values from -6 to -4
Outputs:
- loss_value: float32 [], replicated
- grad_image: float32 [16384, 1152], P(('row', 'col'))
- grad_text: float32 [16384, 1152], P(('row', 'col'))
All inputs are finite; a program needn't handle non-finite values.
Results may differ from a plain program's by a relative error of at most 0.0011.
Values may be sent and summed in bfloat16 or wider, within the bound.
No kernel may reach another device: no remote copies, remote signals or barrier semaphores. Data moves between devices by JAX's collectives and lax.ppermute only.
A program may use at most 128 MiB of HBM per device.

v0:
```python
import jax
import jax.numpy as jnp
from jax import lax
from jax.experimental import pallas as pl
from jax.experimental.pallas import tpu as pltpu
from jax.sharding import PartitionSpec as P

VMEM = pl.BlockSpec(memory_space=pltpu.VMEM)
SMEM = pl.BlockSpec(memory_space=pltpu.SMEM)
HBM = pl.BlockSpec(memory_space=pltpu.HBM)
MIB = 1024 * 1024
TINY = 1.1754944e-38
AXES = ("row", "col")
ROWS, COLS = 16, 8
ONE_CHIP, TWO_CHIPS, FOUR_CHIPS = 0.5, 0.25, 0.125
PARTNERS = {"x": ((0, 1), (8, 1)), "a": ((0, 2), (2, 0)), "b": ((0, 6), (6, 0))}


def exchange(x, bits_of_core):
    pairs = []
    for row in range(ROWS):
        for col in range(COLS):
            row_bits, col_bits = bits_of_core[row & 1]
            pairs.append((row * COLS + col, (row ^ row_bits) * COLS + (col ^ col_bits)))
    return lax.ppermute(x, AXES, pairs)


def move(x, step):
    return exchange(x, PARTNERS[step])


def swap(x, row_bits=1, col_bits=0):
    return exchange(x, ((row_bits, col_bits),) * 2)


def encode(x, shift):
    y = x * shift
    y2 = y * y
    y4 = y2 * y2
    return (y4 * y2 * (y * jnp.abs(y))).astype(jnp.bfloat16)


def decode(e, shift):
    f = e.astype(jnp.float32)
    size = jnp.exp2(jnp.log2(jnp.maximum(jnp.abs(f), TINY)) * 0.125)
    return jnp.where(f < 0.0, -size, size) * (1.0 / shift)


def row_scale(raw):
    return lax.rsqrt(jnp.sum(raw * raw, axis=1, keepdims=True) + 1e-06)


def by_core(core_ref, work):
    pl.when(core_ref[0] == 0)(lambda: work(True))
    pl.when(core_ref[0] != 0)(lambda: work(False))


def normalize_kernel(core_ref, img_ref, txt_ref, keep_ref, give_ref, raw_ref, sems):
    copies = [
        pltpu.make_async_copy(source, raw_ref.at[k], sems.at[k])
        for k, source in enumerate((txt_ref, img_ref))
    ]
    for copy in copies:
        copy.start()

    def low(k):
        raw = raw_ref[k]
        return (raw * row_scale(raw)).astype(jnp.bfloat16)

    for k, copy in enumerate(copies):
        copy.wait()

        def work(is_first, k=k):
            ref = keep_ref if (k == 0) == is_first else give_ref
            ref[...] = low(k)

        by_core(core_ref, work)


def normalize(core, img, txt):
    low = jax.ShapeDtypeStruct(img.shape, jnp.bfloat16)
    return pl.pallas_call(
        normalize_kernel,
        out_shape=(low, low),
        in_specs=[SMEM, HBM, HBM],
        out_specs=(VMEM, VMEM),
        scratch_shapes=[pltpu.VMEM((2, *img.shape), jnp.float32), pltpu.SemaphoreType.DMA((2,))],
        compiler_params=pltpu.CompilerParams(vmem_limit_bytes=6 * MIB),
        name="normalize",
    )(core, img, txt)


def pack_kernel(*refs):
    out_ref = refs[-1]
    start = 0
    for ref in refs[:-1]:
        out_ref[start : start + ref.shape[0]] = ref[...]
        start += ref.shape[0]


def pack(*pieces):
    shape = (sum(p.shape[0] for p in pieces), pieces[0].shape[1])
    return pl.pallas_call(
        pack_kernel,
        out_shape=jax.ShapeDtypeStruct(shape, pieces[0].dtype),
        in_specs=[VMEM] * len(pieces),
        out_specs=VMEM,
        compiler_params=pltpu.CompilerParams(vmem_limit_bytes=8 * MIB),
        name="pack",
    )(*pieces)


def half_kernel(k, in_ref, out_ref):
    rows = out_ref.shape[0]
    out_ref[...] = in_ref[k * rows : (k + 1) * rows]


def half_of(x, k):
    return pl.pallas_call(
        lambda *refs: half_kernel(k, *refs),
        out_shape=jax.ShapeDtypeStruct((x.shape[0] // 2, x.shape[1]), x.dtype),
        in_specs=[VMEM],
        out_specs=VMEM,
        compiler_params=pltpu.CompilerParams(vmem_limit_bytes=4 * MIB),
        name="half_of",
    )(x)


def run_tiles(pair, sharp_ref, bias_ref, jobs):
    sharp_scalar = jnp.max(sharp_ref[...])
    bias = jnp.max(bias_ref[...])
    steps = [(job, k) for job in jobs for k in range(len(job[1]))]

    def products(step):
        job, k = step
        return lax.dot_general(
            job[0][...], job[1][k][0][...], (((1,), (1,)), ((), ())), preferred_element_type=jnp.float32
        )

    loss = jnp.zeros((8, 128), jnp.float32)
    following = products(steps[0])
    for i, (job, k) in enumerate(steps):
        current = following
        if i + 1 < len(steps):
            following = products(steps[i + 1])
        _, blocks, before, out, corner = job
        texts, weights_out = blocks[k]
        rows, cols = current.shape
        sharp = jnp.exp(jnp.full((1, cols), sharp_scalar, jnp.float32))
        logits = current * sharp + bias
        grown = jnp.exp(logits)
        one_more = 1.0 + grown
        weights = sharp * (grown / one_more)
        weights_out[...] = weights.astype(jnp.bfloat16)
        logs = jnp.log(one_more[: rows // 2] * one_more[rows // 2 :])
        logs = jnp.sum(logs.reshape(rows // 16, 8, cols), axis=0)
        if corner is not None:
            row_ids = lax.broadcasted_iota(jnp.int32, (pair, pair), 0)
            col_ids = lax.broadcasted_iota(jnp.int32, (pair, pair), 1)
            wanted = jnp.where(row_ids < pair // 2, row_ids + pair // 2, row_ids - pair // 2)
            same = (wanted == col_ids) & (corner == 0)
            own = weights[:pair, :pair] - jnp.where(same, sharp[:, :pair], 0.0)
            weights_out[:pair, :pair] = own.astype(jnp.bfloat16)
            matched = jnp.where(same, logits[:pair, :pair], 0.0)
            matched = jnp.sum(matched.reshape(pair // 8, 8, pair), axis=0)
            for start in range(0, pair, 128):
                loss = loss - matched[:, start : start + 128]
        for start in range(0, cols, 128):
            loss = loss + logs[:, start : start + 128]
        part = jnp.dot(weights_out[...], texts[...], preferred_element_type=jnp.float32)
        if k == 0:
            total = part if before is None else part + before[...]
        else:
            total = total + part
        if k == len(blocks) - 1:
            out[...] = total
    return loss


def row_blocks(ref, size, rows=None):
    return [ref.at[pl.ds(start, size)] for start in range(0, rows or ref.shape[0], size)]


def near_tile_kernel(core_ref, sharp_ref, bias_ref, near_ref, received_ref, far_ref, img_ref, txt_ref, weights_ref, part_ref, loss_ref):
    pair = far_ref.shape[0] // 3

    def work(is_first):
        if is_first:
            txt_ref[...] = near_ref[...]
            img_ref[...] = received_ref[: 3 * pair]
        else:
            txt_ref[...] = received_ref[...]
            img_ref[:pair] = near_ref[3 * pair :]
            img_ref[pair:] = far_ref[pair:]

    by_core(core_ref, work)
    jobs = []
    for k, rows in enumerate(row_blocks(img_ref, pair)):
        span = pl.ds(k * pair, pair)
        corner = core_ref[0] if k == 0 else None
        jobs.append((rows, [(txt_ref, weights_ref.at[span])], None, part_ref.at[span], corner))
    loss_ref[...] = run_tiles(pair, sharp_ref, bias_ref, jobs)


def far_tile_kernel(
    core_ref, sharp_ref, bias_ref, far_ref, received_ref, near_txt_ref, img_ref, before_ref,
    txt_ref, second_ref, weights_ref, part_ref, near_half_ref, far_half_ref, part_half_ref, loss_ref,
):
    pair = far_ref.shape[0] // 3
    half = pair // 2

    def work(is_first):
        txt_ref[...] = far_ref[...] if is_first else received_ref[...]
        second_ref[...] = received_ref[:half] if is_first else far_ref[half:pair]

    by_core(core_ref, work)
    jobs = []
    for k, rows in enumerate(row_blocks(img_ref, pair)):
        span = pl.ds(k * pair, pair)
        jobs.append((rows, [(txt_ref, weights_ref.at[span])], before_ref.at[span], part_ref.at[span], None))
    blocks = [(near_txt_ref, near_half_ref), (txt_ref, far_half_ref)]
    jobs.append((second_ref, blocks, None, part_half_ref, None))
    loss_ref[...] = run_tiles(pair, sharp_ref, bias_ref, jobs)


def last_tile_kernel(
    core_ref, sharp_ref, bias_ref, last_ref, received_ref, near_txt_ref, far_txt_ref,
    img_ref, second_ref, before_ref, before_half_ref, near_half_ref, far_half_ref,
    weights_ref, part_ref, img_tail_ref, near_tail_ref, far_tail_ref, last_tail_ref, part_tail_ref, loss_ref, txt_ref,
):
    pair = last_ref.shape[0]
    half = pair // 2
    low, high = pl.ds(0, half), pl.ds(half, half)

    def work(is_first):
        txt_ref[...] = last_ref[...] if is_first else received_ref[...]
        img_tail_ref[high] = received_ref[low] if is_first else last_ref[high]

    by_core(core_ref, work)
    img_tail_ref[low] = second_ref[...]
    near_tail_ref[low] = near_half_ref[...]
    far_tail_ref[low] = far_half_ref[...]
    jobs = []
    for k, rows in enumerate(row_blocks(img_ref, pair)):
        span = pl.ds(k * pair, pair)
        jobs.append((rows, [(txt_ref, weights_ref.at[span])], before_ref.at[span], part_ref.at[span], None))
    jobs.append((second_ref, [(txt_ref, last_tail_ref.at[low])], before_half_ref, part_tail_ref.at[low], None))
    blocks = [
        (near_txt_ref, near_tail_ref.at[high]),
        (far_txt_ref, far_tail_ref.at[high]),
        (txt_ref, last_tail_ref.at[high]),
    ]
    jobs.append((img_tail_ref.at[high], blocks, None, part_tail_ref.at[high], None))
    loss_ref[...] = run_tiles(pair, sharp_ref, bias_ref, jobs)


def tile_call(kernel, name, pairs, scalars, arrays, outs, scratch=()):
    features = arrays[0].shape[1]
    return pl.pallas_call(
        kernel,
        out_shape=outs,
        in_specs=[SMEM] + [VMEM] * (len(scalars) - 1 + len(arrays)),
        out_specs=(VMEM,) * len(outs),
        scratch_shapes=[pltpu.VMEM(x.shape, x.dtype) for x in scratch],
        compiler_params=pltpu.CompilerParams(vmem_limit_bytes=16 * MIB),
        cost_estimate=pl.CostEstimate(
            flops=4 * pairs * features,
            bytes_accessed=sum(2 * x.size for x in arrays),
            transcendentals=3 * pairs,
        ),
        name=name,
    )(*scalars, *arrays)


def small_call(kernel, name, core, arrays, outs):
    size = sum(x.size * x.dtype.itemsize for x in (*arrays, *outs))
    return pl.pallas_call(
        kernel,
        out_shape=outs,
        in_specs=[SMEM] + [VMEM] * len(arrays),
        out_specs=(VMEM,) * len(outs),
        compiler_params=pltpu.CompilerParams(vmem_limit_bytes=size + 4 * MIB),
        name=name,
    )(core, *arrays)


CHUNK = 32


def each_chunk(rows, work):
    def step(i, carry):
        first = pl.multiple_of(i * CHUNK, CHUNK)
        work(lambda start=0: pl.ds(start + first, CHUNK))
        return carry

    lax.fori_loop(0, rows // CHUNK, step, 0)


def opposite_kernel(core_ref, txt_ref, img_ref, received_ref, a_ref, b_ref):
    half = a_ref.shape[0]

    def work(is_first):
        def texts(at):
            a_ref[at()] = encode(txt_ref[at()] + decode(received_ref[at()], ONE_CHIP), ONE_CHIP)
            b_ref[at()] = encode(txt_ref[at(half)] + decode(received_ref[at(half)], ONE_CHIP), ONE_CHIP)

        def images(at):
            a_ref[at()] = received_ref[at(half)]
            b_ref[at()] = encode(img_ref[at(half)], ONE_CHIP)

        each_chunk(half, texts if is_first else images)

    by_core(core_ref, work)


def second_kernel(core_ref, txt_ref, txt_received_ref, img_ref, img_received_ref, out_ref):
    pair = out_ref.shape[0]
    half = pair // 2

    def work(is_first):
        def texts(at):
            out_ref[at()] = encode(txt_ref[at()] + decode(txt_received_ref[at()], ONE_CHIP), TWO_CHIPS)

        def images(at):
            out_ref[at()] = encode(decode(img_received_ref[at()], ONE_CHIP), TWO_CHIPS)
            out_ref[at(half)] = encode(img_ref[at()], TWO_CHIPS)

        if is_first:
            each_chunk(pair, texts)
        else:
            each_chunk(half, images)

    by_core(core_ref, work)


def far_kernel(core_ref, txt_ref, img_ref, received_ref, from_a_ref, from_b_ref, x_ref, b_ref):
    half = x_ref.shape[0] // 2

    def work(is_first):
        def rows(at):
            def base(i):
                if is_first:
                    return txt_ref[at(i * half)] + decode(received_ref[at(i * half)], ONE_CHIP)
                return img_ref[at(i * half)]

            x_ref[at()] = encode(base(2), TWO_CHIPS)
            x_ref[at(half)] = encode(base(3) + decode(from_b_ref[at()], ONE_CHIP), TWO_CHIPS)
            b_ref[at()] = encode(base(4) + decode(from_a_ref[at()], ONE_CHIP), TWO_CHIPS)
            b_ref[at(half)] = encode(base(5), TWO_CHIPS)

        each_chunk(half, rows)

    by_core(core_ref, work)


def base_kernel(core_ref, txt_ref, received_ref, img_ref, img_received_ref, out_ref):
    count = out_ref.shape[0]
    three = 3 * count // 4

    def work(is_first):
        def texts(at):
            out_ref[at()] = txt_ref[at()] + decode(received_ref[at()], ONE_CHIP)

        def images(at):
            out_ref[at()] = decode(img_received_ref[at()], ONE_CHIP)

        if is_first:
            each_chunk(count, texts)
        else:
            each_chunk(three, images)
            out_ref[three:] = img_ref[: count - three]

    by_core(core_ref, work)


def near_kernel(k, core_ref, base_ref, received_ref, out_ref):
    pair = out_ref.shape[0]

    def rows(at):
        value = base_ref[at(k * pair)] + decode(received_ref[at()], TWO_CHIPS)
        out_ref[at()] = encode(value, FOUR_CHIPS)

    each_chunk(pair, rows)


def gather_sums_kernel(core_ref, base_ref, a_ref, b_ref, x_ref, keep_ref, give_ref):
    own = keep_ref.shape[0]

    def rows(at):
        for start, ref in ((0, keep_ref), (own, give_ref)):
            total = base_ref[at(start)] + decode(x_ref[at(start)], FOUR_CHIPS)
            total = total + decode(a_ref[at(start)], FOUR_CHIPS)
            ref[at()] = total + decode(b_ref[at(start)], FOUR_CHIPS)

    each_chunk(own, rows)


def finish_kernel(batch, core_ref, img_ref, txt_ref, kept_ref, received_ref, loss_parts_ref, loss_ref, grad_img_ref, grad_txt_ref):
    loss_ref[...] = jnp.full((1, 1), jnp.sum(loss_parts_ref[...]) * (1.0 / batch), jnp.float32)

    def side(at, raw_ref, sum_ref, grad_ref):
        raw = raw_ref[at()]
        scale = row_scale(raw)
        unit = raw * scale
        summed = sum_ref[at()]
        grad_ref[at()] = (summed - unit * jnp.sum(unit * summed, axis=1, keepdims=True)) * scale

    def work(is_first):
        def rows(at):
            side(at, img_ref, received_ref if is_first else kept_ref, grad_img_ref)
            side(at, txt_ref, kept_ref if is_first else received_ref, grad_txt_ref)

        each_chunk(kept_ref.shape[0], rows)

    by_core(core_ref, work)


def transposed_product(weights, img):
    return lax.dot_general(
        weights, img, (((0,), (0,)), ((), ())), preferred_element_type=jnp.float32
    )


def body(image_embed, text_embed, exponent_of_sharpness, bias):
    own, features = image_embed.shape
    pair = 2 * own
    batch = own * ROWS * COLS
    core = lax.axis_index("row") & 1
    core, on_first = lax.optimization_barrier((core.reshape(1), core == 0))

    def array(rows, dtype, columns=features):
        return jax.ShapeDtypeStruct((rows, columns), dtype)

    low_half, low_piece = array(own, jnp.bfloat16), array(pair, jnp.bfloat16)

    keep, give = normalize(core, image_embed, text_embed)
    low = pack(keep, swap(give))
    slot_x, slot_1, slot_3 = move(low, "x"), move(low, "a"), move(low, "b")
    slot_2, slot_x3, slot_x1 = move(slot_3, "a"), move(slot_x, "b"), move(slot_1, "x")
    near = pack(low, slot_x, slot_1, slot_3)
    near_received = swap(near)
    sharpness = jnp.broadcast_to(exponent_of_sharpness.reshape(1, 1), (8, 128))
    shift = jnp.broadcast_to(bias.reshape(1, 1), (8, 128))
    slot_x3, sharpness, shift = lax.optimization_barrier((slot_x3, sharpness, shift))
    last_a = move(half_of(slot_x3, 0), "a")
    last_b = move(half_of(slot_x1, 1), "b")
    far = pack(slot_2, slot_x1, slot_x3)
    far_received = swap(far)

    scalars = (core, sharpness, shift)
    losses = array(8, jnp.float32, 128)
    wide, three = 4 * pair, 3 * pair
    img, near_txt, near_weights, part, near_loss = tile_call(
        near_tile_kernel,
        "tile_near",
        three * wide,
        scalars,
        (near, near_received, far),
        (
            array(three, jnp.bfloat16),
            array(wide, jnp.bfloat16),
            array(three, jnp.bfloat16, wide),
            array(three, jnp.float32),
            losses,
        ),
    )
    last_a, last_b, part = lax.optimization_barrier((last_a, last_b, part))
    last = pack(last_a, last_b)
    last_received = swap(last)
    far_txt, second, far_weights, part, near_half, far_half, part_half, far_loss = tile_call(
        far_tile_kernel,
        "tile_far",
        three * three + own * (wide + three),
        scalars,
        (far, far_received, near_txt, img, part),
        (
            array(three, jnp.bfloat16),
            low_half,
            array(three, jnp.bfloat16, three),
            array(three, jnp.float32),
            array(own, jnp.bfloat16, wide),
            array(own, jnp.bfloat16, three),
            array(own, jnp.float32),
            losses,
        ),
    )
    last_weights, img_part, img_tail, near_tail, far_tail, last_tail, img_part_tail, last_loss = tile_call(
        last_tile_kernel,
        "tile_last",
        (three + own) * pair + own * 2 * wide,
        scalars,
        (last, last_received, near_txt, far_txt, img, second, part, part_half, near_half, far_half),
        (
            array(three, jnp.bfloat16, pair),
            array(three, jnp.float32),
            low_piece,
            array(pair, jnp.bfloat16, wide),
            array(pair, jnp.bfloat16, three),
            array(pair, jnp.bfloat16, pair),
            array(pair, jnp.float32),
            losses,
        ),
        (low_piece,),
    )
    loss = near_loss + far_loss + last_loss

    def text_sums(weights, tail):
        return transposed_product(weights, img) + transposed_product(tail, img_tail)

    loss = loss + swap(loss)
    opposite_part = text_sums(last_weights, last_tail)
    sent = encode(jnp.where(on_first, img_part_tail, opposite_part), ONE_CHIP)
    sent, far_weights, far_tail = lax.optimization_barrier((sent, far_weights, far_tail))
    tail_received = swap(sent)
    far_part = text_sums(far_weights, far_tail)
    sent = encode(jnp.where(on_first, img_part, far_part), ONE_CHIP)
    loss = loss + swap(loss, 0, 1)
    tail_received, sent, loss = lax.optimization_barrier((tail_received, sent, loss))

    a, b = small_call(
        opposite_kernel, "opposite", core, (opposite_part, img_part_tail, tail_received), (low_half, low_half)
    )
    a, b, sent, near_weights, near_tail = lax.optimization_barrier((a, b, sent, near_weights, near_tail))
    from_a, from_b = move(a, "a"), move(b, "b")
    rest_received = swap(sent)
    near_part = text_sums(near_weights, near_tail)
    sent = encode(near_part, ONE_CHIP)
    loss = loss + swap(loss, 8, 1)
    (second,) = small_call(
        second_kernel, "second", core, (far_part, rest_received, img_part_tail, tail_received), (low_piece,)
    )
    from_a, from_b, second, sent, loss = lax.optimization_barrier((from_a, from_b, second, sent, loss))

    second_received = move(second, "a")
    x, b = small_call(
        far_kernel, "far", core, (far_part, img_part, rest_received, from_a, from_b), (low_piece,) * 2
    )
    x, b, sent = lax.optimization_barrier((x, b, sent))
    from_x, from_b = move(x, "x"), move(b, "b")
    near_received = swap(sent)
    (base,) = small_call(
        base_kernel, "base", core, (near_part, near_received, img_part, rest_received), (array(wide, jnp.float32),)
    )
    base, loss = lax.optimization_barrier((base, loss))
    loss = loss + swap(loss, 0, 2)
    second_received, base, loss = lax.optimization_barrier((second_received, base, loss))

    def near_slot(k, received):
        (out,) = small_call(
            lambda *refs: near_kernel(k, *refs), "near", core, (base, received), (low_piece,)
        )
        return out

    from_b, from_x, from_a = (
        move(near_slot(3, second_received), "b"),
        move(near_slot(1, from_b), "x"),
        move(near_slot(2, from_x), "a"),
    )
    loss = loss + swap(loss, 0, 6)
    loss = loss + swap(loss, 2, 0)
    from_x, from_a, from_b, loss = lax.optimization_barrier((from_x, from_a, from_b, loss))
    loss = loss + swap(loss, 6, 0)
    keep, give = small_call(
        gather_sums_kernel, "gather_sums", core, (base, from_a, from_b, from_x), (array(own, jnp.float32),) * 2
    )
    grad = array(own, jnp.float32)
    loss_value, grad_image, grad_text = small_call(
        lambda *refs: finish_kernel(batch, *refs),
        "finish",
        core,
        (image_embed, text_embed, keep, swap(give), loss),
        (array(1, jnp.float32, 1), grad, grad),
    )
    return (loss_value.reshape(()), grad_image, grad_text)


def solution(mesh):
    in_specs = (P(("row", "col"), None), P(("row", "col"), None), P(), P())
    out_specs = (P(), P(("row", "col"), None), P(("row", "col"), None))
    return jax.shard_map(body, mesh=mesh, in_specs=in_specs, out_specs=out_specs, check_vma=False)
```

profile of v0, /device:TPU:1, one launch (start us, length us, event | category | flops | bytes accessed | tf_op | source)
XLA Modules:
  0.0 108.3 jit_solution(15777923323002378627)
XLA Ops:
  0.6 1.1 copy-done
  1.7 1.1 copy-done.2
  3.3 1.5 %collective-permute-start = (bf16[128,1152]{1,0:T(8,128)(2,1)S(1)}, bf16[128,1152]{1,0:T(8,128)(2,1)S(1)}, u32[]{:S(2)}, u32[]{:S(2)}) collective-permute-start(bf16[128,1152]{1,0:T(8,128)(2,1)S(1)} %get-tuple-element.73), channel_id=1, source_target_pairs={{0,8},{1,9},{2,10},{3,11},{4,12},{5,13},{6,14},{7,15},{8,0},{9,1},... | collective-permute-start | bytes 884744 | tf_op jit(solution)/shard_map/ppermute | solution.py:25
  4.8 1.2 %collective-permute-done.refs_1_ = bf16[128,1152]{1,0:T(8,128)(2,1)S(1)} collective-permute-done((bf16[128,1152]{1,0:T(8,128)(2,1)S(1)}, bf16[128,1152]{1,0:T(8,128)(2,1)S(1)}, u32[]{:S(2)}, u32[]{:S(2)}) %collective-permute-start) | collective-permute-done | bytes 294944 | tf_op jit(solution)/shard_map/ppermute | solution.py:25
  6.1 2.6 %collective-permute-start.1 = (bf16[256,1152]{1,0:T(8,128)(2,1)S(1)}, bf16[256,1152]{1,0:T(8,128)(2,1)S(1)}, u32[]{:S(2)}, u32[]{:S(2)}) collective-permute-start(bf16[256,1152]{1,0:T(8,128)(2,1)S(1)} %pack.4.refs_0_), channel_id=1, source_target_pairs={{0,1},{1,0},{2,3},{3,2},{4,5},{5,4},{6,7},{7,6},{8,73},{9,72},{10,... | collective-permute-start | bytes 1769480 | tf_op jit(solution)/shard_map/ppermute | solution.py:25
  8.7 1.6 %collective-permute-start.4 = (bf16[256,1152]{1,0:T(8,128)(2,1)S(1)}, bf16[256,1152]{1,0:T(8,128)(2,1)S(1)}, u32[]{:S(2)}, u32[]{:S(2)}) collective-permute-start(bf16[256,1152]{1,0:T(8,128)(2,1)S(1)} %pack.4.refs_0_), channel_id=1, source_target_pairs={{0,2},{1,3},{2,0},{3,1},{4,6},{5,7},{6,4},{7,5},{8,24},{9,25},{10,... | collective-permute-start | bytes 1769480 | tf_op jit(solution)/shard_map/ppermute | solution.py:25
  10.3 2.2 %collective-permute-start.7 = (bf16[256,1152]{1,0:T(8,128)(2,1)S(1)}, bf16[256,1152]{1,0:T(8,128)(2,1)S(1)}, u32[]{:S(2)}, u32[]{:S(2)}) collective-permute-start(bf16[256,1152]{1,0:T(8,128)(2,1)S(1)} %pack.4.refs_0_), channel_id=1, source_target_pairs={{0,6},{1,7},{2,4},{3,5},{4,2},{5,3},{6,0},{7,1},{8,56},{9,57},{10,... | collective-permute-start | bytes 1769480 | tf_op jit(solution)/shard_map/ppermute | solution.py:25
  12.6 3.8 %collective-permute-done.1.refs_1_ = bf16[256,1152]{1,0:T(8,128)(2,1)S(1)} collective-permute-done((bf16[256,1152]{1,0:T(8,128)(2,1)S(1)}, bf16[256,1152]{1,0:T(8,128)(2,1)S(1)}, u32[]{:S(2)}, u32[]{:S(2)}) %collective-permute-start.1) | collective-permute-done | bytes 589856 | tf_op jit(solution)/shard_map/ppermute | solution.py:25
  16.4 1.5 %collective-permute-done.4.refs_2_ = bf16[256,1152]{1,0:T(8,128)(2,1)S(1)} collective-permute-done((bf16[256,1152]{1,0:T(8,128)(2,1)S(1)}, bf16[256,1152]{1,0:T(8,128)(2,1)S(1)}, u32[]{:S(2)}, u32[]{:S(2)}) %collective-permute-start.4) | collective-permute-done | bytes 589856 | tf_op jit(solution)/shard_map/ppermute | solution.py:25
  17.9 2.5 %collective-permute-done.7.refs_3_ = bf16[256,1152]{1,0:T(8,128)(2,1)S(1)} collective-permute-done((bf16[256,1152]{1,0:T(8,128)(2,1)S(1)}, bf16[256,1152]{1,0:T(8,128)(2,1)S(1)}, u32[]{:S(2)}, u32[]{:S(2)}) %collective-permute-start.7) | collective-permute-done | bytes 589856 | tf_op jit(solution)/shard_map/ppermute | solution.py:25
  21.0 3.8 %collective-permute-start.2 = (bf16[256,1152]{1,0:T(8,128)(2,1)S(1)}, bf16[256,1152]{1,0:T(8,128)(2,1)S(1)}, u32[]{:S(2)}, u32[]{:S(2)}) collective-permute-start(bf16[256,1152]{1,0:T(8,128)(2,1)S(1)} %collective-permute-done.1.refs_1_), channel_id=1, source_target_pairs={{0,6},{1,7},{2,4},{3,5},{4,2},{5,3},{6,0},{7,1},{8,56},{9,57},{10,... | collective-permute-start | bytes 1769480 | tf_op jit(solution)/shard_map/ppermute | solution.py:25
  24.8 1.8 %collective-permute-start.5 = (bf16[256,1152]{1,0:T(8,128)(2,1)S(1)}, bf16[256,1152]{1,0:T(8,128)(2,1)S(1)}, u32[]{:S(2)}, u32[]{:S(2)}) collective-permute-start(bf16[256,1152]{1,0:T(8,128)(2,1)S(1)} %collective-permute-done.4.refs_2_), channel_id=1, source_target_pairs={{0,1},{1,0},{2,3},{3,2},{4,5},{5,4},{6,7},{7,6},{8,73},{9,72},{10,... | collective-permute-start | bytes 1769480 | tf_op jit(solution)/shard_map/ppermute | solution.py:25
  27.9 4.2 %collective-permute-done.2.refs_0_.refs_2_ = bf16[256,1152]{1,0:T(8,128)(2,1)S(1)} collective-permute-done((bf16[256,1152]{1,0:T(8,128)(2,1)S(1)}, bf16[256,1152]{1,0:T(8,128)(2,1)S(1)}, u32[]{:S(2)}, u32[]{:S(2)}) %collective-permute-start.2) | collective-permute-done | bytes 589856 | tf_op jit(solution)/shard_map/ppermute | solution.py:25
  32.1 2.7 %collective-permute-done.5.refs_0_.refs_1_ = bf16[256,1152]{1,0:T(8,128)(2,1)S(1)} collective-permute-done((bf16[256,1152]{1,0:T(8,128)(2,1)S(1)}, bf16[256,1152]{1,0:T(8,128)(2,1)S(1)}, u32[]{:S(2)}, u32[]{:S(2)}) %collective-permute-start.5) | collective-permute-done | bytes 589856 | tf_op jit(solution)/shard_map/ppermute | solution.py:25
  35.7 2.3 %collective-permute-start.6 = (bf16[128,1152]{1,0:T(8,128)(2,1)S(1)}, bf16[128,1152]{1,0:T(8,128)(2,1)S(1)}, u32[]{:S(2)}, u32[]{:S(2)}) collective-permute-start(bf16[128,1152]{1,0:T(8,128)(2,1)S(1)} %half_of.3), channel_id=1, source_target_pairs={{0,6},{1,7},{2,4},{3,5},{4,2},{5,3},{6,0},{7,1},{8,56},{9,57},{10,... | collective-permute-start | bytes 884744 | tf_op jit(solution)/shard_map/ppermute | solution.py:25
  38.0 5.1 %tile_near.1 = (bf16[768,1152]{1,0:T(8,128)(2,1)S(1)}, bf16[1024,1152]{1,0:T(8,128)(2,1)S(1)}, bf16[768,1024]{1,0:T(8,128)(2,1)S(1)}, f32[768,1152]{1,0:T(8,128)S(1)}, f32[8,128]{1,0:T(8,128)S(1)}) custom-call(s32[1]{0:T(128)} %bitcast.core_ref.refs_0_, f32[8,128]{1,0:T(8,128)S(1)} %broadcast_in_dim.15.sharp_ref, f32[8,128]{1,0:T(8,128)S(1)} %broadcast_in_dim.17.bias_ref, ...), custom_call_target="tpu_custom_call" | custom-call | flops 3623878656 | bytes 6488064 | tf_op jit(solution)/shard_map/tile_near/pallas_call | solution.py:259
  43.2 1.2 %collective-permute-start.10 = (bf16[256,1152]{1,0:T(8,128)(2,1)S(1)}, bf16[256,1152]{1,0:T(8,128)(2,1)S(1)}, u32[]{:S(2)}, u32[]{:S(2)}) collective-permute-start(bf16[256,1152]{1,0:T(8,128)(2,1)S(1)} %pack.7.last_ref), channel_id=1, source_target_pairs={{0,8},{1,9},{2,10},{3,11},{4,12},{5,13},{6,14},{7,15},{8,0},{9,1},... | collective-permute-start | bytes 1769480 | tf_op jit(solution)/shard_map/ppermute | solution.py:25
  44.3 6.1 %tile_far.1 = (bf16[768,1152]{1,0:T(8,128)(2,1)S(1)}, bf16[128,1152]{1,0:T(8,128)(2,1)S(1)}, bf16[768,768]{1,0:T(8,128)(2,1)S(1)}, f32[768,1152]{1,0:T(8,128)S(1...) custom-call(s32[1]{0:T(128)} %bitcast.core_ref.refs_0_, ...), custom_call_target="tpu_custom_call" | custom-call | flops 3774873600 | bytes 9437184 | tf_op jit(solution)/shard_map/tile_far/pallas_call | solution.py:259
  50.5 4.1 %tile_last.1 = (bf16[768,256]{1,0:T(8,128)(2,1)S(1)}, f32[768,1152]{1,0:T(8,128)S(1)}, bf16[256,1152]{1,0:T(8,128)(2,1)S(1)}, bf16[256,1024]{1,0:T(8,128)(2,1)S(...) custom-call(s32[1]{0:T(128)} %bitcast.core_ref.refs_0_, ...), custom_call_target="tpu_custom_call" | custom-call | flops 2264924160 | bytes 9895936 | tf_op jit(solution)/shard_map/tile_last/pallas_call | solution.py:259
  55.1 0.9 fusion.5
  56.0 0.7 fusion.7
  57.8 2.5 %fusion.3 = (bf16[768,1152]{1,0:T(8,128)(2,1)S(1)}, f32[768,1152]{1,0:T(8,128)S(1)}) fusion(f32[768,1152]{1,0:T(8,128)S(1)} %get-tuple-element.97.img_ref, pred[]{:T(512)S(6)} %eq.3, f32[768,1152]{1,0:T(8,128)S(1)} %fusion.7, bf16[768,768]{1,0:T(8,128)(2,1)S(1)} %get-tuple-element.98, bf16[768,1152]{1,0:T(8,128)(2,1)S(1)} %get-tuple-element.81.img_ref), kind=kOutput, calls=%fused_computation.9 | convolution fusion | flops 1367801856 | bytes 15335425 | tf_op jit(solution)/shard_map/dot_general | solution.py:419
  60.5 1.6 %collective-permute-start.17 = (bf16[768,1152]{1,0:T(8,128)(2,1)S(1)}, bf16[768,1152]{1,0:T(8,128)(2,1)S(1)}, u32[]{:S(2)}, u32[]{:S(2)}) collective-permute-start(bf16[768,1152]{1,0:T(8,128)(2,1)S(1)} %get-tuple-element.111), channel_id=1, source_target_pairs={{0,8},{1,9},{2,10},{3,11},{4,12},{5,13},{6,14},{7,15},{8,0},{9,1},... | collective-permute-start | bytes 5308424 | tf_op jit(solution)/shard_map/ppermute | solution.py:25
  62.1 1.6 %collective-permute-start.18 = (f32[8,128]{1,0:T(8,128)S(1)}, f32[8,128]{1,0:T(8,128)S(1)}, u32[]{:S(2)}, u32[]{:S(2)}) collective-permute-start(f32[8,128]{1,0:T(8,128)S(1)} %add.41), channel_id=1, source_target_pairs={{0,65},{1,64},{2,67},{3,66},{4,69},{5,68},{6,71},{7,70},{8,73},{9,... | collective-permute-start | bytes 12296 | tf_op jit(solution)/shard_map/ppermute | solution.py:25
  63.7 0.7 collective-permute-start.15
  64.4 2.0 %collective-permute-start.16 = (bf16[128,1152]{1,0:T(8,128)(2,1)S(1)}, bf16[128,1152]{1,0:T(8,128)(2,1)S(1)}, u32[]{:S(2)}, u32[]{:S(2)}) collective-permute-start(bf16[128,1152]{1,0:T(8,128)(2,1)S(1)} %get-tuple-element.110), channel_id=1, source_target_pairs={{0,6},{1,7},{2,4},{3,5},{4,2},{5,3},{6,0},{7,1},{8,56},{9,57},{10,... | collective-permute-start | bytes 884744 | tf_op jit(solution)/shard_map/ppermute | solution.py:25
  66.4 0.9 fusion.8
  67.3 3.1 %fusion.1 = (bf16[1024,1152]{1,0:T(8,128)(2,1)S(1)}, f32[1024,1152]{1,0:T(8,128)S(1)}) fusion(f32[1024,1152]{1,0:T(8,128)S(1)} %fusion.8, bf16[768,1024]{1,0:T(8,128)(2,1)S(1)} %get-tuple-element.112, bf16[768,1152]{1,0:T(8,128)(2,1)S(1)} %get-tuple-element.81.img_ref), kind=kOutput, calls=%fused_computation.5 | convolution fusion | flops 1822556160 | bytes 15138816 | tf_op jit(solution)/shard_map/dot_general | solution.py:419
  71.5 1.1 %far.1 = (bf16[256,1152]{1,0:T(8,128)(2,1)S(1)}, bf16[256,1152]{1,0:T(8,128)(2,1)S(1)}) custom-call(s32[1]{0:T(128)} %bitcast.core_ref.refs_0_, f32[768,1152]{1,0:T(8,128)S(1)} %get-tuple-element.142.txt_ref, f32[768,1152]{1,0:T(8,128)S(1)} %get-tuple-element.97.img_ref, ...), custom_call_target="tpu_custom_call" | custom-call | tf_op jit(solution)/shard_map/far/pallas_call | solution.py:277
  72.6 2.1 %collective-permute-start.20 = (bf16[1024,1152]{1,0:T(8,128)(2,1)S(1)}, bf16[1024,1152]{1,0:T(8,128)(2,1)S(1)}, u32[]{:S(2)}, u32[]{:S(2)}) collective-permute-start(bf16[1024,1152]{1,0:T(8,128)(2,1)S(1)} %get-tuple-element.121), channel_id=1, source_target_pairs={{0,8},{1,9},{2,10},{3,11},{4,12},{5,13},{6,14},{7,15},{8,0},{9,1},... | collective-permute-start | bytes 7077896 | tf_op jit(solution)/shard_map/ppermute | solution.py:25
  74.7 0.8 collective-permute-start.19
  76.2 2.2 %collective-permute-start.22 = (bf16[256,1152]{1,0:T(8,128)(2,1)S(1)}, bf16[256,1152]{1,0:T(8,128)(2,1)S(1)}, u32[]{:S(2)}, u32[]{:S(2)}) collective-permute-start(bf16[256,1152]{1,0:T(8,128)(2,1)S(1)} %get-tuple-element.126), channel_id=1, source_target_pairs={{0,6},{1,7},{2,4},{3,5},{4,2},{5,3},{6,0},{7,1},{8,56},{9,57},{10,... | collective-permute-start | bytes 1769480 | tf_op jit(solution)/shard_map/ppermute | solution.py:25
  78.9 1.5 %base.1.refs_1_.base_ref = f32[1024,1152]{1,0:T(8,128)S(1)} custom-call(s32[1]{0:T(128)} %bitcast.core_ref.refs_0_, f32[1024,1152]{1,0:T(8,128)S(1)} %get-tuple-element.144.txt_ref, bf16[1024,1152]{1,0:T(8,128)(2,1)S(1)} %collective-permute-done.20.received_ref, f32[768,1152]{1,0:T(8,128)S(1)} %get-tuple-element.97.img_ref, ...), custom_call_target="tpu_custom_call" | custom-call | tf_op jit(solution)/shard_map/base/pallas_call | solution.py:277
  80.6 2.8 %collective-permute-done.21 = f32[8,128]{1,0:T(8,128)S(1)} collective-permute-done((f32[8,128]{1,0:T(8,128)S(1)}, f32[8,128]{1,0:T(8,128)S(1)}, u32[]{:S(2)}, u32[]{:S(2)}) %collective-permute-start.21) | collective-permute-done | bytes 4128 | tf_op jit(solution)/shard_map/ppermute | solution.py:25
  83.7 0.8 near.5
  84.6 3.0 %collective-permute-start.26 = (bf16[256,1152]{1,0:T(8,128)(2,1)S(1)}, bf16[256,1152]{1,0:T(8,128)(2,1)S(1)}, u32[]{:S(2)}, u32[]{:S(2)}) collective-permute-start(bf16[256,1152]{1,0:T(8,128)(2,1)S(1)} %near.5), channel_id=1, source_target_pairs={{0,6},{1,7},{2,4},{3,5},{4,2},{5,3},{6,0},{7,1},{8,56},{9,57},{10,... | collective-permute-start | bytes 1769480 | tf_op jit(solution)/shard_map/ppermute | solution.py:25
  87.6 0.8 near.4
  88.5 0.8 near.3
  90.0 1.3 %collective-permute-start.27 = (f32[8,128]{1,0:T(8,128)S(1)}, f32[8,128]{1,0:T(8,128)S(1)}, u32[]{:S(2)}, u32[]{:S(2)}) collective-permute-start(f32[8,128]{1,0:T(8,128)S(1)} %add.44), channel_id=1, source_target_pairs={{0,6},{1,7},{2,4},{3,5},{4,2},{5,3},{6,0},{7,1},{8,14},{9,15},{10,... | collective-permute-start | bytes 12296 | tf_op jit(solution)/shard_map/ppermute | solution.py:25
  91.3 2.8 %collective-permute-done.27 = f32[8,128]{1,0:T(8,128)S(1)} collective-permute-done((f32[8,128]{1,0:T(8,128)S(1)}, f32[8,128]{1,0:T(8,128)S(1)}, u32[]{:S(2)}, u32[]{:S(2)}) %collective-permute-start.27) | collective-permute-done | bytes 4128 | tf_op jit(solution)/shard_map/ppermute | solution.py:25
  94.1 1.4 %collective-permute-start.28 = (f32[8,128]{1,0:T(8,128)S(1)}, f32[8,128]{1,0:T(8,128)S(1)}, u32[]{:S(2)}, u32[]{:S(2)}) collective-permute-start(f32[8,128]{1,0:T(8,128)S(1)} %add.45), channel_id=1, source_target_pairs={{0,16},{1,17},{2,18},{3,19},{4,20},{5,21},{6,22},{7,23},{8,24},{9,... | collective-permute-start | bytes 12296 | tf_op jit(solution)/shard_map/ppermute | solution.py:25
  95.6 2.0 %collective-permute-done.28 = f32[8,128]{1,0:T(8,128)S(1)} collective-permute-done((f32[8,128]{1,0:T(8,128)S(1)}, f32[8,128]{1,0:T(8,128)S(1)}, u32[]{:S(2)}, u32[]{:S(2)}) %collective-permute-start.28) | collective-permute-done | bytes 4128 | tf_op jit(solution)/shard_map/ppermute | solution.py:25
  97.6 1.8 %collective-permute-done.23.x_ref = bf16[256,1152]{1,0:T(8,128)(2,1)S(1)} collective-permute-done((bf16[256,1152]{1,0:T(8,128)(2,1)S(1)}, bf16[256,1152]{1,0:T(8,128)(2,1)S(1)}, u32[]{:S(2)}, u32[]{:S(2)}) %collective-permute-start.23) | collective-permute-done | bytes 589856 | tf_op jit(solution)/shard_map/ppermute | solution.py:25
  99.4 1.3 %gather_sums.1 = (f32[128,1152]{1,0:T(8,128)S(1)}, f32[128,1152]{1,0:T(8,128)S(1)}) custom-call(s32[1]{0:T(128)} %bitcast.core_ref.refs_0_, f32[1024,1152]{1,0:T(8,128)S(1)} %base.1.refs_1_.base_ref, bf16[256,1152]{1,0:T(8,128)(2,1)S(1)} %collective-permute-done.25.a_ref, bf16[256,1152]{1,0:T(8,128)(2,1)S(1)} %collective-permute-done.26.b_ref, ...), custom_call_target="tpu_custom_call" | custom-call | tf_op jit(solution)/shard_map/gather_sums/pallas_call | solution.py:277
  100.7 1.6 %collective-permute-start.29 = (f32[128,1152]{1,0:T(8,128)S(1)}, f32[128,1152]{1,0:T(8,128)S(1)}, u32[]{:S(2)}, u32[]{:S(2)}) collective-permute-start(f32[128,1152]{1,0:T(8,128)S(1)} %get-tuple-element.134), channel_id=1, source_target_pairs={{0,8},{1,9},{2,10},{3,11},{4,12},{5,13},{6,14},{7,15},{8,0},{9,1},... | collective-permute-start | bytes 1769480 | tf_op jit(solution)/shard_map/ppermute | solution.py:25
  102.3 2.9 %collective-permute-start.30 = (f32[8,128]{1,0:T(8,128)S(1)}, f32[8,128]{1,0:T(8,128)S(1)}, u32[]{:S(2)}, u32[]{:S(2)}) collective-permute-start(f32[8,128]{1,0:T(8,128)S(1)} %add.46), channel_id=1, source_target_pairs={{0,48},{1,49},{2,50},{3,51},{4,52},{5,53},{6,54},{7,55},{8,56},{9,... | collective-permute-start | bytes 12296 | tf_op jit(solution)/shard_map/ppermute | solution.py:25
  105.2 1.0 collective-permute-done.30
  106.2 2.0 %finish.1 = (f32[1,1]{1,0:T(1,128)}, f32[128,1152]{1,0:T(8,128)}, f32[128,1152]{1,0:T(8,128)}) custom-call(s32[1]{0:T(128)} %bitcast.core_ref.refs_0_, f32[128,1152]{1,0:T(8,128)S(1)} %copy-done.1, f32[128,1152]{1,0:T(8,128)S(1)} %copy-done.3, f32[128,1152]{1,0:T(8,128)S(1)} %get-tuple-element.133.refs_3_, f32[128,1152]{1,0:T(8,128)S(1)} %collective-permute-done.29.refs_4_, ...), custom_call_target="tpu_custom_call" | custom-call | tf_op jit(solution)/shard_map/finish/pallas_call | solution.py:277
  (57 shorter events, 7.7 us)
Async XLA Ops:
  0.6 1.1 copy-start
  1.7 1.1 copy-start.2
  3.3 2.7 %collective-permute-start = (bf16[128,1152]{1,0:T(8,128)(2,1)S(1)}, bf16[128,1152]{1,0:T(8,128)(2,1)S(1)}, u32[]{:S(2)}, u32[]{:S(2)}) collective-permute-start(bf16[128,1152]{1,0:T(8,128)(2,1)S(1)} %get-tuple-element.73), channel_id=1, source_target_pairs={{0,8},{1,9},{2,10},{3,11},{4,12},{5,13},{6,14},{7,15},{8,0},{9,1},... | collective-permute-start | bytes 884744 | tf_op jit(solution)/shard_map/ppermute | solution.py:25
  6.1 10.3 %collective-permute-start.1 = (bf16[256,1152]{1,0:T(8,128)(2,1)S(1)}, bf16[256,1152]{1,0:T(8,128)(2,1)S(1)}, u32[]{:S(2)}, u32[]{:S(2)}) collective-permute-start(bf16[256,1152]{1,0:T(8,128)(2,1)S(1)} %pack.4.refs_0_), channel_id=1, source_target_pairs={{0,1},{1,0},{2,3},{3,2},{4,5},{5,4},{6,7},{7,6},{8,73},{9,72},{10,... | collective-permute-start | bytes 1769480 | tf_op jit(solution)/shard_map/ppermute | solution.py:25
  8.7 9.2 %collective-permute-start.4 = (bf16[256,1152]{1,0:T(8,128)(2,1)S(1)}, bf16[256,1152]{1,0:T(8,128)(2,1)S(1)}, u32[]{:S(2)}, u32[]{:S(2)}) collective-permute-start(bf16[256,1152]{1,0:T(8,128)(2,1)S(1)} %pack.4.refs_0_), channel_id=1, source_target_pairs={{0,2},{1,3},{2,0},{3,1},{4,6},{5,7},{6,4},{7,5},{8,24},{9,25},{10,... | collective-permute-start | bytes 1769480 | tf_op jit(solution)/shard_map/ppermute | solution.py:25
  10.3 10.0 %collective-permute-start.7 = (bf16[256,1152]{1,0:T(8,128)(2,1)S(1)}, bf16[256,1152]{1,0:T(8,128)(2,1)S(1)}, u32[]{:S(2)}, u32[]{:S(2)}) collective-permute-start(bf16[256,1152]{1,0:T(8,128)(2,1)S(1)} %pack.4.refs_0_), channel_id=1, source_target_pairs={{0,6},{1,7},{2,4},{3,5},{4,2},{5,3},{6,0},{7,1},{8,56},{9,57},{10,... | collective-permute-start | bytes 1769480 | tf_op jit(solution)/shard_map/ppermute | solution.py:25
  20.5 17.5 %collective-permute-start.8 = (bf16[1024,1152]{1,0:T(8,128)(2,1)S(1)}, bf16[1024,1152]{1,0:T(8,128)(2,1)S(1)}, u32[]{:S(2)}, u32[]{:S(2)}) collective-permute-start(bf16[1024,1152]{1,0:T(8,128)(2,1)S(1)} %pack.5.near_ref), channel_id=1, source_target_pairs={{0,8},{1,9},{2,10},{3,11},{4,12},{5,13},{6,14},{7,15},{8,0},{9,1},... | collective-permute-start | bytes 7077896 | tf_op jit(solution)/shard_map/ppermute | solution.py:25
  21.0 11.0 %collective-permute-start.2 = (bf16[256,1152]{1,0:T(8,128)(2,1)S(1)}, bf16[256,1152]{1,0:T(8,128)(2,1)S(1)}, u32[]{:S(2)}, u32[]{:S(2)}) collective-permute-start(bf16[256,1152]{1,0:T(8,128)(2,1)S(1)} %collective-permute-done.1.refs_1_), channel_id=1, source_target_pairs={{0,6},{1,7},{2,4},{3,5},{4,2},{5,3},{6,0},{7,1},{8,56},{9,57},{10,... | collective-permute-start | bytes 1769480 | tf_op jit(solution)/shard_map/ppermute | solution.py:25
  24.8 9.9 %collective-permute-start.5 = (bf16[256,1152]{1,0:T(8,128)(2,1)S(1)}, bf16[256,1152]{1,0:T(8,128)(2,1)S(1)}, u32[]{:S(2)}, u32[]{:S(2)}) collective-permute-start(bf16[256,1152]{1,0:T(8,128)(2,1)S(1)} %collective-permute-done.4.refs_2_), channel_id=1, source_target_pairs={{0,1},{1,0},{2,3},{3,2},{4,5},{5,4},{6,7},{7,6},{8,73},{9,72},{10,... | collective-permute-start | bytes 1769480 | tf_op jit(solution)/shard_map/ppermute | solution.py:25
  26.6 8.7 %collective-permute-start.9 = (bf16[256,1152]{1,0:T(8,128)(2,1)S(1)}, bf16[256,1152]{1,0:T(8,128)(2,1)S(1)}, u32[]{:S(2)}, u32[]{:S(2)}) collective-permute-start(bf16[256,1152]{1,0:T(8,128)(2,1)S(1)} %collective-permute-done.7.refs_3_), channel_id=1, source_target_pairs={{0,2},{1,3},{2,0},{3,1},{4,6},{5,7},{6,4},{7,5},{8,24},{9,25},{10,... | collective-permute-start | bytes 1769480 | tf_op jit(solution)/shard_map/ppermute | solution.py:25
  35.5 8.9 %collective-permute-start.11 = (bf16[768,1152]{1,0:T(8,128)(2,1)S(1)}, bf16[768,1152]{1,0:T(8,128)(2,1)S(1)}, u32[]{:S(2)}, u32[]{:S(2)}) collective-permute-start(bf16[768,1152]{1,0:T(8,128)(2,1)S(1)} %pack.6.far_ref), channel_id=1, source_target_pairs={{0,8},{1,9},{2,10},{3,11},{4,12},{5,13},{6,14},{7,15},{8,0},{9,1},... | collective-permute-start | bytes 5308424 | tf_op jit(solution)/shard_map/ppermute | solution.py:25
  35.6 7.5 %collective-permute-start.3 = (bf16[128,1152]{1,0:T(8,128)(2,1)S(1)}, bf16[128,1152]{1,0:T(8,128)(2,1)S(1)}, u32[]{:S(2)}, u32[]{:S(2)}) collective-permute-start(bf16[128,1152]{1,0:T(8,128)(2,1)S(1)} %half_of.2), channel_id=1, source_target_pairs={{0,2},{1,3},{2,0},{3,1},{4,6},{5,7},{6,4},{7,5},{8,24},{9,25},{10,... | collective-permute-start | bytes 884744 | tf_op jit(solution)/shard_map/ppermute | solution.py:25
  35.7 7.4 %collective-permute-start.6 = (bf16[128,1152]{1,0:T(8,128)(2,1)S(1)}, bf16[128,1152]{1,0:T(8,128)(2,1)S(1)}, u32[]{:S(2)}, u32[]{:S(2)}) collective-permute-start(bf16[128,1152]{1,0:T(8,128)(2,1)S(1)} %half_of.3), channel_id=1, source_target_pairs={{0,6},{1,7},{2,4},{3,5},{4,2},{5,3},{6,0},{7,1},{8,56},{9,57},{10,... | collective-permute-start | bytes 884744 | tf_op jit(solution)/shard_map/ppermute | solution.py:25
  43.2 7.3 %collective-permute-start.10 = (bf16[256,1152]{1,0:T(8,128)(2,1)S(1)}, bf16[256,1152]{1,0:T(8,128)(2,1)S(1)}, u32[]{:S(2)}, u32[]{:S(2)}) collective-permute-start(bf16[256,1152]{1,0:T(8,128)(2,1)S(1)} %pack.7.last_ref), channel_id=1, source_target_pairs={{0,8},{1,9},{2,10},{3,11},{4,12},{5,13},{6,14},{7,15},{8,0},{9,1},... | collective-permute-start | bytes 1769480 | tf_op jit(solution)/shard_map/ppermute | solution.py:25
  54.6 2.7 %collective-permute-start.13 = (f32[8,128]{1,0:T(8,128)S(1)}, f32[8,128]{1,0:T(8,128)S(1)}, u32[]{:S(2)}, u32[]{:S(2)}) collective-permute-start(f32[8,128]{1,0:T(8,128)S(1)} %add_add_fusion), channel_id=1, source_target_pairs={{0,8},{1,9},{2,10},{3,11},{4,12},{5,13},{6,14},{7,15},{8,0},{9,1},... | collective-permute-start | bytes 12296 | tf_op jit(solution)/shard_map/ppermute | solution.py:25
  56.7 3.6 %collective-permute-start.12 = (bf16[256,1152]{1,0:T(8,128)(2,1)S(1)}, bf16[256,1152]{1,0:T(8,128)(2,1)S(1)}, u32[]{:S(2)}, u32[]{:S(2)}) collective-permute-start(bf16[256,1152]{1,0:T(8,128)(2,1)S(1)} %get-tuple-element.96), channel_id=1, source_target_pairs={{0,8},{1,9},{2,10},{3,11},{4,12},{5,13},{6,14},{7,15},{8,0},{9,1},... | collective-permute-start | bytes 1769480 | tf_op jit(solution)/shard_map/ppermute | solution.py:25
  57.3 3.0 %collective-permute-start.14 = (f32[8,128]{1,0:T(8,128)S(1)}, f32[8,128]{1,0:T(8,128)S(1)}, u32[]{:S(2)}, u32[]{:S(2)}) collective-permute-start(f32[8,128]{1,0:T(8,128)S(1)} %add.40), channel_id=1, source_target_pairs={{0,1},{1,0},{2,3},{3,2},{4,5},{5,4},{6,7},{7,6},{8,9},{9,8},{10,11... | collective-permute-start | bytes 12296 | tf_op jit(solution)/shard_map/ppermute | solution.py:25
  60.5 9.8 %collective-permute-start.17 = (bf16[768,1152]{1,0:T(8,128)(2,1)S(1)}, bf16[768,1152]{1,0:T(8,128)(2,1)S(1)}, u32[]{:S(2)}, u32[]{:S(2)}) collective-permute-start(bf16[768,1152]{1,0:T(8,128)(2,1)S(1)} %get-tuple-element.111), channel_id=1, source_target_pairs={{0,8},{1,9},{2,10},{3,11},{4,12},{5,13},{6,14},{7,15},{8,0},{9,1},... | collective-permute-start | bytes 5308424 | tf_op jit(solution)/shard_map/ppermute | solution.py:25
  62.1 8.2 %collective-permute-start.18 = (f32[8,128]{1,0:T(8,128)S(1)}, f32[8,128]{1,0:T(8,128)S(1)}, u32[]{:S(2)}, u32[]{:S(2)}) collective-permute-start(f32[8,128]{1,0:T(8,128)S(1)} %add.41), channel_id=1, source_target_pairs={{0,65},{1,64},{2,67},{3,66},{4,69},{5,68},{6,71},{7,70},{8,73},{9,... | collective-permute-start | bytes 12296 | tf_op jit(solution)/shard_map/ppermute | solution.py:25
  63.7 7.2 %collective-permute-start.15 = (bf16[128,1152]{1,0:T(8,128)(2,1)S(1)}, bf16[128,1152]{1,0:T(8,128)(2,1)S(1)}, u32[]{:S(2)}, u32[]{:S(2)}) collective-permute-start(bf16[128,1152]{1,0:T(8,128)(2,1)S(1)} %get-tuple-element.109), channel_id=1, source_target_pairs={{0,2},{1,3},{2,0},{3,1},{4,6},{5,7},{6,4},{7,5},{8,24},{9,25},{10,... | collective-permute-start | bytes 884744 | tf_op jit(solution)/shard_map/ppermute | solution.py:25
  64.4 7.1 %collective-permute-start.16 = (bf16[128,1152]{1,0:T(8,128)(2,1)S(1)}, bf16[128,1152]{1,0:T(8,128)(2,1)S(1)}, u32[]{:S(2)}, u32[]{:S(2)}) collective-permute-start(bf16[128,1152]{1,0:T(8,128)(2,1)S(1)} %get-tuple-element.110), channel_id=1, source_target_pairs={{0,6},{1,7},{2,4},{3,5},{4,2},{5,3},{6,0},{7,1},{8,56},{9,57},{10,... | collective-permute-start | bytes 884744 | tf_op jit(solution)/shard_map/ppermute | solution.py:25
  72.6 6.3 %collective-permute-start.20 = (bf16[1024,1152]{1,0:T(8,128)(2,1)S(1)}, bf16[1024,1152]{1,0:T(8,128)(2,1)S(1)}, u32[]{:S(2)}, u32[]{:S(2)}) collective-permute-start(bf16[1024,1152]{1,0:T(8,128)(2,1)S(1)} %get-tuple-element.121), channel_id=1, source_target_pairs={{0,8},{1,9},{2,10},{3,11},{4,12},{5,13},{6,14},{7,15},{8,0},{9,1},... | collective-permute-start | bytes 7077896 | tf_op jit(solution)/shard_map/ppermute | solution.py:25
  74.7 9.0 %collective-permute-start.19 = (bf16[256,1152]{1,0:T(8,128)(2,1)S(1)}, bf16[256,1152]{1,0:T(8,128)(2,1)S(1)}, u32[]{:S(2)}, u32[]{:S(2)}) collective-permute-start(bf16[256,1152]{1,0:T(8,128)(2,1)S(1)} %second.1), channel_id=1, source_target_pairs={{0,2},{1,3},{2,0},{3,1},{4,6},{5,7},{6,4},{7,5},{8,24},{9,25},{10,... | collective-permute-start | bytes 1769480 | tf_op jit(solution)/shard_map/ppermute | solution.py:25
  75.5 12.1 %collective-permute-start.24 = (bf16[256,1152]{1,0:T(8,128)(2,1)S(1)}, bf16[256,1152]{1,0:T(8,128)(2,1)S(1)}, u32[]{:S(2)}, u32[]{:S(2)}) collective-permute-start(bf16[256,1152]{1,0:T(8,128)(2,1)S(1)} %get-tuple-element.127), channel_id=1, source_target_pairs={{0,1},{1,0},{2,3},{3,2},{4,5},{5,4},{6,7},{7,6},{8,73},{9,72},{10,... | collective-permute-start | bytes 1769480 | tf_op jit(solution)/shard_map/ppermute | solution.py:25
  76.2 12.3 %collective-permute-start.22 = (bf16[256,1152]{1,0:T(8,128)(2,1)S(1)}, bf16[256,1152]{1,0:T(8,128)(2,1)S(1)}, u32[]{:S(2)}, u32[]{:S(2)}) collective-permute-start(bf16[256,1152]{1,0:T(8,128)(2,1)S(1)} %get-tuple-element.126), channel_id=1, source_target_pairs={{0,6},{1,7},{2,4},{3,5},{4,2},{5,3},{6,0},{7,1},{8,56},{9,57},{10,... | collective-permute-start | bytes 1769480 | tf_op jit(solution)/shard_map/ppermute | solution.py:25
  80.4 2.9 %collective-permute-start.21 = (f32[8,128]{1,0:T(8,128)S(1)}, f32[8,128]{1,0:T(8,128)S(1)}, u32[]{:S(2)}, u32[]{:S(2)}) collective-permute-start(f32[8,128]{1,0:T(8,128)S(1)} %add.43), channel_id=1, source_target_pairs={{0,2},{1,3},{2,0},{3,1},{4,6},{5,7},{6,4},{7,5},{8,10},{9,11},{10,... | collective-permute-start | bytes 12296 | tf_op jit(solution)/shard_map/ppermute | solution.py:25
  84.6 13.0 %collective-permute-start.26 = (bf16[256,1152]{1,0:T(8,128)(2,1)S(1)}, bf16[256,1152]{1,0:T(8,128)(2,1)S(1)}, u32[]{:S(2)}, u32[]{:S(2)}) collective-permute-start(bf16[256,1152]{1,0:T(8,128)(2,1)S(1)} %near.5), channel_id=1, source_target_pairs={{0,6},{1,7},{2,4},{3,5},{4,2},{5,3},{6,0},{7,1},{8,56},{9,57},{10,... | collective-permute-start | bytes 1769480 | tf_op jit(solution)/shard_map/ppermute | solution.py:25
  88.4 9.2 %collective-permute-start.25 = (bf16[256,1152]{1,0:T(8,128)(2,1)S(1)}, bf16[256,1152]{1,0:T(8,128)(2,1)S(1)}, u32[]{:S(2)}, u32[]{:S(2)}) collective-permute-start(bf16[256,1152]{1,0:T(8,128)(2,1)S(1)} %near.4), channel_id=1, source_target_pairs={{0,2},{1,3},{2,0},{3,1},{4,6},{5,7},{6,4},{7,5},{8,24},{9,25},{10,... | collective-permute-start | bytes 1769480 | tf_op jit(solution)/shard_map/ppermute | solution.py:25
  89.4 10.0 %collective-permute-start.23 = (bf16[256,1152]{1,0:T(8,128)(2,1)S(1)}, bf16[256,1152]{1,0:T(8,128)(2,1)S(1)}, u32[]{:S(2)}, u32[]{:S(2)}) collective-permute-start(bf16[256,1152]{1,0:T(8,128)(2,1)S(1)} %near.3), channel_id=1, source_target_pairs={{0,1},{1,0},{2,3},{3,2},{4,5},{5,4},{6,7},{7,6},{8,73},{9,72},{10,... | collective-permute-start | bytes 1769480 | tf_op jit(solution)/shard_map/ppermute | solution.py:25
  90.0 4.1 %collective-permute-start.27 = (f32[8,128]{1,0:T(8,128)S(1)}, f32[8,128]{1,0:T(8,128)S(1)}, u32[]{:S(2)}, u32[]{:S(2)}) collective-permute-start(f32[8,128]{1,0:T(8,128)S(1)} %add.44), channel_id=1, source_target_pairs={{0,6},{1,7},{2,4},{3,5},{4,2},{5,3},{6,0},{7,1},{8,14},{9,15},{10,... | collective-permute-start | bytes 12296 | tf_op jit(solution)/shard_map/ppermute | solution.py:25
  94.1 3.4 %collective-permute-start.28 = (f32[8,128]{1,0:T(8,128)S(1)}, f32[8,128]{1,0:T(8,128)S(1)}, u32[]{:S(2)}, u32[]{:S(2)}) collective-permute-start(f32[8,128]{1,0:T(8,128)S(1)} %add.45), channel_id=1, source_target_pairs={{0,16},{1,17},{2,18},{3,19},{4,20},{5,21},{6,22},{7,23},{8,24},{9,... | collective-permute-start | bytes 12296 | tf_op jit(solution)/shard_map/ppermute | solution.py:25
  97.6 8.6 %copy-start.1 = (f32[128,1152]{1,0:T(8,128)S(1)}, f32[128,1152]{1,0:T(8,128)}, u32[]{:S(2)}) copy-start(f32[128,1152]{1,0:T(8,128)} %refs_1_.1) | copy-start | bytes 1769476
  97.6 8.7 %copy-start.3 = (f32[128,1152]{1,0:T(8,128)S(1)}, f32[128,1152]{1,0:T(8,128)}, u32[]{:S(2)}) copy-start(f32[128,1152]{1,0:T(8,128)} %refs_2_.1) | copy-start | bytes 1769476
  100.7 5.5 %collective-permute-start.29 = (f32[128,1152]{1,0:T(8,128)S(1)}, f32[128,1152]{1,0:T(8,128)S(1)}, u32[]{:S(2)}, u32[]{:S(2)}) collective-permute-start(f32[128,1152]{1,0:T(8,128)S(1)} %get-tuple-element.134), channel_id=1, source_target_pairs={{0,8},{1,9},{2,10},{3,11},{4,12},{5,13},{6,14},{7,15},{8,0},{9,1},... | collective-permute-start | bytes 1769480 | tf_op jit(solution)/shard_map/ppermute | solution.py:25
  102.3 3.9 %collective-permute-start.30 = (f32[8,128]{1,0:T(8,128)S(1)}, f32[8,128]{1,0:T(8,128)S(1)}, u32[]{:S(2)}, u32[]{:S(2)}) collective-permute-start(f32[8,128]{1,0:T(8,128)S(1)} %add.46), channel_id=1, source_target_pairs={{0,48},{1,49},{2,50},{3,51},{4,52},{5,53},{6,54},{7,55},{8,56},{9,... | collective-permute-start | bytes 12296 | tf_op jit(solution)/shard_map/ppermute | solution.py:25
where the time goes:
time: 108 us
  starting transfers between devices  41.6 us (39%)
  waiting for transfers between devices  28.3 us (26%)
  Pallas kernels  25.5 us (24%)
  matrix products  8.42 us (8%)
  between operations  2.25 us (2%)
  local copies, waits for them, and re-layouts  2.13 us (2%)
    ppermute x31, starting transfers between devices, exchange(): return lax.ppermute(x, AXES, pairs)  41.6 us
    ppermute x31, waiting for transfers between devices, exchange(): return lax.ppermute(x, AXES, pairs)  28.3 us
    pallas_call x3, Pallas kernels, tile_call(): pl.pallas_call(kernel, out_shape=outs, in_specs=[SMEM] + [VMEM] * (len(sc...  15.3 us
    pallas_call x9, Pallas kernels, small_call(): pl.pallas_call(kernel, out_shape=outs, in_specs=[SMEM] + [VMEM] * len(arr...  9.22 us
    dot_general x6, matrix products, transposed_product(): lax.dot_general(weights, img, (((0,), (0,)), ((), ())), preferred_element...  8.42 us
  transfers between devices with their start and end apart: 31, of which 15 were waited for; matrix products, arithmetic and copies ran while one was open for 8% of the time, Pallas kernels for 15%

commit v1 on v0

--- a/solution.py
+++ b/solution.py
@@ -202,55 +202,40 @@
     loss_ref[...] = run_tiles(pair, sharp_ref, bias_ref, jobs)
 
 
-def far_tile_kernel(
-    core_ref, sharp_ref, bias_ref, far_ref, received_ref, near_txt_ref, img_ref, before_ref,
-    txt_ref, second_ref, weights_ref, part_ref, near_half_ref, far_half_ref, part_half_ref, loss_ref,
-):
+def far_tile_kernel(core_ref, sharp_ref, bias_ref, far_ref, received_ref, img_ref, before_ref, txt_ref, weights_ref, part_ref, loss_ref):
     pair = far_ref.shape[0] // 3
-    half = pair // 2
 
     def work(is_first):
         txt_ref[...] = far_ref[...] if is_first else received_ref[...]
-        second_ref[...] = received_ref[:half] if is_first else far_ref[half:pair]
 
     by_core(core_ref, work)
     jobs = []
     for k, rows in enumerate(row_blocks(img_ref, pair)):
         span = pl.ds(k * pair, pair)
         jobs.append((rows, [(txt_ref, weights_ref.at[span])], before_ref.at[span], part_ref.at[span], None))
-    blocks = [(near_txt_ref, near_half_ref), (txt_ref, far_half_ref)]
-    jobs.append((second_ref, blocks, None, part_half_ref, None))
     loss_ref[...] = run_tiles(pair, sharp_ref, bias_ref, jobs)
 
 
 def last_tile_kernel(
-    core_ref, sharp_ref, bias_ref, last_ref, received_ref, near_txt_ref, far_txt_ref,
-    img_ref, second_ref, before_ref, before_half_ref, near_half_ref, far_half_ref,
+    core_ref, sharp_ref, bias_ref, last_ref, received_ref, far_ref, far_received_ref, near_txt_ref, far_txt_ref,
+    img_ref, before_ref,
     weights_ref, part_ref, img_tail_ref, near_tail_ref, far_tail_ref, last_tail_ref, part_tail_ref, loss_ref, txt_ref,
 ):
     pair = last_ref.shape[0]
     half = pair // 2
-    low, high = pl.ds(0, half), pl.ds(half, half)
 
     def work(is_first):
         txt_ref[...] = last_ref[...] if is_first else received_ref[...]
-        img_tail_ref[high] = received_ref[low] if is_first else last_ref[high]
-
-    by_core(core_ref, work)
-    img_tail_ref[low] = second_ref[...]
-    near_tail_ref[low] = near_half_ref[...]
-    far_tail_ref[low] = far_half_ref[...]
+        img_tail_ref[:half] = far_received_ref[:half] if is_first else far_ref[half:pair]
+        img_tail_ref[half:] = received_ref[:half] if is_first else last_ref[half:]
+
+    by_core(core_ref, work)
     jobs = []
     for k, rows in enumerate(row_blocks(img_ref, pair)):
         span = pl.ds(k * pair, pair)
         jobs.append((rows, [(txt_ref, weights_ref.at[span])], before_ref.at[span], part_ref.at[span], None))
-    jobs.append((second_ref, [(txt_ref, last_tail_ref.at[low])], before_half_ref, part_tail_ref.at[low], None))
-    blocks = [
-        (near_txt_ref, near_tail_ref.at[high]),
-        (far_txt_ref, far_tail_ref.at[high]),
-        (txt_ref, last_tail_ref.at[high]),
-    ]
-    jobs.append((img_tail_ref.at[high], blocks, None, part_tail_ref.at[high], None))
+    blocks = [(near_txt_ref, near_tail_ref), (far_txt_ref, far_tail_ref), (txt_ref, last_tail_ref)]
+    jobs.append((img_tail_ref, blocks, None, part_tail_ref, None))
     loss_ref[...] = run_tiles(pair, sharp_ref, bias_ref, jobs)
 
 
@@ -383,8 +368,10 @@
     each_chunk(pair, rows)
 
 
-def gather_sums_kernel(core_ref, base_ref, a_ref, b_ref, x_ref, keep_ref, give_ref):
+def gather_sums_kernel(core_ref, base_ref, a_ref, b_ref, x_ref, loss_ref, keep_ref, give_ref):
     own = keep_ref.shape[0]
+    give_ref[own:] = jnp.zeros((8, give_ref.shape[1]), jnp.float32)
+    give_ref[own:, :128] = loss_ref[...]
 
     def rows(at):
         for start, ref in ((0, keep_ref), (own, give_ref)):
@@ -396,7 +383,9 @@
 
 
 def finish_kernel(batch, core_ref, img_ref, txt_ref, kept_ref, received_ref, loss_parts_ref, loss_ref, grad_img_ref, grad_txt_ref):
-    loss_ref[...] = jnp.full((1, 1), jnp.sum(loss_parts_ref[...]) * (1.0 / batch), jnp.float32)
+    own = kept_ref.shape[0]
+    both = loss_parts_ref[...] + received_ref[own:, :128]
+    loss_ref[...] = jnp.full((1, 1), jnp.sum(both) * (1.0 / batch), jnp.float32)
 
     def side(at, raw_ref, sum_ref, grad_ref):
         raw = raw_ref[at()]
@@ -410,7 +399,7 @@
             side(at, img_ref, received_ref if is_first else kept_ref, grad_img_ref)
             side(at, txt_ref, kept_ref if is_first else received_ref, grad_txt_ref)
 
-        each_chunk(kept_ref.shape[0], rows)
+        each_chunk(own, rows)
 
     by_core(core_ref, work)
 
@@ -467,29 +456,20 @@
     last_a, last_b, part = lax.optimization_barrier((last_a, last_b, part))
     last = pack(last_a, last_b)
     last_received = swap(last)
-    far_txt, second, far_weights, part, near_half, far_half, part_half, far_loss = tile_call(
+    far_txt, far_weights, part, far_loss = tile_call(
         far_tile_kernel,
         "tile_far",
-        three * three + own * (wide + three),
+        three * three,
         scalars,
-        (far, far_received, near_txt, img, part),
-        (
-            array(three, jnp.bfloat16),
-            low_half,
-            array(three, jnp.bfloat16, three),
-            array(three, jnp.float32),
-            array(own, jnp.bfloat16, wide),
-            array(own, jnp.bfloat16, three),
-            array(own, jnp.float32),
-            losses,
-        ),
+        (far, far_received, img, part),
+        (array(three, jnp.bfloat16), array(three, jnp.bfloat16, three), array(three, jnp.float32), losses),
     )
     last_weights, img_part, img_tail, near_tail, far_tail, last_tail, img_part_tail, last_loss = tile_call(
         last_tile_kernel,
         "tile_last",
-        (three + own) * pair + own * 2 * wide,
+        three * pair + pair * 2 * wide,
         scalars,
-        (last, last_received, near_txt, far_txt, img, second, part, part_half, near_half, far_half),
+        (last, last_received, far, far_received, near_txt, far_txt, img, part),
         (
             array(three, jnp.bfloat16, pair),
             array(three, jnp.float32),
@@ -507,14 +487,14 @@
     def text_sums(weights, tail):
         return transposed_product(weights, img) + transposed_product(tail, img_tail)
 
-    loss = loss + swap(loss)
+    loss = loss + swap(loss, 0, 1)
     opposite_part = text_sums(last_weights, last_tail)
     sent = encode(jnp.where(on_first, img_part_tail, opposite_part), ONE_CHIP)
-    sent, far_weights, far_tail = lax.optimization_barrier((sent, far_weights, far_tail))
+    sent, far_weights, far_tail, loss = lax.optimization_barrier((sent, far_weights, far_tail, loss))
     tail_received = swap(sent)
     far_part = text_sums(far_weights, far_tail)
     sent = encode(jnp.where(on_first, img_part, far_part), ONE_CHIP)
-    loss = loss + swap(loss, 0, 1)
+    loss = loss + swap(loss, 8, 1)
     tail_received, sent, loss = lax.optimization_barrier((tail_received, sent, loss))
 
     a, b = small_call(
@@ -525,7 +505,7 @@
     rest_received = swap(sent)
     near_part = text_sums(near_weights, near_tail)
     sent = encode(near_part, ONE_CHIP)
-    loss = loss + swap(loss, 8, 1)
+    loss = loss + swap(loss, 0, 2)
     (second,) = small_call(
         second_kernel, "second", core, (far_part, rest_received, img_part_tail, tail_received), (low_piece,)
     )
@@ -542,7 +522,7 @@
         base_kernel, "base", core, (near_part, near_received, img_part, rest_received), (array(wide, jnp.float32),)
     )
     base, loss = lax.optimization_barrier((base, loss))
-    loss = loss + swap(loss, 0, 2)
+    loss = loss + swap(loss, 0, 6)
     second_received, base, loss = lax.optimization_barrier((second_received, base, loss))
 
     def near_slot(k, received):
@@ -556,12 +536,14 @@
         move(near_slot(1, from_b), "x"),
         move(near_slot(2, from_x), "a"),
     )
-    loss = loss + swap(loss, 0, 6)
     loss = loss + swap(loss, 2, 0)
-    from_x, from_a, from_b, loss = lax.optimization_barrier((from_x, from_a, from_b, loss))
     loss = loss + swap(loss, 6, 0)
     keep, give = small_call(
-        gather_sums_kernel, "gather_sums", core, (base, from_a, from_b, from_x), (array(own, jnp.float32),) * 2
+        gather_sums_kernel,
+        "gather_sums",
+        core,
+        (base, from_a, from_b, from_x, loss),
+        (array(own, jnp.float32), array(own + 8, jnp.float32)),
     )
     grad = array(own, jnp.float32)
     loss_value, grad_image, grad_text = small_call(

time: 108 us -> 108 us (level)
  Pallas kernels: 25.5 us -> 23.9 us
    pallas_call x3, Pallas kernels: 15.3 us -> 13.7 us  [tile_call(): pl.pallas_call(kernel, out_shape=outs, in_specs=[SMEM] + [VMEM] * (len(sc...]
    ppermute x31 -> x30, starting transfers between devices: 41.6 us -> 42.4 us  [exchange(): return lax.ppermute(x, AXES, pairs)]
    ppermute x31 -> x30, waiting for transfers between devices: 28.3 us -> 28.3 us  [exchange(): return lax.ppermute(x, AXES, pairs)]
  transfers between devices with their start and end apart: 31 -> 30, of which waited for: 15 -> 16; matrix products, arithmetic and copies ran while one was open for 8% -> 8% of each run, Pallas kernels for 15% -> 13%
where the time goes in v1:
time: 108 us; the launch traced here: 107 us
  starting transfers between devices  42.4 us (39%)
  waiting for transfers between devices  28.3 us (26%)
  Pallas kernels  23.9 us (22%)
  matrix products  8.43 us (8%)
  between operations  2.2 us (2%)
  local copies, waits for them, and re-layouts  2.13 us (2%)
    ppermute x30, starting transfers between devices, exchange(): return lax.ppermute(x, AXES, pairs)  42.4 us
    ppermute x30, waiting for transfers between devices, exchange(): return lax.ppermute(x, AXES, pairs)  28.3 us
    pallas_call x3, Pallas kernels, tile_call(): pl.pallas_call(kernel, out_shape=outs, in_specs=[SMEM] + [VMEM] * (len(sc...  13.7 us
    pallas_call x9, Pallas kernels, small_call(): pl.pallas_call(kernel, out_shape=outs, in_specs=[SMEM] + [VMEM] * len(arr...  9.2 us
    dot_general x6, matrix products, transposed_product(): lax.dot_general(weights, img, (((0,), (0,)), ((), ())), preferred_element...  8.43 us
  transfers between devices with their start and end apart: 30, of which 16 were waited for; matrix products, arithmetic and copies ran while one was open for 8% of the time, Pallas kernels for 13%

profile of v1, /device:TPU:1, one launch (start us, length us, event | category | flops | bytes accessed | tf_op | source)
XLA Modules:
  0.0 107.4 jit_solution(8809724954445518687)
XLA Ops:
  0.6 1.1 copy-done
  1.7 1.1 copy-done.2
  3.3 1.5 %collective-permute-start = (bf16[128,1152]{1,0:T(8,128)(2,1)S(1)}, bf16[128,1152]{1,0:T(8,128)(2,1)S(1)}, u32[]{:S(2)}, u32[]{:S(2)}) collective-permute-start(bf16[128,1152]{1,0:T(8,128)(2,1)S(1)} %get-tuple-element.66), channel_id=1, source_target_pairs={{0,8},{1,9},{2,10},{3,11},{4,12},{5,13},{6,14},{7,15},{8,0},{9,1},... | collective-permute-start | bytes 884744 | tf_op jit(solution)/shard_map/ppermute | solution.py:25
  4.8 1.2 %collective-permute-done.refs_1_ = bf16[128,1152]{1,0:T(8,128)(2,1)S(1)} collective-permute-done((bf16[128,1152]{1,0:T(8,128)(2,1)S(1)}, bf16[128,1152]{1,0:T(8,128)(2,1)S(1)}, u32[]{:S(2)}, u32[]{:S(2)}) %collective-permute-start) | collective-permute-done | bytes 294944 | tf_op jit(solution)/shard_map/ppermute | solution.py:25
  6.1 3.9 %collective-permute-start.7 = (bf16[256,1152]{1,0:T(8,128)(2,1)S(1)}, bf16[256,1152]{1,0:T(8,128)(2,1)S(1)}, u32[]{:S(2)}, u32[]{:S(2)}) collective-permute-start(bf16[256,1152]{1,0:T(8,128)(2,1)S(1)} %pack.4.refs_0_), channel_id=1, source_target_pairs={{0,6},{1,7},{2,4},{3,5},{4,2},{5,3},{6,0},{7,1},{8,56},{9,57},{10,... | collective-permute-start | bytes 1769480 | tf_op jit(solution)/shard_map/ppermute | solution.py:25
  10.0 2.5 %collective-permute-start.1 = (bf16[256,1152]{1,0:T(8,128)(2,1)S(1)}, bf16[256,1152]{1,0:T(8,128)(2,1)S(1)}, u32[]{:S(2)}, u32[]{:S(2)}) collective-permute-start(bf16[256,1152]{1,0:T(8,128)(2,1)S(1)} %pack.4.refs_0_), channel_id=1, source_target_pairs={{0,1},{1,0},{2,3},{3,2},{4,5},{5,4},{6,7},{7,6},{8,73},{9,72},{10,... | collective-permute-start | bytes 1769480 | tf_op jit(solution)/shard_map/ppermute | solution.py:25
  12.5 4.8 %collective-permute-done.7.refs_3_ = bf16[256,1152]{1,0:T(8,128)(2,1)S(1)} collective-permute-done((bf16[256,1152]{1,0:T(8,128)(2,1)S(1)}, bf16[256,1152]{1,0:T(8,128)(2,1)S(1)}, u32[]{:S(2)}, u32[]{:S(2)}) %collective-permute-start.7) | collective-permute-done | bytes 589856 | tf_op jit(solution)/shard_map/ppermute | solution.py:25
  17.3 1.8 %collective-permute-done.4.refs_2_ = bf16[256,1152]{1,0:T(8,128)(2,1)S(1)} collective-permute-done((bf16[256,1152]{1,0:T(8,128)(2,1)S(1)}, bf16[256,1152]{1,0:T(8,128)(2,1)S(1)}, u32[]{:S(2)}, u32[]{:S(2)}) %collective-permute-start.4) | collective-permute-done | bytes 589856 | tf_op jit(solution)/shard_map/ppermute | solution.py:25
  19.0 0.9 collective-permute-done.1.refs_1_
  20.2 3.4 %collective-permute-start.2 = (bf16[256,1152]{1,0:T(8,128)(2,1)S(1)}, bf16[256,1152]{1,0:T(8,128)(2,1)S(1)}, u32[]{:S(2)}, u32[]{:S(2)}) collective-permute-start(bf16[256,1152]{1,0:T(8,128)(2,1)S(1)} %collective-permute-done.1.refs_1_), channel_id=1, source_target_pairs={{0,6},{1,7},{2,4},{3,5},{4,2},{5,3},{6,0},{7,1},{8,56},{9,57},{10,... | collective-permute-start | bytes 1769480 | tf_op jit(solution)/shard_map/ppermute | solution.py:25
  23.7 2.5 %collective-permute-start.5 = (bf16[256,1152]{1,0:T(8,128)(2,1)S(1)}, bf16[256,1152]{1,0:T(8,128)(2,1)S(1)}, u32[]{:S(2)}, u32[]{:S(2)}) collective-permute-start(bf16[256,1152]{1,0:T(8,128)(2,1)S(1)} %collective-permute-done.4.refs_2_), channel_id=1, source_target_pairs={{0,1},{1,0},{2,3},{3,2},{4,5},{5,4},{6,7},{7,6},{8,73},{9,72},{10,... | collective-permute-start | bytes 1769480 | tf_op jit(solution)/shard_map/ppermute | solution.py:25
  27.4 3.8 %collective-permute-done.2.refs_0_.refs_2_ = bf16[256,1152]{1,0:T(8,128)(2,1)S(1)} collective-permute-done((bf16[256,1152]{1,0:T(8,128)(2,1)S(1)}, bf16[256,1152]{1,0:T(8,128)(2,1)S(1)}, u32[]{:S(2)}, u32[]{:S(2)}) %collective-permute-start.2) | collective-permute-done | bytes 589856 | tf_op jit(solution)/shard_map/ppermute | solution.py:25
  31.2 1.5 %collective-permute-done.9.refs_0_ = bf16[256,1152]{1,0:T(8,128)(2,1)S(1)} collective-permute-done((bf16[256,1152]{1,0:T(8,128)(2,1)S(1)}, bf16[256,1152]{1,0:T(8,128)(2,1)S(1)}, u32[]{:S(2)}, u32[]{:S(2)}) %collective-permute-start.9) | collective-permute-done | bytes 589856 | tf_op jit(solution)/shard_map/ppermute | solution.py:25
  32.7 0.9 collective-permute-done.5.refs_0_.refs_1_
  34.0 2.0 %collective-permute-start.6 = (bf16[128,1152]{1,0:T(8,128)(2,1)S(1)}, bf16[128,1152]{1,0:T(8,128)(2,1)S(1)}, u32[]{:S(2)}, u32[]{:S(2)}) collective-permute-start(bf16[128,1152]{1,0:T(8,128)(2,1)S(1)} %half_of.3), channel_id=1, source_target_pairs={{0,6},{1,7},{2,4},{3,5},{4,2},{5,3},{6,0},{7,1},{8,56},{9,57},{10,... | collective-permute-start | bytes 884744 | tf_op jit(solution)/shard_map/ppermute | solution.py:25
  36.0 5.1 %tile_near.1 = (bf16[768,1152]{1,0:T(8,128)(2,1)S(1)}, bf16[1024,1152]{1,0:T(8,128)(2,1)S(1)}, bf16[768,1024]{1,0:T(8,128)(2,1)S(1)}, f32[768,1152]{1,0:T(8,128)S(1)}, f32[8,128]{1,0:T(8,128)S(1)}) custom-call(s32[1]{0:T(128)} %bitcast.core_ref.refs_0_, f32[8,128]{1,0:T(8,128)S(1)} %broadcast_in_dim.15.sharp_ref, f32[8,128]{1,0:T(8,128)S(1)} %broadcast_in_dim.17.bias_ref, ...), custom_call_target="tpu_custom_call" | custom-call | flops 3623878656 | bytes 6488064 | tf_op jit(solution)/shard_map/tile_near/pallas_call | solution.py:244
  42.5 3.9 %tile_far.1 = (bf16[768,1152]{1,0:T(8,128)(2,1)S(1)}, bf16[768,768]{1,0:T(8,128)(2,1)S(1)}, f32[768,1152]{1,0:T(8,128)S(1)}, f32[8,128]{1,0:T(8,128)S(1)}) custom-call(s32[1]{0:T(128)} %bitcast.core_ref.refs_0_, f32[8,128]{1,0:T(8,128)S(1)} %broadcast_in_dim.15.sharp_ref, f32[8,128]{1,0:T(8,128)S(1)} %broadcast_in_dim.17.bias_ref, ...), custom_call_target="tpu_custom_call" | custom-call | flops 2717908992 | bytes 7077888 | tf_op jit(solution)/shard_map/tile_far/pallas_call | solution.py:244
  46.5 4.7 %tile_last.1 = (bf16[768,256]{1,0:T(8,128)(2,1)S(1)}, f32[768,1152]{1,0:T(8,128)S(1)}, bf16[256,1152]{1,0:T(8,128)(2,1)S(1)}, bf16[256,1024]{1,0:T(8,128)(2,1)S(...) custom-call(s32[1]{0:T(128)} %bitcast.core_ref.refs_0_, ...), custom_call_target="tpu_custom_call" | custom-call | flops 3321888768 | bytes 12386304 | tf_op jit(solution)/shard_map/tile_last/pallas_call | solution.py:244
  52.1 0.9 fusion.5
  53.8 2.5 %collective-permute-start.14 = (f32[8,128]{1,0:T(8,128)S(1)}, f32[8,128]{1,0:T(8,128)S(1)}, u32[]{:S(2)}, u32[]{:S(2)}) collective-permute-start(f32[8,128]{1,0:T(8,128)S(1)} %add.36), channel_id=1, source_target_pairs={{0,65},{1,64},{2,67},{3,66},{4,69},{5,68},{6,71},{7,70},{8,73},{9,... | collective-permute-start | bytes 12296 | tf_op jit(solution)/shard_map/ppermute | solution.py:25
  56.2 1.5 %collective-permute-start.13 = (bf16[256,1152]{1,0:T(8,128)(2,1)S(1)}, bf16[256,1152]{1,0:T(8,128)(2,1)S(1)}, u32[]{:S(2)}, u32[]{:S(2)}) collective-permute-start(bf16[256,1152]{1,0:T(8,128)(2,1)S(1)} %get-tuple-element.88), channel_id=1, source_target_pairs={{0,8},{1,9},{2,10},{3,11},{4,12},{5,13},{6,14},{7,15},{8,0},{9,1},... | collective-permute-start | bytes 1769480 | tf_op jit(solution)/shard_map/ppermute | solution.py:25
  58.4 2.5 %fusion.3 = (bf16[768,1152]{1,0:T(8,128)(2,1)S(1)}, f32[768,1152]{1,0:T(8,128)S(1)}) fusion(f32[768,1152]{1,0:T(8,128)S(1)} %get-tuple-element.89.img_ref, pred[]{:T(512)S(6)} %eq.3, f32[768,1152]{1,0:T(8,128)S(1)} %fusion.7, bf16[768,768]{1,0:T(8,128)(2,1)S(1)} %get-tuple-element.90, bf16[768,1152]{1,0:T(8,128)(2,1)S(1)} %get-tuple-element.74.img_ref), kind=kOutput, calls=%fused_computation.9 | convolution fusion | flops 1367801856 | bytes 15335425 | tf_op jit(solution)/shard_map/dot_general | solution.py:408
  61.2 0.9 collective-permute-start.17
  62.7 1.3 %collective-permute-start.15 = (bf16[128,1152]{1,0:T(8,128)(2,1)S(1)}, bf16[128,1152]{1,0:T(8,128)(2,1)S(1)}, u32[]{:S(2)}, u32[]{:S(2)}) collective-permute-start(bf16[128,1152]{1,0:T(8,128)(2,1)S(1)} %get-tuple-element.99), channel_id=1, source_target_pairs={{0,2},{1,3},{2,0},{3,1},{4,6},{5,7},{6,4},{7,5},{8,24},{9,25},{10,... | collective-permute-start | bytes 884744 | tf_op jit(solution)/shard_map/ppermute | solution.py:25
  64.0 1.2 %collective-permute-start.16 = (bf16[128,1152]{1,0:T(8,128)(2,1)S(1)}, bf16[128,1152]{1,0:T(8,128)(2,1)S(1)}, u32[]{:S(2)}, u32[]{:S(2)}) collective-permute-start(bf16[128,1152]{1,0:T(8,128)(2,1)S(1)} %get-tuple-element.100), channel_id=1, source_target_pairs={{0,6},{1,7},{2,4},{3,5},{4,2},{5,3},{6,0},{7,1},{8,56},{9,57},{10,... | collective-permute-start | bytes 884744 | tf_op jit(solution)/shard_map/ppermute | solution.py:25
  65.2 0.9 fusion.8
  66.1 3.1 %fusion.1 = (bf16[1024,1152]{1,0:T(8,128)(2,1)S(1)}, f32[1024,1152]{1,0:T(8,128)S(1)}) fusion(f32[1024,1152]{1,0:T(8,128)S(1)} %fusion.8, bf16[768,1024]{1,0:T(8,128)(2,1)S(1)} %get-tuple-element.102, bf16[768,1152]{1,0:T(8,128)(2,1)S(1)} %get-tuple-element.74.img_ref), kind=kOutput, calls=%fused_computation.5 | convolution fusion | flops 1822556160 | bytes 15138816 | tf_op jit(solution)/shard_map/dot_general | solution.py:408
  69.7 1.4 %collective-permute-done.16.from_b_ref = bf16[128,1152]{1,0:T(8,128)(2,1)S(1)} collective-permute-done((bf16[128,1152]{1,0:T(8,128)(2,1)S(1)}, bf16[128,1152]{1,0:T(8,128)(2,1)S(1)}, u32[]{:S(2)}, u32[]{:S(2)}) %collective-permute-start.16) | collective-permute-done | bytes 294944 | tf_op jit(solution)/shard_map/ppermute | solution.py:25
  71.1 1.1 %far.1 = (bf16[256,1152]{1,0:T(8,128)(2,1)S(1)}, bf16[256,1152]{1,0:T(8,128)(2,1)S(1)}) custom-call(s32[1]{0:T(128)} %bitcast.core_ref.refs_0_, f32[768,1152]{1,0:T(8,128)S(1)} %get-tuple-element.128.txt_ref, f32[768,1152]{1,0:T(8,128)S(1)} %get-tuple-element.89.img_ref, ...), custom_call_target="tpu_custom_call" | custom-call | tf_op jit(solution)/shard_map/far/pallas_call | solution.py:262
  72.2 2.2 %collective-permute-start.20 = (bf16[1024,1152]{1,0:T(8,128)(2,1)S(1)}, bf16[1024,1152]{1,0:T(8,128)(2,1)S(1)}, u32[]{:S(2)}, u32[]{:S(2)}) collective-permute-start(bf16[1024,1152]{1,0:T(8,128)(2,1)S(1)} %get-tuple-element.111), channel_id=1, source_target_pairs={{0,8},{1,9},{2,10},{3,11},{4,12},{5,13},{6,14},{7,15},{8,0},{9,1},... | collective-permute-start | bytes 7077896 | tf_op jit(solution)/shard_map/ppermute | solution.py:25
  74.4 1.5 %collective-permute-start.19 = (bf16[256,1152]{1,0:T(8,128)(2,1)S(1)}, bf16[256,1152]{1,0:T(8,128)(2,1)S(1)}, u32[]{:S(2)}, u32[]{:S(2)}) collective-permute-start(bf16[256,1152]{1,0:T(8,128)(2,1)S(1)} %second.1), channel_id=1, source_target_pairs={{0,2},{1,3},{2,0},{3,1},{4,6},{5,7},{6,4},{7,5},{8,24},{9,25},{10,... | collective-permute-start | bytes 1769480 | tf_op jit(solution)/shard_map/ppermute | solution.py:25
  75.9 1.3 %collective-permute-start.22 = (bf16[256,1152]{1,0:T(8,128)(2,1)S(1)}, bf16[256,1152]{1,0:T(8,128)(2,1)S(1)}, u32[]{:S(2)}, u32[]{:S(2)}) collective-permute-start(bf16[256,1152]{1,0:T(8,128)(2,1)S(1)} %get-tuple-element.116), channel_id=1, source_target_pairs={{0,1},{1,0},{2,3},{3,2},{4,5},{5,4},{6,7},{7,6},{8,73},{9,72},{10,... | collective-permute-start | bytes 1769480 | tf_op jit(solution)/shard_map/ppermute | solution.py:25
  77.2 1.5 %collective-permute-start.25 = (bf16[256,1152]{1,0:T(8,128)(2,1)S(1)}, bf16[256,1152]{1,0:T(8,128)(2,1)S(1)}, u32[]{:S(2)}, u32[]{:S(2)}) collective-permute-start(bf16[256,1152]{1,0:T(8,128)(2,1)S(1)} %get-tuple-element.118), channel_id=1, source_target_pairs={{0,6},{1,7},{2,4},{3,5},{4,2},{5,3},{6,0},{7,1},{8,56},{9,57},{10,... | collective-permute-start | bytes 1769480 | tf_op jit(solution)/shard_map/ppermute | solution.py:25
  78.7 1.5 %base.1.refs_1_.base_ref = f32[1024,1152]{1,0:T(8,128)S(1)} custom-call(s32[1]{0:T(128)} %bitcast.core_ref.refs_0_, f32[1024,1152]{1,0:T(8,128)S(1)} %get-tuple-element.130.txt_ref, bf16[1024,1152]{1,0:T(8,128)(2,1)S(1)} %collective-permute-done.20.received_ref, f32[768,1152]{1,0:T(8,128)S(1)} %get-tuple-element.89.img_ref, ...), custom_call_target="tpu_custom_call" | custom-call | tf_op jit(solution)/shard_map/base/pallas_call | solution.py:262
  80.2 1.9 %collective-permute-start.21 = (f32[8,128]{1,0:T(8,128)S(1)}, f32[8,128]{1,0:T(8,128)S(1)}, u32[]{:S(2)}, u32[]{:S(2)}) collective-permute-start(f32[8,128]{1,0:T(8,128)S(1)} %add.40), channel_id=1, source_target_pairs={{0,6},{1,7},{2,4},{3,5},{4,2},{5,3},{6,0},{7,1},{8,14},{9,15},{10,... | collective-permute-start | bytes 12296 | tf_op jit(solution)/shard_map/ppermute | solution.py:25
  82.1 2.3 %collective-permute-done.21 = f32[8,128]{1,0:T(8,128)S(1)} collective-permute-done((f32[8,128]{1,0:T(8,128)S(1)}, f32[8,128]{1,0:T(8,128)S(1)}, u32[]{:S(2)}, u32[]{:S(2)}) %collective-permute-start.21) | collective-permute-done | bytes 4128 | tf_op jit(solution)/shard_map/ppermute | solution.py:25
  84.4 0.8 near.4
  85.8 0.8 near.3
  86.7 0.8 collective-permute-start.23
  88.4 1.4 %collective-permute-start.26 = (bf16[256,1152]{1,0:T(8,128)(2,1)S(1)}, bf16[256,1152]{1,0:T(8,128)(2,1)S(1)}, u32[]{:S(2)}, u32[]{:S(2)}) collective-permute-start(bf16[256,1152]{1,0:T(8,128)(2,1)S(1)} %near.5), channel_id=1, source_target_pairs={{0,1},{1,0},{2,3},{3,2},{4,5},{5,4},{6,7},{7,6},{8,73},{9,72},{10,... | collective-permute-start | bytes 1769480 | tf_op jit(solution)/shard_map/ppermute | solution.py:25
  89.7 2.1 %collective-permute-start.24 = (bf16[256,1152]{1,0:T(8,128)(2,1)S(1)}, bf16[256,1152]{1,0:T(8,128)(2,1)S(1)}, u32[]{:S(2)}, u32[]{:S(2)}) collective-permute-start(bf16[256,1152]{1,0:T(8,128)(2,1)S(1)} %near.4), channel_id=1, source_target_pairs={{0,6},{1,7},{2,4},{3,5},{4,2},{5,3},{6,0},{7,1},{8,56},{9,57},{10,... | collective-permute-start | bytes 1769480 | tf_op jit(solution)/shard_map/ppermute | solution.py:25
  92.0 3.9 %collective-permute-done.27 = f32[8,128]{1,0:T(8,128)S(1)} collective-permute-done((f32[8,128]{1,0:T(8,128)S(1)}, f32[8,128]{1,0:T(8,128)S(1)}, u32[]{:S(2)}, u32[]{:S(2)}) %collective-permute-start.27) | collective-permute-done | bytes 4128 | tf_op jit(solution)/shard_map/ppermute | solution.py:25
  95.8 2.1 %collective-permute-start.28 = (f32[8,128]{1,0:T(8,128)S(1)}, f32[8,128]{1,0:T(8,128)S(1)}, u32[]{:S(2)}, u32[]{:S(2)}) collective-permute-start(f32[8,128]{1,0:T(8,128)S(1)} %add.42), channel_id=1, source_target_pairs={{0,48},{1,49},{2,50},{3,51},{4,52},{5,53},{6,54},{7,55},{8,56},{9,... | collective-permute-start | bytes 12296 | tf_op jit(solution)/shard_map/ppermute | solution.py:25
  98.0 2.0 %collective-permute-done.28 = f32[8,128]{1,0:T(8,128)S(1)} collective-permute-done((f32[8,128]{1,0:T(8,128)S(1)}, f32[8,128]{1,0:T(8,128)S(1)}, u32[]{:S(2)}, u32[]{:S(2)}) %collective-permute-start.28) | collective-permute-done | bytes 4128 | tf_op jit(solution)/shard_map/ppermute | solution.py:25
  100.0 1.3 %gather_sums.1 = (f32[128,1152]{1,0:T(8,128)S(1)}, f32[136,1152]{1,0:T(8,128)S(1)}) custom-call(s32[1]{0:T(128)} %bitcast.core_ref.refs_0_, f32[1024,1152]{1,0:T(8,128)S(1)} %base.1.refs_1_.base_ref, bf16[256,1152]{1,0:T(8,128)(2,1)S(1)} %collective-permute-done.23.a_ref, bf16[256,1152]{1,0:T(8,128)(2,1)S(1)} %collective-permute-done.24.b_ref, ...), custom_call_target="tpu_custom_call" | custom-call | tf_op jit(solution)/shard_map/gather_sums/pallas_call | solution.py:262
  101.4 2.4 %collective-permute-start.29 = (f32[136,1152]{1,0:T(8,128)S(1)}, f32[136,1152]{1,0:T(8,128)S(1)}, u32[]{:S(2)}, u32[]{:S(2)}) collective-permute-start(f32[136,1152]{1,0:T(8,128)S(1)} %get-tuple-element.121), channel_id=1, source_target_pairs={{0,8},{1,9},{2,10},{3,11},{4,12},{5,13},{6,14},{7,15},{8,0},{9,1},... | collective-permute-start | bytes 1880072 | tf_op jit(solution)/shard_map/ppermute | solution.py:25
  103.7 1.7 %collective-permute-done.29.refs_4_ = f32[136,1152]{1,0:T(8,128)S(1)} collective-permute-done((f32[136,1152]{1,0:T(8,128)S(1)}, f32[136,1152]{1,0:T(8,128)S(1)}, u32[]{:S(2)}, u32[]{:S(2)}) %collective-permute-start.29) | collective-permute-done | bytes 626720 | tf_op jit(solution)/shard_map/ppermute | solution.py:25
  105.4 2.0 %finish.1 = (f32[1,1]{1,0:T(1,128)}, f32[128,1152]{1,0:T(8,128)}, f32[128,1152]{1,0:T(8,128)}) custom-call(s32[1]{0:T(128)} %bitcast.core_ref.refs_0_, f32[128,1152]{1,0:T(8,128)S(1)} %copy-done.1, f32[128,1152]{1,0:T(8,128)S(1)} %copy-done.3, f32[128,1152]{1,0:T(8,128)S(1)} %get-tuple-element.120.refs_3_, f32[136,1152]{1,0:T(8,128)S(1)} %collective-permute-done.29.refs_4_, ...), custom_call_target="tpu_custom_call" | custom-call | tf_op jit(solution)/shard_map/finish/pallas_call | solution.py:262
  (54 shorter events, 8.1 us)
Async XLA Ops:
  0.6 1.1 copy-start
  1.7 1.1 copy-start.2
  3.3 2.7 %collective-permute-start = (bf16[128,1152]{1,0:T(8,128)(2,1)S(1)}, bf16[128,1152]{1,0:T(8,128)(2,1)S(1)}, u32[]{:S(2)}, u32[]{:S(2)}) collective-permute-start(bf16[128,1152]{1,0:T(8,128)(2,1)S(1)} %get-tuple-element.66), channel_id=1, source_target_pairs={{0,8},{1,9},{2,10},{3,11},{4,12},{5,13},{6,14},{7,15},{8,0},{9,1},... | collective-permute-start | bytes 884744 | tf_op jit(solution)/shard_map/ppermute | solution.py:25
  6.1 11.2 %collective-permute-start.7 = (bf16[256,1152]{1,0:T(8,128)(2,1)S(1)}, bf16[256,1152]{1,0:T(8,128)(2,1)S(1)}, u32[]{:S(2)}, u32[]{:S(2)}) collective-permute-start(bf16[256,1152]{1,0:T(8,128)(2,1)S(1)} %pack.4.refs_0_), channel_id=1, source_target_pairs={{0,6},{1,7},{2,4},{3,5},{4,2},{5,3},{6,0},{7,1},{8,56},{9,57},{10,... | collective-permute-start | bytes 1769480 | tf_op jit(solution)/shard_map/ppermute | solution.py:25
  10.0 9.0 %collective-permute-start.4 = (bf16[256,1152]{1,0:T(8,128)(2,1)S(1)}, bf16[256,1152]{1,0:T(8,128)(2,1)S(1)}, u32[]{:S(2)}, u32[]{:S(2)}) collective-permute-start(bf16[256,1152]{1,0:T(8,128)(2,1)S(1)} %pack.4.refs_0_), channel_id=1, source_target_pairs={{0,2},{1,3},{2,0},{3,1},{4,6},{5,7},{6,4},{7,5},{8,24},{9,25},{10,... | collective-permute-start | bytes 1769480 | tf_op jit(solution)/shard_map/ppermute | solution.py:25
  10.0 9.9 %collective-permute-start.1 = (bf16[256,1152]{1,0:T(8,128)(2,1)S(1)}, bf16[256,1152]{1,0:T(8,128)(2,1)S(1)}, u32[]{:S(2)}, u32[]{:S(2)}) collective-permute-start(bf16[256,1152]{1,0:T(8,128)(2,1)S(1)} %pack.4.refs_0_), channel_id=1, source_target_pairs={{0,1},{1,0},{2,3},{3,2},{4,5},{5,4},{6,7},{7,6},{8,73},{9,72},{10,... | collective-permute-start | bytes 1769480 | tf_op jit(solution)/shard_map/ppermute | solution.py:25
  20.1 15.9 %collective-permute-start.8 = (bf16[1024,1152]{1,0:T(8,128)(2,1)S(1)}, bf16[1024,1152]{1,0:T(8,128)(2,1)S(1)}, u32[]{:S(2)}, u32[]{:S(2)}) collective-permute-start(bf16[1024,1152]{1,0:T(8,128)(2,1)S(1)} %pack.5.near_ref), channel_id=1, source_target_pairs={{0,8},{1,9},{2,10},{3,11},{4,12},{5,13},{6,14},{7,15},{8,0},{9,1},... | collective-permute-start | bytes 7077896 | tf_op jit(solution)/shard_map/ppermute | solution.py:25
  20.2 11.0 %collective-permute-start.2 = (bf16[256,1152]{1,0:T(8,128)(2,1)S(1)}, bf16[256,1152]{1,0:T(8,128)(2,1)S(1)}, u32[]{:S(2)}, u32[]{:S(2)}) collective-permute-start(bf16[256,1152]{1,0:T(8,128)(2,1)S(1)} %collective-permute-done.1.refs_1_), channel_id=1, source_target_pairs={{0,6},{1,7},{2,4},{3,5},{4,2},{5,3},{6,0},{7,1},{8,56},{9,57},{10,... | collective-permute-start | bytes 1769480 | tf_op jit(solution)/shard_map/ppermute | solution.py:25
  23.7 9.0 %collective-permute-start.9 = (bf16[256,1152]{1,0:T(8,128)(2,1)S(1)}, bf16[256,1152]{1,0:T(8,128)(2,1)S(1)}, u32[]{:S(2)}, u32[]{:S(2)}) collective-permute-start(bf16[256,1152]{1,0:T(8,128)(2,1)S(1)} %collective-permute-done.7.refs_3_), channel_id=1, source_target_pairs={{0,2},{1,3},{2,0},{3,1},{4,6},{5,7},{6,4},{7,5},{8,24},{9,25},{10,... | collective-permute-start | bytes 1769480 | tf_op jit(solution)/shard_map/ppermute | solution.py:25
  23.7 9.9 %collective-permute-start.5 = (bf16[256,1152]{1,0:T(8,128)(2,1)S(1)}, bf16[256,1152]{1,0:T(8,128)(2,1)S(1)}, u32[]{:S(2)}, u32[]{:S(2)}) collective-permute-start(bf16[256,1152]{1,0:T(8,128)(2,1)S(1)} %collective-permute-done.4.refs_2_), channel_id=1, source_target_pairs={{0,1},{1,0},{2,3},{3,2},{4,5},{5,4},{6,7},{7,6},{8,73},{9,72},{10,... | collective-permute-start | bytes 1769480 | tf_op jit(solution)/shard_map/ppermute | solution.py:25
  33.7 8.8 %collective-permute-start.11 = (bf16[768,1152]{1,0:T(8,128)(2,1)S(1)}, bf16[768,1152]{1,0:T(8,128)(2,1)S(1)}, u32[]{:S(2)}, u32[]{:S(2)}) collective-permute-start(bf16[768,1152]{1,0:T(8,128)(2,1)S(1)} %pack.6.far_ref), channel_id=1, source_target_pairs={{0,8},{1,9},{2,10},{3,11},{4,12},{5,13},{6,14},{7,15},{8,0},{9,1},... | collective-permute-start | bytes 5308424 | tf_op jit(solution)/shard_map/ppermute | solution.py:25
  34.0 7.2 %collective-permute-start.6 = (bf16[128,1152]{1,0:T(8,128)(2,1)S(1)}, bf16[128,1152]{1,0:T(8,128)(2,1)S(1)}, u32[]{:S(2)}, u32[]{:S(2)}) collective-permute-start(bf16[128,1152]{1,0:T(8,128)(2,1)S(1)} %half_of.3), channel_id=1, source_target_pairs={{0,6},{1,7},{2,4},{3,5},{4,2},{5,3},{6,0},{7,1},{8,56},{9,57},{10,... | collective-permute-start | bytes 884744 | tf_op jit(solution)/shard_map/ppermute | solution.py:25
  36.0 5.9 %collective-permute-start.3 = (bf16[128,1152]{1,0:T(8,128)(2,1)S(1)}, bf16[128,1152]{1,0:T(8,128)(2,1)S(1)}, u32[]{:S(2)}, u32[]{:S(2)}) collective-permute-start(bf16[128,1152]{1,0:T(8,128)(2,1)S(1)} %half_of.2), channel_id=1, source_target_pairs={{0,2},{1,3},{2,0},{3,1},{4,6},{5,7},{6,4},{7,5},{8,24},{9,25},{10,... | collective-permute-start | bytes 884744 | tf_op jit(solution)/shard_map/ppermute | solution.py:25
  41.9 4.6 %collective-permute-start.10 = (bf16[256,1152]{1,0:T(8,128)(2,1)S(1)}, bf16[256,1152]{1,0:T(8,128)(2,1)S(1)}, u32[]{:S(2)}, u32[]{:S(2)}) collective-permute-start(bf16[256,1152]{1,0:T(8,128)(2,1)S(1)} %pack.7.last_ref), channel_id=1, source_target_pairs={{0,8},{1,9},{2,10},{3,11},{4,12},{5,13},{6,14},{7,15},{8,0},{9,1},... | collective-permute-start | bytes 1769480 | tf_op jit(solution)/shard_map/ppermute | solution.py:25
  51.2 2.5 %collective-permute-start.12 = (f32[8,128]{1,0:T(8,128)S(1)}, f32[8,128]{1,0:T(8,128)S(1)}, u32[]{:S(2)}, u32[]{:S(2)}) collective-permute-start(f32[8,128]{1,0:T(8,128)S(1)} %add_add_fusion), channel_id=1, source_target_pairs={{0,1},{1,0},{2,3},{3,2},{4,5},{5,4},{6,7},{7,6},{8,9},{9,8},{10,11... | collective-permute-start | bytes 12296 | tf_op jit(solution)/shard_map/ppermute | solution.py:25
  53.8 7.2 %collective-permute-start.14 = (f32[8,128]{1,0:T(8,128)S(1)}, f32[8,128]{1,0:T(8,128)S(1)}, u32[]{:S(2)}, u32[]{:S(2)}) collective-permute-start(f32[8,128]{1,0:T(8,128)S(1)} %add.36), channel_id=1, source_target_pairs={{0,65},{1,64},{2,67},{3,66},{4,69},{5,68},{6,71},{7,70},{8,73},{9,... | collective-permute-start | bytes 12296 | tf_op jit(solution)/shard_map/ppermute | solution.py:25
  56.2 4.7 %collective-permute-start.13 = (bf16[256,1152]{1,0:T(8,128)(2,1)S(1)}, bf16[256,1152]{1,0:T(8,128)(2,1)S(1)}, u32[]{:S(2)}, u32[]{:S(2)}) collective-permute-start(bf16[256,1152]{1,0:T(8,128)(2,1)S(1)} %get-tuple-element.88), channel_id=1, source_target_pairs={{0,8},{1,9},{2,10},{3,11},{4,12},{5,13},{6,14},{7,15},{8,0},{9,1},... | collective-permute-start | bytes 1769480 | tf_op jit(solution)/shard_map/ppermute | solution.py:25
  61.2 8.0 %collective-permute-start.17 = (bf16[768,1152]{1,0:T(8,128)(2,1)S(1)}, bf16[768,1152]{1,0:T(8,128)(2,1)S(1)}, u32[]{:S(2)}, u32[]{:S(2)}) collective-permute-start(bf16[768,1152]{1,0:T(8,128)(2,1)S(1)} %get-tuple-element.101), channel_id=1, source_target_pairs={{0,8},{1,9},{2,10},{3,11},{4,12},{5,13},{6,14},{7,15},{8,0},{9,1},... | collective-permute-start | bytes 5308424 | tf_op jit(solution)/shard_map/ppermute | solution.py:25
  62.1 7.1 %collective-permute-start.18 = (f32[8,128]{1,0:T(8,128)S(1)}, f32[8,128]{1,0:T(8,128)S(1)}, u32[]{:S(2)}, u32[]{:S(2)}) collective-permute-start(f32[8,128]{1,0:T(8,128)S(1)} %add.38), channel_id=1, source_target_pairs={{0,2},{1,3},{2,0},{3,1},{4,6},{5,7},{6,4},{7,5},{8,10},{9,11},{10,... | collective-permute-start | bytes 12296 | tf_op jit(solution)/shard_map/ppermute | solution.py:25
  62.7 7.0 %collective-permute-start.15 = (bf16[128,1152]{1,0:T(8,128)(2,1)S(1)}, bf16[128,1152]{1,0:T(8,128)(2,1)S(1)}, u32[]{:S(2)}, u32[]{:S(2)}) collective-permute-start(bf16[128,1152]{1,0:T(8,128)(2,1)S(1)} %get-tuple-element.99), channel_id=1, source_target_pairs={{0,2},{1,3},{2,0},{3,1},{4,6},{5,7},{6,4},{7,5},{8,24},{9,25},{10,... | collective-permute-start | bytes 884744 | tf_op jit(solution)/shard_map/ppermute | solution.py:25
  64.0 7.1 %collective-permute-start.16 = (bf16[128,1152]{1,0:T(8,128)(2,1)S(1)}, bf16[128,1152]{1,0:T(8,128)(2,1)S(1)}, u32[]{:S(2)}, u32[]{:S(2)}) collective-permute-start(bf16[128,1152]{1,0:T(8,128)(2,1)S(1)} %get-tuple-element.100), channel_id=1, source_target_pairs={{0,6},{1,7},{2,4},{3,5},{4,2},{5,3},{6,0},{7,1},{8,56},{9,57},{10,... | collective-permute-start | bytes 884744 | tf_op jit(solution)/shard_map/ppermute | solution.py:25
  72.2 6.4 %collective-permute-start.20 = (bf16[1024,1152]{1,0:T(8,128)(2,1)S(1)}, bf16[1024,1152]{1,0:T(8,128)(2,1)S(1)}, u32[]{:S(2)}, u32[]{:S(2)}) collective-permute-start(bf16[1024,1152]{1,0:T(8,128)(2,1)S(1)} %get-tuple-element.111), channel_id=1, source_target_pairs={{0,8},{1,9},{2,10},{3,11},{4,12},{5,13},{6,14},{7,15},{8,0},{9,1},... | collective-permute-start | bytes 7077896 | tf_op jit(solution)/shard_map/ppermute | solution.py:25
  74.4 9.9 %collective-permute-start.19 = (bf16[256,1152]{1,0:T(8,128)(2,1)S(1)}, bf16[256,1152]{1,0:T(8,128)(2,1)S(1)}, u32[]{:S(2)}, u32[]{:S(2)}) collective-permute-start(bf16[256,1152]{1,0:T(8,128)(2,1)S(1)} %second.1), channel_id=1, source_target_pairs={{0,2},{1,3},{2,0},{3,1},{4,6},{5,7},{6,4},{7,5},{8,24},{9,25},{10,... | collective-permute-start | bytes 1769480 | tf_op jit(solution)/shard_map/ppermute | solution.py:25
  75.9 9.9 %collective-permute-start.22 = (bf16[256,1152]{1,0:T(8,128)(2,1)S(1)}, bf16[256,1152]{1,0:T(8,128)(2,1)S(1)}, u32[]{:S(2)}, u32[]{:S(2)}) collective-permute-start(bf16[256,1152]{1,0:T(8,128)(2,1)S(1)} %get-tuple-element.116), channel_id=1, source_target_pairs={{0,1},{1,0},{2,3},{3,2},{4,5},{5,4},{6,7},{7,6},{8,73},{9,72},{10,... | collective-permute-start | bytes 1769480 | tf_op jit(solution)/shard_map/ppermute | solution.py:25
  77.2 10.3 %collective-permute-start.25 = (bf16[256,1152]{1,0:T(8,128)(2,1)S(1)}, bf16[256,1152]{1,0:T(8,128)(2,1)S(1)}, u32[]{:S(2)}, u32[]{:S(2)}) collective-permute-start(bf16[256,1152]{1,0:T(8,128)(2,1)S(1)} %get-tuple-element.118), channel_id=1, source_target_pairs={{0,6},{1,7},{2,4},{3,5},{4,2},{5,3},{6,0},{7,1},{8,56},{9,57},{10,... | collective-permute-start | bytes 1769480 | tf_op jit(solution)/shard_map/ppermute | solution.py:25
  80.2 4.1 %collective-permute-start.21 = (f32[8,128]{1,0:T(8,128)S(1)}, f32[8,128]{1,0:T(8,128)S(1)}, u32[]{:S(2)}, u32[]{:S(2)}) collective-permute-start(f32[8,128]{1,0:T(8,128)S(1)} %add.40), channel_id=1, source_target_pairs={{0,6},{1,7},{2,4},{3,5},{4,2},{5,3},{6,0},{7,1},{8,14},{9,15},{10,... | collective-permute-start | bytes 12296 | tf_op jit(solution)/shard_map/ppermute | solution.py:25
  86.7 13.3 %collective-permute-start.23 = (bf16[256,1152]{1,0:T(8,128)(2,1)S(1)}, bf16[256,1152]{1,0:T(8,128)(2,1)S(1)}, u32[]{:S(2)}, u32[]{:S(2)}) collective-permute-start(bf16[256,1152]{1,0:T(8,128)(2,1)S(1)} %near.3), channel_id=1, source_target_pairs={{0,2},{1,3},{2,0},{3,1},{4,6},{5,7},{6,4},{7,5},{8,24},{9,25},{10,... | collective-permute-start | bytes 1769480 | tf_op jit(solution)/shard_map/ppermute | solution.py:25
  88.4 11.7 %collective-permute-start.26 = (bf16[256,1152]{1,0:T(8,128)(2,1)S(1)}, bf16[256,1152]{1,0:T(8,128)(2,1)S(1)}, u32[]{:S(2)}, u32[]{:S(2)}) collective-permute-start(bf16[256,1152]{1,0:T(8,128)(2,1)S(1)} %near.5), channel_id=1, source_target_pairs={{0,1},{1,0},{2,3},{3,2},{4,5},{5,4},{6,7},{7,6},{8,73},{9,72},{10,... | collective-permute-start | bytes 1769480 | tf_op jit(solution)/shard_map/ppermute | solution.py:25
  89.7 10.3 %collective-permute-start.24 = (bf16[256,1152]{1,0:T(8,128)(2,1)S(1)}, bf16[256,1152]{1,0:T(8,128)(2,1)S(1)}, u32[]{:S(2)}, u32[]{:S(2)}) collective-permute-start(bf16[256,1152]{1,0:T(8,128)(2,1)S(1)} %near.4), channel_id=1, source_target_pairs={{0,6},{1,7},{2,4},{3,5},{4,2},{5,3},{6,0},{7,1},{8,56},{9,57},{10,... | collective-permute-start | bytes 1769480 | tf_op jit(solution)/shard_map/ppermute | solution.py:25
  91.8 4.0 %collective-permute-start.27 = (f32[8,128]{1,0:T(8,128)S(1)}, f32[8,128]{1,0:T(8,128)S(1)}, u32[]{:S(2)}, u32[]{:S(2)}) collective-permute-start(f32[8,128]{1,0:T(8,128)S(1)} %add.41), channel_id=1, source_target_pairs={{0,16},{1,17},{2,18},{3,19},{4,20},{5,21},{6,22},{7,23},{8,24},{9,... | collective-permute-start | bytes 12296 | tf_op jit(solution)/shard_map/ppermute | solution.py:25
  95.8 4.2 %collective-permute-start.28 = (f32[8,128]{1,0:T(8,128)S(1)}, f32[8,128]{1,0:T(8,128)S(1)}, u32[]{:S(2)}, u32[]{:S(2)}) collective-permute-start(f32[8,128]{1,0:T(8,128)S(1)} %add.42), channel_id=1, source_target_pairs={{0,48},{1,49},{2,50},{3,51},{4,52},{5,53},{6,54},{7,55},{8,56},{9,... | collective-permute-start | bytes 12296 | tf_op jit(solution)/shard_map/ppermute | solution.py:25
  100.0 5.4 %copy-start.1 = (f32[128,1152]{1,0:T(8,128)S(1)}, f32[128,1152]{1,0:T(8,128)}, u32[]{:S(2)}) copy-start(f32[128,1152]{1,0:T(8,128)} %refs_1_.1) | copy-start | bytes 1769476
  100.0 5.4 %copy-start.3 = (f32[128,1152]{1,0:T(8,128)S(1)}, f32[128,1152]{1,0:T(8,128)}, u32[]{:S(2)}) copy-start(f32[128,1152]{1,0:T(8,128)} %refs_2_.1) | copy-start | bytes 1769476
  101.4 4.1 %collective-permute-start.29 = (f32[136,1152]{1,0:T(8,128)S(1)}, f32[136,1152]{1,0:T(8,128)S(1)}, u32[]{:S(2)}, u32[]{:S(2)}) collective-permute-start(f32[136,1152]{1,0:T(8,128)S(1)} %get-tuple-element.121), channel_id=1, source_target_pairs={{0,8},{1,9},{2,10},{3,11},{4,12},{5,13},{6,14},{7,15},{8,0},{9,1},... | collective-permute-start | bytes 1880072 | tf_op jit(solution)/shard_map/ppermute | solution.py:25

commit v2 on v1

--- a/solution.py
+++ b/solution.py
@@ -42,7 +42,7 @@
 
 def decode(e, shift):
     f = e.astype(jnp.float32)
-    size = jnp.exp2(jnp.log2(jnp.maximum(jnp.abs(f), TINY)) * 0.125)
+    size = jnp.exp(jnp.log(jnp.maximum(jnp.abs(f), TINY)) * 0.125)
     return jnp.where(f < 0.0, -size, size) * (1.0 / shift)
 
 
@@ -181,17 +181,13 @@
     return [ref.at[pl.ds(start, size)] for start in range(0, rows or ref.shape[0], size)]
 
 
-def near_tile_kernel(core_ref, sharp_ref, bias_ref, near_ref, received_ref, far_ref, img_ref, txt_ref, weights_ref, part_ref, loss_ref):
-    pair = far_ref.shape[0] // 3
-
-    def work(is_first):
-        if is_first:
-            txt_ref[...] = near_ref[...]
-            img_ref[...] = received_ref[: 3 * pair]
-        else:
-            txt_ref[...] = received_ref[...]
-            img_ref[:pair] = near_ref[3 * pair :]
-            img_ref[pair:] = far_ref[pair:]
+def near_tile_kernel(core_ref, sharp_ref, bias_ref, near_ref, received_ref, img_ref, txt_ref, weights_ref, part_ref, loss_ref):
+    count = img_ref.shape[0]
+    pair = count // 2
+
+    def work(is_first):
+        txt_ref[...] = near_ref[...] if is_first else received_ref[...]
+        img_ref[...] = received_ref[:count] if is_first else near_ref[count:]
 
     by_core(core_ref, work)
     jobs = []
@@ -202,17 +198,37 @@
     loss_ref[...] = run_tiles(pair, sharp_ref, bias_ref, jobs)
 
 
-def far_tile_kernel(core_ref, sharp_ref, bias_ref, far_ref, received_ref, img_ref, before_ref, txt_ref, weights_ref, part_ref, loss_ref):
-    pair = far_ref.shape[0] // 3
+def middle_tile_kernel(core_ref, sharp_ref, bias_ref, far_ref, received_ref, txt_ref, img_ref, weights_ref, part_ref, loss_ref):
+    pair = img_ref.shape[0]
+
+    def work(is_first):
+        img_ref[...] = received_ref[:pair] if is_first else far_ref[2 * pair :]
+
+    by_core(core_ref, work)
+    loss_ref[...] = run_tiles(pair, sharp_ref, bias_ref, [(img_ref, [(txt_ref, weights_ref)], None, part_ref, None)])
+
+
+def far_tile_kernel(
+    core_ref, sharp_ref, bias_ref, far_ref, received_ref, near_img_ref, far_img_ref, near_before_ref, far_before_ref,
+    near_weights_ref, middle_weights_ref,
+    txt_ref, img_ref, all_weights_ref, weights_ref, part_ref, loss_ref,
+):
+    pair = far_img_ref.shape[0]
 
     def work(is_first):
         txt_ref[...] = far_ref[...] if is_first else received_ref[...]
 
     by_core(core_ref, work)
+    img_ref[: 2 * pair] = near_img_ref[...]
+    img_ref[2 * pair :] = far_img_ref[...]
+    all_weights_ref[: 2 * pair] = near_weights_ref[...]
+    all_weights_ref[2 * pair :] = middle_weights_ref[...]
     jobs = []
-    for k, rows in enumerate(row_blocks(img_ref, pair)):
+    images = row_blocks(near_img_ref, pair) + [far_img_ref]
+    before = row_blocks(near_before_ref, pair) + [far_before_ref]
+    for k in range(3):
         span = pl.ds(k * pair, pair)
-        jobs.append((rows, [(txt_ref, weights_ref.at[span])], before_ref.at[span], part_ref.at[span], None))
+        jobs.append((images[k], [(txt_ref, weights_ref.at[span])], before[k], part_ref.at[span], None))
     loss_ref[...] = run_tiles(pair, sharp_ref, bias_ref, jobs)
 
 
@@ -226,7 +242,7 @@
 
     def work(is_first):
         txt_ref[...] = last_ref[...] if is_first else received_ref[...]
-        img_tail_ref[:half] = far_received_ref[:half] if is_first else far_ref[half:pair]
+        img_tail_ref[:half] = far_received_ref[pair : pair + half] if is_first else far_ref[pair + half : 2 * pair]
         img_tail_ref[half:] = received_ref[:half] if is_first else last_ref[half:]
 
     by_core(core_ref, work)
@@ -298,35 +314,36 @@
     by_core(core_ref, work)
 
 
-def second_kernel(core_ref, txt_ref, txt_received_ref, img_ref, img_received_ref, out_ref):
+def second_kernel(core_ref, txt_ref, received_ref, out_ref):
     pair = out_ref.shape[0]
+
+    def work(is_first):
+        def rows(at):
+            if is_first:
+                value = txt_ref[at()] + decode(received_ref[at()], ONE_CHIP)
+            else:
+                value = decode(received_ref[at(2 * pair)], ONE_CHIP)
+            out_ref[at()] = encode(value, TWO_CHIPS)
+
+        each_chunk(pair, rows)
+
+    by_core(core_ref, work)
+
+
+def far_kernel(
+    core_ref, txt_ref, txt_received_ref, img_ref, img_tail_ref, tail_received_ref, from_a_ref, from_b_ref, x_ref, b_ref
+):
+    pair = x_ref.shape[0]
     half = pair // 2
-
-    def work(is_first):
-        def texts(at):
-            out_ref[at()] = encode(txt_ref[at()] + decode(txt_received_ref[at()], ONE_CHIP), TWO_CHIPS)
-
-        def images(at):
-            out_ref[at()] = encode(decode(img_received_ref[at()], ONE_CHIP), TWO_CHIPS)
-            out_ref[at(half)] = encode(img_ref[at()], TWO_CHIPS)
-
-        if is_first:
-            each_chunk(pair, texts)
-        else:
-            each_chunk(half, images)
-
-    by_core(core_ref, work)
-
-
-def far_kernel(core_ref, txt_ref, img_ref, received_ref, from_a_ref, from_b_ref, x_ref, b_ref):
-    half = x_ref.shape[0] // 2
 
     def work(is_first):
         def rows(at):
             def base(i):
                 if is_first:
-                    return txt_ref[at(i * half)] + decode(received_ref[at(i * half)], ONE_CHIP)
-                return img_ref[at(i * half)]
+                    return txt_ref[at(i * half)] + decode(txt_received_ref[at(i * half)], ONE_CHIP)
+                if i == 2:
+                    return decode(tail_received_ref[at()], ONE_CHIP)
+                return img_tail_ref[at()] if i == 3 else img_ref[at(i * half)]
 
             x_ref[at()] = encode(base(2), TWO_CHIPS)
             x_ref[at(half)] = encode(base(3) + decode(from_b_ref[at()], ONE_CHIP), TWO_CHIPS)
@@ -340,7 +357,7 @@
 
 def base_kernel(core_ref, txt_ref, received_ref, img_ref, img_received_ref, out_ref):
     count = out_ref.shape[0]
-    three = 3 * count // 4
+    two = count // 2
 
     def work(is_first):
         def texts(at):
@@ -352,8 +369,8 @@
         if is_first:
             each_chunk(count, texts)
         else:
-            each_chunk(three, images)
-            out_ref[three:] = img_ref[: count - three]
+            each_chunk(two, images)
+            out_ref[two:] = img_ref[:two]
 
     by_core(core_ref, work)
 
@@ -430,39 +447,54 @@
     near_received = swap(near)
     sharpness = jnp.broadcast_to(exponent_of_sharpness.reshape(1, 1), (8, 128))
     shift = jnp.broadcast_to(bias.reshape(1, 1), (8, 128))
-    slot_x3, sharpness, shift = lax.optimization_barrier((slot_x3, sharpness, shift))
+
+    scalars = (core, sharpness, shift)
+    losses = array(8, jnp.float32, 128)
+    wide, three, two = 4 * pair, 3 * pair, 2 * pair
+    near_img, near_txt, near_weights, near_part, near_loss = tile_call(
+        near_tile_kernel,
+        "tile_near",
+        two * wide,
+        scalars,
+        (near, near_received),
+        (
+            array(two, jnp.bfloat16),
+            array(wide, jnp.bfloat16),
+            array(two, jnp.bfloat16, wide),
+            array(two, jnp.float32),
+            losses,
+        ),
+    )
+    slot_2, slot_x3, slot_x1, near_part = lax.optimization_barrier((slot_2, slot_x3, slot_x1, near_part))
     last_a = move(half_of(slot_x3, 0), "a")
     last_b = move(half_of(slot_x1, 1), "b")
     far = pack(slot_2, slot_x1, slot_x3)
     far_received = swap(far)
-
-    scalars = (core, sharpness, shift)
-    losses = array(8, jnp.float32, 128)
-    wide, three = 4 * pair, 3 * pair
-    img, near_txt, near_weights, part, near_loss = tile_call(
-        near_tile_kernel,
-        "tile_near",
-        three * wide,
+    far_img, middle_weights, middle_part, middle_loss = tile_call(
+        middle_tile_kernel,
+        "tile_middle",
+        pair * wide,
         scalars,
-        (near, near_received, far),
-        (
-            array(three, jnp.bfloat16),
-            array(wide, jnp.bfloat16),
-            array(three, jnp.bfloat16, wide),
-            array(three, jnp.float32),
-            losses,
-        ),
-    )
-    last_a, last_b, part = lax.optimization_barrier((last_a, last_b, part))
+        (far, far_received, near_txt),
+        (low_piece, array(pair, jnp.bfloat16, wide), array(pair, jnp.float32), losses),
+    )
+    last_a, last_b, middle_part = lax.optimization_barrier((last_a, last_b, middle_part))
     last = pack(last_a, last_b)
     last_received = swap(last)
-    far_txt, far_weights, part, far_loss = tile_call(
+    far_txt, img, near_weights, far_weights, part, far_loss = tile_call(
         far_tile_kernel,
         "tile_far",
         three * three,
         scalars,
-        (far, far_received, img, part),
-        (array(three, jnp.bfloat16), array(three, jnp.bfloat16, three), array(three, jnp.float32), losses),
+        (far, far_received, near_img, far_img, near_part, middle_part, near_weights, middle_weights),
+        (
+            array(three, jnp.bfloat16),
+            array(three, jnp.bfloat16),
+            array(three, jnp.bfloat16, wide),
+            array(three, jnp.bfloat16, three),
+            array(three, jnp.float32),
+            losses,
+        ),
     )
     last_weights, img_part, img_tail, near_tail, far_tail, last_tail, img_part_tail, last_loss = tile_call(
         last_tile_kernel,
@@ -482,7 +514,7 @@
         ),
         (low_piece,),
     )
-    loss = near_loss + far_loss + last_loss
+    loss = near_loss + middle_loss + far_loss + last_loss
 
     def text_sums(weights, tail):
         return transposed_product(weights, img) + transposed_product(tail, img_tail)
@@ -507,13 +539,17 @@
     sent = encode(near_part, ONE_CHIP)
     loss = loss + swap(loss, 0, 2)
     (second,) = small_call(
-        second_kernel, "second", core, (far_part, rest_received, img_part_tail, tail_received), (low_piece,)
+        second_kernel, "second", core, (far_part, rest_received), (low_piece,)
     )
     from_a, from_b, second, sent, loss = lax.optimization_barrier((from_a, from_b, second, sent, loss))
 
     second_received = move(second, "a")
     x, b = small_call(
-        far_kernel, "far", core, (far_part, img_part, rest_received, from_a, from_b), (low_piece,) * 2
+        far_kernel,
+        "far",
+        core,
+        (far_part, rest_received, img_part, img_part_tail, tail_received, from_a, from_b),
+        (low_piece,) * 2,
     )
     x, b, sent = lax.optimization_barrier((x, b, sent))
     from_x, from_b = move(x, "x"), move(b, "b")

time: 108 us -> 110 us (1.019)
  waiting for transfers between devices: 28.3 us -> 38 us
  starting transfers between devices: 42.4 us -> 34 us
  Pallas kernels: 23.9 us -> 25.2 us
    ppermute x30, waiting for transfers between devices: 28.3 us -> 38 us  [exchange(): return lax.ppermute(x, AXES, pairs)]
    ppermute x30, starting transfers between devices: 42.4 us -> 34 us  [exchange(): return lax.ppermute(x, AXES, pairs)]
    pallas_call x3 -> x4, Pallas kernels: 13.7 us -> 14.1 us  [tile_call(): pl.pallas_call(kernel, out_shape=outs, in_specs=[SMEM] + [VMEM] * (len(sc...]
  transfers between devices with their start and end apart: 30 -> 30, of which waited for: 16 -> 17; matrix products, arithmetic and copies ran while one was open for 8% -> 8% of each run, Pallas kernels for 13% -> 13%
where the time goes in v2:
time: 110 us
  waiting for transfers between devices  38 us (35%)
  starting transfers between devices  34 us (31%)
  Pallas kernels  25.2 us (23%)
  matrix products  8.37 us (8%)
  between operations  2.27 us (2%)
  local copies, waits for them, and re-layouts  2.14 us (2%)
    ppermute x30, waiting for transfers between devices, exchange(): return lax.ppermute(x, AXES, pairs)  38 us
    ppermute x30, starting transfers between devices, exchange(): return lax.ppermute(x, AXES, pairs)  34 us
    pallas_call x4, Pallas kernels, tile_call(): pl.pallas_call(kernel, out_shape=outs, in_specs=[SMEM] + [VMEM] * (len(sc...  14.1 us
    pallas_call x9, Pallas kernels, small_call(): pl.pallas_call(kernel, out_shape=outs, in_specs=[SMEM] + [VMEM] * len(arr...  10.2 us
    dot_general x6, matrix products, transposed_product(): lax.dot_general(weights, img, (((0,), (0,)), ((), ())), preferred_element...  8.37 us
  transfers between devices with their start and end apart: 30, of which 17 were waited for; matrix products, arithmetic and copies ran while one was open for 8% of the time, Pallas kernels for 13%

profile of v2, /device:TPU:1, one launch (start us, length us, event | category | flops | bytes accessed | tf_op | source)
XLA Modules:
  0.0 110.1 jit_solution(13505626602270709451)
XLA Ops:
  0.6 1.1 copy-done
  1.7 1.1 copy-done.2
  3.3 1.5 %collective-permute-start = (bf16[128,1152]{1,0:T(8,128)(2,1)S(1)}, bf16[128,1152]{1,0:T(8,128)(2,1)S(1)}, u32[]{:S(2)}, u32[]{:S(2)}) collective-permute-start(bf16[128,1152]{1,0:T(8,128)(2,1)S(1)} %get-tuple-element.73), channel_id=1, source_target_pairs={{0,8},{1,9},{2,10},{3,11},{4,12},{5,13},{6,14},{7,15},{8,0},{9,1},... | collective-permute-start | bytes 884744 | tf_op jit(solution)/shard_map/ppermute | solution.py:25
  4.8 1.2 %collective-permute-done.refs_1_ = bf16[128,1152]{1,0:T(8,128)(2,1)S(1)} collective-permute-done((bf16[128,1152]{1,0:T(8,128)(2,1)S(1)}, bf16[128,1152]{1,0:T(8,128)(2,1)S(1)}, u32[]{:S(2)}, u32[]{:S(2)}) %collective-permute-start) | collective-permute-done | bytes 294944 | tf_op jit(solution)/shard_map/ppermute | solution.py:25
  6.1 3.9 %collective-permute-start.1 = (bf16[256,1152]{1,0:T(8,128)(2,1)S(1)}, bf16[256,1152]{1,0:T(8,128)(2,1)S(1)}, u32[]{:S(2)}, u32[]{:S(2)}) collective-permute-start(bf16[256,1152]{1,0:T(8,128)(2,1)S(1)} %pack.4.refs_0_), channel_id=1, source_target_pairs={{0,6},{1,7},{2,4},{3,5},{4,2},{5,3},{6,0},{7,1},{8,56},{9,57},{10,... | collective-permute-start | bytes 1769480 | tf_op jit(solution)/shard_map/ppermute | solution.py:25
  10.0 2.5 %collective-permute-start.3 = (bf16[256,1152]{1,0:T(8,128)(2,1)S(1)}, bf16[256,1152]{1,0:T(8,128)(2,1)S(1)}, u32[]{:S(2)}, u32[]{:S(2)}) collective-permute-start(bf16[256,1152]{1,0:T(8,128)(2,1)S(1)} %pack.4.refs_0_), channel_id=1, source_target_pairs={{0,1},{1,0},{2,3},{3,2},{4,5},{5,4},{6,7},{7,6},{8,73},{9,72},{10,... | collective-permute-start | bytes 1769480 | tf_op jit(solution)/shard_map/ppermute | solution.py:25
  12.5 4.8 %collective-permute-done.1.refs_3_ = bf16[256,1152]{1,0:T(8,128)(2,1)S(1)} collective-permute-done((bf16[256,1152]{1,0:T(8,128)(2,1)S(1)}, bf16[256,1152]{1,0:T(8,128)(2,1)S(1)}, u32[]{:S(2)}, u32[]{:S(2)}) %collective-permute-start.1) | collective-permute-done | bytes 589856 | tf_op jit(solution)/shard_map/ppermute | solution.py:25
  17.3 2.7 %collective-permute-done.3.refs_1_ = bf16[256,1152]{1,0:T(8,128)(2,1)S(1)} collective-permute-done((bf16[256,1152]{1,0:T(8,128)(2,1)S(1)}, bf16[256,1152]{1,0:T(8,128)(2,1)S(1)}, u32[]{:S(2)}, u32[]{:S(2)}) %collective-permute-start.3) | collective-permute-done | bytes 589856 | tf_op jit(solution)/shard_map/ppermute | solution.py:25
  19.9 1.3 %collective-permute-done.5.refs_2_ = bf16[256,1152]{1,0:T(8,128)(2,1)S(1)} collective-permute-done((bf16[256,1152]{1,0:T(8,128)(2,1)S(1)}, bf16[256,1152]{1,0:T(8,128)(2,1)S(1)}, u32[]{:S(2)}, u32[]{:S(2)}) %collective-permute-start.5) | collective-permute-done | bytes 589856 | tf_op jit(solution)/shard_map/ppermute | solution.py:25
  21.5 1.4 %collective-permute-start.2 = (bf16[256,1152]{1,0:T(8,128)(2,1)S(1)}, bf16[256,1152]{1,0:T(8,128)(2,1)S(1)}, u32[]{:S(2)}, u32[]{:S(2)}) collective-permute-start(bf16[256,1152]{1,0:T(8,128)(2,1)S(1)} %collective-permute-done.1.refs_3_), channel_id=1, source_target_pairs={{0,2},{1,3},{2,0},{3,1},{4,6},{5,7},{6,4},{7,5},{8,24},{9,25},{10,... | collective-permute-start | bytes 1769480 | tf_op jit(solution)/shard_map/ppermute | solution.py:25
  22.9 2.2 %collective-permute-start.4 = (bf16[256,1152]{1,0:T(8,128)(2,1)S(1)}, bf16[256,1152]{1,0:T(8,128)(2,1)S(1)}, u32[]{:S(2)}, u32[]{:S(2)}) collective-permute-start(bf16[256,1152]{1,0:T(8,128)(2,1)S(1)} %collective-permute-done.3.refs_1_), channel_id=1, source_target_pairs={{0,6},{1,7},{2,4},{3,5},{4,2},{5,3},{6,0},{7,1},{8,56},{9,57},{10,... | collective-permute-start | bytes 1769480 | tf_op jit(solution)/shard_map/ppermute | solution.py:25
  25.1 1.8 %collective-permute-start.6 = (bf16[256,1152]{1,0:T(8,128)(2,1)S(1)}, bf16[256,1152]{1,0:T(8,128)(2,1)S(1)}, u32[]{:S(2)}, u32[]{:S(2)}) collective-permute-start(bf16[256,1152]{1,0:T(8,128)(2,1)S(1)} %collective-permute-done.5.refs_2_), channel_id=1, source_target_pairs={{0,1},{1,0},{2,3},{3,2},{4,5},{5,4},{6,7},{7,6},{8,73},{9,72},{10,... | collective-permute-start | bytes 1769480 | tf_op jit(solution)/shard_map/ppermute | solution.py:25
  28.3 3.5 %tile_near.1 = (bf16[512,1152]{1,0:T(8,128)(2,1)S(1)}, bf16[1024,1152]{1,0:T(8,128)(2,1)S(1)}, bf16[512,1024]{1,0:T(8,128)(2,1)S(1)}, f32[512,1152]{1,0:T(8,128)S(1)}, f32[8,128]{1,0:T(8,128)S(1)}) custom-call(s32[1]{0:T(128)} %bitcast.core_ref.refs_0_, f32[8,128]{1,0:T(8,128)S(1)} %broadcast_in_dim.15.sharp_ref, f32[8,128]{1,0:T(8,128)S(1)} %broadcast_in_dim.17.bias_ref, ...), custom_call_target="tpu_custom_call" | custom-call | flops 2415919104 | bytes 4718592 | tf_op jit(solution)/shard_map/tile_near/pallas_call | solution.py:260
  31.8 1.3 %collective-permute-done.4.refs_0_.refs_2_ = bf16[256,1152]{1,0:T(8,128)(2,1)S(1)} collective-permute-done((bf16[256,1152]{1,0:T(8,128)(2,1)S(1)}, bf16[256,1152]{1,0:T(8,128)(2,1)S(1)}, u32[]{:S(2)}, u32[]{:S(2)}) %collective-permute-start.4) | collective-permute-done | bytes 589856 | tf_op jit(solution)/shard_map/ppermute | solution.py:25
  33.1 1.9 %collective-permute-done.6.refs_0_.refs_1_ = bf16[256,1152]{1,0:T(8,128)(2,1)S(1)} collective-permute-done((bf16[256,1152]{1,0:T(8,128)(2,1)S(1)}, bf16[256,1152]{1,0:T(8,128)(2,1)S(1)}, u32[]{:S(2)}, u32[]{:S(2)}) %collective-permute-start.6) | collective-permute-done | bytes 589856 | tf_op jit(solution)/shard_map/ppermute | solution.py:25
  36.8 2.3 %collective-permute-done.10.received_ref.far_received_ref = bf16[768,1152]{1,0:T(8,128)(2,1)S(1)} collective-permute-done((bf16[768,1152]{1,0:T(8,128)(2,1)S(1)}, bf16[768,1152]{1,0:T(8,128)(2,1)S(1)}, u32[]{:S(2)}, u32[]{:S(2)}) %collective-permute-start.10) | collective-permute-done | bytes 1769504 | tf_op jit(solution)/shard_map/ppermute | solution.py:25
  39.1 1.8 %tile_middle.1 = (bf16[256,1152]{1,0:T(8,128)(2,1)S(1)}, bf16[256,1024]{1,0:T(8,128)(2,1)S(1)}, f32[256,1152]{1,0:T(8,128)S(1)}, f32[8,128]{1,0:T(8,128)S(1)}) custom-call(s32[1]{0:T(128)} %bitcast.core_ref.refs_0_, f32[8,128]{1,0:T(8,128)S(1)} %broadcast_in_dim.15.sharp_ref, f32[8,128]{1,0:T(8,128)S(1)} %broadcast_in_dim.17.bias_ref, ...), custom_call_target="tpu_custom_call" | custom-call | flops 1207959552 | bytes 5898240 | tf_op jit(solution)/shard_map/tile_middle/pallas_call | solution.py:260
  40.9 0.9 collective-permute-done.8.refs_0_
  41.8 1.4 %collective-permute-done.9.refs_1_ = bf16[128,1152]{1,0:T(8,128)(2,1)S(1)} collective-permute-done((bf16[128,1152]{1,0:T(8,128)(2,1)S(1)}, bf16[128,1152]{1,0:T(8,128)(2,1)S(1)}, u32[]{:S(2)}, u32[]{:S(2)}) %collective-permute-start.9) | collective-permute-done | bytes 294944 | tf_op jit(solution)/shard_map/ppermute | solution.py:25
  43.3 1.4 %collective-permute-start.11 = (bf16[256,1152]{1,0:T(8,128)(2,1)S(1)}, bf16[256,1152]{1,0:T(8,128)(2,1)S(1)}, u32[]{:S(2)}, u32[]{:S(2)}) collective-permute-start(bf16[256,1152]{1,0:T(8,128)(2,1)S(1)} %pack.7.last_ref), channel_id=1, source_target_pairs={{0,8},{1,9},{2,10},{3,11},{4,12},{5,13},{6,14},{7,15},{8,0},{9,1},... | collective-permute-start | bytes 1769480 | tf_op jit(solution)/shard_map/ppermute | solution.py:25
  44.7 4.0 %tile_far.1 = (bf16[768,1152]{1,0:T(8,128)(2,1)S(1)}, bf16[768,1152]{1,0:T(8,128)(2,1)S(1)}, bf16[768,1024]{1,0:T(8,128)(2,1)S(1)}, bf16[768,768]{1,0:T(8,128)(2...) custom-call(s32[1]{0:T(128)} %bitcast.core_ref.refs_0_, f32[8,128]{1,0:T(8,128)S(1)} %broadcast_in_dim.15.sharp_ref, ...), custom_call_target="tpu_custom_call" | custom-call | flops 2717908992 | bytes 8650752 | tf_op jit(solution)/shard_map/tile_far/pallas_call | solution.py:260
  48.8 4.7 %tile_last.1 = (bf16[768,256]{1,0:T(8,128)(2,1)S(1)}, f32[768,1152]{1,0:T(8,128)S(1)}, bf16[256,1152]{1,0:T(8,128)(2,1)S(1)}, bf16[256,1024]{1,0:T(8,128)(2,1)S(...) custom-call(s32[1]{0:T(128)} %bitcast.core_ref.refs_0_, ...), custom_call_target="tpu_custom_call" | custom-call | flops 3321888768 | bytes 12386304 | tf_op jit(solution)/shard_map/tile_last/pallas_call | solution.py:260
  54.0 0.9 fusion.5
  54.9 1.2 %collective-permute-done.12 = f32[8,128]{1,0:T(8,128)S(1)} collective-permute-done((f32[8,128]{1,0:T(8,128)S(1)}, f32[8,128]{1,0:T(8,128)S(1)}, u32[]{:S(2)}, u32[]{:S(2)}) %collective-permute-start.12) | collective-permute-done | bytes 4128 | tf_op jit(solution)/shard_map/ppermute | solution.py:25
  56.1 1.2 %collective-permute-start.14 = (f32[8,128]{1,0:T(8,128)S(1)}, f32[8,128]{1,0:T(8,128)S(1)}, u32[]{:S(2)}, u32[]{:S(2)}) collective-permute-start(f32[8,128]{1,0:T(8,128)S(1)} %add.40), channel_id=1, source_target_pairs={{0,65},{1,64},{2,67},{3,66},{4,69},{5,68},{6,71},{7,70},{8,73},{9,... | collective-permute-start | bytes 12296 | tf_op jit(solution)/shard_map/ppermute | solution.py:25
  58.0 1.6 %collective-permute-start.13 = (bf16[256,1152]{1,0:T(8,128)(2,1)S(1)}, bf16[256,1152]{1,0:T(8,128)(2,1)S(1)}, u32[]{:S(2)}, u32[]{:S(2)}) collective-permute-start(bf16[256,1152]{1,0:T(8,128)(2,1)S(1)} %get-tuple-element.102), channel_id=1, source_target_pairs={{0,8},{1,9},{2,10},{3,11},{4,12},{5,13},{6,14},{7,15},{8,0},{9,1},... | collective-permute-start | bytes 1769480 | tf_op jit(solution)/shard_map/ppermute | solution.py:25
  59.5 2.4 %fusion.3 = (bf16[768,1152]{1,0:T(8,128)(2,1)S(1)}, f32[768,1152]{1,0:T(8,128)S(1)}) fusion(f32[768,1152]{1,0:T(8,128)S(1)} %get-tuple-element.103.img_ref, pred[]{:T(512)S(6)} %eq.3, f32[768,1152]{1,0:T(8,128)S(1)} %fusion.7, bf16[768,768]{1,0:T(8,128)(2,1)S(1)} %get-tuple-element.104, bf16[768,1152]{1,0:T(8,128)(2,1)S(1)} %get-tuple-element.89.img_ref), kind=kOutput, calls=%fused_computation.9 | convolution fusion | flops 1367801856 | bytes 15335425 | tf_op jit(solution)/shard_map/dot_general | solution.py:425
  65.0 0.9 fusion.8
  65.9 3.0 %fusion.1 = (bf16[1024,1152]{1,0:T(8,128)(2,1)S(1)}, f32[1024,1152]{1,0:T(8,128)S(1)}) fusion(f32[1024,1152]{1,0:T(8,128)S(1)} %fusion.8, bf16[768,1024]{1,0:T(8,128)(2,1)S(1)} %get-tuple-element.116, bf16[768,1152]{1,0:T(8,128)(2,1)S(1)} %get-tuple-element.89.img_ref), kind=kOutput, calls=%fused_computation.5 | convolution fusion | flops 1822556160 | bytes 15138816 | tf_op jit(solution)/shard_map/dot_general | solution.py:425
  69.8 1.6 %collective-permute-done.16.from_b_ref = bf16[128,1152]{1,0:T(8,128)(2,1)S(1)} collective-permute-done((bf16[128,1152]{1,0:T(8,128)(2,1)S(1)}, bf16[128,1152]{1,0:T(8,128)(2,1)S(1)}, u32[]{:S(2)}, u32[]{:S(2)}) %collective-permute-start.16) | collective-permute-done | bytes 294944 | tf_op jit(solution)/shard_map/ppermute | solution.py:25
  71.4 1.5 %far.1 = (bf16[256,1152]{1,0:T(8,128)(2,1)S(1)}, bf16[256,1152]{1,0:T(8,128)(2,1)S(1)}) custom-call(s32[1]{0:T(128)} %bitcast.core_ref.refs_0_, f32[768,1152]{1,0:T(8,128)S(1)} %get-tuple-element.142.txt_ref, bf16[768,1152]{1,0:T(8,128)(2,1)S(1)} %collective-permute-done.17.received_ref.txt_received_ref.img_received_ref, ...), custom_call_target="tpu_custom_call" | custom-call | tf_op jit(solution)/shard_map/far/pallas_call | solution.py:278
  72.9 2.9 %collective-permute-start.20 = (bf16[1024,1152]{1,0:T(8,128)(2,1)S(1)}, bf16[1024,1152]{1,0:T(8,128)(2,1)S(1)}, u32[]{:S(2)}, u32[]{:S(2)}) collective-permute-start(bf16[1024,1152]{1,0:T(8,128)(2,1)S(1)} %get-tuple-element.125), channel_id=1, source_target_pairs={{0,8},{1,9},{2,10},{3,11},{4,12},{5,13},{6,14},{7,15},{8,0},{9,1},... | collective-permute-start | bytes 7077896 | tf_op jit(solution)/shard_map/ppermute | solution.py:25
  77.2 1.2 %collective-permute-start.22 = (bf16[256,1152]{1,0:T(8,128)(2,1)S(1)}, bf16[256,1152]{1,0:T(8,128)(2,1)S(1)}, u32[]{:S(2)}, u32[]{:S(2)}) collective-permute-start(bf16[256,1152]{1,0:T(8,128)(2,1)S(1)} %get-tuple-element.130), channel_id=1, source_target_pairs={{0,1},{1,0},{2,3},{3,2},{4,5},{5,4},{6,7},{7,6},{8,73},{9,72},{10,... | collective-permute-start | bytes 1769480 | tf_op jit(solution)/shard_map/ppermute | solution.py:25
  78.4 1.5 %collective-permute-done.20.received_ref = bf16[1024,1152]{1,0:T(8,128)(2,1)S(1)} collective-permute-done((bf16[1024,1152]{1,0:T(8,128)(2,1)S(1)}, bf16[1024,1152]{1,0:T(8,128)(2,1)S(1)}, u32[]{:S(2)}, u32[]{:S(2)}) %collective-permute-start.20) | collective-permute-done | bytes 2359328 | tf_op jit(solution)/shard_map/ppermute | solution.py:25
  79.9 1.3 %base.1.refs_1_.base_ref = f32[1024,1152]{1,0:T(8,128)S(1)} custom-call(s32[1]{0:T(128)} %bitcast.core_ref.refs_0_, f32[1024,1152]{1,0:T(8,128)S(1)} %get-tuple-element.144.txt_ref, bf16[1024,1152]{1,0:T(8,128)(2,1)S(1)} %collective-permute-done.20.received_ref, f32[768,1152]{1,0:T(8,128)S(1)} %get-tuple-element.103.img_ref, ...), custom_call_target="tpu_custom_call" | custom-call | tf_op jit(solution)/shard_map/base/pallas_call | solution.py:278
  81.2 0.9 collective-permute-start.21
  82.1 3.2 %collective-permute-done.21 = f32[8,128]{1,0:T(8,128)S(1)} collective-permute-done((f32[8,128]{1,0:T(8,128)S(1)}, f32[8,128]{1,0:T(8,128)S(1)}, u32[]{:S(2)}, u32[]{:S(2)}) %collective-permute-start.21) | collective-permute-done | bytes 4128 | tf_op jit(solution)/shard_map/ppermute | solution.py:25
  85.3 1.3 %collective-permute-done.25.refs_2_ = bf16[256,1152]{1,0:T(8,128)(2,1)S(1)} collective-permute-done((bf16[256,1152]{1,0:T(8,128)(2,1)S(1)}, bf16[256,1152]{1,0:T(8,128)(2,1)S(1)}, u32[]{:S(2)}, u32[]{:S(2)}) %collective-permute-start.25) | collective-permute-done | bytes 589856 | tf_op jit(solution)/shard_map/ppermute | solution.py:25
  86.7 0.9 near.5
  87.6 1.4 %collective-permute-start.26 = (bf16[256,1152]{1,0:T(8,128)(2,1)S(1)}, bf16[256,1152]{1,0:T(8,128)(2,1)S(1)}, u32[]{:S(2)}, u32[]{:S(2)}) collective-permute-start(bf16[256,1152]{1,0:T(8,128)(2,1)S(1)} %near.5), channel_id=1, source_target_pairs={{0,1},{1,0},{2,3},{3,2},{4,5},{5,4},{6,7},{7,6},{8,73},{9,72},{10,... | collective-permute-start | bytes 1769480 | tf_op jit(solution)/shard_map/ppermute | solution.py:25
  90.6 0.9 near.3
  91.6 1.5 %collective-permute-start.27 = (f32[8,128]{1,0:T(8,128)S(1)}, f32[8,128]{1,0:T(8,128)S(1)}, u32[]{:S(2)}, u32[]{:S(2)}) collective-permute-start(f32[8,128]{1,0:T(8,128)S(1)} %add.45), channel_id=1, source_target_pairs={{0,16},{1,17},{2,18},{3,19},{4,20},{5,21},{6,22},{7,23},{8,24},{9,... | collective-permute-start | bytes 12296 | tf_op jit(solution)/shard_map/ppermute | solution.py:25
  93.0 7.6 %collective-permute-done.27 = f32[8,128]{1,0:T(8,128)S(1)} collective-permute-done((f32[8,128]{1,0:T(8,128)S(1)}, f32[8,128]{1,0:T(8,128)S(1)}, u32[]{:S(2)}, u32[]{:S(2)}) %collective-permute-start.27) | collective-permute-done | bytes 4128 | tf_op jit(solution)/shard_map/ppermute | solution.py:25
  100.7 2.0 %collective-permute-start.28 = (f32[8,128]{1,0:T(8,128)S(1)}, f32[8,128]{1,0:T(8,128)S(1)}, u32[]{:S(2)}, u32[]{:S(2)}) collective-permute-start(f32[8,128]{1,0:T(8,128)S(1)} %add.46), channel_id=1, source_target_pairs={{0,48},{1,49},{2,50},{3,51},{4,52},{5,53},{6,54},{7,55},{8,56},{9,... | collective-permute-start | bytes 12296 | tf_op jit(solution)/shard_map/ppermute | solution.py:25
  102.7 1.7 %collective-permute-done.28 = f32[8,128]{1,0:T(8,128)S(1)} collective-permute-done((f32[8,128]{1,0:T(8,128)S(1)}, f32[8,128]{1,0:T(8,128)S(1)}, u32[]{:S(2)}, u32[]{:S(2)}) %collective-permute-start.28) | collective-permute-done | bytes 4128 | tf_op jit(solution)/shard_map/ppermute | solution.py:25
  104.4 1.5 %gather_sums.1 = (f32[128,1152]{1,0:T(8,128)S(1)}, f32[136,1152]{1,0:T(8,128)S(1)}) custom-call(s32[1]{0:T(128)} %bitcast.core_ref.refs_0_, f32[1024,1152]{1,0:T(8,128)S(1)} %base.1.refs_1_.base_ref, bf16[256,1152]{1,0:T(8,128)(2,1)S(1)} %collective-permute-done.23.a_ref, bf16[256,1152]{1,0:T(8,128)(2,1)S(1)} %collective-permute-done.24.b_ref, ...), custom_call_target="tpu_custom_call" | custom-call | tf_op jit(solution)/shard_map/gather_sums/pallas_call | solution.py:278
  106.0 2.0 %collective-permute-done.29.refs_4_ = f32[136,1152]{1,0:T(8,128)S(1)} collective-permute-done((f32[136,1152]{1,0:T(8,128)S(1)}, f32[136,1152]{1,0:T(8,128)S(1)}, u32[]{:S(2)}, u32[]{:S(2)}) %collective-permute-start.29) | collective-permute-done | bytes 626720 | tf_op jit(solution)/shard_map/ppermute | solution.py:25
  108.1 2.0 %finish.1 = (f32[1,1]{1,0:T(1,128)}, f32[128,1152]{1,0:T(8,128)}, f32[128,1152]{1,0:T(8,128)}) custom-call(s32[1]{0:T(128)} %bitcast.core_ref.refs_0_, f32[128,1152]{1,0:T(8,128)S(1)} %copy-done.1, f32[128,1152]{1,0:T(8,128)S(1)} %copy-done.3, f32[128,1152]{1,0:T(8,128)S(1)} %get-tuple-element.134.refs_3_, f32[136,1152]{1,0:T(8,128)S(1)} %collective-permute-done.29.refs_4_, ...), custom_call_target="tpu_custom_call" | custom-call | tf_op jit(solution)/shard_map/finish/pallas_call | solution.py:278
  (55 shorter events, 10.9 us)
Async XLA Ops:
  0.6 1.1 copy-start
  1.7 1.1 copy-start.2
  3.3 2.7 %collective-permute-start = (bf16[128,1152]{1,0:T(8,128)(2,1)S(1)}, bf16[128,1152]{1,0:T(8,128)(2,1)S(1)}, u32[]{:S(2)}, u32[]{:S(2)}) collective-permute-start(bf16[128,1152]{1,0:T(8,128)(2,1)S(1)} %get-tuple-element.73), channel_id=1, source_target_pairs={{0,8},{1,9},{2,10},{3,11},{4,12},{5,13},{6,14},{7,15},{8,0},{9,1},... | collective-permute-start | bytes 884744 | tf_op jit(solution)/shard_map/ppermute | solution.py:25
  6.1 11.2 %collective-permute-start.1 = (bf16[256,1152]{1,0:T(8,128)(2,1)S(1)}, bf16[256,1152]{1,0:T(8,128)(2,1)S(1)}, u32[]{:S(2)}, u32[]{:S(2)}) collective-permute-start(bf16[256,1152]{1,0:T(8,128)(2,1)S(1)} %pack.4.refs_0_), channel_id=1, source_target_pairs={{0,6},{1,7},{2,4},{3,5},{4,2},{5,3},{6,0},{7,1},{8,56},{9,57},{10,... | collective-permute-start | bytes 1769480 | tf_op jit(solution)/shard_map/ppermute | solution.py:25
  10.0 9.9 %collective-permute-start.3 = (bf16[256,1152]{1,0:T(8,128)(2,1)S(1)}, bf16[256,1152]{1,0:T(8,128)(2,1)S(1)}, u32[]{:S(2)}, u32[]{:S(2)}) collective-permute-start(bf16[256,1152]{1,0:T(8,128)(2,1)S(1)} %pack.4.refs_0_), channel_id=1, source_target_pairs={{0,1},{1,0},{2,3},{3,2},{4,5},{5,4},{6,7},{7,6},{8,73},{9,72},{10,... | collective-permute-start | bytes 1769480 | tf_op jit(solution)/shard_map/ppermute | solution.py:25
  12.5 8.7 %collective-permute-start.5 = (bf16[256,1152]{1,0:T(8,128)(2,1)S(1)}, bf16[256,1152]{1,0:T(8,128)(2,1)S(1)}, u32[]{:S(2)}, u32[]{:S(2)}) collective-permute-start(bf16[256,1152]{1,0:T(8,128)(2,1)S(1)} %pack.4.refs_0_), channel_id=1, source_target_pairs={{0,2},{1,3},{2,0},{3,1},{4,6},{5,7},{6,4},{7,5},{8,24},{9,25},{10,... | collective-permute-start | bytes 1769480 | tf_op jit(solution)/shard_map/ppermute | solution.py:25
  21.4 6.9 %collective-permute-start.7 = (bf16[1024,1152]{1,0:T(8,128)(2,1)S(1)}, bf16[1024,1152]{1,0:T(8,128)(2,1)S(1)}, u32[]{:S(2)}, u32[]{:S(2)}) collective-permute-start(bf16[1024,1152]{1,0:T(8,128)(2,1)S(1)} %pack.5.near_ref), channel_id=1, source_target_pairs={{0,8},{1,9},{2,10},{3,11},{4,12},{5,13},{6,14},{7,15},{8,0},{9,1},... | collective-permute-start | bytes 7077896 | tf_op jit(solution)/shard_map/ppermute | solution.py:25
  21.5 10.3 %collective-permute-start.2 = (bf16[256,1152]{1,0:T(8,128)(2,1)S(1)}, bf16[256,1152]{1,0:T(8,128)(2,1)S(1)}, u32[]{:S(2)}, u32[]{:S(2)}) collective-permute-start(bf16[256,1152]{1,0:T(8,128)(2,1)S(1)} %collective-permute-done.1.refs_3_), channel_id=1, source_target_pairs={{0,2},{1,3},{2,0},{3,1},{4,6},{5,7},{6,4},{7,5},{8,24},{9,25},{10,... | collective-permute-start | bytes 1769480 | tf_op jit(solution)/shard_map/ppermute | solution.py:25
  22.9 10.2 %collective-permute-start.4 = (bf16[256,1152]{1,0:T(8,128)(2,1)S(1)}, bf16[256,1152]{1,0:T(8,128)(2,1)S(1)}, u32[]{:S(2)}, u32[]{:S(2)}) collective-permute-start(bf16[256,1152]{1,0:T(8,128)(2,1)S(1)} %collective-permute-done.3.refs_1_), channel_id=1, source_target_pairs={{0,6},{1,7},{2,4},{3,5},{4,2},{5,3},{6,0},{7,1},{8,56},{9,57},{10,... | collective-permute-start | bytes 1769480 | tf_op jit(solution)/shard_map/ppermute | solution.py:25
  25.1 9.9 %collective-permute-start.6 = (bf16[256,1152]{1,0:T(8,128)(2,1)S(1)}, bf16[256,1152]{1,0:T(8,128)(2,1)S(1)}, u32[]{:S(2)}, u32[]{:S(2)}) collective-permute-start(bf16[256,1152]{1,0:T(8,128)(2,1)S(1)} %collective-permute-done.5.refs_2_), channel_id=1, source_target_pairs={{0,1},{1,0},{2,3},{3,2},{4,5},{5,4},{6,7},{7,6},{8,73},{9,72},{10,... | collective-permute-start | bytes 1769480 | tf_op jit(solution)/shard_map/ppermute | solution.py:25
  35.2 3.9 %collective-permute-start.10 = (bf16[768,1152]{1,0:T(8,128)(2,1)S(1)}, bf16[768,1152]{1,0:T(8,128)(2,1)S(1)}, u32[]{:S(2)}, u32[]{:S(2)}) collective-permute-start(bf16[768,1152]{1,0:T(8,128)(2,1)S(1)} %pack.6.far_ref), channel_id=1, source_target_pairs={{0,8},{1,9},{2,10},{3,11},{4,12},{5,13},{6,14},{7,15},{8,0},{9,1},... | collective-permute-start | bytes 5308424 | tf_op jit(solution)/shard_map/ppermute | solution.py:25
  35.9 5.9 %collective-permute-start.8 = (bf16[128,1152]{1,0:T(8,128)(2,1)S(1)}, bf16[128,1152]{1,0:T(8,128)(2,1)S(1)}, u32[]{:S(2)}, u32[]{:S(2)}) collective-permute-start(bf16[128,1152]{1,0:T(8,128)(2,1)S(1)} %half_of.2), channel_id=1, source_target_pairs={{0,2},{1,3},{2,0},{3,1},{4,6},{5,7},{6,4},{7,5},{8,24},{9,25},{10,... | collective-permute-start | bytes 884744 | tf_op jit(solution)/shard_map/ppermute | solution.py:25
  36.2 7.1 %collective-permute-start.9 = (bf16[128,1152]{1,0:T(8,128)(2,1)S(1)}, bf16[128,1152]{1,0:T(8,128)(2,1)S(1)}, u32[]{:S(2)}, u32[]{:S(2)}) collective-permute-start(bf16[128,1152]{1,0:T(8,128)(2,1)S(1)} %half_of.3), channel_id=1, source_target_pairs={{0,6},{1,7},{2,4},{3,5},{4,2},{5,3},{6,0},{7,1},{8,56},{9,57},{10,... | collective-permute-start | bytes 884744 | tf_op jit(solution)/shard_map/ppermute | solution.py:25
  43.3 5.5 %collective-permute-start.11 = (bf16[256,1152]{1,0:T(8,128)(2,1)S(1)}, bf16[256,1152]{1,0:T(8,128)(2,1)S(1)}, u32[]{:S(2)}, u32[]{:S(2)}) collective-permute-start(bf16[256,1152]{1,0:T(8,128)(2,1)S(1)} %pack.7.last_ref), channel_id=1, source_target_pairs={{0,8},{1,9},{2,10},{3,11},{4,12},{5,13},{6,14},{7,15},{8,0},{9,1},... | collective-permute-start | bytes 1769480 | tf_op jit(solution)/shard_map/ppermute | solution.py:25
  53.5 2.5 %collective-permute-start.12 = (f32[8,128]{1,0:T(8,128)S(1)}, f32[8,128]{1,0:T(8,128)S(1)}, u32[]{:S(2)}, u32[]{:S(2)}) collective-permute-start(f32[8,128]{1,0:T(8,128)S(1)} %add_add_fusion), channel_id=1, source_target_pairs={{0,1},{1,0},{2,3},{3,2},{4,5},{5,4},{6,7},{7,6},{8,9},{9,8},{10,11... | collective-permute-start | bytes 12296 | tf_op jit(solution)/shard_map/ppermute | solution.py:25
  56.1 5.9 %collective-permute-start.14 = (f32[8,128]{1,0:T(8,128)S(1)}, f32[8,128]{1,0:T(8,128)S(1)}, u32[]{:S(2)}, u32[]{:S(2)}) collective-permute-start(f32[8,128]{1,0:T(8,128)S(1)} %add.40), channel_id=1, source_target_pairs={{0,65},{1,64},{2,67},{3,66},{4,69},{5,68},{6,71},{7,70},{8,73},{9,... | collective-permute-start | bytes 12296 | tf_op jit(solution)/shard_map/ppermute | solution.py:25
  58.0 4.0 %collective-permute-start.13 = (bf16[256,1152]{1,0:T(8,128)(2,1)S(1)}, bf16[256,1152]{1,0:T(8,128)(2,1)S(1)}, u32[]{:S(2)}, u32[]{:S(2)}) collective-permute-start(bf16[256,1152]{1,0:T(8,128)(2,1)S(1)} %get-tuple-element.102), channel_id=1, source_target_pairs={{0,8},{1,9},{2,10},{3,11},{4,12},{5,13},{6,14},{7,15},{8,0},{9,1},... | collective-permute-start | bytes 1769480 | tf_op jit(solution)/shard_map/ppermute | solution.py:25
  62.5 6.5 %collective-permute-start.17 = (bf16[768,1152]{1,0:T(8,128)(2,1)S(1)}, bf16[768,1152]{1,0:T(8,128)(2,1)S(1)}, u32[]{:S(2)}, u32[]{:S(2)}) collective-permute-start(bf16[768,1152]{1,0:T(8,128)(2,1)S(1)} %get-tuple-element.115), channel_id=1, source_target_pairs={{0,8},{1,9},{2,10},{3,11},{4,12},{5,13},{6,14},{7,15},{8,0},{9,1},... | collective-permute-start | bytes 5308424 | tf_op jit(solution)/shard_map/ppermute | solution.py:25
  63.2 5.7 %collective-permute-start.18 = (f32[8,128]{1,0:T(8,128)S(1)}, f32[8,128]{1,0:T(8,128)S(1)}, u32[]{:S(2)}, u32[]{:S(2)}) collective-permute-start(f32[8,128]{1,0:T(8,128)S(1)} %add.42), channel_id=1, source_target_pairs={{0,2},{1,3},{2,0},{3,1},{4,6},{5,7},{6,4},{7,5},{8,10},{9,11},{10,... | collective-permute-start | bytes 12296 | tf_op jit(solution)/shard_map/ppermute | solution.py:25
  63.6 6.2 %collective-permute-start.15 = (bf16[128,1152]{1,0:T(8,128)(2,1)S(1)}, bf16[128,1152]{1,0:T(8,128)(2,1)S(1)}, u32[]{:S(2)}, u32[]{:S(2)}) collective-permute-start(bf16[128,1152]{1,0:T(8,128)(2,1)S(1)} %get-tuple-element.113), channel_id=1, source_target_pairs={{0,2},{1,3},{2,0},{3,1},{4,6},{5,7},{6,4},{7,5},{8,24},{9,25},{10,... | collective-permute-start | bytes 884744 | tf_op jit(solution)/shard_map/ppermute | solution.py:25
  64.3 7.1 %collective-permute-start.16 = (bf16[128,1152]{1,0:T(8,128)(2,1)S(1)}, bf16[128,1152]{1,0:T(8,128)(2,1)S(1)}, u32[]{:S(2)}, u32[]{:S(2)}) collective-permute-start(bf16[128,1152]{1,0:T(8,128)(2,1)S(1)} %get-tuple-element.114), channel_id=1, source_target_pairs={{0,6},{1,7},{2,4},{3,5},{4,2},{5,3},{6,0},{7,1},{8,56},{9,57},{10,... | collective-permute-start | bytes 884744 | tf_op jit(solution)/shard_map/ppermute | solution.py:25
  72.9 7.0 %collective-permute-start.20 = (bf16[1024,1152]{1,0:T(8,128)(2,1)S(1)}, bf16[1024,1152]{1,0:T(8,128)(2,1)S(1)}, u32[]{:S(2)}, u32[]{:S(2)}) collective-permute-start(bf16[1024,1152]{1,0:T(8,128)(2,1)S(1)} %get-tuple-element.125), channel_id=1, source_target_pairs={{0,8},{1,9},{2,10},{3,11},{4,12},{5,13},{6,14},{7,15},{8,0},{9,1},... | collective-permute-start | bytes 7077896 | tf_op jit(solution)/shard_map/ppermute | solution.py:25
  75.8 9.6 %collective-permute-start.19 = (bf16[256,1152]{1,0:T(8,128)(2,1)S(1)}, bf16[256,1152]{1,0:T(8,128)(2,1)S(1)}, u32[]{:S(2)}, u32[]{:S(2)}) collective-permute-start(bf16[256,1152]{1,0:T(8,128)(2,1)S(1)} %second.1), channel_id=1, source_target_pairs={{0,2},{1,3},{2,0},{3,1},{4,6},{5,7},{6,4},{7,5},{8,24},{9,25},{10,... | collective-permute-start | bytes 1769480 | tf_op jit(solution)/shard_map/ppermute | solution.py:25
  76.5 10.2 %collective-permute-start.25 = (bf16[256,1152]{1,0:T(8,128)(2,1)S(1)}, bf16[256,1152]{1,0:T(8,128)(2,1)S(1)}, u32[]{:S(2)}, u32[]{:S(2)}) collective-permute-start(bf16[256,1152]{1,0:T(8,128)(2,1)S(1)} %get-tuple-element.132), channel_id=1, source_target_pairs={{0,6},{1,7},{2,4},{3,5},{4,2},{5,3},{6,0},{7,1},{8,56},{9,57},{10,... | collective-permute-start | bytes 1769480 | tf_op jit(solution)/shard_map/ppermute | solution.py:25
  77.2 13.4 %collective-permute-start.22 = (bf16[256,1152]{1,0:T(8,128)(2,1)S(1)}, bf16[256,1152]{1,0:T(8,128)(2,1)S(1)}, u32[]{:S(2)}, u32[]{:S(2)}) collective-permute-start(bf16[256,1152]{1,0:T(8,128)(2,1)S(1)} %get-tuple-element.130), channel_id=1, source_target_pairs={{0,1},{1,0},{2,3},{3,2},{4,5},{5,4},{6,7},{7,6},{8,73},{9,72},{10,... | collective-permute-start | bytes 1769480 | tf_op jit(solution)/shard_map/ppermute | solution.py:25
  81.2 4.1 %collective-permute-start.21 = (f32[8,128]{1,0:T(8,128)S(1)}, f32[8,128]{1,0:T(8,128)S(1)}, u32[]{:S(2)}, u32[]{:S(2)}) collective-permute-start(f32[8,128]{1,0:T(8,128)S(1)} %add.44), channel_id=1, source_target_pairs={{0,6},{1,7},{2,4},{3,5},{4,2},{5,3},{6,0},{7,1},{8,14},{9,15},{10,... | collective-permute-start | bytes 12296 | tf_op jit(solution)/shard_map/ppermute | solution.py:25
  87.6 16.8 %collective-permute-start.26 = (bf16[256,1152]{1,0:T(8,128)(2,1)S(1)}, bf16[256,1152]{1,0:T(8,128)(2,1)S(1)}, u32[]{:S(2)}, u32[]{:S(2)}) collective-permute-start(bf16[256,1152]{1,0:T(8,128)(2,1)S(1)} %near.5), channel_id=1, source_target_pairs={{0,1},{1,0},{2,3},{3,2},{4,5},{5,4},{6,7},{7,6},{8,73},{9,72},{10,... | collective-permute-start | bytes 1769480 | tf_op jit(solution)/shard_map/ppermute | solution.py:25
  89.8 14.6 %collective-permute-start.24 = (bf16[256,1152]{1,0:T(8,128)(2,1)S(1)}, bf16[256,1152]{1,0:T(8,128)(2,1)S(1)}, u32[]{:S(2)}, u32[]{:S(2)}) collective-permute-start(bf16[256,1152]{1,0:T(8,128)(2,1)S(1)} %near.4), channel_id=1, source_target_pairs={{0,6},{1,7},{2,4},{3,5},{4,2},{5,3},{6,0},{7,1},{8,56},{9,57},{10,... | collective-permute-start | bytes 1769480 | tf_op jit(solution)/shard_map/ppermute | solution.py:25
  91.5 12.9 %collective-permute-start.23 = (bf16[256,1152]{1,0:T(8,128)(2,1)S(1)}, bf16[256,1152]{1,0:T(8,128)(2,1)S(1)}, u32[]{:S(2)}, u32[]{:S(2)}) collective-permute-start(bf16[256,1152]{1,0:T(8,128)(2,1)S(1)} %near.3), channel_id=1, source_target_pairs={{0,2},{1,3},{2,0},{3,1},{4,6},{5,7},{6,4},{7,5},{8,24},{9,25},{10,... | collective-permute-start | bytes 1769480 | tf_op jit(solution)/shard_map/ppermute | solution.py:25
  91.6 9.1 %collective-permute-start.27 = (f32[8,128]{1,0:T(8,128)S(1)}, f32[8,128]{1,0:T(8,128)S(1)}, u32[]{:S(2)}, u32[]{:S(2)}) collective-permute-start(f32[8,128]{1,0:T(8,128)S(1)} %add.45), channel_id=1, source_target_pairs={{0,16},{1,17},{2,18},{3,19},{4,20},{5,21},{6,22},{7,23},{8,24},{9,... | collective-permute-start | bytes 12296 | tf_op jit(solution)/shard_map/ppermute | solution.py:25
  100.7 3.7 %collective-permute-start.28 = (f32[8,128]{1,0:T(8,128)S(1)}, f32[8,128]{1,0:T(8,128)S(1)}, u32[]{:S(2)}, u32[]{:S(2)}) collective-permute-start(f32[8,128]{1,0:T(8,128)S(1)} %add.46), channel_id=1, source_target_pairs={{0,48},{1,49},{2,50},{3,51},{4,52},{5,53},{6,54},{7,55},{8,56},{9,... | collective-permute-start | bytes 12296 | tf_op jit(solution)/shard_map/ppermute | solution.py:25
  104.4 3.7 %copy-start.1 = (f32[128,1152]{1,0:T(8,128)S(1)}, f32[128,1152]{1,0:T(8,128)}, u32[]{:S(2)}) copy-start(f32[128,1152]{1,0:T(8,128)} %refs_1_.1) | copy-start | bytes 1769476
  104.4 3.7 %copy-start.3 = (f32[128,1152]{1,0:T(8,128)S(1)}, f32[128,1152]{1,0:T(8,128)}, u32[]{:S(2)}) copy-start(f32[128,1152]{1,0:T(8,128)} %refs_2_.1) | copy-start | bytes 1769476
  105.9 2.1 %collective-permute-start.29 = (f32[136,1152]{1,0:T(8,128)S(1)}, f32[136,1152]{1,0:T(8,128)S(1)}, u32[]{:S(2)}, u32[]{:S(2)}) collective-permute-start(f32[136,1152]{1,0:T(8,128)S(1)} %get-tuple-element.135), channel_id=1, source_target_pairs={{0,8},{1,9},{2,10},{3,11},{4,12},{5,13},{6,14},{7,15},{8,0},{9,1},... | collective-permute-start | bytes 1880072 | tf_op jit(solution)/shard_map/ppermute | solution.py:25

commit v3 on v2

--- a/solution.py
+++ b/solution.py
@@ -42,7 +42,7 @@
 
 def decode(e, shift):
     f = e.astype(jnp.float32)
-    size = jnp.exp(jnp.log(jnp.maximum(jnp.abs(f), TINY)) * 0.125)
+    size = jnp.exp2(jnp.log2(jnp.maximum(jnp.abs(f), TINY)) * 0.125)
     return jnp.where(f < 0.0, -size, size) * (1.0 / shift)
 
 
@@ -85,7 +85,7 @@
         in_specs=[SMEM, HBM, HBM],
         out_specs=(VMEM, VMEM),
         scratch_shapes=[pltpu.VMEM((2, *img.shape), jnp.float32), pltpu.SemaphoreType.DMA((2,))],
-        compiler_params=pltpu.CompilerParams(vmem_limit_bytes=6 * MIB),
+        compiler_params=pltpu.CompilerParams(vmem_limit_bytes=59 * MIB),
         name="normalize",
     )(core, img, txt)
 
@@ -285,7 +285,7 @@
     )(core, *arrays)
 
 
-CHUNK = 32
+CHUNK = 64
 
 
 def each_chunk(rows, work):
@@ -478,9 +478,6 @@
         (far, far_received, near_txt),
         (low_piece, array(pair, jnp.bfloat16, wide), array(pair, jnp.float32), losses),
     )
-    last_a, last_b, middle_part = lax.optimization_barrier((last_a, last_b, middle_part))
-    last = pack(last_a, last_b)
-    last_received = swap(last)
     far_txt, img, near_weights, far_weights, part, far_loss = tile_call(
         far_tile_kernel,
         "tile_far",
@@ -496,6 +493,9 @@
             losses,
         ),
     )
+    last_a, last_b, part = lax.optimization_barrier((last_a, last_b, part))
+    last = pack(last_a, last_b)
+    last_received = swap(last)
     last_weights, img_part, img_tail, near_tail, far_tail, last_tail, img_part_tail, last_loss = tile_call(
         last_tile_kernel,
         "tile_last",

time: 110 us -> 107 us (0.973)
  waiting for transfers between devices: 38 us -> 27.4 us
  starting transfers between devices: 34 us -> 42.5 us
  local copies, waits for them, and re-layouts: 2.14 us -> 0.97 us
    ppermute x30, waiting for transfers between devices: 38 us -> 27.4 us  [exchange(): return lax.ppermute(x, AXES, pairs)]
    ppermute x30, starting transfers between devices: 34 us -> 42.5 us  [exchange(): return lax.ppermute(x, AXES, pairs)]
    pallas_call x9, Pallas kernels: 10.2 us -> 8.41 us  [small_call(): pl.pallas_call(kernel, out_shape=outs, in_specs=[SMEM] + [VMEM] * len(arr...]
    pallas_call x1, Pallas kernels: 0.54 us -> 2.2 us  [normalize(): pl.pallas_call(normalize_kernel, out_shape=(low, low), in_specs=[SMEM, HB...]
    unnamed x8 -> x6, local copies, waits for them, and re-layouts: 2.13 us -> 0.97 us
  transfers between devices with their start and end apart: 30 -> 30, of which waited for: 17 -> 15; matrix products, arithmetic and copies ran while one was open for 8% -> 8% of each run, Pallas kernels for 13% -> 13%
where the time goes in v3:
time: 107 us
  starting transfers between devices  42.5 us (40%)
  waiting for transfers between devices  27.4 us (26%)
  Pallas kernels  25.1 us (23%)
  matrix products  8.36 us (8%)
  between operations  2.24 us (2%)
    ppermute x30, starting transfers between devices, exchange(): return lax.ppermute(x, AXES, pairs)  42.5 us
    ppermute x30, waiting for transfers between devices, exchange(): return lax.ppermute(x, AXES, pairs)  27.4 us
    pallas_call x4, Pallas kernels, tile_call(): pl.pallas_call(kernel, out_shape=outs, in_specs=[SMEM] + [VMEM] * (len(sc...  14 us
    pallas_call x9, Pallas kernels, small_call(): pl.pallas_call(kernel, out_shape=outs, in_specs=[SMEM] + [VMEM] * len(arr...  8.41 us
    dot_general x6, matrix products, transposed_product(): lax.dot_general(weights, img, (((0,), (0,)), ((), ())), preferred_element...  8.36 us
    pallas_call x1, Pallas kernels, normalize(): pl.pallas_call(normalize_kernel, out_shape=(low, low), in_specs=[SMEM, HB...  2.2 us
  transfers between devices with their start and end apart: 30, of which 15 were waited for; matrix products, arithmetic and copies ran while one was open for 8% of the time, Pallas kernels for 13%

profile of v3, /device:TPU:1, one launch (start us, length us, event | category | flops | bytes accessed | tf_op | source)
XLA Modules:
  0.0 106.6 jit_solution(251273520863671080)
XLA Ops:
  0.6 2.2 %normalize.1 = (bf16[128,1152]{1,0:T(8,128)(2,1)}, bf16[128,1152]{1,0:T(8,128)(2,1)}) custom-call(s32[1]{0:T(128)} %bitcast.core_ref.refs_0_, f32[128,1152]{1,0:T(8,128)} %refs_1_.1, f32[128,1152]{1,0:T(8,128)} %refs_2_.1), custom_call_target="tpu_custom_call" | custom-call | tf_op jit(solution)/shard_map/normalize/pallas_call | solution.py:82
  2.8 1.5 %collective-permute-start = (bf16[128,1152]{1,0:T(8,128)(2,1)}, bf16[128,1152]{1,0:T(8,128)(2,1)S(1)}, u32[]{:S(2)}, u32[]{:S(2)}) collective-permute-start(bf16[128,1152]{1,0:T(8,128)(2,1)} %get-tuple-element.73), channel_id=1, source_target_pairs={{0,8},{1,9},{2,10},{3,11},{4,12},{5,13},{6,14},{7,15},{8,0},{9,1},... | collective-permute-start | bytes 884744 | tf_op jit(solution)/shard_map/ppermute | solution.py:25
  4.4 1.4 %collective-permute-done.refs_1_ = bf16[128,1152]{1,0:T(8,128)(2,1)S(1)} collective-permute-done((bf16[128,1152]{1,0:T(8,128)(2,1)}, bf16[128,1152]{1,0:T(8,128)(2,1)S(1)}, u32[]{:S(2)}, u32[]{:S(2)}) %collective-permute-start) | collective-permute-done | bytes 294944 | tf_op jit(solution)/shard_map/ppermute | solution.py:25
  5.8 1.0 copy-done.2
  6.8 1.8 %collective-permute-start.5 = (bf16[256,1152]{1,0:T(8,128)(2,1)S(1)}, bf16[256,1152]{1,0:T(8,128)(2,1)S(1)}, u32[]{:S(2)}, u32[]{:S(2)}) collective-permute-start(bf16[256,1152]{1,0:T(8,128)(2,1)S(1)} %pack.4.refs_0_), channel_id=1, source_target_pairs={{0,2},{1,3},{2,0},{3,1},{4,6},{5,7},{6,4},{7,5},{8,24},{9,25},{10,... | collective-permute-start | bytes 1769480 | tf_op jit(solution)/shard_map/ppermute | solution.py:25
  8.6 2.5 %collective-permute-start.3 = (bf16[256,1152]{1,0:T(8,128)(2,1)S(1)}, bf16[256,1152]{1,0:T(8,128)(2,1)S(1)}, u32[]{:S(2)}, u32[]{:S(2)}) collective-permute-start(bf16[256,1152]{1,0:T(8,128)(2,1)S(1)} %pack.4.refs_0_), channel_id=1, source_target_pairs={{0,1},{1,0},{2,3},{3,2},{4,5},{5,4},{6,7},{7,6},{8,73},{9,72},{10,... | collective-permute-start | bytes 1769480 | tf_op jit(solution)/shard_map/ppermute | solution.py:25
  11.1 2.2 %collective-permute-start.1 = (bf16[256,1152]{1,0:T(8,128)(2,1)S(1)}, bf16[256,1152]{1,0:T(8,128)(2,1)S(1)}, u32[]{:S(2)}, u32[]{:S(2)}) collective-permute-start(bf16[256,1152]{1,0:T(8,128)(2,1)S(1)} %pack.4.refs_0_), channel_id=1, source_target_pairs={{0,6},{1,7},{2,4},{3,5},{4,2},{5,3},{6,0},{7,1},{8,56},{9,57},{10,... | collective-permute-start | bytes 1769480 | tf_op jit(solution)/shard_map/ppermute | solution.py:25
  13.3 2.8 %collective-permute-done.5.refs_2_ = bf16[256,1152]{1,0:T(8,128)(2,1)S(1)} collective-permute-done((bf16[256,1152]{1,0:T(8,128)(2,1)S(1)}, bf16[256,1152]{1,0:T(8,128)(2,1)S(1)}, u32[]{:S(2)}, u32[]{:S(2)}) %collective-permute-start.5) | collective-permute-done | bytes 589856 | tf_op jit(solution)/shard_map/ppermute | solution.py:25
  16.1 2.7 %collective-permute-done.3.refs_1_ = bf16[256,1152]{1,0:T(8,128)(2,1)S(1)} collective-permute-done((bf16[256,1152]{1,0:T(8,128)(2,1)S(1)}, bf16[256,1152]{1,0:T(8,128)(2,1)S(1)}, u32[]{:S(2)}, u32[]{:S(2)}) %collective-permute-start.3) | collective-permute-done | bytes 589856 | tf_op jit(solution)/shard_map/ppermute | solution.py:25
  18.8 2.3 %collective-permute-done.1.refs_3_ = bf16[256,1152]{1,0:T(8,128)(2,1)S(1)} collective-permute-done((bf16[256,1152]{1,0:T(8,128)(2,1)S(1)}, bf16[256,1152]{1,0:T(8,128)(2,1)S(1)}, u32[]{:S(2)}, u32[]{:S(2)}) %collective-permute-start.1) | collective-permute-done | bytes 589856 | tf_op jit(solution)/shard_map/ppermute | solution.py:25
  21.7 1.8 %collective-permute-start.6 = (bf16[256,1152]{1,0:T(8,128)(2,1)S(1)}, bf16[256,1152]{1,0:T(8,128)(2,1)S(1)}, u32[]{:S(2)}, u32[]{:S(2)}) collective-permute-start(bf16[256,1152]{1,0:T(8,128)(2,1)S(1)} %collective-permute-done.5.refs_2_), channel_id=1, source_target_pairs={{0,1},{1,0},{2,3},{3,2},{4,5},{5,4},{6,7},{7,6},{8,73},{9,72},{10,... | collective-permute-start | bytes 1769480 | tf_op jit(solution)/shard_map/ppermute | solution.py:25
  23.6 3.8 %collective-permute-start.4 = (bf16[256,1152]{1,0:T(8,128)(2,1)S(1)}, bf16[256,1152]{1,0:T(8,128)(2,1)S(1)}, u32[]{:S(2)}, u32[]{:S(2)}) collective-permute-start(bf16[256,1152]{1,0:T(8,128)(2,1)S(1)} %collective-permute-done.3.refs_1_), channel_id=1, source_target_pairs={{0,6},{1,7},{2,4},{3,5},{4,2},{5,3},{6,0},{7,1},{8,56},{9,57},{10,... | collective-permute-start | bytes 1769480 | tf_op jit(solution)/shard_map/ppermute | solution.py:25
  28.6 3.5 %tile_near.1 = (bf16[512,1152]{1,0:T(8,128)(2,1)S(1)}, bf16[1024,1152]{1,0:T(8,128)(2,1)S(1)}, bf16[512,1024]{1,0:T(8,128)(2,1)S(1)}, f32[512,1152]{1,0:T(8,128)S(1)}, f32[8,128]{1,0:T(8,128)S(1)}) custom-call(s32[1]{0:T(128)} %bitcast.core_ref.refs_0_, f32[8,128]{1,0:T(8,128)S(1)} %broadcast_in_dim.15.sharp_ref, f32[8,128]{1,0:T(8,128)S(1)} %broadcast_in_dim.17.bias_ref, ...), custom_call_target="tpu_custom_call" | custom-call | flops 2415919104 | bytes 4718592 | tf_op jit(solution)/shard_map/tile_near/pallas_call | solution.py:260
  32.2 2.4 %collective-permute-done.4.refs_0_.refs_2_ = bf16[256,1152]{1,0:T(8,128)(2,1)S(1)} collective-permute-done((bf16[256,1152]{1,0:T(8,128)(2,1)S(1)}, bf16[256,1152]{1,0:T(8,128)(2,1)S(1)}, u32[]{:S(2)}, u32[]{:S(2)}) %collective-permute-start.4) | collective-permute-done | bytes 589856 | tf_op jit(solution)/shard_map/ppermute | solution.py:25
  34.6 1.5 %collective-permute-done.2.refs_0_ = bf16[256,1152]{1,0:T(8,128)(2,1)S(1)} collective-permute-done((bf16[256,1152]{1,0:T(8,128)(2,1)S(1)}, bf16[256,1152]{1,0:T(8,128)(2,1)S(1)}, u32[]{:S(2)}, u32[]{:S(2)}) %collective-permute-start.2) | collective-permute-done | bytes 589856 | tf_op jit(solution)/shard_map/ppermute | solution.py:25
  36.3 2.2 %collective-permute-start.9 = (bf16[128,1152]{1,0:T(8,128)(2,1)S(1)}, bf16[128,1152]{1,0:T(8,128)(2,1)S(1)}, u32[]{:S(2)}, u32[]{:S(2)}) collective-permute-start(bf16[128,1152]{1,0:T(8,128)(2,1)S(1)} %half_of.3), channel_id=1, source_target_pairs={{0,6},{1,7},{2,4},{3,5},{4,2},{5,3},{6,0},{7,1},{8,56},{9,57},{10,... | collective-permute-start | bytes 884744 | tf_op jit(solution)/shard_map/ppermute | solution.py:25
  38.5 1.4 %collective-permute-done.10.received_ref.far_received_ref = bf16[768,1152]{1,0:T(8,128)(2,1)S(1)} collective-permute-done((bf16[768,1152]{1,0:T(8,128)(2,1)S(1)}, bf16[768,1152]{1,0:T(8,128)(2,1)S(1)}, u32[]{:S(2)}, u32[]{:S(2)}) %collective-permute-start.10) | collective-permute-done | bytes 1769504 | tf_op jit(solution)/shard_map/ppermute | solution.py:25
  39.9 1.8 %tile_middle.1 = (bf16[256,1152]{1,0:T(8,128)(2,1)S(1)}, bf16[256,1024]{1,0:T(8,128)(2,1)S(1)}, f32[256,1152]{1,0:T(8,128)S(1)}, f32[8,128]{1,0:T(8,128)S(1)}) custom-call(s32[1]{0:T(128)} %bitcast.core_ref.refs_0_, f32[8,128]{1,0:T(8,128)S(1)} %broadcast_in_dim.15.sharp_ref, f32[8,128]{1,0:T(8,128)S(1)} %broadcast_in_dim.17.bias_ref, ...), custom_call_target="tpu_custom_call" | custom-call | flops 1207959552 | bytes 5898240 | tf_op jit(solution)/shard_map/tile_middle/pallas_call | solution.py:260
  41.8 4.0 %tile_far.1 = (bf16[768,1152]{1,0:T(8,128)(2,1)S(1)}, bf16[768,1152]{1,0:T(8,128)(2,1)S(1)}, bf16[768,1024]{1,0:T(8,128)(2,1)S(1)}, bf16[768,768]{1,0:T(8,128)(2...) custom-call(s32[1]{0:T(128)} %bitcast.core_ref.refs_0_, f32[8,128]{1,0:T(8,128)S(1)} %broadcast_in_dim.15.sharp_ref, ...), custom_call_target="tpu_custom_call" | custom-call | flops 2717908992 | bytes 8650752 | tf_op jit(solution)/shard_map/tile_far/pallas_call | solution.py:260
  46.1 1.9 %collective-permute-done.11.received_ref = bf16[256,1152]{1,0:T(8,128)(2,1)S(1)} collective-permute-done((bf16[256,1152]{1,0:T(8,128)(2,1)S(1)}, bf16[256,1152]{1,0:T(8,128)(2,1)S(1)}, u32[]{:S(2)}, u32[]{:S(2)}) %collective-permute-start.11) | collective-permute-done | bytes 589856 | tf_op jit(solution)/shard_map/ppermute | solution.py:25
  48.0 4.7 %tile_last.1 = (bf16[768,256]{1,0:T(8,128)(2,1)S(1)}, f32[768,1152]{1,0:T(8,128)S(1)}, bf16[256,1152]{1,0:T(8,128)(2,1)S(1)}, bf16[256,1024]{1,0:T(8,128)(2,1)S(...) custom-call(s32[1]{0:T(128)} %bitcast.core_ref.refs_0_, ...), custom_call_target="tpu_custom_call" | custom-call | flops 3321888768 | bytes 12386304 | tf_op jit(solution)/shard_map/tile_last/pallas_call | solution.py:260
  53.4 0.9 fusion.5
  54.3 0.9 collective-permute-done.12
  55.2 1.1 %collective-permute-start.14 = (f32[8,128]{1,0:T(8,128)S(1)}, f32[8,128]{1,0:T(8,128)S(1)}, u32[]{:S(2)}, u32[]{:S(2)}) collective-permute-start(f32[8,128]{1,0:T(8,128)S(1)} %add.40), channel_id=1, source_target_pairs={{0,65},{1,64},{2,67},{3,66},{4,69},{5,68},{6,71},{7,70},{8,73},{9,... | collective-permute-start | bytes 12296 | tf_op jit(solution)/shard_map/ppermute | solution.py:25
  56.3 1.6 %collective-permute-start.13 = (bf16[256,1152]{1,0:T(8,128)(2,1)S(1)}, bf16[256,1152]{1,0:T(8,128)(2,1)S(1)}, u32[]{:S(2)}, u32[]{:S(2)}) collective-permute-start(bf16[256,1152]{1,0:T(8,128)(2,1)S(1)} %get-tuple-element.102), channel_id=1, source_target_pairs={{0,8},{1,9},{2,10},{3,11},{4,12},{5,13},{6,14},{7,15},{8,0},{9,1},... | collective-permute-start | bytes 1769480 | tf_op jit(solution)/shard_map/ppermute | solution.py:25
  58.6 2.4 %fusion.3 = (bf16[768,1152]{1,0:T(8,128)(2,1)S(1)}, f32[768,1152]{1,0:T(8,128)S(1)}) fusion(f32[768,1152]{1,0:T(8,128)S(1)} %get-tuple-element.103.img_ref, pred[]{:T(512)S(6)} %eq.3, f32[768,1152]{1,0:T(8,128)S(1)} %fusion.7, bf16[768,768]{1,0:T(8,128)(2,1)S(1)} %get-tuple-element.104, bf16[768,1152]{1,0:T(8,128)(2,1)S(1)} %get-tuple-element.89.img_ref), kind=kOutput, calls=%fused_computation.9 | convolution fusion | flops 1367801856 | bytes 15335425 | tf_op jit(solution)/shard_map/dot_general | solution.py:425
  61.3 0.9 collective-permute-start.17
  63.4 2.1 %collective-permute-start.16 = (bf16[128,1152]{1,0:T(8,128)(2,1)S(1)}, bf16[128,1152]{1,0:T(8,128)(2,1)S(1)}, u32[]{:S(2)}, u32[]{:S(2)}) collective-permute-start(bf16[128,1152]{1,0:T(8,128)(2,1)S(1)} %get-tuple-element.114), channel_id=1, source_target_pairs={{0,6},{1,7},{2,4},{3,5},{4,2},{5,3},{6,0},{7,1},{8,56},{9,57},{10,... | collective-permute-start | bytes 884744 | tf_op jit(solution)/shard_map/ppermute | solution.py:25
  65.4 0.9 fusion.8
  66.3 3.0 %fusion.1 = (bf16[1024,1152]{1,0:T(8,128)(2,1)S(1)}, f32[1024,1152]{1,0:T(8,128)S(1)}) fusion(f32[1024,1152]{1,0:T(8,128)S(1)} %fusion.8, bf16[768,1024]{1,0:T(8,128)(2,1)S(1)} %get-tuple-element.116, bf16[768,1152]{1,0:T(8,128)(2,1)S(1)} %get-tuple-element.89.img_ref), kind=kOutput, calls=%fused_computation.5 | convolution fusion | flops 1822556160 | bytes 15138816 | tf_op jit(solution)/shard_map/dot_general | solution.py:425
  70.5 1.2 %far.1 = (bf16[256,1152]{1,0:T(8,128)(2,1)S(1)}, bf16[256,1152]{1,0:T(8,128)(2,1)S(1)}) custom-call(s32[1]{0:T(128)} %bitcast.core_ref.refs_0_, f32[768,1152]{1,0:T(8,128)S(1)} %get-tuple-element.142.txt_ref, bf16[768,1152]{1,0:T(8,128)(2,1)S(1)} %collective-permute-done.17.received_ref.txt_received_ref.img_received_ref, ...), custom_call_target="tpu_custom_call" | custom-call | tf_op jit(solution)/shard_map/far/pallas_call | solution.py:278
  71.7 2.5 %collective-permute-start.20 = (bf16[1024,1152]{1,0:T(8,128)(2,1)S(1)}, bf16[1024,1152]{1,0:T(8,128)(2,1)S(1)}, u32[]{:S(2)}, u32[]{:S(2)}) collective-permute-start(bf16[1024,1152]{1,0:T(8,128)(2,1)S(1)} %get-tuple-element.125), channel_id=1, source_target_pairs={{0,8},{1,9},{2,10},{3,11},{4,12},{5,13},{6,14},{7,15},{8,0},{9,1},... | collective-permute-start | bytes 7077896 | tf_op jit(solution)/shard_map/ppermute | solution.py:25
  74.2 1.2 %collective-permute-start.19 = (bf16[256,1152]{1,0:T(8,128)(2,1)S(1)}, bf16[256,1152]{1,0:T(8,128)(2,1)S(1)}, u32[]{:S(2)}, u32[]{:S(2)}) collective-permute-start(bf16[256,1152]{1,0:T(8,128)(2,1)S(1)} %second.1), channel_id=1, source_target_pairs={{0,2},{1,3},{2,0},{3,1},{4,6},{5,7},{6,4},{7,5},{8,24},{9,25},{10,... | collective-permute-start | bytes 1769480 | tf_op jit(solution)/shard_map/ppermute | solution.py:25
  75.4 1.3 %collective-permute-start.22 = (bf16[256,1152]{1,0:T(8,128)(2,1)S(1)}, bf16[256,1152]{1,0:T(8,128)(2,1)S(1)}, u32[]{:S(2)}, u32[]{:S(2)}) collective-permute-start(bf16[256,1152]{1,0:T(8,128)(2,1)S(1)} %get-tuple-element.130), channel_id=1, source_target_pairs={{0,1},{1,0},{2,3},{3,2},{4,5},{5,4},{6,7},{7,6},{8,73},{9,72},{10,... | collective-permute-start | bytes 1769480 | tf_op jit(solution)/shard_map/ppermute | solution.py:25
  76.7 2.1 %collective-permute-start.25 = (bf16[256,1152]{1,0:T(8,128)(2,1)S(1)}, bf16[256,1152]{1,0:T(8,128)(2,1)S(1)}, u32[]{:S(2)}, u32[]{:S(2)}) collective-permute-start(bf16[256,1152]{1,0:T(8,128)(2,1)S(1)} %get-tuple-element.132), channel_id=1, source_target_pairs={{0,6},{1,7},{2,4},{3,5},{4,2},{5,3},{6,0},{7,1},{8,56},{9,57},{10,... | collective-permute-start | bytes 1769480 | tf_op jit(solution)/shard_map/ppermute | solution.py:25
  78.8 1.0 base.1.refs_1_.base_ref
  79.8 1.8 %collective-permute-start.21 = (f32[8,128]{1,0:T(8,128)S(1)}, f32[8,128]{1,0:T(8,128)S(1)}, u32[]{:S(2)}, u32[]{:S(2)}) collective-permute-start(f32[8,128]{1,0:T(8,128)S(1)} %add.44), channel_id=1, source_target_pairs={{0,6},{1,7},{2,4},{3,5},{4,2},{5,3},{6,0},{7,1},{8,14},{9,15},{10,... | collective-permute-start | bytes 12296 | tf_op jit(solution)/shard_map/ppermute | solution.py:25
  81.6 2.6 %collective-permute-done.21 = f32[8,128]{1,0:T(8,128)S(1)} collective-permute-done((f32[8,128]{1,0:T(8,128)S(1)}, f32[8,128]{1,0:T(8,128)S(1)}, u32[]{:S(2)}, u32[]{:S(2)}) %collective-permute-start.21) | collective-permute-done | bytes 4128 | tf_op jit(solution)/shard_map/ppermute | solution.py:25
  84.2 0.8 near.4
  87.5 1.4 %collective-permute-start.26 = (bf16[256,1152]{1,0:T(8,128)(2,1)S(1)}, bf16[256,1152]{1,0:T(8,128)(2,1)S(1)}, u32[]{:S(2)}, u32[]{:S(2)}) collective-permute-start(bf16[256,1152]{1,0:T(8,128)(2,1)S(1)} %near.5), channel_id=1, source_target_pairs={{0,1},{1,0},{2,3},{3,2},{4,5},{5,4},{6,7},{7,6},{8,73},{9,72},{10,... | collective-permute-start | bytes 1769480 | tf_op jit(solution)/shard_map/ppermute | solution.py:25
  88.9 2.8 %collective-permute-start.24 = (bf16[256,1152]{1,0:T(8,128)(2,1)S(1)}, bf16[256,1152]{1,0:T(8,128)(2,1)S(1)}, u32[]{:S(2)}, u32[]{:S(2)}) collective-permute-start(bf16[256,1152]{1,0:T(8,128)(2,1)S(1)} %near.4), channel_id=1, source_target_pairs={{0,6},{1,7},{2,4},{3,5},{4,2},{5,3},{6,0},{7,1},{8,56},{9,57},{10,... | collective-permute-start | bytes 1769480 | tf_op jit(solution)/shard_map/ppermute | solution.py:25
  91.8 3.5 %collective-permute-done.27 = f32[8,128]{1,0:T(8,128)S(1)} collective-permute-done((f32[8,128]{1,0:T(8,128)S(1)}, f32[8,128]{1,0:T(8,128)S(1)}, u32[]{:S(2)}, u32[]{:S(2)}) %collective-permute-start.27) | collective-permute-done | bytes 4128 | tf_op jit(solution)/shard_map/ppermute | solution.py:25
  95.3 2.4 %collective-permute-start.28 = (f32[8,128]{1,0:T(8,128)S(1)}, f32[8,128]{1,0:T(8,128)S(1)}, u32[]{:S(2)}, u32[]{:S(2)}) collective-permute-start(f32[8,128]{1,0:T(8,128)S(1)} %add.46), channel_id=1, source_target_pairs={{0,48},{1,49},{2,50},{3,51},{4,52},{5,53},{6,54},{7,55},{8,56},{9,... | collective-permute-start | bytes 12296 | tf_op jit(solution)/shard_map/ppermute | solution.py:25
  97.6 1.7 %collective-permute-done.28 = f32[8,128]{1,0:T(8,128)S(1)} collective-permute-done((f32[8,128]{1,0:T(8,128)S(1)}, f32[8,128]{1,0:T(8,128)S(1)}, u32[]{:S(2)}, u32[]{:S(2)}) %collective-permute-start.28) | collective-permute-done | bytes 4128 | tf_op jit(solution)/shard_map/ppermute | solution.py:25
  99.4 1.3 %gather_sums.1 = (f32[128,1152]{1,0:T(8,128)S(1)}, f32[136,1152]{1,0:T(8,128)S(1)}) custom-call(s32[1]{0:T(128)} %bitcast.core_ref.refs_0_, f32[1024,1152]{1,0:T(8,128)S(1)} %base.1.refs_1_.base_ref, bf16[256,1152]{1,0:T(8,128)(2,1)S(1)} %collective-permute-done.23.a_ref, bf16[256,1152]{1,0:T(8,128)(2,1)S(1)} %collective-permute-done.24.b_ref, ...), custom_call_target="tpu_custom_call" | custom-call | tf_op jit(solution)/shard_map/gather_sums/pallas_call | solution.py:278
  100.7 2.5 %collective-permute-start.29 = (f32[136,1152]{1,0:T(8,128)S(1)}, f32[136,1152]{1,0:T(8,128)S(1)}, u32[]{:S(2)}, u32[]{:S(2)}) collective-permute-start(f32[136,1152]{1,0:T(8,128)S(1)} %get-tuple-element.135), channel_id=1, source_target_pairs={{0,8},{1,9},{2,10},{3,11},{4,12},{5,13},{6,14},{7,15},{8,0},{9,1},... | collective-permute-start | bytes 1880072 | tf_op jit(solution)/shard_map/ppermute | solution.py:25
  103.2 1.7 %collective-permute-done.29.refs_4_ = f32[136,1152]{1,0:T(8,128)S(1)} collective-permute-done((f32[136,1152]{1,0:T(8,128)S(1)}, f32[136,1152]{1,0:T(8,128)S(1)}, u32[]{:S(2)}, u32[]{:S(2)}) %collective-permute-start.29) | collective-permute-done | bytes 626720 | tf_op jit(solution)/shard_map/ppermute | solution.py:25
  104.9 1.7 %finish.1 = (f32[1,1]{1,0:T(1,128)}, f32[128,1152]{1,0:T(8,128)}, f32[128,1152]{1,0:T(8,128)}) custom-call(s32[1]{0:T(128)} %bitcast.core_ref.refs_0_, f32[128,1152]{1,0:T(8,128)S(1)} %copy-done, f32[128,1152]{1,0:T(8,128)S(1)} %copy-done.1, f32[128,1152]{1,0:T(8,128)S(1)} %get-tuple-element.134.refs_3_, f32[136,1152]{1,0:T(8,128)S(1)} %collective-permute-done.29.refs_4_, ...), custom_call_target="tpu_custom_call" | custom-call | tf_op jit(solution)/shard_map/finish/pallas_call | solution.py:278
  (53 shorter events, 7.7 us)
Async XLA Ops:
  2.8 2.9 %collective-permute-start = (bf16[128,1152]{1,0:T(8,128)(2,1)}, bf16[128,1152]{1,0:T(8,128)(2,1)S(1)}, u32[]{:S(2)}, u32[]{:S(2)}) collective-permute-start(bf16[128,1152]{1,0:T(8,128)(2,1)} %get-tuple-element.73), channel_id=1, source_target_pairs={{0,8},{1,9},{2,10},{3,11},{4,12},{5,13},{6,14},{7,15},{8,0},{9,1},... | collective-permute-start | bytes 884744 | tf_op jit(solution)/shard_map/ppermute | solution.py:25
  5.8 1.0 copy-start.2
  6.8 9.4 %collective-permute-start.5 = (bf16[256,1152]{1,0:T(8,128)(2,1)S(1)}, bf16[256,1152]{1,0:T(8,128)(2,1)S(1)}, u32[]{:S(2)}, u32[]{:S(2)}) collective-permute-start(bf16[256,1152]{1,0:T(8,128)(2,1)S(1)} %pack.4.refs_0_), channel_id=1, source_target_pairs={{0,2},{1,3},{2,0},{3,1},{4,6},{5,7},{6,4},{7,5},{8,24},{9,25},{10,... | collective-permute-start | bytes 1769480 | tf_op jit(solution)/shard_map/ppermute | solution.py:25
  8.6 10.2 %collective-permute-start.3 = (bf16[256,1152]{1,0:T(8,128)(2,1)S(1)}, bf16[256,1152]{1,0:T(8,128)(2,1)S(1)}, u32[]{:S(2)}, u32[]{:S(2)}) collective-permute-start(bf16[256,1152]{1,0:T(8,128)(2,1)S(1)} %pack.4.refs_0_), channel_id=1, source_target_pairs={{0,1},{1,0},{2,3},{3,2},{4,5},{5,4},{6,7},{7,6},{8,73},{9,72},{10,... | collective-permute-start | bytes 1769480 | tf_op jit(solution)/shard_map/ppermute | solution.py:25
  11.1 10.0 %collective-permute-start.1 = (bf16[256,1152]{1,0:T(8,128)(2,1)S(1)}, bf16[256,1152]{1,0:T(8,128)(2,1)S(1)}, u32[]{:S(2)}, u32[]{:S(2)}) collective-permute-start(bf16[256,1152]{1,0:T(8,128)(2,1)S(1)} %pack.4.refs_0_), channel_id=1, source_target_pairs={{0,6},{1,7},{2,4},{3,5},{4,2},{5,3},{6,0},{7,1},{8,56},{9,57},{10,... | collective-permute-start | bytes 1769480 | tf_op jit(solution)/shard_map/ppermute | solution.py:25
  21.3 7.4 %collective-permute-start.7 = (bf16[1024,1152]{1,0:T(8,128)(2,1)S(1)}, bf16[1024,1152]{1,0:T(8,128)(2,1)S(1)}, u32[]{:S(2)}, u32[]{:S(2)}) collective-permute-start(bf16[1024,1152]{1,0:T(8,128)(2,1)S(1)} %pack.5.near_ref), channel_id=1, source_target_pairs={{0,8},{1,9},{2,10},{3,11},{4,12},{5,13},{6,14},{7,15},{8,0},{9,1},... | collective-permute-start | bytes 7077896 | tf_op jit(solution)/shard_map/ppermute | solution.py:25
  21.7 10.4 %collective-permute-start.6 = (bf16[256,1152]{1,0:T(8,128)(2,1)S(1)}, bf16[256,1152]{1,0:T(8,128)(2,1)S(1)}, u32[]{:S(2)}, u32[]{:S(2)}) collective-permute-start(bf16[256,1152]{1,0:T(8,128)(2,1)S(1)} %collective-permute-done.5.refs_2_), channel_id=1, source_target_pairs={{0,1},{1,0},{2,3},{3,2},{4,5},{5,4},{6,7},{7,6},{8,73},{9,72},{10,... | collective-permute-start | bytes 1769480 | tf_op jit(solution)/shard_map/ppermute | solution.py:25
  23.6 11.0 %collective-permute-start.4 = (bf16[256,1152]{1,0:T(8,128)(2,1)S(1)}, bf16[256,1152]{1,0:T(8,128)(2,1)S(1)}, u32[]{:S(2)}, u32[]{:S(2)}) collective-permute-start(bf16[256,1152]{1,0:T(8,128)(2,1)S(1)} %collective-permute-done.3.refs_1_), channel_id=1, source_target_pairs={{0,6},{1,7},{2,4},{3,5},{4,2},{5,3},{6,0},{7,1},{8,56},{9,57},{10,... | collective-permute-start | bytes 1769480 | tf_op jit(solution)/shard_map/ppermute | solution.py:25
  27.3 8.7 %collective-permute-start.2 = (bf16[256,1152]{1,0:T(8,128)(2,1)S(1)}, bf16[256,1152]{1,0:T(8,128)(2,1)S(1)}, u32[]{:S(2)}, u32[]{:S(2)}) collective-permute-start(bf16[256,1152]{1,0:T(8,128)(2,1)S(1)} %collective-permute-done.1.refs_3_), channel_id=1, source_target_pairs={{0,2},{1,3},{2,0},{3,1},{4,6},{5,7},{6,4},{7,5},{8,24},{9,25},{10,... | collective-permute-start | bytes 1769480 | tf_op jit(solution)/shard_map/ppermute | solution.py:25
  36.2 3.8 %collective-permute-start.10 = (bf16[768,1152]{1,0:T(8,128)(2,1)S(1)}, bf16[768,1152]{1,0:T(8,128)(2,1)S(1)}, u32[]{:S(2)}, u32[]{:S(2)}) collective-permute-start(bf16[768,1152]{1,0:T(8,128)(2,1)S(1)} %pack.6.far_ref), channel_id=1, source_target_pairs={{0,8},{1,9},{2,10},{3,11},{4,12},{5,13},{6,14},{7,15},{8,0},{9,1},... | collective-permute-start | bytes 5308424 | tf_op jit(solution)/shard_map/ppermute | solution.py:25
  36.3 9.5 %collective-permute-start.9 = (bf16[128,1152]{1,0:T(8,128)(2,1)S(1)}, bf16[128,1152]{1,0:T(8,128)(2,1)S(1)}, u32[]{:S(2)}, u32[]{:S(2)}) collective-permute-start(bf16[128,1152]{1,0:T(8,128)(2,1)S(1)} %half_of.3), channel_id=1, source_target_pairs={{0,6},{1,7},{2,4},{3,5},{4,2},{5,3},{6,0},{7,1},{8,56},{9,57},{10,... | collective-permute-start | bytes 884744 | tf_op jit(solution)/shard_map/ppermute | solution.py:25
  38.5 7.3 %collective-permute-start.8 = (bf16[128,1152]{1,0:T(8,128)(2,1)S(1)}, bf16[128,1152]{1,0:T(8,128)(2,1)S(1)}, u32[]{:S(2)}, u32[]{:S(2)}) collective-permute-start(bf16[128,1152]{1,0:T(8,128)(2,1)S(1)} %half_of.2), channel_id=1, source_target_pairs={{0,2},{1,3},{2,0},{3,1},{4,6},{5,7},{6,4},{7,5},{8,24},{9,25},{10,... | collective-permute-start | bytes 884744 | tf_op jit(solution)/shard_map/ppermute | solution.py:25
  45.9 2.1 %collective-permute-start.11 = (bf16[256,1152]{1,0:T(8,128)(2,1)S(1)}, bf16[256,1152]{1,0:T(8,128)(2,1)S(1)}, u32[]{:S(2)}, u32[]{:S(2)}) collective-permute-start(bf16[256,1152]{1,0:T(8,128)(2,1)S(1)} %pack.7.last_ref), channel_id=1, source_target_pairs={{0,8},{1,9},{2,10},{3,11},{4,12},{5,13},{6,14},{7,15},{8,0},{9,1},... | collective-permute-start | bytes 1769480 | tf_op jit(solution)/shard_map/ppermute | solution.py:25
  52.7 2.5 %collective-permute-start.12 = (f32[8,128]{1,0:T(8,128)S(1)}, f32[8,128]{1,0:T(8,128)S(1)}, u32[]{:S(2)}, u32[]{:S(2)}) collective-permute-start(f32[8,128]{1,0:T(8,128)S(1)} %add_add_fusion), channel_id=1, source_target_pairs={{0,1},{1,0},{2,3},{3,2},{4,5},{5,4},{6,7},{7,6},{8,9},{9,8},{10,11... | collective-permute-start | bytes 12296 | tf_op jit(solution)/shard_map/ppermute | solution.py:25
  55.2 5.8 %collective-permute-start.14 = (f32[8,128]{1,0:T(8,128)S(1)}, f32[8,128]{1,0:T(8,128)S(1)}, u32[]{:S(2)}, u32[]{:S(2)}) collective-permute-start(f32[8,128]{1,0:T(8,128)S(1)} %add.40), channel_id=1, source_target_pairs={{0,65},{1,64},{2,67},{3,66},{4,69},{5,68},{6,71},{7,70},{8,73},{9,... | collective-permute-start | bytes 12296 | tf_op jit(solution)/shard_map/ppermute | solution.py:25
  56.3 4.8 %collective-permute-start.13 = (bf16[256,1152]{1,0:T(8,128)(2,1)S(1)}, bf16[256,1152]{1,0:T(8,128)(2,1)S(1)}, u32[]{:S(2)}, u32[]{:S(2)}) collective-permute-start(bf16[256,1152]{1,0:T(8,128)(2,1)S(1)} %get-tuple-element.102), channel_id=1, source_target_pairs={{0,8},{1,9},{2,10},{3,11},{4,12},{5,13},{6,14},{7,15},{8,0},{9,1},... | collective-permute-start | bytes 1769480 | tf_op jit(solution)/shard_map/ppermute | solution.py:25
  61.3 8.1 %collective-permute-start.17 = (bf16[768,1152]{1,0:T(8,128)(2,1)S(1)}, bf16[768,1152]{1,0:T(8,128)(2,1)S(1)}, u32[]{:S(2)}, u32[]{:S(2)}) collective-permute-start(bf16[768,1152]{1,0:T(8,128)(2,1)S(1)} %get-tuple-element.115), channel_id=1, source_target_pairs={{0,8},{1,9},{2,10},{3,11},{4,12},{5,13},{6,14},{7,15},{8,0},{9,1},... | collective-permute-start | bytes 5308424 | tf_op jit(solution)/shard_map/ppermute | solution.py:25
  62.2 7.2 %collective-permute-start.18 = (f32[8,128]{1,0:T(8,128)S(1)}, f32[8,128]{1,0:T(8,128)S(1)}, u32[]{:S(2)}, u32[]{:S(2)}) collective-permute-start(f32[8,128]{1,0:T(8,128)S(1)} %add.42), channel_id=1, source_target_pairs={{0,2},{1,3},{2,0},{3,1},{4,6},{5,7},{6,4},{7,5},{8,10},{9,11},{10,... | collective-permute-start | bytes 12296 | tf_op jit(solution)/shard_map/ppermute | solution.py:25
  62.9 7.2 %collective-permute-start.15 = (bf16[128,1152]{1,0:T(8,128)(2,1)S(1)}, bf16[128,1152]{1,0:T(8,128)(2,1)S(1)}, u32[]{:S(2)}, u32[]{:S(2)}) collective-permute-start(bf16[128,1152]{1,0:T(8,128)(2,1)S(1)} %get-tuple-element.113), channel_id=1, source_target_pairs={{0,2},{1,3},{2,0},{3,1},{4,6},{5,7},{6,4},{7,5},{8,24},{9,25},{10,... | collective-permute-start | bytes 884744 | tf_op jit(solution)/shard_map/ppermute | solution.py:25
  63.4 7.1 %collective-permute-start.16 = (bf16[128,1152]{1,0:T(8,128)(2,1)S(1)}, bf16[128,1152]{1,0:T(8,128)(2,1)S(1)}, u32[]{:S(2)}, u32[]{:S(2)}) collective-permute-start(bf16[128,1152]{1,0:T(8,128)(2,1)S(1)} %get-tuple-element.114), channel_id=1, source_target_pairs={{0,6},{1,7},{2,4},{3,5},{4,2},{5,3},{6,0},{7,1},{8,56},{9,57},{10,... | collective-permute-start | bytes 884744 | tf_op jit(solution)/shard_map/ppermute | solution.py:25
  71.7 7.1 %collective-permute-start.20 = (bf16[1024,1152]{1,0:T(8,128)(2,1)S(1)}, bf16[1024,1152]{1,0:T(8,128)(2,1)S(1)}, u32[]{:S(2)}, u32[]{:S(2)}) collective-permute-start(bf16[1024,1152]{1,0:T(8,128)(2,1)S(1)} %get-tuple-element.125), channel_id=1, source_target_pairs={{0,8},{1,9},{2,10},{3,11},{4,12},{5,13},{6,14},{7,15},{8,0},{9,1},... | collective-permute-start | bytes 7077896 | tf_op jit(solution)/shard_map/ppermute | solution.py:25
  74.2 10.0 %collective-permute-start.19 = (bf16[256,1152]{1,0:T(8,128)(2,1)S(1)}, bf16[256,1152]{1,0:T(8,128)(2,1)S(1)}, u32[]{:S(2)}, u32[]{:S(2)}) collective-permute-start(bf16[256,1152]{1,0:T(8,128)(2,1)S(1)} %second.1), channel_id=1, source_target_pairs={{0,2},{1,3},{2,0},{3,1},{4,6},{5,7},{6,4},{7,5},{8,24},{9,25},{10,... | collective-permute-start | bytes 1769480 | tf_op jit(solution)/shard_map/ppermute | solution.py:25
  75.4 10.0 %collective-permute-start.22 = (bf16[256,1152]{1,0:T(8,128)(2,1)S(1)}, bf16[256,1152]{1,0:T(8,128)(2,1)S(1)}, u32[]{:S(2)}, u32[]{:S(2)}) collective-permute-start(bf16[256,1152]{1,0:T(8,128)(2,1)S(1)} %get-tuple-element.130), channel_id=1, source_target_pairs={{0,1},{1,0},{2,3},{3,2},{4,5},{5,4},{6,7},{7,6},{8,73},{9,72},{10,... | collective-permute-start | bytes 1769480 | tf_op jit(solution)/shard_map/ppermute | solution.py:25
  76.7 10.0 %collective-permute-start.25 = (bf16[256,1152]{1,0:T(8,128)(2,1)S(1)}, bf16[256,1152]{1,0:T(8,128)(2,1)S(1)}, u32[]{:S(2)}, u32[]{:S(2)}) collective-permute-start(bf16[256,1152]{1,0:T(8,128)(2,1)S(1)} %get-tuple-element.132), channel_id=1, source_target_pairs={{0,6},{1,7},{2,4},{3,5},{4,2},{5,3},{6,0},{7,1},{8,56},{9,57},{10,... | collective-permute-start | bytes 1769480 | tf_op jit(solution)/shard_map/ppermute | solution.py:25
  79.8 4.4 %collective-permute-start.21 = (f32[8,128]{1,0:T(8,128)S(1)}, f32[8,128]{1,0:T(8,128)S(1)}, u32[]{:S(2)}, u32[]{:S(2)}) collective-permute-start(f32[8,128]{1,0:T(8,128)S(1)} %add.44), channel_id=1, source_target_pairs={{0,6},{1,7},{2,4},{3,5},{4,2},{5,3},{6,0},{7,1},{8,14},{9,15},{10,... | collective-permute-start | bytes 12296 | tf_op jit(solution)/shard_map/ppermute | solution.py:25
  86.1 13.3 %collective-permute-start.23 = (bf16[256,1152]{1,0:T(8,128)(2,1)S(1)}, bf16[256,1152]{1,0:T(8,128)(2,1)S(1)}, u32[]{:S(2)}, u32[]{:S(2)}) collective-permute-start(bf16[256,1152]{1,0:T(8,128)(2,1)S(1)} %near.3), channel_id=1, source_target_pairs={{0,2},{1,3},{2,0},{3,1},{4,6},{5,7},{6,4},{7,5},{8,24},{9,25},{10,... | collective-permute-start | bytes 1769480 | tf_op jit(solution)/shard_map/ppermute | solution.py:25
  87.5 11.9 %collective-permute-start.26 = (bf16[256,1152]{1,0:T(8,128)(2,1)S(1)}, bf16[256,1152]{1,0:T(8,128)(2,1)S(1)}, u32[]{:S(2)}, u32[]{:S(2)}) collective-permute-start(bf16[256,1152]{1,0:T(8,128)(2,1)S(1)} %near.5), channel_id=1, source_target_pairs={{0,1},{1,0},{2,3},{3,2},{4,5},{5,4},{6,7},{7,6},{8,73},{9,72},{10,... | collective-permute-start | bytes 1769480 | tf_op jit(solution)/shard_map/ppermute | solution.py:25
  88.9 10.5 %collective-permute-start.24 = (bf16[256,1152]{1,0:T(8,128)(2,1)S(1)}, bf16[256,1152]{1,0:T(8,128)(2,1)S(1)}, u32[]{:S(2)}, u32[]{:S(2)}) collective-permute-start(bf16[256,1152]{1,0:T(8,128)(2,1)S(1)} %near.4), channel_id=1, source_target_pairs={{0,6},{1,7},{2,4},{3,5},{4,2},{5,3},{6,0},{7,1},{8,56},{9,57},{10,... | collective-permute-start | bytes 1769480 | tf_op jit(solution)/shard_map/ppermute | solution.py:25
  91.8 3.5 %collective-permute-start.27 = (f32[8,128]{1,0:T(8,128)S(1)}, f32[8,128]{1,0:T(8,128)S(1)}, u32[]{:S(2)}, u32[]{:S(2)}) collective-permute-start(f32[8,128]{1,0:T(8,128)S(1)} %add.45), channel_id=1, source_target_pairs={{0,16},{1,17},{2,18},{3,19},{4,20},{5,21},{6,22},{7,23},{8,24},{9,... | collective-permute-start | bytes 12296 | tf_op jit(solution)/shard_map/ppermute | solution.py:25
  95.3 4.1 %collective-permute-start.28 = (f32[8,128]{1,0:T(8,128)S(1)}, f32[8,128]{1,0:T(8,128)S(1)}, u32[]{:S(2)}, u32[]{:S(2)}) collective-permute-start(f32[8,128]{1,0:T(8,128)S(1)} %add.46), channel_id=1, source_target_pairs={{0,48},{1,49},{2,50},{3,51},{4,52},{5,53},{6,54},{7,55},{8,56},{9,... | collective-permute-start | bytes 12296 | tf_op jit(solution)/shard_map/ppermute | solution.py:25
  99.4 5.5 %copy-start = (f32[128,1152]{1,0:T(8,128)S(1)}, f32[128,1152]{1,0:T(8,128)}, u32[]{:S(2)}) copy-start(f32[128,1152]{1,0:T(8,128)} %refs_1_.1) | copy-start | bytes 1769476
  99.4 5.5 %copy-start.1 = (f32[128,1152]{1,0:T(8,128)S(1)}, f32[128,1152]{1,0:T(8,128)}, u32[]{:S(2)}) copy-start(f32[128,1152]{1,0:T(8,128)} %refs_2_.1) | copy-start | bytes 1769476
  100.7 4.2 %collective-permute-start.29 = (f32[136,1152]{1,0:T(8,128)S(1)}, f32[136,1152]{1,0:T(8,128)S(1)}, u32[]{:S(2)}, u32[]{:S(2)}) collective-permute-start(f32[136,1152]{1,0:T(8,128)S(1)} %get-tuple-element.135), channel_id=1, source_target_pairs={{0,8},{1,9},{2,10},{3,11},{4,12},{5,13},{6,14},{7,15},{8,0},{9,1},... | collective-permute-start | bytes 1880072 | tf_op jit(solution)/shard_map/ppermute | solution.py:25

commit v4 on v3

--- a/solution.py
+++ b/solution.py
@@ -85,7 +85,7 @@
         in_specs=[SMEM, HBM, HBM],
         out_specs=(VMEM, VMEM),
         scratch_shapes=[pltpu.VMEM((2, *img.shape), jnp.float32), pltpu.SemaphoreType.DMA((2,))],
-        compiler_params=pltpu.CompilerParams(vmem_limit_bytes=59 * MIB),
+        compiler_params=pltpu.CompilerParams(vmem_limit_bytes=6 * MIB),
         name="normalize",
     )(core, img, txt)
 
@@ -198,43 +198,40 @@
     loss_ref[...] = run_tiles(pair, sharp_ref, bias_ref, jobs)
 
 
-def middle_tile_kernel(core_ref, sharp_ref, bias_ref, far_ref, received_ref, txt_ref, img_ref, weights_ref, part_ref, loss_ref):
-    pair = img_ref.shape[0]
-
-    def work(is_first):
-        img_ref[...] = received_ref[:pair] if is_first else far_ref[2 * pair :]
-
-    by_core(core_ref, work)
-    loss_ref[...] = run_tiles(pair, sharp_ref, bias_ref, [(img_ref, [(txt_ref, weights_ref)], None, part_ref, None)])
-
-
 def far_tile_kernel(
-    core_ref, sharp_ref, bias_ref, far_ref, received_ref, near_img_ref, far_img_ref, near_before_ref, far_before_ref,
-    near_weights_ref, middle_weights_ref,
-    txt_ref, img_ref, all_weights_ref, weights_ref, part_ref, loss_ref,
+    core_ref, sharp_ref, bias_ref, far_ref, received_ref, near_img_ref, near_before_ref,
+    txt_ref, img_ref, weights_ref, part_ref, loss_ref,
 ):
-    pair = far_img_ref.shape[0]
+    count = near_img_ref.shape[0]
+    pair = count // 2
 
     def work(is_first):
         txt_ref[...] = far_ref[...] if is_first else received_ref[...]
-
-    by_core(core_ref, work)
-    img_ref[: 2 * pair] = near_img_ref[...]
-    img_ref[2 * pair :] = far_img_ref[...]
-    all_weights_ref[: 2 * pair] = near_weights_ref[...]
-    all_weights_ref[2 * pair :] = middle_weights_ref[...]
+        img_ref[count:] = received_ref[:pair] if is_first else far_ref[count:]
+
+    by_core(core_ref, work)
+    img_ref[:count] = near_img_ref[...]
     jobs = []
-    images = row_blocks(near_img_ref, pair) + [far_img_ref]
-    before = row_blocks(near_before_ref, pair) + [far_before_ref]
-    for k in range(3):
+    before = row_blocks(near_before_ref, pair) + [None]
+    for k, rows in enumerate(row_blocks(img_ref, pair)):
         span = pl.ds(k * pair, pair)
-        jobs.append((images[k], [(txt_ref, weights_ref.at[span])], before[k], part_ref.at[span], None))
+        jobs.append((rows, [(txt_ref, weights_ref.at[span])], before[k], part_ref.at[span], None))
     loss_ref[...] = run_tiles(pair, sharp_ref, bias_ref, jobs)
+
+
+def middle_tile_kernel(
+    core_ref, sharp_ref, bias_ref, img_ref, txt_ref, before_ref, near_weights_ref, weights_ref, part_ref, loss_ref
+):
+    pair = part_ref.shape[0]
+    span = pl.ds(2 * pair, pair)
+    weights_ref[: 2 * pair] = near_weights_ref[...]
+    job = (img_ref.at[span], [(txt_ref, weights_ref.at[span])], before_ref.at[span], part_ref, None)
+    loss_ref[...] = run_tiles(pair, sharp_ref, bias_ref, [job])
 
 
 def last_tile_kernel(
     core_ref, sharp_ref, bias_ref, last_ref, received_ref, far_ref, far_received_ref, near_txt_ref, far_txt_ref,
-    img_ref, before_ref,
+    img_ref, before_ref, middle_before_ref,
     weights_ref, part_ref, img_tail_ref, near_tail_ref, far_tail_ref, last_tail_ref, part_tail_ref, loss_ref, txt_ref,
 ):
     pair = last_ref.shape[0]
@@ -247,9 +244,10 @@
 
     by_core(core_ref, work)
     jobs = []
+    before = row_blocks(before_ref, pair, 2 * pair) + [middle_before_ref]
     for k, rows in enumerate(row_blocks(img_ref, pair)):
         span = pl.ds(k * pair, pair)
-        jobs.append((rows, [(txt_ref, weights_ref.at[span])], before_ref.at[span], part_ref.at[span], None))
+        jobs.append((rows, [(txt_ref, weights_ref.at[span])], before[k], part_ref.at[span], None))
     blocks = [(near_txt_ref, near_tail_ref), (far_txt_ref, far_tail_ref), (txt_ref, last_tail_ref)]
     jobs.append((img_tail_ref, blocks, None, part_tail_ref, None))
     loss_ref[...] = run_tiles(pair, sharp_ref, bias_ref, jobs)
@@ -470,38 +468,37 @@
     last_b = move(half_of(slot_x1, 1), "b")
     far = pack(slot_2, slot_x1, slot_x3)
     far_received = swap(far)
-    far_img, middle_weights, middle_part, middle_loss = tile_call(
+    far_txt, img, far_weights, part, far_loss = tile_call(
+        far_tile_kernel,
+        "tile_far",
+        three * three,
+        scalars,
+        (far, far_received, near_img, near_part),
+        (
+            array(three, jnp.bfloat16),
+            array(three, jnp.bfloat16),
+            array(three, jnp.bfloat16, three),
+            array(three, jnp.float32),
+            losses,
+        ),
+    )
+    last_a, last_b, part = lax.optimization_barrier((last_a, last_b, part))
+    last = pack(last_a, last_b)
+    last_received = swap(last)
+    near_weights, middle_part, middle_loss = tile_call(
         middle_tile_kernel,
         "tile_middle",
         pair * wide,
         scalars,
-        (far, far_received, near_txt),
-        (low_piece, array(pair, jnp.bfloat16, wide), array(pair, jnp.float32), losses),
-    )
-    far_txt, img, near_weights, far_weights, part, far_loss = tile_call(
-        far_tile_kernel,
-        "tile_far",
-        three * three,
-        scalars,
-        (far, far_received, near_img, far_img, near_part, middle_part, near_weights, middle_weights),
-        (
-            array(three, jnp.bfloat16),
-            array(three, jnp.bfloat16),
-            array(three, jnp.bfloat16, wide),
-            array(three, jnp.bfloat16, three),
-            array(three, jnp.float32),
-            losses,
-        ),
-    )
-    last_a, last_b, part = lax.optimization_barrier((last_a, last_b, part))
-    last = pack(last_a, last_b)
-    last_received = swap(last)
+        (img, near_txt, part, near_weights),
+        (array(three, jnp.bfloat16, wide), array(pair, jnp.float32), losses),
+    )
     last_weights, img_part, img_tail, near_tail, far_tail, last_tail, img_part_tail, last_loss = tile_call(
         last_tile_kernel,
         "tile_last",
         three * pair + pair * 2 * wide,
         scalars,
-        (last, last_received, far, far_received, near_txt, far_txt, img, part),
+        (last, last_received, far, far_received, near_txt, far_txt, img, part, middle_part),
         (
             array(three, jnp.bfloat16, pair),
             array(three, jnp.float32),
@@ -559,7 +556,6 @@
     )
     base, loss = lax.optimization_barrier((base, loss))
     loss = loss + swap(loss, 0, 6)
-    second_received, base, loss = lax.optimization_barrier((second_received, base, loss))
 
     def near_slot(k, received):
         (out,) = small_call(

time: 107 us -> 110 us (1.028)
  waiting for transfers between devices: 27.4 us -> 31.3 us
  Pallas kernels: 25.1 us -> 23 us
  local copies, waits for them, and re-layouts: 0.97 us -> 2.14 us
    ppermute x30, waiting for transfers between devices: 27.4 us -> 31.3 us  [exchange(): return lax.ppermute(x, AXES, pairs)]
    pallas_call x1, Pallas kernels: 2.2 us -> 0.54 us  [normalize(): pl.pallas_call(normalize_kernel, out_shape=(low, low), in_specs=[SMEM, HB...]
    unnamed x6 -> x8, local copies, waits for them, and re-layouts: 0.97 us -> 2.13 us
  transfers between devices with their start and end apart: 30 -> 30, of which waited for: 15 -> 16; matrix products, arithmetic and copies ran while one was open for 8% -> 8% of each run, Pallas kernels for 13% -> 12%
where the time goes in v4:
time: 110 us; the launch traced here: 109 us
  starting transfers between devices  42.4 us (39%)
  waiting for transfers between devices  31.3 us (28%)
  Pallas kernels  23 us (21%)
  matrix products  8.31 us (8%)
  between operations  2.25 us (2%)
  local copies, waits for them, and re-layouts  2.14 us (2%)
    ppermute x30, starting transfers between devices, exchange(): return lax.ppermute(x, AXES, pairs)  42.4 us
    ppermute x30, waiting for transfers between devices, exchange(): return lax.ppermute(x, AXES, pairs)  31.3 us
    pallas_call x4, Pallas kernels, tile_call(): pl.pallas_call(kernel, out_shape=outs, in_specs=[SMEM] + [VMEM] * (len(sc...  13.7 us
    pallas_call x9, Pallas kernels, small_call(): pl.pallas_call(kernel, out_shape=outs, in_specs=[SMEM] + [VMEM] * len(arr...  8.41 us
    dot_general x6, matrix products, transposed_product(): lax.dot_general(weights, img, (((0,), (0,)), ((), ())), preferred_element...  8.31 us
  transfers between devices with their start and end apart: 30, of which 16 were waited for; matrix products, arithmetic and copies ran while one was open for 8% of the time, Pallas kernels for 12%

profile of v4, /device:TPU:1, one launch (start us, length us, event | category | flops | bytes accessed | tf_op | source)
XLA Modules:
  0.0 109.5 jit_solution(2854156322889833116)
XLA Ops:
  0.6 1.1 copy-done
  1.7 1.1 copy-done.2
  3.3 1.5 %collective-permute-start = (bf16[128,1152]{1,0:T(8,128)(2,1)S(1)}, bf16[128,1152]{1,0:T(8,128)(2,1)S(1)}, u32[]{:S(2)}, u32[]{:S(2)}) collective-permute-start(bf16[128,1152]{1,0:T(8,128)(2,1)S(1)} %get-tuple-element.68), channel_id=1, source_target_pairs={{0,8},{1,9},{2,10},{3,11},{4,12},{5,13},{6,14},{7,15},{8,0},{9,1},... | collective-permute-start | bytes 884744 | tf_op jit(solution)/shard_map/ppermute | solution.py:25
  4.8 1.2 %collective-permute-done.refs_1_ = bf16[128,1152]{1,0:T(8,128)(2,1)S(1)} collective-permute-done((bf16[128,1152]{1,0:T(8,128)(2,1)S(1)}, bf16[128,1152]{1,0:T(8,128)(2,1)S(1)}, u32[]{:S(2)}, u32[]{:S(2)}) %collective-permute-start) | collective-permute-done | bytes 294944 | tf_op jit(solution)/shard_map/ppermute | solution.py:25
  6.1 1.8 %collective-permute-start.5 = (bf16[256,1152]{1,0:T(8,128)(2,1)S(1)}, bf16[256,1152]{1,0:T(8,128)(2,1)S(1)}, u32[]{:S(2)}, u32[]{:S(2)}) collective-permute-start(bf16[256,1152]{1,0:T(8,128)(2,1)S(1)} %pack.4.refs_0_), channel_id=1, source_target_pairs={{0,2},{1,3},{2,0},{3,1},{4,6},{5,7},{6,4},{7,5},{8,24},{9,25},{10,... | collective-permute-start | bytes 1769480 | tf_op jit(solution)/shard_map/ppermute | solution.py:25
  7.9 2.5 %collective-permute-start.3 = (bf16[256,1152]{1,0:T(8,128)(2,1)S(1)}, bf16[256,1152]{1,0:T(8,128)(2,1)S(1)}, u32[]{:S(2)}, u32[]{:S(2)}) collective-permute-start(bf16[256,1152]{1,0:T(8,128)(2,1)S(1)} %pack.4.refs_0_), channel_id=1, source_target_pairs={{0,1},{1,0},{2,3},{3,2},{4,5},{5,4},{6,7},{7,6},{8,73},{9,72},{10,... | collective-permute-start | bytes 1769480 | tf_op jit(solution)/shard_map/ppermute | solution.py:25
  10.3 2.2 %collective-permute-start.1 = (bf16[256,1152]{1,0:T(8,128)(2,1)S(1)}, bf16[256,1152]{1,0:T(8,128)(2,1)S(1)}, u32[]{:S(2)}, u32[]{:S(2)}) collective-permute-start(bf16[256,1152]{1,0:T(8,128)(2,1)S(1)} %pack.4.refs_0_), channel_id=1, source_target_pairs={{0,6},{1,7},{2,4},{3,5},{4,2},{5,3},{6,0},{7,1},{8,56},{9,57},{10,... | collective-permute-start | bytes 1769480 | tf_op jit(solution)/shard_map/ppermute | solution.py:25
  12.6 2.8 %collective-permute-done.5.refs_2_ = bf16[256,1152]{1,0:T(8,128)(2,1)S(1)} collective-permute-done((bf16[256,1152]{1,0:T(8,128)(2,1)S(1)}, bf16[256,1152]{1,0:T(8,128)(2,1)S(1)}, u32[]{:S(2)}, u32[]{:S(2)}) %collective-permute-start.5) | collective-permute-done | bytes 589856 | tf_op jit(solution)/shard_map/ppermute | solution.py:25
  15.4 2.7 %collective-permute-done.3.refs_1_ = bf16[256,1152]{1,0:T(8,128)(2,1)S(1)} collective-permute-done((bf16[256,1152]{1,0:T(8,128)(2,1)S(1)}, bf16[256,1152]{1,0:T(8,128)(2,1)S(1)}, u32[]{:S(2)}, u32[]{:S(2)}) %collective-permute-start.3) | collective-permute-done | bytes 589856 | tf_op jit(solution)/shard_map/ppermute | solution.py:25
  18.1 2.3 %collective-permute-done.1.refs_3_ = bf16[256,1152]{1,0:T(8,128)(2,1)S(1)} collective-permute-done((bf16[256,1152]{1,0:T(8,128)(2,1)S(1)}, bf16[256,1152]{1,0:T(8,128)(2,1)S(1)}, u32[]{:S(2)}, u32[]{:S(2)}) %collective-permute-start.1) | collective-permute-done | bytes 589856 | tf_op jit(solution)/shard_map/ppermute | solution.py:25
  21.0 1.8 %collective-permute-start.6 = (bf16[256,1152]{1,0:T(8,128)(2,1)S(1)}, bf16[256,1152]{1,0:T(8,128)(2,1)S(1)}, u32[]{:S(2)}, u32[]{:S(2)}) collective-permute-start(bf16[256,1152]{1,0:T(8,128)(2,1)S(1)} %collective-permute-done.5.refs_2_), channel_id=1, source_target_pairs={{0,1},{1,0},{2,3},{3,2},{4,5},{5,4},{6,7},{7,6},{8,73},{9,72},{10,... | collective-permute-start | bytes 1769480 | tf_op jit(solution)/shard_map/ppermute | solution.py:25
  22.8 3.8 %collective-permute-start.4 = (bf16[256,1152]{1,0:T(8,128)(2,1)S(1)}, bf16[256,1152]{1,0:T(8,128)(2,1)S(1)}, u32[]{:S(2)}, u32[]{:S(2)}) collective-permute-start(bf16[256,1152]{1,0:T(8,128)(2,1)S(1)} %collective-permute-done.3.refs_1_), channel_id=1, source_target_pairs={{0,6},{1,7},{2,4},{3,5},{4,2},{5,3},{6,0},{7,1},{8,56},{9,57},{10,... | collective-permute-start | bytes 1769480 | tf_op jit(solution)/shard_map/ppermute | solution.py:25
  27.9 3.5 %tile_near.1 = (bf16[512,1152]{1,0:T(8,128)(2,1)S(1)}, bf16[1024,1152]{1,0:T(8,128)(2,1)S(1)}, bf16[512,1024]{1,0:T(8,128)(2,1)S(1)}, f32[512,1152]{1,0:T(8,128)S(1)}, f32[8,128]{1,0:T(8,128)S(1)}) custom-call(s32[1]{0:T(128)} %bitcast.core_ref.refs_0_, f32[8,128]{1,0:T(8,128)S(1)} %broadcast_in_dim.15.sharp_ref, f32[8,128]{1,0:T(8,128)S(1)} %broadcast_in_dim.17.bias_ref, ...), custom_call_target="tpu_custom_call" | custom-call | flops 2415919104 | bytes 4718592 | tf_op jit(solution)/shard_map/tile_near/pallas_call | solution.py:258
  31.4 2.4 %collective-permute-done.4.refs_0_.refs_2_ = bf16[256,1152]{1,0:T(8,128)(2,1)S(1)} collective-permute-done((bf16[256,1152]{1,0:T(8,128)(2,1)S(1)}, bf16[256,1152]{1,0:T(8,128)(2,1)S(1)}, u32[]{:S(2)}, u32[]{:S(2)}) %collective-permute-start.4) | collective-permute-done | bytes 589856 | tf_op jit(solution)/shard_map/ppermute | solution.py:25
  33.9 1.5 %collective-permute-done.2.refs_0_ = bf16[256,1152]{1,0:T(8,128)(2,1)S(1)} collective-permute-done((bf16[256,1152]{1,0:T(8,128)(2,1)S(1)}, bf16[256,1152]{1,0:T(8,128)(2,1)S(1)}, u32[]{:S(2)}, u32[]{:S(2)}) %collective-permute-start.2) | collective-permute-done | bytes 589856 | tf_op jit(solution)/shard_map/ppermute | solution.py:25
  35.6 2.2 %collective-permute-start.9 = (bf16[128,1152]{1,0:T(8,128)(2,1)S(1)}, bf16[128,1152]{1,0:T(8,128)(2,1)S(1)}, u32[]{:S(2)}, u32[]{:S(2)}) collective-permute-start(bf16[128,1152]{1,0:T(8,128)(2,1)S(1)} %half_of.3), channel_id=1, source_target_pairs={{0,6},{1,7},{2,4},{3,5},{4,2},{5,3},{6,0},{7,1},{8,56},{9,57},{10,... | collective-permute-start | bytes 884744 | tf_op jit(solution)/shard_map/ppermute | solution.py:25
  37.8 1.4 %collective-permute-done.10.received_ref.far_received_ref = bf16[768,1152]{1,0:T(8,128)(2,1)S(1)} collective-permute-done((bf16[768,1152]{1,0:T(8,128)(2,1)S(1)}, bf16[768,1152]{1,0:T(8,128)(2,1)S(1)}, u32[]{:S(2)}, u32[]{:S(2)}) %collective-permute-start.10) | collective-permute-done | bytes 1769504 | tf_op jit(solution)/shard_map/ppermute | solution.py:25
  39.2 3.7 %tile_far.1 = (bf16[768,1152]{1,0:T(8,128)(2,1)S(1)}, bf16[768,1152]{1,0:T(8,128)(2,1)S(1)}, bf16[768,768]{1,0:T(8,128)(2,1)S(1)}, f32[768,1152]{1,0:T(8,128)S(1)}, f32[8,128]{1,0:T(8,128)S(1)}) custom-call(s32[1]{0:T(128)} %bitcast.core_ref.refs_0_, f32[8,128]{1,0:T(8,128)S(1)} %broadcast_in_dim.15.sharp_ref, f32[8,128]{1,0:T(8,128)S(1)} %broadcast_in_dim.17.bias_ref, ...), custom_call_target="tpu_custom_call" | custom-call | flops 2717908992 | bytes 5898240 | tf_op jit(solution)/shard_map/tile_far/pallas_call | solution.py:258
  43.7 1.7 %collective-permute-start.11 = (bf16[256,1152]{1,0:T(8,128)(2,1)S(1)}, bf16[256,1152]{1,0:T(8,128)(2,1)S(1)}, u32[]{:S(2)}, u32[]{:S(2)}) collective-permute-start(bf16[256,1152]{1,0:T(8,128)(2,1)S(1)} %pack.7.last_ref), channel_id=1, source_target_pairs={{0,8},{1,9},{2,10},{3,11},{4,12},{5,13},{6,14},{7,15},{8,0},{9,1},... | collective-permute-start | bytes 1769480 | tf_op jit(solution)/shard_map/ppermute | solution.py:25
  45.4 1.9 %tile_middle.1 = (bf16[768,1024]{1,0:T(8,128)(2,1)S(1)}, f32[256,1152]{1,0:T(8,128)S(1)}, f32[8,128]{1,0:T(8,128)S(1)}) custom-call(s32[1]{0:T(128)} %bitcast.core_ref.refs_0_, f32[8,128]{1,0:T(8,128)S(1)} %broadcast_in_dim.15.sharp_ref, f32[8,128]{1,0:T(8,128)S(1)} %broadcast_in_dim.17.bias_ref, bf16[768,1152]{1,0:T(8,128)(2,1)S(1)} %get-tuple-element.80.img_ref, ...), custom_call_target="tpu_custom_call" | custom-call | flops 1207959552 | bytes 6946816 | tf_op jit(solution)/shard_map/tile_middle/pallas_call | solution.py:258
  47.3 4.6 %tile_last.1 = (bf16[768,256]{1,0:T(8,128)(2,1)S(1)}, f32[768,1152]{1,0:T(8,128)S(1)}, bf16[256,1152]{1,0:T(8,128)(2,1)S(1)}, bf16[256,1024]{1,0:T(8,128)(2,1)S(...) custom-call(s32[1]{0:T(128)} %bitcast.core_ref.refs_0_, ...), custom_call_target="tpu_custom_call" | custom-call | flops 3321888768 | bytes 12976128 | tf_op jit(solution)/shard_map/tile_last/pallas_call | solution.py:258
  52.7 0.9 fusion.5
  53.6 0.9 collective-permute-done.12
  54.5 0.9 collective-permute-start.14
  55.4 1.8 %collective-permute-start.13 = (bf16[256,1152]{1,0:T(8,128)(2,1)S(1)}, bf16[256,1152]{1,0:T(8,128)(2,1)S(1)}, u32[]{:S(2)}, u32[]{:S(2)}) collective-permute-start(bf16[256,1152]{1,0:T(8,128)(2,1)S(1)} %get-tuple-element.95), channel_id=1, source_target_pairs={{0,8},{1,9},{2,10},{3,11},{4,12},{5,13},{6,14},{7,15},{8,0},{9,1},... | collective-permute-start | bytes 1769480 | tf_op jit(solution)/shard_map/ppermute | solution.py:25
  57.9 2.5 %fusion.3 = (bf16[768,1152]{1,0:T(8,128)(2,1)S(1)}, f32[768,1152]{1,0:T(8,128)S(1)}) fusion(f32[768,1152]{1,0:T(8,128)S(1)} %get-tuple-element.96.img_ref, pred[]{:T(512)S(6)} %eq.3, f32[768,1152]{1,0:T(8,128)S(1)} %fusion.7, bf16[768,768]{1,0:T(8,128)(2,1)S(1)} %get-tuple-element.97, bf16[768,1152]{1,0:T(8,128)(2,1)S(1)} %get-tuple-element.80.img_ref), kind=kOutput, calls=%fused_computation.9 | convolution fusion | flops 1367801856 | bytes 15335425 | tf_op jit(solution)/shard_map/dot_general | solution.py:423
  60.6 0.8 collective-permute-start.15
  61.4 1.9 %collective-permute-start.17 = (bf16[128,1152]{1,0:T(8,128)(2,1)S(1)}, bf16[128,1152]{1,0:T(8,128)(2,1)S(1)}, u32[]{:S(2)}, u32[]{:S(2)}) collective-permute-start(bf16[128,1152]{1,0:T(8,128)(2,1)S(1)} %get-tuple-element.110), channel_id=1, source_target_pairs={{0,6},{1,7},{2,4},{3,5},{4,2},{5,3},{6,0},{7,1},{8,56},{9,57},{10,... | collective-permute-start | bytes 884744 | tf_op jit(solution)/shard_map/ppermute | solution.py:25
  63.4 0.9 fusion.8
  64.3 3.0 %fusion.1 = (bf16[1024,1152]{1,0:T(8,128)(2,1)S(1)}, f32[1024,1152]{1,0:T(8,128)S(1)}) fusion(f32[1024,1152]{1,0:T(8,128)S(1)} %fusion.8, bf16[768,1024]{1,0:T(8,128)(2,1)S(1)} %get-tuple-element.106, bf16[768,1152]{1,0:T(8,128)(2,1)S(1)} %get-tuple-element.80.img_ref), kind=kOutput, calls=%fused_computation.5 | convolution fusion | flops 1822556160 | bytes 15138816 | tf_op jit(solution)/shard_map/dot_general | solution.py:423
  68.5 1.2 %far.1 = (bf16[256,1152]{1,0:T(8,128)(2,1)S(1)}, bf16[256,1152]{1,0:T(8,128)(2,1)S(1)}) custom-call(s32[1]{0:T(128)} %bitcast.core_ref.refs_0_, f32[768,1152]{1,0:T(8,128)S(1)} %get-tuple-element.132.txt_ref, bf16[768,1152]{1,0:T(8,128)(2,1)S(1)} %collective-permute-done.15.received_ref.txt_received_ref.img_received_ref, ...), custom_call_target="tpu_custom_call" | custom-call | tf_op jit(solution)/shard_map/far/pallas_call | solution.py:276
  69.7 3.7 %collective-permute-start.19 = (bf16[1024,1152]{1,0:T(8,128)(2,1)S(1)}, bf16[1024,1152]{1,0:T(8,128)(2,1)S(1)}, u32[]{:S(2)}, u32[]{:S(2)}) collective-permute-start(bf16[1024,1152]{1,0:T(8,128)(2,1)S(1)} %get-tuple-element.117), channel_id=1, source_target_pairs={{0,8},{1,9},{2,10},{3,11},{4,12},{5,13},{6,14},{7,15},{8,0},{9,1},... | collective-permute-start | bytes 7077896 | tf_op jit(solution)/shard_map/ppermute | solution.py:25
  73.4 1.4 %collective-permute-start.20 = (bf16[256,1152]{1,0:T(8,128)(2,1)S(1)}, bf16[256,1152]{1,0:T(8,128)(2,1)S(1)}, u32[]{:S(2)}, u32[]{:S(2)}) collective-permute-start(bf16[256,1152]{1,0:T(8,128)(2,1)S(1)} %get-tuple-element.120), channel_id=1, source_target_pairs={{0,1},{1,0},{2,3},{3,2},{4,5},{5,4},{6,7},{7,6},{8,73},{9,72},{10,... | collective-permute-start | bytes 1769480 | tf_op jit(solution)/shard_map/ppermute | solution.py:25
  74.8 1.9 %collective-permute-start.24 = (bf16[256,1152]{1,0:T(8,128)(2,1)S(1)}, bf16[256,1152]{1,0:T(8,128)(2,1)S(1)}, u32[]{:S(2)}, u32[]{:S(2)}) collective-permute-start(bf16[256,1152]{1,0:T(8,128)(2,1)S(1)} %get-tuple-element.122), channel_id=1, source_target_pairs={{0,6},{1,7},{2,4},{3,5},{4,2},{5,3},{6,0},{7,1},{8,56},{9,57},{10,... | collective-permute-start | bytes 1769480 | tf_op jit(solution)/shard_map/ppermute | solution.py:25
  76.7 0.9 collective-permute-done.19.received_ref
  77.6 1.0 base.1.refs_1_.base_ref
  78.6 5.1 %collective-permute-done.20.refs_2_ = bf16[256,1152]{1,0:T(8,128)(2,1)S(1)} collective-permute-done((bf16[256,1152]{1,0:T(8,128)(2,1)S(1)}, bf16[256,1152]{1,0:T(8,128)(2,1)S(1)}, u32[]{:S(2)}, u32[]{:S(2)}) %collective-permute-start.20) | collective-permute-done | bytes 589856 | tf_op jit(solution)/shard_map/ppermute | solution.py:25
  85.3 2.0 %collective-permute-start.23 = (bf16[256,1152]{1,0:T(8,128)(2,1)S(1)}, bf16[256,1152]{1,0:T(8,128)(2,1)S(1)}, u32[]{:S(2)}, u32[]{:S(2)}) collective-permute-start(bf16[256,1152]{1,0:T(8,128)(2,1)S(1)} %near.4), channel_id=1, source_target_pairs={{0,6},{1,7},{2,4},{3,5},{4,2},{5,3},{6,0},{7,1},{8,56},{9,57},{10,... | collective-permute-start | bytes 1769480 | tf_op jit(solution)/shard_map/ppermute | solution.py:25
  88.1 1.4 %collective-permute-start.25 = (bf16[256,1152]{1,0:T(8,128)(2,1)S(1)}, bf16[256,1152]{1,0:T(8,128)(2,1)S(1)}, u32[]{:S(2)}, u32[]{:S(2)}) collective-permute-start(bf16[256,1152]{1,0:T(8,128)(2,1)S(1)} %near.5), channel_id=1, source_target_pairs={{0,1},{1,0},{2,3},{3,2},{4,5},{5,4},{6,7},{7,6},{8,73},{9,72},{10,... | collective-permute-start | bytes 1769480 | tf_op jit(solution)/shard_map/ppermute | solution.py:25
  89.5 1.7 %collective-permute-start.26 = (f32[8,128]{1,0:T(8,128)S(1)}, f32[8,128]{1,0:T(8,128)S(1)}, u32[]{:S(2)}, u32[]{:S(2)}) collective-permute-start(f32[8,128]{1,0:T(8,128)S(1)} %add.44), channel_id=1, source_target_pairs={{0,6},{1,7},{2,4},{3,5},{4,2},{5,3},{6,0},{7,1},{8,14},{9,15},{10,... | collective-permute-start | bytes 12296 | tf_op jit(solution)/shard_map/ppermute | solution.py:25
  91.2 2.3 %collective-permute-done.26 = f32[8,128]{1,0:T(8,128)S(1)} collective-permute-done((f32[8,128]{1,0:T(8,128)S(1)}, f32[8,128]{1,0:T(8,128)S(1)}, u32[]{:S(2)}, u32[]{:S(2)}) %collective-permute-start.26) | collective-permute-done | bytes 4128 | tf_op jit(solution)/shard_map/ppermute | solution.py:25
  94.3 2.0 %collective-permute-done.27 = f32[8,128]{1,0:T(8,128)S(1)} collective-permute-done((f32[8,128]{1,0:T(8,128)S(1)}, f32[8,128]{1,0:T(8,128)S(1)}, u32[]{:S(2)}, u32[]{:S(2)}) %collective-permute-start.27) | collective-permute-done | bytes 4128 | tf_op jit(solution)/shard_map/ppermute | solution.py:25
  96.3 0.8 collective-permute-start.28
  97.1 2.9 %collective-permute-done.28 = f32[8,128]{1,0:T(8,128)S(1)} collective-permute-done((f32[8,128]{1,0:T(8,128)S(1)}, f32[8,128]{1,0:T(8,128)S(1)}, u32[]{:S(2)}, u32[]{:S(2)}) %collective-permute-start.28) | collective-permute-done | bytes 4128 | tf_op jit(solution)/shard_map/ppermute | solution.py:25
  100.0 1.3 %gather_sums.1 = (f32[128,1152]{1,0:T(8,128)S(1)}, f32[136,1152]{1,0:T(8,128)S(1)}) custom-call(s32[1]{0:T(128)} %bitcast.core_ref.refs_0_, f32[1024,1152]{1,0:T(8,128)S(1)} %base.1.refs_1_.base_ref, bf16[256,1152]{1,0:T(8,128)(2,1)S(1)} %collective-permute-done.21.a_ref, bf16[256,1152]{1,0:T(8,128)(2,1)S(1)} %collective-permute-done.23.b_ref, ...), custom_call_target="tpu_custom_call" | custom-call | tf_op jit(solution)/shard_map/gather_sums/pallas_call | solution.py:276
  101.3 4.8 %collective-permute-start.29 = (f32[136,1152]{1,0:T(8,128)S(1)}, f32[136,1152]{1,0:T(8,128)S(1)}, u32[]{:S(2)}, u32[]{:S(2)}) collective-permute-start(f32[136,1152]{1,0:T(8,128)S(1)} %get-tuple-element.125), channel_id=1, source_target_pairs={{0,8},{1,9},{2,10},{3,11},{4,12},{5,13},{6,14},{7,15},{8,0},{9,1},... | collective-permute-start | bytes 1880072 | tf_op jit(solution)/shard_map/ppermute | solution.py:25
  106.1 1.7 %collective-permute-done.29.refs_4_ = f32[136,1152]{1,0:T(8,128)S(1)} collective-permute-done((f32[136,1152]{1,0:T(8,128)S(1)}, f32[136,1152]{1,0:T(8,128)S(1)}, u32[]{:S(2)}, u32[]{:S(2)}) %collective-permute-start.29) | collective-permute-done | bytes 626720 | tf_op jit(solution)/shard_map/ppermute | solution.py:25
  107.8 1.7 %finish.1 = (f32[1,1]{1,0:T(1,128)}, f32[128,1152]{1,0:T(8,128)}, f32[128,1152]{1,0:T(8,128)}) custom-call(s32[1]{0:T(128)} %bitcast.core_ref.refs_0_, f32[128,1152]{1,0:T(8,128)S(1)} %copy-done.1, f32[128,1152]{1,0:T(8,128)S(1)} %copy-done.3, f32[128,1152]{1,0:T(8,128)S(1)} %get-tuple-element.124.refs_3_, f32[136,1152]{1,0:T(8,128)S(1)} %collective-permute-done.29.refs_4_, ...), custom_call_target="tpu_custom_call" | custom-call | tf_op jit(solution)/shard_map/finish/pallas_call | solution.py:276
  (55 shorter events, 8.5 us)
Async XLA Ops:
  0.6 1.1 copy-start
  1.7 1.1 copy-start.2
  3.3 2.7 %collective-permute-start = (bf16[128,1152]{1,0:T(8,128)(2,1)S(1)}, bf16[128,1152]{1,0:T(8,128)(2,1)S(1)}, u32[]{:S(2)}, u32[]{:S(2)}) collective-permute-start(bf16[128,1152]{1,0:T(8,128)(2,1)S(1)} %get-tuple-element.68), channel_id=1, source_target_pairs={{0,8},{1,9},{2,10},{3,11},{4,12},{5,13},{6,14},{7,15},{8,0},{9,1},... | collective-permute-start | bytes 884744 | tf_op jit(solution)/shard_map/ppermute | solution.py:25
  6.1 9.4 %collective-permute-start.5 = (bf16[256,1152]{1,0:T(8,128)(2,1)S(1)}, bf16[256,1152]{1,0:T(8,128)(2,1)S(1)}, u32[]{:S(2)}, u32[]{:S(2)}) collective-permute-start(bf16[256,1152]{1,0:T(8,128)(2,1)S(1)} %pack.4.refs_0_), channel_id=1, source_target_pairs={{0,2},{1,3},{2,0},{3,1},{4,6},{5,7},{6,4},{7,5},{8,24},{9,25},{10,... | collective-permute-start | bytes 1769480 | tf_op jit(solution)/shard_map/ppermute | solution.py:25
  7.9 10.2 %collective-permute-start.3 = (bf16[256,1152]{1,0:T(8,128)(2,1)S(1)}, bf16[256,1152]{1,0:T(8,128)(2,1)S(1)}, u32[]{:S(2)}, u32[]{:S(2)}) collective-permute-start(bf16[256,1152]{1,0:T(8,128)(2,1)S(1)} %pack.4.refs_0_), channel_id=1, source_target_pairs={{0,1},{1,0},{2,3},{3,2},{4,5},{5,4},{6,7},{7,6},{8,73},{9,72},{10,... | collective-permute-start | bytes 1769480 | tf_op jit(solution)/shard_map/ppermute | solution.py:25
  10.3 10.0 %collective-permute-start.1 = (bf16[256,1152]{1,0:T(8,128)(2,1)S(1)}, bf16[256,1152]{1,0:T(8,128)(2,1)S(1)}, u32[]{:S(2)}, u32[]{:S(2)}) collective-permute-start(bf16[256,1152]{1,0:T(8,128)(2,1)S(1)} %pack.4.refs_0_), channel_id=1, source_target_pairs={{0,6},{1,7},{2,4},{3,5},{4,2},{5,3},{6,0},{7,1},{8,56},{9,57},{10,... | collective-permute-start | bytes 1769480 | tf_op jit(solution)/shard_map/ppermute | solution.py:25
  20.5 7.4 %collective-permute-start.7 = (bf16[1024,1152]{1,0:T(8,128)(2,1)S(1)}, bf16[1024,1152]{1,0:T(8,128)(2,1)S(1)}, u32[]{:S(2)}, u32[]{:S(2)}) collective-permute-start(bf16[1024,1152]{1,0:T(8,128)(2,1)S(1)} %pack.5.near_ref), channel_id=1, source_target_pairs={{0,8},{1,9},{2,10},{3,11},{4,12},{5,13},{6,14},{7,15},{8,0},{9,1},... | collective-permute-start | bytes 7077896 | tf_op jit(solution)/shard_map/ppermute | solution.py:25
  21.0 10.4 %collective-permute-start.6 = (bf16[256,1152]{1,0:T(8,128)(2,1)S(1)}, bf16[256,1152]{1,0:T(8,128)(2,1)S(1)}, u32[]{:S(2)}, u32[]{:S(2)}) collective-permute-start(bf16[256,1152]{1,0:T(8,128)(2,1)S(1)} %collective-permute-done.5.refs_2_), channel_id=1, source_target_pairs={{0,1},{1,0},{2,3},{3,2},{4,5},{5,4},{6,7},{7,6},{8,73},{9,72},{10,... | collective-permute-start | bytes 1769480 | tf_op jit(solution)/shard_map/ppermute | solution.py:25
  22.8 11.0 %collective-permute-start.4 = (bf16[256,1152]{1,0:T(8,128)(2,1)S(1)}, bf16[256,1152]{1,0:T(8,128)(2,1)S(1)}, u32[]{:S(2)}, u32[]{:S(2)}) collective-permute-start(bf16[256,1152]{1,0:T(8,128)(2,1)S(1)} %collective-permute-done.3.refs_1_), channel_id=1, source_target_pairs={{0,6},{1,7},{2,4},{3,5},{4,2},{5,3},{6,0},{7,1},{8,56},{9,57},{10,... | collective-permute-start | bytes 1769480 | tf_op jit(solution)/shard_map/ppermute | solution.py:25
  26.6 8.7 %collective-permute-start.2 = (bf16[256,1152]{1,0:T(8,128)(2,1)S(1)}, bf16[256,1152]{1,0:T(8,128)(2,1)S(1)}, u32[]{:S(2)}, u32[]{:S(2)}) collective-permute-start(bf16[256,1152]{1,0:T(8,128)(2,1)S(1)} %collective-permute-done.1.refs_3_), channel_id=1, source_target_pairs={{0,2},{1,3},{2,0},{3,1},{4,6},{5,7},{6,4},{7,5},{8,24},{9,25},{10,... | collective-permute-start | bytes 1769480 | tf_op jit(solution)/shard_map/ppermute | solution.py:25
  35.5 3.8 %collective-permute-start.10 = (bf16[768,1152]{1,0:T(8,128)(2,1)S(1)}, bf16[768,1152]{1,0:T(8,128)(2,1)S(1)}, u32[]{:S(2)}, u32[]{:S(2)}) collective-permute-start(bf16[768,1152]{1,0:T(8,128)(2,1)S(1)} %pack.6.far_ref), channel_id=1, source_target_pairs={{0,8},{1,9},{2,10},{3,11},{4,12},{5,13},{6,14},{7,15},{8,0},{9,1},... | collective-permute-start | bytes 5308424 | tf_op jit(solution)/shard_map/ppermute | solution.py:25
  35.6 7.3 %collective-permute-start.9 = (bf16[128,1152]{1,0:T(8,128)(2,1)S(1)}, bf16[128,1152]{1,0:T(8,128)(2,1)S(1)}, u32[]{:S(2)}, u32[]{:S(2)}) collective-permute-start(bf16[128,1152]{1,0:T(8,128)(2,1)S(1)} %half_of.3), channel_id=1, source_target_pairs={{0,6},{1,7},{2,4},{3,5},{4,2},{5,3},{6,0},{7,1},{8,56},{9,57},{10,... | collective-permute-start | bytes 884744 | tf_op jit(solution)/shard_map/ppermute | solution.py:25
  37.8 5.9 %collective-permute-start.8 = (bf16[128,1152]{1,0:T(8,128)(2,1)S(1)}, bf16[128,1152]{1,0:T(8,128)(2,1)S(1)}, u32[]{:S(2)}, u32[]{:S(2)}) collective-permute-start(bf16[128,1152]{1,0:T(8,128)(2,1)S(1)} %half_of.2), channel_id=1, source_target_pairs={{0,2},{1,3},{2,0},{3,1},{4,6},{5,7},{6,4},{7,5},{8,24},{9,25},{10,... | collective-permute-start | bytes 884744 | tf_op jit(solution)/shard_map/ppermute | solution.py:25
  43.7 3.5 %collective-permute-start.11 = (bf16[256,1152]{1,0:T(8,128)(2,1)S(1)}, bf16[256,1152]{1,0:T(8,128)(2,1)S(1)}, u32[]{:S(2)}, u32[]{:S(2)}) collective-permute-start(bf16[256,1152]{1,0:T(8,128)(2,1)S(1)} %pack.7.last_ref), channel_id=1, source_target_pairs={{0,8},{1,9},{2,10},{3,11},{4,12},{5,13},{6,14},{7,15},{8,0},{9,1},... | collective-permute-start | bytes 1769480 | tf_op jit(solution)/shard_map/ppermute | solution.py:25
  51.9 2.6 %collective-permute-start.12 = (f32[8,128]{1,0:T(8,128)S(1)}, f32[8,128]{1,0:T(8,128)S(1)}, u32[]{:S(2)}, u32[]{:S(2)}) collective-permute-start(f32[8,128]{1,0:T(8,128)S(1)} %add_add_fusion), channel_id=1, source_target_pairs={{0,1},{1,0},{2,3},{3,2},{4,5},{5,4},{6,7},{7,6},{8,9},{9,8},{10,11... | collective-permute-start | bytes 12296 | tf_op jit(solution)/shard_map/ppermute | solution.py:25
  54.5 5.9 %collective-permute-start.14 = (f32[8,128]{1,0:T(8,128)S(1)}, f32[8,128]{1,0:T(8,128)S(1)}, u32[]{:S(2)}, u32[]{:S(2)}) collective-permute-start(f32[8,128]{1,0:T(8,128)S(1)} %add.40), channel_id=1, source_target_pairs={{0,65},{1,64},{2,67},{3,66},{4,69},{5,68},{6,71},{7,70},{8,73},{9,... | collective-permute-start | bytes 12296 | tf_op jit(solution)/shard_map/ppermute | solution.py:25
  55.4 5.0 %collective-permute-start.13 = (bf16[256,1152]{1,0:T(8,128)(2,1)S(1)}, bf16[256,1152]{1,0:T(8,128)(2,1)S(1)}, u32[]{:S(2)}, u32[]{:S(2)}) collective-permute-start(bf16[256,1152]{1,0:T(8,128)(2,1)S(1)} %get-tuple-element.95), channel_id=1, source_target_pairs={{0,8},{1,9},{2,10},{3,11},{4,12},{5,13},{6,14},{7,15},{8,0},{9,1},... | collective-permute-start | bytes 1769480 | tf_op jit(solution)/shard_map/ppermute | solution.py:25
  60.6 6.6 %collective-permute-start.15 = (bf16[768,1152]{1,0:T(8,128)(2,1)S(1)}, bf16[768,1152]{1,0:T(8,128)(2,1)S(1)}, u32[]{:S(2)}, u32[]{:S(2)}) collective-permute-start(bf16[768,1152]{1,0:T(8,128)(2,1)S(1)} %get-tuple-element.108), channel_id=1, source_target_pairs={{0,8},{1,9},{2,10},{3,11},{4,12},{5,13},{6,14},{7,15},{8,0},{9,1},... | collective-permute-start | bytes 5308424 | tf_op jit(solution)/shard_map/ppermute | solution.py:25
  61.4 5.8 %collective-permute-start.18 = (f32[8,128]{1,0:T(8,128)S(1)}, f32[8,128]{1,0:T(8,128)S(1)}, u32[]{:S(2)}, u32[]{:S(2)}) collective-permute-start(f32[8,128]{1,0:T(8,128)S(1)} %add.42), channel_id=1, source_target_pairs={{0,2},{1,3},{2,0},{3,1},{4,6},{5,7},{6,4},{7,5},{8,10},{9,11},{10,... | collective-permute-start | bytes 12296 | tf_op jit(solution)/shard_map/ppermute | solution.py:25
  61.4 6.6 %collective-permute-start.16 = (bf16[128,1152]{1,0:T(8,128)(2,1)S(1)}, bf16[128,1152]{1,0:T(8,128)(2,1)S(1)}, u32[]{:S(2)}, u32[]{:S(2)}) collective-permute-start(bf16[128,1152]{1,0:T(8,128)(2,1)S(1)} %get-tuple-element.109), channel_id=1, source_target_pairs={{0,2},{1,3},{2,0},{3,1},{4,6},{5,7},{6,4},{7,5},{8,24},{9,25},{10,... | collective-permute-start | bytes 884744 | tf_op jit(solution)/shard_map/ppermute | solution.py:25
  61.4 7.1 %collective-permute-start.17 = (bf16[128,1152]{1,0:T(8,128)(2,1)S(1)}, bf16[128,1152]{1,0:T(8,128)(2,1)S(1)}, u32[]{:S(2)}, u32[]{:S(2)}) collective-permute-start(bf16[128,1152]{1,0:T(8,128)(2,1)S(1)} %get-tuple-element.110), channel_id=1, source_target_pairs={{0,6},{1,7},{2,4},{3,5},{4,2},{5,3},{6,0},{7,1},{8,56},{9,57},{10,... | collective-permute-start | bytes 884744 | tf_op jit(solution)/shard_map/ppermute | solution.py:25
  69.7 7.9 %collective-permute-start.19 = (bf16[1024,1152]{1,0:T(8,128)(2,1)S(1)}, bf16[1024,1152]{1,0:T(8,128)(2,1)S(1)}, u32[]{:S(2)}, u32[]{:S(2)}) collective-permute-start(bf16[1024,1152]{1,0:T(8,128)(2,1)S(1)} %get-tuple-element.117), channel_id=1, source_target_pairs={{0,8},{1,9},{2,10},{3,11},{4,12},{5,13},{6,14},{7,15},{8,0},{9,1},... | collective-permute-start | bytes 7077896 | tf_op jit(solution)/shard_map/ppermute | solution.py:25
  73.4 10.2 %collective-permute-start.20 = (bf16[256,1152]{1,0:T(8,128)(2,1)S(1)}, bf16[256,1152]{1,0:T(8,128)(2,1)S(1)}, u32[]{:S(2)}, u32[]{:S(2)}) collective-permute-start(bf16[256,1152]{1,0:T(8,128)(2,1)S(1)} %get-tuple-element.120), channel_id=1, source_target_pairs={{0,1},{1,0},{2,3},{3,2},{4,5},{5,4},{6,7},{7,6},{8,73},{9,72},{10,... | collective-permute-start | bytes 1769480 | tf_op jit(solution)/shard_map/ppermute | solution.py:25
  74.7 9.8 %collective-permute-start.22 = (bf16[256,1152]{1,0:T(8,128)(2,1)S(1)}, bf16[256,1152]{1,0:T(8,128)(2,1)S(1)}, u32[]{:S(2)}, u32[]{:S(2)}) collective-permute-start(bf16[256,1152]{1,0:T(8,128)(2,1)S(1)} %second.1), channel_id=1, source_target_pairs={{0,2},{1,3},{2,0},{3,1},{4,6},{5,7},{6,4},{7,5},{8,24},{9,25},{10,... | collective-permute-start | bytes 1769480 | tf_op jit(solution)/shard_map/ppermute | solution.py:25
  74.8 12.5 %collective-permute-start.24 = (bf16[256,1152]{1,0:T(8,128)(2,1)S(1)}, bf16[256,1152]{1,0:T(8,128)(2,1)S(1)}, u32[]{:S(2)}, u32[]{:S(2)}) collective-permute-start(bf16[256,1152]{1,0:T(8,128)(2,1)S(1)} %get-tuple-element.122), channel_id=1, source_target_pairs={{0,6},{1,7},{2,4},{3,5},{4,2},{5,3},{6,0},{7,1},{8,56},{9,57},{10,... | collective-permute-start | bytes 1769480 | tf_op jit(solution)/shard_map/ppermute | solution.py:25
  84.4 15.6 %collective-permute-start.21 = (bf16[256,1152]{1,0:T(8,128)(2,1)S(1)}, bf16[256,1152]{1,0:T(8,128)(2,1)S(1)}, u32[]{:S(2)}, u32[]{:S(2)}) collective-permute-start(bf16[256,1152]{1,0:T(8,128)(2,1)S(1)} %near.3), channel_id=1, source_target_pairs={{0,2},{1,3},{2,0},{3,1},{4,6},{5,7},{6,4},{7,5},{8,24},{9,25},{10,... | collective-permute-start | bytes 1769480 | tf_op jit(solution)/shard_map/ppermute | solution.py:25
  85.3 14.7 %collective-permute-start.23 = (bf16[256,1152]{1,0:T(8,128)(2,1)S(1)}, bf16[256,1152]{1,0:T(8,128)(2,1)S(1)}, u32[]{:S(2)}, u32[]{:S(2)}) collective-permute-start(bf16[256,1152]{1,0:T(8,128)(2,1)S(1)} %near.4), channel_id=1, source_target_pairs={{0,6},{1,7},{2,4},{3,5},{4,2},{5,3},{6,0},{7,1},{8,56},{9,57},{10,... | collective-permute-start | bytes 1769480 | tf_op jit(solution)/shard_map/ppermute | solution.py:25
  88.1 11.9 %collective-permute-start.25 = (bf16[256,1152]{1,0:T(8,128)(2,1)S(1)}, bf16[256,1152]{1,0:T(8,128)(2,1)S(1)}, u32[]{:S(2)}, u32[]{:S(2)}) collective-permute-start(bf16[256,1152]{1,0:T(8,128)(2,1)S(1)} %near.5), channel_id=1, source_target_pairs={{0,1},{1,0},{2,3},{3,2},{4,5},{5,4},{6,7},{7,6},{8,73},{9,72},{10,... | collective-permute-start | bytes 1769480 | tf_op jit(solution)/shard_map/ppermute | solution.py:25
  89.5 4.1 %collective-permute-start.26 = (f32[8,128]{1,0:T(8,128)S(1)}, f32[8,128]{1,0:T(8,128)S(1)}, u32[]{:S(2)}, u32[]{:S(2)}) collective-permute-start(f32[8,128]{1,0:T(8,128)S(1)} %add.44), channel_id=1, source_target_pairs={{0,6},{1,7},{2,4},{3,5},{4,2},{5,3},{6,0},{7,1},{8,14},{9,15},{10,... | collective-permute-start | bytes 12296 | tf_op jit(solution)/shard_map/ppermute | solution.py:25
  93.6 2.8 %collective-permute-start.27 = (f32[8,128]{1,0:T(8,128)S(1)}, f32[8,128]{1,0:T(8,128)S(1)}, u32[]{:S(2)}, u32[]{:S(2)}) collective-permute-start(f32[8,128]{1,0:T(8,128)S(1)} %add.45), channel_id=1, source_target_pairs={{0,16},{1,17},{2,18},{3,19},{4,20},{5,21},{6,22},{7,23},{8,24},{9,... | collective-permute-start | bytes 12296 | tf_op jit(solution)/shard_map/ppermute | solution.py:25
  96.3 3.7 %collective-permute-start.28 = (f32[8,128]{1,0:T(8,128)S(1)}, f32[8,128]{1,0:T(8,128)S(1)}, u32[]{:S(2)}, u32[]{:S(2)}) collective-permute-start(f32[8,128]{1,0:T(8,128)S(1)} %add.46), channel_id=1, source_target_pairs={{0,48},{1,49},{2,50},{3,51},{4,52},{5,53},{6,54},{7,55},{8,56},{9,... | collective-permute-start | bytes 12296 | tf_op jit(solution)/shard_map/ppermute | solution.py:25
  100.0 7.8 %copy-start.1 = (f32[128,1152]{1,0:T(8,128)S(1)}, f32[128,1152]{1,0:T(8,128)}, u32[]{:S(2)}) copy-start(f32[128,1152]{1,0:T(8,128)} %refs_1_.1) | copy-start | bytes 1769476
  100.0 7.8 %copy-start.3 = (f32[128,1152]{1,0:T(8,128)S(1)}, f32[128,1152]{1,0:T(8,128)}, u32[]{:S(2)}) copy-start(f32[128,1152]{1,0:T(8,128)} %refs_2_.1) | copy-start | bytes 1769476
  101.3 6.5 %collective-permute-start.29 = (f32[136,1152]{1,0:T(8,128)S(1)}, f32[136,1152]{1,0:T(8,128)S(1)}, u32[]{:S(2)}, u32[]{:S(2)}) collective-permute-start(f32[136,1152]{1,0:T(8,128)S(1)} %get-tuple-element.125), channel_id=1, source_target_pairs={{0,8},{1,9},{2,10},{3,11},{4,12},{5,13},{6,14},{7,15},{8,0},{9,1},... | collective-permute-start | bytes 1880072 | tf_op jit(solution)/shard_map/ppermute | solution.py:25

commit v5 on v4

--- a/solution.py
+++ b/solution.py
@@ -519,11 +519,10 @@
     loss = loss + swap(loss, 0, 1)
     opposite_part = text_sums(last_weights, last_tail)
     sent = encode(jnp.where(on_first, img_part_tail, opposite_part), ONE_CHIP)
-    sent, far_weights, far_tail, loss = lax.optimization_barrier((sent, far_weights, far_tail, loss))
+    sent, far_weights, far_tail = lax.optimization_barrier((sent, far_weights, far_tail))
     tail_received = swap(sent)
     far_part = text_sums(far_weights, far_tail)
     sent = encode(jnp.where(on_first, img_part, far_part), ONE_CHIP)
-    loss = loss + swap(loss, 8, 1)
     tail_received, sent, loss = lax.optimization_barrier((tail_received, sent, loss))
 
     a, b = small_call(
@@ -534,6 +533,7 @@
     rest_received = swap(sent)
     near_part = text_sums(near_weights, near_tail)
     sent = encode(near_part, ONE_CHIP)
+    loss = loss + swap(loss, 8, 1)
     loss = loss + swap(loss, 0, 2)
     (second,) = small_call(
         second_kernel, "second", core, (far_part, rest_received), (low_piece,)
@@ -556,6 +556,7 @@
     )
     base, loss = lax.optimization_barrier((base, loss))
     loss = loss + swap(loss, 0, 6)
+    base, loss = lax.optimization_barrier((base, loss))
 
     def near_slot(k, received):
         (out,) = small_call(

time: 110 us -> 102 us (0.927)
  starting transfers between devices: 42.4 us -> 38.3 us
  waiting for transfers between devices: 31.3 us -> 27.2 us
    ppermute x30, waiting for transfers between devices: 31.3 us -> 27.2 us  [exchange(): return lax.ppermute(x, AXES, pairs)]
    ppermute x30, starting transfers between devices: 42.4 us -> 38.3 us  [exchange(): return lax.ppermute(x, AXES, pairs)]
  transfers between devices with their start and end apart: 30 -> 30, of which waited for: 16 -> 16; matrix products, arithmetic and copies ran while one was open for 8% -> 8% of each run, Pallas kernels for 12% -> 13%
where the time goes in v5:
time: 102 us; the launch traced here: 101 us
  starting transfers between devices  38.3 us (38%)
  waiting for transfers between devices  27.2 us (27%)
  Pallas kernels  23 us (23%)
  matrix products  8.31 us (8%)
  between operations  2.26 us (2%)
  local copies, waits for them, and re-layouts  2.14 us (2%)
    ppermute x30, starting transfers between devices, exchange(): return lax.ppermute(x, AXES, pairs)  38.3 us
    ppermute x30, waiting for transfers between devices, exchange(): return lax.ppermute(x, AXES, pairs)  27.2 us
    pallas_call x4, Pallas kernels, tile_call(): pl.pallas_call(kernel, out_shape=outs, in_specs=[SMEM] + [VMEM] * (len(sc...  13.7 us
    pallas_call x9, Pallas kernels, small_call(): pl.pallas_call(kernel, out_shape=outs, in_specs=[SMEM] + [VMEM] * len(arr...  8.4 us
    dot_general x6, matrix products, transposed_product(): lax.dot_general(weights, img, (((0,), (0,)), ((), ())), preferred_element...  8.31 us
    unnamed x8, local copies, waits for them, and re-layouts  2.13 us
  transfers between devices with their start and end apart: 30, of which 16 were waited for; matrix products, arithmetic and copies ran while one was open for 8% of the time, Pallas kernels for 13%

profile of v5, /device:TPU:1, one launch (start us, length us, event | category | flops | bytes accessed | tf_op | source)
XLA Modules:
  0.0 101.3 jit_solution(5221275461674176926)
XLA Ops:
  0.6 1.1 %copy-done = f32[128,1152]{1,0:T(8,128)S(1)} copy-done((f32[128,1152]{1,0:T(8,128)S(1)}, f32[128,1152]{1,0:T(8,128)}, u32[]{:S(2)}) %copy-start) | copy-done | bytes 589848
  1.7 1.1 %copy-done.2 = f32[128,1152]{1,0:T(8,128)S(1)} copy-done((f32[128,1152]{1,0:T(8,128)S(1)}, f32[128,1152]{1,0:T(8,128)}, u32[]{:S(2)}) %copy-start.2) | copy-done | bytes 589848
  3.3 1.5 %collective-permute-start = (bf16[128,1152]{1,0:T(8,128)(2,1)S(1)}, bf16[128,1152]{1,0:T(8,128)(2,1)S(1)}, u32[]{:S(2)}, u32[]{:S(2)}) collective-permute-start(bf16[128,1152]{1,0:T(8,128)(2,1)S(1)} %get-tuple-element.69), channel_id=1, source_target_pairs={{0,8},{1,9},{2,10},{3,11},{4,12},{5,13},{6,14},{7,15},{8,0},{9,1},... | collective-permute-start | bytes 884744 | tf_op jit(solution)/shard_map/ppermute | solution.py:25
  4.8 1.2 %collective-permute-done.refs_1_ = bf16[128,1152]{1,0:T(8,128)(2,1)S(1)} collective-permute-done((bf16[128,1152]{1,0:T(8,128)(2,1)S(1)}, bf16[128,1152]{1,0:T(8,128)(2,1)S(1)}, u32[]{:S(2)}, u32[]{:S(2)}) %collective-permute-start) | collective-permute-done | bytes 294944 | tf_op jit(solution)/shard_map/ppermute | solution.py:25
  6.1 1.8 %collective-permute-start.5 = (bf16[256,1152]{1,0:T(8,128)(2,1)S(1)}, bf16[256,1152]{1,0:T(8,128)(2,1)S(1)}, u32[]{:S(2)}, u32[]{:S(2)}) collective-permute-start(bf16[256,1152]{1,0:T(8,128)(2,1)S(1)} %pack.4.refs_0_), channel_id=1, source_target_pairs={{0,2},{1,3},{2,0},{3,1},{4,6},{5,7},{6,4},{7,5},{8,24},{9,25},{10,... | collective-permute-start | bytes 1769480 | tf_op jit(solution)/shard_map/ppermute | solution.py:25
  7.9 2.5 %collective-permute-start.3 = (bf16[256,1152]{1,0:T(8,128)(2,1)S(1)}, bf16[256,1152]{1,0:T(8,128)(2,1)S(1)}, u32[]{:S(2)}, u32[]{:S(2)}) collective-permute-start(bf16[256,1152]{1,0:T(8,128)(2,1)S(1)} %pack.4.refs_0_), channel_id=1, source_target_pairs={{0,1},{1,0},{2,3},{3,2},{4,5},{5,4},{6,7},{7,6},{8,73},{9,72},{10,... | collective-permute-start | bytes 1769480 | tf_op jit(solution)/shard_map/ppermute | solution.py:25
  10.3 2.2 %collective-permute-start.1 = (bf16[256,1152]{1,0:T(8,128)(2,1)S(1)}, bf16[256,1152]{1,0:T(8,128)(2,1)S(1)}, u32[]{:S(2)}, u32[]{:S(2)}) collective-permute-start(bf16[256,1152]{1,0:T(8,128)(2,1)S(1)} %pack.4.refs_0_), channel_id=1, source_target_pairs={{0,6},{1,7},{2,4},{3,5},{4,2},{5,3},{6,0},{7,1},{8,56},{9,57},{10,... | collective-permute-start | bytes 1769480 | tf_op jit(solution)/shard_map/ppermute | solution.py:25
  12.6 2.8 %collective-permute-done.5.refs_2_ = bf16[256,1152]{1,0:T(8,128)(2,1)S(1)} collective-permute-done((bf16[256,1152]{1,0:T(8,128)(2,1)S(1)}, bf16[256,1152]{1,0:T(8,128)(2,1)S(1)}, u32[]{:S(2)}, u32[]{:S(2)}) %collective-permute-start.5) | collective-permute-done | bytes 589856 | tf_op jit(solution)/shard_map/ppermute | solution.py:25
  15.4 2.7 %collective-permute-done.3.refs_1_ = bf16[256,1152]{1,0:T(8,128)(2,1)S(1)} collective-permute-done((bf16[256,1152]{1,0:T(8,128)(2,1)S(1)}, bf16[256,1152]{1,0:T(8,128)(2,1)S(1)}, u32[]{:S(2)}, u32[]{:S(2)}) %collective-permute-start.3) | collective-permute-done | bytes 589856 | tf_op jit(solution)/shard_map/ppermute | solution.py:25
  18.1 2.3 %collective-permute-done.1.refs_3_ = bf16[256,1152]{1,0:T(8,128)(2,1)S(1)} collective-permute-done((bf16[256,1152]{1,0:T(8,128)(2,1)S(1)}, bf16[256,1152]{1,0:T(8,128)(2,1)S(1)}, u32[]{:S(2)}, u32[]{:S(2)}) %collective-permute-start.1) | collective-permute-done | bytes 589856 | tf_op jit(solution)/shard_map/ppermute | solution.py:25
  21.0 1.8 %collective-permute-start.6 = (bf16[256,1152]{1,0:T(8,128)(2,1)S(1)}, bf16[256,1152]{1,0:T(8,128)(2,1)S(1)}, u32[]{:S(2)}, u32[]{:S(2)}) collective-permute-start(bf16[256,1152]{1,0:T(8,128)(2,1)S(1)} %collective-permute-done.5.refs_2_), channel_id=1, source_target_pairs={{0,1},{1,0},{2,3},{3,2},{4,5},{5,4},{6,7},{7,6},{8,73},{9,72},{10,... | collective-permute-start | bytes 1769480 | tf_op jit(solution)/shard_map/ppermute | solution.py:25
  22.8 3.8 %collective-permute-start.4 = (bf16[256,1152]{1,0:T(8,128)(2,1)S(1)}, bf16[256,1152]{1,0:T(8,128)(2,1)S(1)}, u32[]{:S(2)}, u32[]{:S(2)}) collective-permute-start(bf16[256,1152]{1,0:T(8,128)(2,1)S(1)} %collective-permute-done.3.refs_1_), channel_id=1, source_target_pairs={{0,6},{1,7},{2,4},{3,5},{4,2},{5,3},{6,0},{7,1},{8,56},{9,57},{10,... | collective-permute-start | bytes 1769480 | tf_op jit(solution)/shard_map/ppermute | solution.py:25
  27.9 3.5 %tile_near.1 = (bf16[512,1152]{1,0:T(8,128)(2,1)S(1)}, bf16[1024,1152]{1,0:T(8,128)(2,1)S(1)}, bf16[512,1024]{1,0:T(8,128)(2,1)S(1)}, f32[512,1152]{1,0:T(8,128)S(1)}, f32[8,128]{1,0:T(8,128)S(1)}) custom-call(s32[1]{0:T(128)} %bitcast.core_ref.refs_0_, f32[8,128]{1,0:T(8,128)S(1)} %broadcast_in_dim.15.sharp_ref, f32[8,128]{1,0:T(8,128)S(1)} %broadcast_in_dim.17.bias_ref, ...), custom_call_target="tpu_custom_call" | custom-call | flops 2415919104 | bytes 4718592 | tf_op jit(solution)/shard_map/tile_near/pallas_call | solution.py:258
  31.4 2.4 %collective-permute-done.4.refs_0_.refs_2_ = bf16[256,1152]{1,0:T(8,128)(2,1)S(1)} collective-permute-done((bf16[256,1152]{1,0:T(8,128)(2,1)S(1)}, bf16[256,1152]{1,0:T(8,128)(2,1)S(1)}, u32[]{:S(2)}, u32[]{:S(2)}) %collective-permute-start.4) | collective-permute-done | bytes 589856 | tf_op jit(solution)/shard_map/ppermute | solution.py:25
  33.9 1.5 %collective-permute-done.2.refs_0_ = bf16[256,1152]{1,0:T(8,128)(2,1)S(1)} collective-permute-done((bf16[256,1152]{1,0:T(8,128)(2,1)S(1)}, bf16[256,1152]{1,0:T(8,128)(2,1)S(1)}, u32[]{:S(2)}, u32[]{:S(2)}) %collective-permute-start.2) | collective-permute-done | bytes 589856 | tf_op jit(solution)/shard_map/ppermute | solution.py:25
  35.6 2.2 %collective-permute-start.9 = (bf16[128,1152]{1,0:T(8,128)(2,1)S(1)}, bf16[128,1152]{1,0:T(8,128)(2,1)S(1)}, u32[]{:S(2)}, u32[]{:S(2)}) collective-permute-start(bf16[128,1152]{1,0:T(8,128)(2,1)S(1)} %half_of.3), channel_id=1, source_target_pairs={{0,6},{1,7},{2,4},{3,5},{4,2},{5,3},{6,0},{7,1},{8,56},{9,57},{10,... | collective-permute-start | bytes 884744 | tf_op jit(solution)/shard_map/ppermute | solution.py:25
  37.8 1.4 %collective-permute-done.10.received_ref.far_received_ref = bf16[768,1152]{1,0:T(8,128)(2,1)S(1)} collective-permute-done((bf16[768,1152]{1,0:T(8,128)(2,1)S(1)}, bf16[768,1152]{1,0:T(8,128)(2,1)S(1)}, u32[]{:S(2)}, u32[]{:S(2)}) %collective-permute-start.10) | collective-permute-done | bytes 1769504 | tf_op jit(solution)/shard_map/ppermute | solution.py:25
  39.2 3.7 %tile_far.1 = (bf16[768,1152]{1,0:T(8,128)(2,1)S(1)}, bf16[768,1152]{1,0:T(8,128)(2,1)S(1)}, bf16[768,768]{1,0:T(8,128)(2,1)S(1)}, f32[768,1152]{1,0:T(8,128)S(1)}, f32[8,128]{1,0:T(8,128)S(1)}) custom-call(s32[1]{0:T(128)} %bitcast.core_ref.refs_0_, f32[8,128]{1,0:T(8,128)S(1)} %broadcast_in_dim.15.sharp_ref, f32[8,128]{1,0:T(8,128)S(1)} %broadcast_in_dim.17.bias_ref, ...), custom_call_target="tpu_custom_call" | custom-call | flops 2717908992 | bytes 5898240 | tf_op jit(solution)/shard_map/tile_far/pallas_call | solution.py:258
  43.7 1.7 %collective-permute-start.11 = (bf16[256,1152]{1,0:T(8,128)(2,1)S(1)}, bf16[256,1152]{1,0:T(8,128)(2,1)S(1)}, u32[]{:S(2)}, u32[]{:S(2)}) collective-permute-start(bf16[256,1152]{1,0:T(8,128)(2,1)S(1)} %pack.7.last_ref), channel_id=1, source_target_pairs={{0,8},{1,9},{2,10},{3,11},{4,12},{5,13},{6,14},{7,15},{8,0},{9,1},... | collective-permute-start | bytes 1769480 | tf_op jit(solution)/shard_map/ppermute | solution.py:25
  45.4 1.9 %tile_middle.1 = (bf16[768,1024]{1,0:T(8,128)(2,1)S(1)}, f32[256,1152]{1,0:T(8,128)S(1)}, f32[8,128]{1,0:T(8,128)S(1)}) custom-call(s32[1]{0:T(128)} %bitcast.core_ref.refs_0_, f32[8,128]{1,0:T(8,128)S(1)} %broadcast_in_dim.15.sharp_ref, f32[8,128]{1,0:T(8,128)S(1)} %broadcast_in_dim.17.bias_ref, bf16[768,1152]{1,0:T(8,128)(2,1)S(1)} %get-tuple-element.81.img_ref, ...), custom_call_target="tpu_custom_call" | custom-call | flops 1207959552 | bytes 6946816 | tf_op jit(solution)/shard_map/tile_middle/pallas_call | solution.py:258
  47.3 4.6 %tile_last.1 = (bf16[768,256]{1,0:T(8,128)(2,1)S(1)}, f32[768,1152]{1,0:T(8,128)S(1)}, bf16[256,1152]{1,0:T(8,128)(2,1)S(1)}, bf16[256,1024]{1,0:T(8,128)(2,1)S(...) custom-call(s32[1]{0:T(128)} %bitcast.core_ref.refs_0_, ...), custom_call_target="tpu_custom_call" | custom-call | flops 3321888768 | bytes 12976128 | tf_op jit(solution)/shard_map/tile_last/pallas_call | solution.py:258
  52.7 0.9 fusion.5
  54.8 2.5 %fusion.3 = (bf16[768,1152]{1,0:T(8,128)(2,1)S(1)}, f32[768,1152]{1,0:T(8,128)S(1)}) fusion(f32[768,1152]{1,0:T(8,128)S(1)} %get-tuple-element.93.img_ref, pred[]{:T(512)S(6)} %eq.3, f32[768,1152]{1,0:T(8,128)S(1)} %fusion.7, bf16[768,768]{1,0:T(8,128)(2,1)S(1)} %get-tuple-element.94, bf16[768,1152]{1,0:T(8,128)(2,1)S(1)} %get-tuple-element.81.img_ref), kind=kOutput, calls=%fused_computation.9 | convolution fusion | flops 1367801856 | bytes 15335425 | tf_op jit(solution)/shard_map/dot_general | solution.py:423
  58.2 1.3 %collective-permute-start.17 = (f32[8,128]{1,0:T(8,128)S(1)}, f32[8,128]{1,0:T(8,128)S(1)}, u32[]{:S(2)}, u32[]{:S(2)}) collective-permute-start(f32[8,128]{1,0:T(8,128)S(1)} %add.41), channel_id=1, source_target_pairs={{0,65},{1,64},{2,67},{3,66},{4,69},{5,68},{6,71},{7,70},{8,73},{9,... | collective-permute-start | bytes 12296 | tf_op jit(solution)/shard_map/ppermute | solution.py:25
  59.6 2.2 %collective-permute-start.16 = (bf16[128,1152]{1,0:T(8,128)(2,1)S(1)}, bf16[128,1152]{1,0:T(8,128)(2,1)S(1)}, u32[]{:S(2)}, u32[]{:S(2)}) collective-permute-start(bf16[128,1152]{1,0:T(8,128)(2,1)S(1)} %get-tuple-element.110), channel_id=1, source_target_pairs={{0,6},{1,7},{2,4},{3,5},{4,2},{5,3},{6,0},{7,1},{8,56},{9,57},{10,... | collective-permute-start | bytes 884744 | tf_op jit(solution)/shard_map/ppermute | solution.py:25
  61.8 0.9 fusion.8
  62.8 3.0 %fusion.1 = (bf16[1024,1152]{1,0:T(8,128)(2,1)S(1)}, f32[1024,1152]{1,0:T(8,128)S(1)}) fusion(f32[1024,1152]{1,0:T(8,128)S(1)} %fusion.8, bf16[768,1024]{1,0:T(8,128)(2,1)S(1)} %get-tuple-element.106, bf16[768,1152]{1,0:T(8,128)(2,1)S(1)} %get-tuple-element.81.img_ref), kind=kOutput, calls=%fused_computation.5 | convolution fusion | flops 1822556160 | bytes 15138816 | tf_op jit(solution)/shard_map/dot_general | solution.py:423
  66.7 1.2 %far.1 = (bf16[256,1152]{1,0:T(8,128)(2,1)S(1)}, bf16[256,1152]{1,0:T(8,128)(2,1)S(1)}) custom-call(s32[1]{0:T(128)} %bitcast.core_ref.refs_0_, f32[768,1152]{1,0:T(8,128)S(1)} %get-tuple-element.134.txt_ref, bf16[768,1152]{1,0:T(8,128)(2,1)S(1)} %collective-permute-done.14.received_ref.txt_received_ref.img_received_ref, ...), custom_call_target="tpu_custom_call" | custom-call | tf_op jit(solution)/shard_map/far/pallas_call | solution.py:276
  67.9 2.0 %collective-permute-start.19 = (bf16[1024,1152]{1,0:T(8,128)(2,1)S(1)}, bf16[1024,1152]{1,0:T(8,128)(2,1)S(1)}, u32[]{:S(2)}, u32[]{:S(2)}) collective-permute-start(bf16[1024,1152]{1,0:T(8,128)(2,1)S(1)} %get-tuple-element.117), channel_id=1, source_target_pairs={{0,8},{1,9},{2,10},{3,11},{4,12},{5,13},{6,14},{7,15},{8,0},{9,1},... | collective-permute-start | bytes 7077896 | tf_op jit(solution)/shard_map/ppermute | solution.py:25
  69.8 1.3 %collective-permute-start.21 = (bf16[256,1152]{1,0:T(8,128)(2,1)S(1)}, bf16[256,1152]{1,0:T(8,128)(2,1)S(1)}, u32[]{:S(2)}, u32[]{:S(2)}) collective-permute-start(bf16[256,1152]{1,0:T(8,128)(2,1)S(1)} %get-tuple-element.122), channel_id=1, source_target_pairs={{0,1},{1,0},{2,3},{3,2},{4,5},{5,4},{6,7},{7,6},{8,73},{9,72},{10,... | collective-permute-start | bytes 1769480 | tf_op jit(solution)/shard_map/ppermute | solution.py:25
  71.2 2.0 %collective-permute-start.25 = (bf16[256,1152]{1,0:T(8,128)(2,1)S(1)}, bf16[256,1152]{1,0:T(8,128)(2,1)S(1)}, u32[]{:S(2)}, u32[]{:S(2)}) collective-permute-start(bf16[256,1152]{1,0:T(8,128)(2,1)S(1)} %get-tuple-element.124), channel_id=1, source_target_pairs={{0,6},{1,7},{2,4},{3,5},{4,2},{5,3},{6,0},{7,1},{8,56},{9,57},{10,... | collective-permute-start | bytes 1769480 | tf_op jit(solution)/shard_map/ppermute | solution.py:25
  74.0 1.0 base.1.refs_1_.base_ref
  75.0 1.4 %collective-permute-start.20 = (f32[8,128]{1,0:T(8,128)S(1)}, f32[8,128]{1,0:T(8,128)S(1)}, u32[]{:S(2)}, u32[]{:S(2)}) collective-permute-start(f32[8,128]{1,0:T(8,128)S(1)} %add.44), channel_id=1, source_target_pairs={{0,6},{1,7},{2,4},{3,5},{4,2},{5,3},{6,0},{7,1},{8,14},{9,15},{10,... | collective-permute-start | bytes 12296 | tf_op jit(solution)/shard_map/ppermute | solution.py:25
  76.4 2.8 %collective-permute-done.20 = f32[8,128]{1,0:T(8,128)S(1)} collective-permute-done((f32[8,128]{1,0:T(8,128)S(1)}, f32[8,128]{1,0:T(8,128)S(1)}, u32[]{:S(2)}, u32[]{:S(2)}) %collective-permute-start.20) | collective-permute-done | bytes 4128 | tf_op jit(solution)/shard_map/ppermute | solution.py:25
  79.2 0.9 collective-permute-done.21.refs_2_
  80.1 0.8 near.3
  81.3 0.8 near.4
  82.0 2.3 %collective-permute-start.24 = (bf16[256,1152]{1,0:T(8,128)(2,1)S(1)}, bf16[256,1152]{1,0:T(8,128)(2,1)S(1)}, u32[]{:S(2)}, u32[]{:S(2)}) collective-permute-start(bf16[256,1152]{1,0:T(8,128)(2,1)S(1)} %near.4), channel_id=1, source_target_pairs={{0,6},{1,7},{2,4},{3,5},{4,2},{5,3},{6,0},{7,1},{8,56},{9,57},{10,... | collective-permute-start | bytes 1769480 | tf_op jit(solution)/shard_map/ppermute | solution.py:25
  84.4 0.8 near.5
  85.1 0.9 collective-permute-start.26
  86.8 3.2 %collective-permute-done.27 = f32[8,128]{1,0:T(8,128)S(1)} collective-permute-done((f32[8,128]{1,0:T(8,128)S(1)}, f32[8,128]{1,0:T(8,128)S(1)}, u32[]{:S(2)}, u32[]{:S(2)}) %collective-permute-start.27) | collective-permute-done | bytes 4128 | tf_op jit(solution)/shard_map/ppermute | solution.py:25
  90.0 2.4 %collective-permute-start.28 = (f32[8,128]{1,0:T(8,128)S(1)}, f32[8,128]{1,0:T(8,128)S(1)}, u32[]{:S(2)}, u32[]{:S(2)}) collective-permute-start(f32[8,128]{1,0:T(8,128)S(1)} %add.46), channel_id=1, source_target_pairs={{0,48},{1,49},{2,50},{3,51},{4,52},{5,53},{6,54},{7,55},{8,56},{9,... | collective-permute-start | bytes 12296 | tf_op jit(solution)/shard_map/ppermute | solution.py:25
  92.4 1.5 %collective-permute-done.28 = f32[8,128]{1,0:T(8,128)S(1)} collective-permute-done((f32[8,128]{1,0:T(8,128)S(1)}, f32[8,128]{1,0:T(8,128)S(1)}, u32[]{:S(2)}, u32[]{:S(2)}) %collective-permute-start.28) | collective-permute-done | bytes 4128 | tf_op jit(solution)/shard_map/ppermute | solution.py:25
  94.0 1.2 %collective-permute-done.26.x_ref = bf16[256,1152]{1,0:T(8,128)(2,1)S(1)} collective-permute-done((bf16[256,1152]{1,0:T(8,128)(2,1)S(1)}, bf16[256,1152]{1,0:T(8,128)(2,1)S(1)}, u32[]{:S(2)}, u32[]{:S(2)}) %collective-permute-start.26) | collective-permute-done | bytes 589856 | tf_op jit(solution)/shard_map/ppermute | solution.py:25
  95.2 1.3 %gather_sums.1 = (f32[128,1152]{1,0:T(8,128)S(1)}, f32[136,1152]{1,0:T(8,128)S(1)}) custom-call(s32[1]{0:T(128)} %bitcast.core_ref.refs_0_, f32[1024,1152]{1,0:T(8,128)S(1)} %base.1.refs_1_.base_ref, bf16[256,1152]{1,0:T(8,128)(2,1)S(1)} %collective-permute-done.22.a_ref, bf16[256,1152]{1,0:T(8,128)(2,1)S(1)} %collective-permute-done.24.b_ref, ...), custom_call_target="tpu_custom_call" | custom-call | tf_op jit(solution)/shard_map/gather_sums/pallas_call | solution.py:276
  96.4 1.5 %collective-permute-start.29 = (f32[136,1152]{1,0:T(8,128)S(1)}, f32[136,1152]{1,0:T(8,128)S(1)}, u32[]{:S(2)}, u32[]{:S(2)}) collective-permute-start(f32[136,1152]{1,0:T(8,128)S(1)} %get-tuple-element.127), channel_id=1, source_target_pairs={{0,8},{1,9},{2,10},{3,11},{4,12},{5,13},{6,14},{7,15},{8,0},{9,1},... | collective-permute-start | bytes 1880072 | tf_op jit(solution)/shard_map/ppermute | solution.py:25
  97.9 1.7 %collective-permute-done.29.refs_4_ = f32[136,1152]{1,0:T(8,128)S(1)} collective-permute-done((f32[136,1152]{1,0:T(8,128)S(1)}, f32[136,1152]{1,0:T(8,128)S(1)}, u32[]{:S(2)}, u32[]{:S(2)}) %collective-permute-start.29) | collective-permute-done | bytes 626720 | tf_op jit(solution)/shard_map/ppermute | solution.py:25
  99.6 1.7 %finish.1 = (f32[1,1]{1,0:T(1,128)}, f32[128,1152]{1,0:T(8,128)}, f32[128,1152]{1,0:T(8,128)}) custom-call(s32[1]{0:T(128)} %bitcast.core_ref.refs_0_, f32[128,1152]{1,0:T(8,128)S(1)} %copy-done.1, f32[128,1152]{1,0:T(8,128)S(1)} %copy-done.3, f32[128,1152]{1,0:T(8,128)S(1)} %get-tuple-element.126.refs_3_, f32[136,1152]{1,0:T(8,128)S(1)} %collective-permute-done.29.refs_4_, ...), custom_call_target="tpu_custom_call" | custom-call | tf_op jit(solution)/shard_map/finish/pallas_call | solution.py:276
  (55 shorter events, 8.2 us)
Async XLA Ops:
  0.6 1.1 %copy-start = (f32[128,1152]{1,0:T(8,128)S(1)}, f32[128,1152]{1,0:T(8,128)}, u32[]{:S(2)}) copy-start(f32[128,1152]{1,0:T(8,128)} %refs_1_.1) | copy-start | bytes 1769476
  1.7 1.1 %copy-start.2 = (f32[128,1152]{1,0:T(8,128)S(1)}, f32[128,1152]{1,0:T(8,128)}, u32[]{:S(2)}) copy-start(f32[128,1152]{1,0:T(8,128)} %refs_2_.1) | copy-start | bytes 1769476
  3.3 2.7 %collective-permute-start = (bf16[128,1152]{1,0:T(8,128)(2,1)S(1)}, bf16[128,1152]{1,0:T(8,128)(2,1)S(1)}, u32[]{:S(2)}, u32[]{:S(2)}) collective-permute-start(bf16[128,1152]{1,0:T(8,128)(2,1)S(1)} %get-tuple-element.69), channel_id=1, source_target_pairs={{0,8},{1,9},{2,10},{3,11},{4,12},{5,13},{6,14},{7,15},{8,0},{9,1},... | collective-permute-start | bytes 884744 | tf_op jit(solution)/shard_map/ppermute | solution.py:25
  6.1 9.4 %collective-permute-start.5 = (bf16[256,1152]{1,0:T(8,128)(2,1)S(1)}, bf16[256,1152]{1,0:T(8,128)(2,1)S(1)}, u32[]{:S(2)}, u32[]{:S(2)}) collective-permute-start(bf16[256,1152]{1,0:T(8,128)(2,1)S(1)} %pack.4.refs_0_), channel_id=1, source_target_pairs={{0,2},{1,3},{2,0},{3,1},{4,6},{5,7},{6,4},{7,5},{8,24},{9,25},{10,... | collective-permute-start | bytes 1769480 | tf_op jit(solution)/shard_map/ppermute | solution.py:25
  7.9 10.2 %collective-permute-start.3 = (bf16[256,1152]{1,0:T(8,128)(2,1)S(1)}, bf16[256,1152]{1,0:T(8,128)(2,1)S(1)}, u32[]{:S(2)}, u32[]{:S(2)}) collective-permute-start(bf16[256,1152]{1,0:T(8,128)(2,1)S(1)} %pack.4.refs_0_), channel_id=1, source_target_pairs={{0,1},{1,0},{2,3},{3,2},{4,5},{5,4},{6,7},{7,6},{8,73},{9,72},{10,... | collective-permute-start | bytes 1769480 | tf_op jit(solution)/shard_map/ppermute | solution.py:25
  10.3 10.0 %collective-permute-start.1 = (bf16[256,1152]{1,0:T(8,128)(2,1)S(1)}, bf16[256,1152]{1,0:T(8,128)(2,1)S(1)}, u32[]{:S(2)}, u32[]{:S(2)}) collective-permute-start(bf16[256,1152]{1,0:T(8,128)(2,1)S(1)} %pack.4.refs_0_), channel_id=1, source_target_pairs={{0,6},{1,7},{2,4},{3,5},{4,2},{5,3},{6,0},{7,1},{8,56},{9,57},{10,... | collective-permute-start | bytes 1769480 | tf_op jit(solution)/shard_map/ppermute | solution.py:25
  20.5 7.4 %collective-permute-start.7 = (bf16[1024,1152]{1,0:T(8,128)(2,1)S(1)}, bf16[1024,1152]{1,0:T(8,128)(2,1)S(1)}, u32[]{:S(2)}, u32[]{:S(2)}) collective-permute-start(bf16[1024,1152]{1,0:T(8,128)(2,1)S(1)} %pack.5.near_ref), channel_id=1, source_target_pairs={{0,8},{1,9},{2,10},{3,11},{4,12},{5,13},{6,14},{7,15},{8,0},{9,1},... | collective-permute-start | bytes 7077896 | tf_op jit(solution)/shard_map/ppermute | solution.py:25
  21.0 10.4 %collective-permute-start.6 = (bf16[256,1152]{1,0:T(8,128)(2,1)S(1)}, bf16[256,1152]{1,0:T(8,128)(2,1)S(1)}, u32[]{:S(2)}, u32[]{:S(2)}) collective-permute-start(bf16[256,1152]{1,0:T(8,128)(2,1)S(1)} %collective-permute-done.5.refs_2_), channel_id=1, source_target_pairs={{0,1},{1,0},{2,3},{3,2},{4,5},{5,4},{6,7},{7,6},{8,73},{9,72},{10,... | collective-permute-start | bytes 1769480 | tf_op jit(solution)/shard_map/ppermute | solution.py:25
  22.8 11.0 %collective-permute-start.4 = (bf16[256,1152]{1,0:T(8,128)(2,1)S(1)}, bf16[256,1152]{1,0:T(8,128)(2,1)S(1)}, u32[]{:S(2)}, u32[]{:S(2)}) collective-permute-start(bf16[256,1152]{1,0:T(8,128)(2,1)S(1)} %collective-permute-done.3.refs_1_), channel_id=1, source_target_pairs={{0,6},{1,7},{2,4},{3,5},{4,2},{5,3},{6,0},{7,1},{8,56},{9,57},{10,... | collective-permute-start | bytes 1769480 | tf_op jit(solution)/shard_map/ppermute | solution.py:25
  26.6 8.7 %collective-permute-start.2 = (bf16[256,1152]{1,0:T(8,128)(2,1)S(1)}, bf16[256,1152]{1,0:T(8,128)(2,1)S(1)}, u32[]{:S(2)}, u32[]{:S(2)}) collective-permute-start(bf16[256,1152]{1,0:T(8,128)(2,1)S(1)} %collective-permute-done.1.refs_3_), channel_id=1, source_target_pairs={{0,2},{1,3},{2,0},{3,1},{4,6},{5,7},{6,4},{7,5},{8,24},{9,25},{10,... | collective-permute-start | bytes 1769480 | tf_op jit(solution)/shard_map/ppermute | solution.py:25
  35.5 3.8 %collective-permute-start.10 = (bf16[768,1152]{1,0:T(8,128)(2,1)S(1)}, bf16[768,1152]{1,0:T(8,128)(2,1)S(1)}, u32[]{:S(2)}, u32[]{:S(2)}) collective-permute-start(bf16[768,1152]{1,0:T(8,128)(2,1)S(1)} %pack.6.far_ref), channel_id=1, source_target_pairs={{0,8},{1,9},{2,10},{3,11},{4,12},{5,13},{6,14},{7,15},{8,0},{9,1},... | collective-permute-start | bytes 5308424 | tf_op jit(solution)/shard_map/ppermute | solution.py:25
  35.6 7.3 %collective-permute-start.9 = (bf16[128,1152]{1,0:T(8,128)(2,1)S(1)}, bf16[128,1152]{1,0:T(8,128)(2,1)S(1)}, u32[]{:S(2)}, u32[]{:S(2)}) collective-permute-start(bf16[128,1152]{1,0:T(8,128)(2,1)S(1)} %half_of.3), channel_id=1, source_target_pairs={{0,6},{1,7},{2,4},{3,5},{4,2},{5,3},{6,0},{7,1},{8,56},{9,57},{10,... | collective-permute-start | bytes 884744 | tf_op jit(solution)/shard_map/ppermute | solution.py:25
  37.8 5.9 %collective-permute-start.8 = (bf16[128,1152]{1,0:T(8,128)(2,1)S(1)}, bf16[128,1152]{1,0:T(8,128)(2,1)S(1)}, u32[]{:S(2)}, u32[]{:S(2)}) collective-permute-start(bf16[128,1152]{1,0:T(8,128)(2,1)S(1)} %half_of.2), channel_id=1, source_target_pairs={{0,2},{1,3},{2,0},{3,1},{4,6},{5,7},{6,4},{7,5},{8,24},{9,25},{10,... | collective-permute-start | bytes 884744 | tf_op jit(solution)/shard_map/ppermute | solution.py:25
  43.7 3.5 %collective-permute-start.11 = (bf16[256,1152]{1,0:T(8,128)(2,1)S(1)}, bf16[256,1152]{1,0:T(8,128)(2,1)S(1)}, u32[]{:S(2)}, u32[]{:S(2)}) collective-permute-start(bf16[256,1152]{1,0:T(8,128)(2,1)S(1)} %pack.7.last_ref), channel_id=1, source_target_pairs={{0,8},{1,9},{2,10},{3,11},{4,12},{5,13},{6,14},{7,15},{8,0},{9,1},... | collective-permute-start | bytes 1769480 | tf_op jit(solution)/shard_map/ppermute | solution.py:25
  51.9 5.4 %collective-permute-start.13 = (f32[8,128]{1,0:T(8,128)S(1)}, f32[8,128]{1,0:T(8,128)S(1)}, u32[]{:S(2)}, u32[]{:S(2)}) collective-permute-start(f32[8,128]{1,0:T(8,128)S(1)} %add_add_fusion), channel_id=1, source_target_pairs={{0,1},{1,0},{2,3},{3,2},{4,5},{5,4},{6,7},{7,6},{8,9},{9,8},{10,11... | collective-permute-start | bytes 12296 | tf_op jit(solution)/shard_map/ppermute | solution.py:25
  53.6 3.7 %collective-permute-start.12 = (bf16[256,1152]{1,0:T(8,128)(2,1)S(1)}, bf16[256,1152]{1,0:T(8,128)(2,1)S(1)}, u32[]{:S(2)}, u32[]{:S(2)}) collective-permute-start(bf16[256,1152]{1,0:T(8,128)(2,1)S(1)} %get-tuple-element.92), channel_id=1, source_target_pairs={{0,8},{1,9},{2,10},{3,11},{4,12},{5,13},{6,14},{7,15},{8,0},{9,1},... | collective-permute-start | bytes 1769480 | tf_op jit(solution)/shard_map/ppermute | solution.py:25
  57.5 8.3 %collective-permute-start.14 = (bf16[768,1152]{1,0:T(8,128)(2,1)S(1)}, bf16[768,1152]{1,0:T(8,128)(2,1)S(1)}, u32[]{:S(2)}, u32[]{:S(2)}) collective-permute-start(bf16[768,1152]{1,0:T(8,128)(2,1)S(1)} %get-tuple-element.108), channel_id=1, source_target_pairs={{0,8},{1,9},{2,10},{3,11},{4,12},{5,13},{6,14},{7,15},{8,0},{9,1},... | collective-permute-start | bytes 5308424 | tf_op jit(solution)/shard_map/ppermute | solution.py:25
  58.2 4.4 %collective-permute-start.17 = (f32[8,128]{1,0:T(8,128)S(1)}, f32[8,128]{1,0:T(8,128)S(1)}, u32[]{:S(2)}, u32[]{:S(2)}) collective-permute-start(f32[8,128]{1,0:T(8,128)S(1)} %add.41), channel_id=1, source_target_pairs={{0,65},{1,64},{2,67},{3,66},{4,69},{5,68},{6,71},{7,70},{8,73},{9,... | collective-permute-start | bytes 12296 | tf_op jit(solution)/shard_map/ppermute | solution.py:25
  59.6 7.0 %collective-permute-start.15 = (bf16[128,1152]{1,0:T(8,128)(2,1)S(1)}, bf16[128,1152]{1,0:T(8,128)(2,1)S(1)}, u32[]{:S(2)}, u32[]{:S(2)}) collective-permute-start(bf16[128,1152]{1,0:T(8,128)(2,1)S(1)} %get-tuple-element.109), channel_id=1, source_target_pairs={{0,2},{1,3},{2,0},{3,1},{4,6},{5,7},{6,4},{7,5},{8,24},{9,25},{10,... | collective-permute-start | bytes 884744 | tf_op jit(solution)/shard_map/ppermute | solution.py:25
  59.6 7.1 %collective-permute-start.16 = (bf16[128,1152]{1,0:T(8,128)(2,1)S(1)}, bf16[128,1152]{1,0:T(8,128)(2,1)S(1)}, u32[]{:S(2)}, u32[]{:S(2)}) collective-permute-start(bf16[128,1152]{1,0:T(8,128)(2,1)S(1)} %get-tuple-element.110), channel_id=1, source_target_pairs={{0,6},{1,7},{2,4},{3,5},{4,2},{5,3},{6,0},{7,1},{8,56},{9,57},{10,... | collective-permute-start | bytes 884744 | tf_op jit(solution)/shard_map/ppermute | solution.py:25
  62.7 3.1 %collective-permute-start.18 = (f32[8,128]{1,0:T(8,128)S(1)}, f32[8,128]{1,0:T(8,128)S(1)}, u32[]{:S(2)}, u32[]{:S(2)}) collective-permute-start(f32[8,128]{1,0:T(8,128)S(1)} %add.43), channel_id=1, source_target_pairs={{0,2},{1,3},{2,0},{3,1},{4,6},{5,7},{6,4},{7,5},{8,10},{9,11},{10,... | collective-permute-start | bytes 12296 | tf_op jit(solution)/shard_map/ppermute | solution.py:25
  67.9 6.1 %collective-permute-start.19 = (bf16[1024,1152]{1,0:T(8,128)(2,1)S(1)}, bf16[1024,1152]{1,0:T(8,128)(2,1)S(1)}, u32[]{:S(2)}, u32[]{:S(2)}) collective-permute-start(bf16[1024,1152]{1,0:T(8,128)(2,1)S(1)} %get-tuple-element.117), channel_id=1, source_target_pairs={{0,8},{1,9},{2,10},{3,11},{4,12},{5,13},{6,14},{7,15},{8,0},{9,1},... | collective-permute-start | bytes 7077896 | tf_op jit(solution)/shard_map/ppermute | solution.py:25
  69.8 10.2 %collective-permute-start.21 = (bf16[256,1152]{1,0:T(8,128)(2,1)S(1)}, bf16[256,1152]{1,0:T(8,128)(2,1)S(1)}, u32[]{:S(2)}, u32[]{:S(2)}) collective-permute-start(bf16[256,1152]{1,0:T(8,128)(2,1)S(1)} %get-tuple-element.122), channel_id=1, source_target_pairs={{0,1},{1,0},{2,3},{3,2},{4,5},{5,4},{6,7},{7,6},{8,73},{9,72},{10,... | collective-permute-start | bytes 1769480 | tf_op jit(solution)/shard_map/ppermute | solution.py:25
  71.2 10.1 %collective-permute-start.23 = (bf16[256,1152]{1,0:T(8,128)(2,1)S(1)}, bf16[256,1152]{1,0:T(8,128)(2,1)S(1)}, u32[]{:S(2)}, u32[]{:S(2)}) collective-permute-start(bf16[256,1152]{1,0:T(8,128)(2,1)S(1)} %second.1), channel_id=1, source_target_pairs={{0,2},{1,3},{2,0},{3,1},{4,6},{5,7},{6,4},{7,5},{8,24},{9,25},{10,... | collective-permute-start | bytes 1769480 | tf_op jit(solution)/shard_map/ppermute | solution.py:25
  71.2 13.1 %collective-permute-start.25 = (bf16[256,1152]{1,0:T(8,128)(2,1)S(1)}, bf16[256,1152]{1,0:T(8,128)(2,1)S(1)}, u32[]{:S(2)}, u32[]{:S(2)}) collective-permute-start(bf16[256,1152]{1,0:T(8,128)(2,1)S(1)} %get-tuple-element.124), channel_id=1, source_target_pairs={{0,6},{1,7},{2,4},{3,5},{4,2},{5,3},{6,0},{7,1},{8,56},{9,57},{10,... | collective-permute-start | bytes 1769480 | tf_op jit(solution)/shard_map/ppermute | solution.py:25
  75.0 4.2 %collective-permute-start.20 = (f32[8,128]{1,0:T(8,128)S(1)}, f32[8,128]{1,0:T(8,128)S(1)}, u32[]{:S(2)}, u32[]{:S(2)}) collective-permute-start(f32[8,128]{1,0:T(8,128)S(1)} %add.44), channel_id=1, source_target_pairs={{0,6},{1,7},{2,4},{3,5},{4,2},{5,3},{6,0},{7,1},{8,14},{9,15},{10,... | collective-permute-start | bytes 12296 | tf_op jit(solution)/shard_map/ppermute | solution.py:25
  80.8 13.1 %collective-permute-start.22 = (bf16[256,1152]{1,0:T(8,128)(2,1)S(1)}, bf16[256,1152]{1,0:T(8,128)(2,1)S(1)}, u32[]{:S(2)}, u32[]{:S(2)}) collective-permute-start(bf16[256,1152]{1,0:T(8,128)(2,1)S(1)} %near.3), channel_id=1, source_target_pairs={{0,2},{1,3},{2,0},{3,1},{4,6},{5,7},{6,4},{7,5},{8,24},{9,25},{10,... | collective-permute-start | bytes 1769480 | tf_op jit(solution)/shard_map/ppermute | solution.py:25
  82.0 12.0 %collective-permute-start.24 = (bf16[256,1152]{1,0:T(8,128)(2,1)S(1)}, bf16[256,1152]{1,0:T(8,128)(2,1)S(1)}, u32[]{:S(2)}, u32[]{:S(2)}) collective-permute-start(bf16[256,1152]{1,0:T(8,128)(2,1)S(1)} %near.4), channel_id=1, source_target_pairs={{0,6},{1,7},{2,4},{3,5},{4,2},{5,3},{6,0},{7,1},{8,56},{9,57},{10,... | collective-permute-start | bytes 1769480 | tf_op jit(solution)/shard_map/ppermute | solution.py:25
  85.1 10.0 %collective-permute-start.26 = (bf16[256,1152]{1,0:T(8,128)(2,1)S(1)}, bf16[256,1152]{1,0:T(8,128)(2,1)S(1)}, u32[]{:S(2)}, u32[]{:S(2)}) collective-permute-start(bf16[256,1152]{1,0:T(8,128)(2,1)S(1)} %near.5), channel_id=1, source_target_pairs={{0,1},{1,0},{2,3},{3,2},{4,5},{5,4},{6,7},{7,6},{8,73},{9,72},{10,... | collective-permute-start | bytes 1769480 | tf_op jit(solution)/shard_map/ppermute | solution.py:25
  86.0 4.0 %collective-permute-start.27 = (f32[8,128]{1,0:T(8,128)S(1)}, f32[8,128]{1,0:T(8,128)S(1)}, u32[]{:S(2)}, u32[]{:S(2)}) collective-permute-start(f32[8,128]{1,0:T(8,128)S(1)} %add.45), channel_id=1, source_target_pairs={{0,16},{1,17},{2,18},{3,19},{4,20},{5,21},{6,22},{7,23},{8,24},{9,... | collective-permute-start | bytes 12296 | tf_op jit(solution)/shard_map/ppermute | solution.py:25
  90.0 4.0 %collective-permute-start.28 = (f32[8,128]{1,0:T(8,128)S(1)}, f32[8,128]{1,0:T(8,128)S(1)}, u32[]{:S(2)}, u32[]{:S(2)}) collective-permute-start(f32[8,128]{1,0:T(8,128)S(1)} %add.46), channel_id=1, source_target_pairs={{0,48},{1,49},{2,50},{3,51},{4,52},{5,53},{6,54},{7,55},{8,56},{9,... | collective-permute-start | bytes 12296 | tf_op jit(solution)/shard_map/ppermute | solution.py:25
  94.0 5.6 %copy-start.1 = (f32[128,1152]{1,0:T(8,128)S(1)}, f32[128,1152]{1,0:T(8,128)}, u32[]{:S(2)}) copy-start(f32[128,1152]{1,0:T(8,128)} %refs_1_.1) | copy-start | bytes 1769476
  94.0 5.6 %copy-start.3 = (f32[128,1152]{1,0:T(8,128)S(1)}, f32[128,1152]{1,0:T(8,128)}, u32[]{:S(2)}) copy-start(f32[128,1152]{1,0:T(8,128)} %refs_2_.1) | copy-start | bytes 1769476
  96.4 3.2 %collective-permute-start.29 = (f32[136,1152]{1,0:T(8,128)S(1)}, f32[136,1152]{1,0:T(8,128)S(1)}, u32[]{:S(2)}, u32[]{:S(2)}) collective-permute-start(f32[136,1152]{1,0:T(8,128)S(1)} %get-tuple-element.127), channel_id=1, source_target_pairs={{0,8},{1,9},{2,10},{3,11},{4,12},{5,13},{6,14},{7,15},{8,0},{9,1},... | collective-permute-start | bytes 1880072 | tf_op jit(solution)/shard_map/ppermute | solution.py:25

commit v6 on v5

--- a/solution.py
+++ b/solution.py
@@ -554,9 +554,9 @@
     (base,) = small_call(
         base_kernel, "base", core, (near_part, near_received, img_part, rest_received), (array(wide, jnp.float32),)
     )
-    base, loss = lax.optimization_barrier((base, loss))
-    loss = loss + swap(loss, 0, 6)
-    base, loss = lax.optimization_barrier((base, loss))
+    more = swap(loss, 0, 6)
+    base, more = lax.optimization_barrier((base, more))
+    loss = loss + more
 
     def near_slot(k, received):
         (out,) = small_call(

time: 102 us -> 102 us (level)
  transfers between devices with their start and end apart: 30 -> 30, of which waited for: 16 -> 15; matrix products, arithmetic and copies ran while one was open for 8% -> 8% of each run, Pallas kernels for 13% -> 13%
where the time goes in v6:
time: 102 us; the launch traced here: 101 us
  starting transfers between devices  38.6 us (38%)
  waiting for transfers between devices  27 us (26%)
  Pallas kernels  23 us (23%)
  matrix products  8.31 us (8%)
  between operations  2.26 us (2%)
  local copies, waits for them, and re-layouts  2.14 us (2%)
    ppermute x30, starting transfers between devices, exchange(): return lax.ppermute(x, AXES, pairs)  38.6 us
    ppermute x30, waiting for transfers between devices, exchange(): return lax.ppermute(x, AXES, pairs)  27 us
    pallas_call x4, Pallas kernels, tile_call(): pl.pallas_call(kernel, out_shape=outs, in_specs=[SMEM] + [VMEM] * (len(sc...  13.7 us
    pallas_call x9, Pallas kernels, small_call(): pl.pallas_call(kernel, out_shape=outs, in_specs=[SMEM] + [VMEM] * len(arr...  8.4 us
    dot_general x6, matrix products, transposed_product(): lax.dot_general(weights, img, (((0,), (0,)), ((), ())), preferred_element...  8.31 us
    unnamed x8, local copies, waits for them, and re-layouts  2.13 us
  transfers between devices with their start and end apart: 30, of which 15 were waited for; matrix products, arithmetic and copies ran while one was open for 8% of the time, Pallas kernels for 13%

profile of v6, /device:TPU:1, one launch (start us, length us, event | category | flops | bytes accessed | tf_op | source)
XLA Modules:
  0.0 101.3 jit_solution(9835774777632247933)
XLA Ops:
  0.6 1.1 %copy-done = f32[128,1152]{1,0:T(8,128)S(1)} copy-done((f32[128,1152]{1,0:T(8,128)S(1)}, f32[128,1152]{1,0:T(8,128)}, u32[]{:S(2)}) %copy-start) | copy-done | bytes 589848
  1.7 1.1 %copy-done.2 = f32[128,1152]{1,0:T(8,128)S(1)} copy-done((f32[128,1152]{1,0:T(8,128)S(1)}, f32[128,1152]{1,0:T(8,128)}, u32[]{:S(2)}) %copy-start.2) | copy-done | bytes 589848
  3.3 1.5 %collective-permute-start = (bf16[128,1152]{1,0:T(8,128)(2,1)S(1)}, bf16[128,1152]{1,0:T(8,128)(2,1)S(1)}, u32[]{:S(2)}, u32[]{:S(2)}) collective-permute-start(bf16[128,1152]{1,0:T(8,128)(2,1)S(1)} %get-tuple-element.67), channel_id=1, source_target_pairs={{0,8},{1,9},{2,10},{3,11},{4,12},{5,13},{6,14},{7,15},{8,0},{9,1},... | collective-permute-start | bytes 884744 | tf_op jit(solution)/shard_map/ppermute | solution.py:25
  4.8 1.2 %collective-permute-done.refs_1_ = bf16[128,1152]{1,0:T(8,128)(2,1)S(1)} collective-permute-done((bf16[128,1152]{1,0:T(8,128)(2,1)S(1)}, bf16[128,1152]{1,0:T(8,128)(2,1)S(1)}, u32[]{:S(2)}, u32[]{:S(2)}) %collective-permute-start) | collective-permute-done | bytes 294944 | tf_op jit(solution)/shard_map/ppermute | solution.py:25
  6.1 1.8 %collective-permute-start.5 = (bf16[256,1152]{1,0:T(8,128)(2,1)S(1)}, bf16[256,1152]{1,0:T(8,128)(2,1)S(1)}, u32[]{:S(2)}, u32[]{:S(2)}) collective-permute-start(bf16[256,1152]{1,0:T(8,128)(2,1)S(1)} %pack.4.refs_0_), channel_id=1, source_target_pairs={{0,2},{1,3},{2,0},{3,1},{4,6},{5,7},{6,4},{7,5},{8,24},{9,25},{10,... | collective-permute-start | bytes 1769480 | tf_op jit(solution)/shard_map/ppermute | solution.py:25
  7.9 2.5 %collective-permute-start.3 = (bf16[256,1152]{1,0:T(8,128)(2,1)S(1)}, bf16[256,1152]{1,0:T(8,128)(2,1)S(1)}, u32[]{:S(2)}, u32[]{:S(2)}) collective-permute-start(bf16[256,1152]{1,0:T(8,128)(2,1)S(1)} %pack.4.refs_0_), channel_id=1, source_target_pairs={{0,1},{1,0},{2,3},{3,2},{4,5},{5,4},{6,7},{7,6},{8,73},{9,72},{10,... | collective-permute-start | bytes 1769480 | tf_op jit(solution)/shard_map/ppermute | solution.py:25
  10.3 2.2 %collective-permute-start.1 = (bf16[256,1152]{1,0:T(8,128)(2,1)S(1)}, bf16[256,1152]{1,0:T(8,128)(2,1)S(1)}, u32[]{:S(2)}, u32[]{:S(2)}) collective-permute-start(bf16[256,1152]{1,0:T(8,128)(2,1)S(1)} %pack.4.refs_0_), channel_id=1, source_target_pairs={{0,6},{1,7},{2,4},{3,5},{4,2},{5,3},{6,0},{7,1},{8,56},{9,57},{10,... | collective-permute-start | bytes 1769480 | tf_op jit(solution)/shard_map/ppermute | solution.py:25
  12.6 2.8 %collective-permute-done.5.refs_2_ = bf16[256,1152]{1,0:T(8,128)(2,1)S(1)} collective-permute-done((bf16[256,1152]{1,0:T(8,128)(2,1)S(1)}, bf16[256,1152]{1,0:T(8,128)(2,1)S(1)}, u32[]{:S(2)}, u32[]{:S(2)}) %collective-permute-start.5) | collective-permute-done | bytes 589856 | tf_op jit(solution)/shard_map/ppermute | solution.py:25
  15.4 2.7 %collective-permute-done.3.refs_1_ = bf16[256,1152]{1,0:T(8,128)(2,1)S(1)} collective-permute-done((bf16[256,1152]{1,0:T(8,128)(2,1)S(1)}, bf16[256,1152]{1,0:T(8,128)(2,1)S(1)}, u32[]{:S(2)}, u32[]{:S(2)}) %collective-permute-start.3) | collective-permute-done | bytes 589856 | tf_op jit(solution)/shard_map/ppermute | solution.py:25
  18.1 2.3 %collective-permute-done.1.refs_3_ = bf16[256,1152]{1,0:T(8,128)(2,1)S(1)} collective-permute-done((bf16[256,1152]{1,0:T(8,128)(2,1)S(1)}, bf16[256,1152]{1,0:T(8,128)(2,1)S(1)}, u32[]{:S(2)}, u32[]{:S(2)}) %collective-permute-start.1) | collective-permute-done | bytes 589856 | tf_op jit(solution)/shard_map/ppermute | solution.py:25
  21.0 1.8 %collective-permute-start.6 = (bf16[256,1152]{1,0:T(8,128)(2,1)S(1)}, bf16[256,1152]{1,0:T(8,128)(2,1)S(1)}, u32[]{:S(2)}, u32[]{:S(2)}) collective-permute-start(bf16[256,1152]{1,0:T(8,128)(2,1)S(1)} %collective-permute-done.5.refs_2_), channel_id=1, source_target_pairs={{0,1},{1,0},{2,3},{3,2},{4,5},{5,4},{6,7},{7,6},{8,73},{9,72},{10,... | collective-permute-start | bytes 1769480 | tf_op jit(solution)/shard_map/ppermute | solution.py:25
  22.8 3.8 %collective-permute-start.4 = (bf16[256,1152]{1,0:T(8,128)(2,1)S(1)}, bf16[256,1152]{1,0:T(8,128)(2,1)S(1)}, u32[]{:S(2)}, u32[]{:S(2)}) collective-permute-start(bf16[256,1152]{1,0:T(8,128)(2,1)S(1)} %collective-permute-done.3.refs_1_), channel_id=1, source_target_pairs={{0,6},{1,7},{2,4},{3,5},{4,2},{5,3},{6,0},{7,1},{8,56},{9,57},{10,... | collective-permute-start | bytes 1769480 | tf_op jit(solution)/shard_map/ppermute | solution.py:25
  27.9 3.5 %tile_near.1 = (bf16[512,1152]{1,0:T(8,128)(2,1)S(1)}, bf16[1024,1152]{1,0:T(8,128)(2,1)S(1)}, bf16[512,1024]{1,0:T(8,128)(2,1)S(1)}, f32[512,1152]{1,0:T(8,128)S(1)}, f32[8,128]{1,0:T(8,128)S(1)}) custom-call(s32[1]{0:T(128)} %bitcast.core_ref.refs_0_, f32[8,128]{1,0:T(8,128)S(1)} %broadcast_in_dim.15.sharp_ref, f32[8,128]{1,0:T(8,128)S(1)} %broadcast_in_dim.17.bias_ref, ...), custom_call_target="tpu_custom_call" | custom-call | flops 2415919104 | bytes 4718592 | tf_op jit(solution)/shard_map/tile_near/pallas_call | solution.py:258
  31.4 2.4 %collective-permute-done.4.refs_0_.refs_2_ = bf16[256,1152]{1,0:T(8,128)(2,1)S(1)} collective-permute-done((bf16[256,1152]{1,0:T(8,128)(2,1)S(1)}, bf16[256,1152]{1,0:T(8,128)(2,1)S(1)}, u32[]{:S(2)}, u32[]{:S(2)}) %collective-permute-start.4) | collective-permute-done | bytes 589856 | tf_op jit(solution)/shard_map/ppermute | solution.py:25
  33.9 1.5 %collective-permute-done.2.refs_0_ = bf16[256,1152]{1,0:T(8,128)(2,1)S(1)} collective-permute-done((bf16[256,1152]{1,0:T(8,128)(2,1)S(1)}, bf16[256,1152]{1,0:T(8,128)(2,1)S(1)}, u32[]{:S(2)}, u32[]{:S(2)}) %collective-permute-start.2) | collective-permute-done | bytes 589856 | tf_op jit(solution)/shard_map/ppermute | solution.py:25
  35.6 2.2 %collective-permute-start.9 = (bf16[128,1152]{1,0:T(8,128)(2,1)S(1)}, bf16[128,1152]{1,0:T(8,128)(2,1)S(1)}, u32[]{:S(2)}, u32[]{:S(2)}) collective-permute-start(bf16[128,1152]{1,0:T(8,128)(2,1)S(1)} %half_of.3), channel_id=1, source_target_pairs={{0,6},{1,7},{2,4},{3,5},{4,2},{5,3},{6,0},{7,1},{8,56},{9,57},{10,... | collective-permute-start | bytes 884744 | tf_op jit(solution)/shard_map/ppermute | solution.py:25
  37.8 1.4 %collective-permute-done.10.received_ref.far_received_ref = bf16[768,1152]{1,0:T(8,128)(2,1)S(1)} collective-permute-done((bf16[768,1152]{1,0:T(8,128)(2,1)S(1)}, bf16[768,1152]{1,0:T(8,128)(2,1)S(1)}, u32[]{:S(2)}, u32[]{:S(2)}) %collective-permute-start.10) | collective-permute-done | bytes 1769504 | tf_op jit(solution)/shard_map/ppermute | solution.py:25
  39.2 3.7 %tile_far.1 = (bf16[768,1152]{1,0:T(8,128)(2,1)S(1)}, bf16[768,1152]{1,0:T(8,128)(2,1)S(1)}, bf16[768,768]{1,0:T(8,128)(2,1)S(1)}, f32[768,1152]{1,0:T(8,128)S(1)}, f32[8,128]{1,0:T(8,128)S(1)}) custom-call(s32[1]{0:T(128)} %bitcast.core_ref.refs_0_, f32[8,128]{1,0:T(8,128)S(1)} %broadcast_in_dim.15.sharp_ref, f32[8,128]{1,0:T(8,128)S(1)} %broadcast_in_dim.17.bias_ref, ...), custom_call_target="tpu_custom_call" | custom-call | flops 2717908992 | bytes 5898240 | tf_op jit(solution)/shard_map/tile_far/pallas_call | solution.py:258
  43.7 1.7 %collective-permute-start.11 = (bf16[256,1152]{1,0:T(8,128)(2,1)S(1)}, bf16[256,1152]{1,0:T(8,128)(2,1)S(1)}, u32[]{:S(2)}, u32[]{:S(2)}) collective-permute-start(bf16[256,1152]{1,0:T(8,128)(2,1)S(1)} %pack.7.last_ref), channel_id=1, source_target_pairs={{0,8},{1,9},{2,10},{3,11},{4,12},{5,13},{6,14},{7,15},{8,0},{9,1},... | collective-permute-start | bytes 1769480 | tf_op jit(solution)/shard_map/ppermute | solution.py:25
  45.4 1.9 %tile_middle.1 = (bf16[768,1024]{1,0:T(8,128)(2,1)S(1)}, f32[256,1152]{1,0:T(8,128)S(1)}, f32[8,128]{1,0:T(8,128)S(1)}) custom-call(s32[1]{0:T(128)} %bitcast.core_ref.refs_0_, f32[8,128]{1,0:T(8,128)S(1)} %broadcast_in_dim.15.sharp_ref, f32[8,128]{1,0:T(8,128)S(1)} %broadcast_in_dim.17.bias_ref, bf16[768,1152]{1,0:T(8,128)(2,1)S(1)} %get-tuple-element.79.img_ref, ...), custom_call_target="tpu_custom_call" | custom-call | flops 1207959552 | bytes 6946816 | tf_op jit(solution)/shard_map/tile_middle/pallas_call | solution.py:258
  47.3 4.6 %tile_last.1 = (bf16[768,256]{1,0:T(8,128)(2,1)S(1)}, f32[768,1152]{1,0:T(8,128)S(1)}, bf16[256,1152]{1,0:T(8,128)(2,1)S(1)}, bf16[256,1024]{1,0:T(8,128)(2,1)S(...) custom-call(s32[1]{0:T(128)} %bitcast.core_ref.refs_0_, ...), custom_call_target="tpu_custom_call" | custom-call | flops 3321888768 | bytes 12976128 | tf_op jit(solution)/shard_map/tile_last/pallas_call | solution.py:258
  52.7 0.9 fusion.5
  54.8 2.5 %fusion.3 = (bf16[768,1152]{1,0:T(8,128)(2,1)S(1)}, f32[768,1152]{1,0:T(8,128)S(1)}) fusion(f32[768,1152]{1,0:T(8,128)S(1)} %get-tuple-element.91.img_ref, pred[]{:T(512)S(6)} %eq.3, f32[768,1152]{1,0:T(8,128)S(1)} %fusion.7, bf16[768,768]{1,0:T(8,128)(2,1)S(1)} %get-tuple-element.92, bf16[768,1152]{1,0:T(8,128)(2,1)S(1)} %get-tuple-element.79.img_ref), kind=kOutput, calls=%fused_computation.9 | convolution fusion | flops 1367801856 | bytes 15335425 | tf_op jit(solution)/shard_map/dot_general | solution.py:423
  58.2 1.3 %collective-permute-start.17 = (f32[8,128]{1,0:T(8,128)S(1)}, f32[8,128]{1,0:T(8,128)S(1)}, u32[]{:S(2)}, u32[]{:S(2)}) collective-permute-start(f32[8,128]{1,0:T(8,128)S(1)} %add.41), channel_id=1, source_target_pairs={{0,65},{1,64},{2,67},{3,66},{4,69},{5,68},{6,71},{7,70},{8,73},{9,... | collective-permute-start | bytes 12296 | tf_op jit(solution)/shard_map/ppermute | solution.py:25
  59.6 2.2 %collective-permute-start.16 = (bf16[128,1152]{1,0:T(8,128)(2,1)S(1)}, bf16[128,1152]{1,0:T(8,128)(2,1)S(1)}, u32[]{:S(2)}, u32[]{:S(2)}) collective-permute-start(bf16[128,1152]{1,0:T(8,128)(2,1)S(1)} %get-tuple-element.108), channel_id=1, source_target_pairs={{0,6},{1,7},{2,4},{3,5},{4,2},{5,3},{6,0},{7,1},{8,56},{9,57},{10,... | collective-permute-start | bytes 884744 | tf_op jit(solution)/shard_map/ppermute | solution.py:25
  61.8 0.9 fusion.8
  62.8 3.0 %fusion.1 = (bf16[1024,1152]{1,0:T(8,128)(2,1)S(1)}, f32[1024,1152]{1,0:T(8,128)S(1)}) fusion(f32[1024,1152]{1,0:T(8,128)S(1)} %fusion.8, bf16[768,1024]{1,0:T(8,128)(2,1)S(1)} %get-tuple-element.104, bf16[768,1152]{1,0:T(8,128)(2,1)S(1)} %get-tuple-element.79.img_ref), kind=kOutput, calls=%fused_computation.5 | convolution fusion | flops 1822556160 | bytes 15138816 | tf_op jit(solution)/shard_map/dot_general | solution.py:423
  66.7 1.2 %far.1 = (bf16[256,1152]{1,0:T(8,128)(2,1)S(1)}, bf16[256,1152]{1,0:T(8,128)(2,1)S(1)}) custom-call(s32[1]{0:T(128)} %bitcast.core_ref.refs_0_, f32[768,1152]{1,0:T(8,128)S(1)} %get-tuple-element.130.txt_ref, bf16[768,1152]{1,0:T(8,128)(2,1)S(1)} %collective-permute-done.14.received_ref.txt_received_ref.img_received_ref, ...), custom_call_target="tpu_custom_call" | custom-call | tf_op jit(solution)/shard_map/far/pallas_call | solution.py:276
  67.9 2.0 %collective-permute-start.19 = (bf16[1024,1152]{1,0:T(8,128)(2,1)S(1)}, bf16[1024,1152]{1,0:T(8,128)(2,1)S(1)}, u32[]{:S(2)}, u32[]{:S(2)}) collective-permute-start(bf16[1024,1152]{1,0:T(8,128)(2,1)S(1)} %get-tuple-element.115), channel_id=1, source_target_pairs={{0,8},{1,9},{2,10},{3,11},{4,12},{5,13},{6,14},{7,15},{8,0},{9,1},... | collective-permute-start | bytes 7077896 | tf_op jit(solution)/shard_map/ppermute | solution.py:25
  69.8 1.3 %collective-permute-start.21 = (bf16[256,1152]{1,0:T(8,128)(2,1)S(1)}, bf16[256,1152]{1,0:T(8,128)(2,1)S(1)}, u32[]{:S(2)}, u32[]{:S(2)}) collective-permute-start(bf16[256,1152]{1,0:T(8,128)(2,1)S(1)} %get-tuple-element.118), channel_id=1, source_target_pairs={{0,1},{1,0},{2,3},{3,2},{4,5},{5,4},{6,7},{7,6},{8,73},{9,72},{10,... | collective-permute-start | bytes 1769480 | tf_op jit(solution)/shard_map/ppermute | solution.py:25
  71.2 2.0 %collective-permute-start.25 = (bf16[256,1152]{1,0:T(8,128)(2,1)S(1)}, bf16[256,1152]{1,0:T(8,128)(2,1)S(1)}, u32[]{:S(2)}, u32[]{:S(2)}) collective-permute-start(bf16[256,1152]{1,0:T(8,128)(2,1)S(1)} %get-tuple-element.120), channel_id=1, source_target_pairs={{0,6},{1,7},{2,4},{3,5},{4,2},{5,3},{6,0},{7,1},{8,56},{9,57},{10,... | collective-permute-start | bytes 1769480 | tf_op jit(solution)/shard_map/ppermute | solution.py:25
  73.2 1.6 %collective-permute-start.20 = (f32[8,128]{1,0:T(8,128)S(1)}, f32[8,128]{1,0:T(8,128)S(1)}, u32[]{:S(2)}, u32[]{:S(2)}) collective-permute-start(f32[8,128]{1,0:T(8,128)S(1)} %add.44), channel_id=1, source_target_pairs={{0,6},{1,7},{2,4},{3,5},{4,2},{5,3},{6,0},{7,1},{8,14},{9,15},{10,... | collective-permute-start | bytes 12296 | tf_op jit(solution)/shard_map/ppermute | solution.py:25
  74.9 1.0 base.1.refs_1_.base_ref
  75.9 1.4 %collective-permute-done.20 = f32[8,128]{1,0:T(8,128)S(1)} collective-permute-done((f32[8,128]{1,0:T(8,128)S(1)}, f32[8,128]{1,0:T(8,128)S(1)}, u32[]{:S(2)}, u32[]{:S(2)}) %collective-permute-start.20) | collective-permute-done | bytes 4128 | tf_op jit(solution)/shard_map/ppermute | solution.py:25
  77.3 2.8 %collective-permute-done.21.refs_2_ = bf16[256,1152]{1,0:T(8,128)(2,1)S(1)} collective-permute-done((bf16[256,1152]{1,0:T(8,128)(2,1)S(1)}, bf16[256,1152]{1,0:T(8,128)(2,1)S(1)}, u32[]{:S(2)}, u32[]{:S(2)}) %collective-permute-start.21) | collective-permute-done | bytes 589856 | tf_op jit(solution)/shard_map/ppermute | solution.py:25
  80.1 0.8 near.3
  81.3 0.8 near.4
  82.0 2.3 %collective-permute-start.24 = (bf16[256,1152]{1,0:T(8,128)(2,1)S(1)}, bf16[256,1152]{1,0:T(8,128)(2,1)S(1)}, u32[]{:S(2)}, u32[]{:S(2)}) collective-permute-start(bf16[256,1152]{1,0:T(8,128)(2,1)S(1)} %near.4), channel_id=1, source_target_pairs={{0,6},{1,7},{2,4},{3,5},{4,2},{5,3},{6,0},{7,1},{8,56},{9,57},{10,... | collective-permute-start | bytes 1769480 | tf_op jit(solution)/shard_map/ppermute | solution.py:25
  84.4 0.8 near.5
  85.1 0.9 collective-permute-start.26
  86.8 3.2 %collective-permute-done.27 = f32[8,128]{1,0:T(8,128)S(1)} collective-permute-done((f32[8,128]{1,0:T(8,128)S(1)}, f32[8,128]{1,0:T(8,128)S(1)}, u32[]{:S(2)}, u32[]{:S(2)}) %collective-permute-start.27) | collective-permute-done | bytes 4128 | tf_op jit(solution)/shard_map/ppermute | solution.py:25
  90.0 2.4 %collective-permute-start.28 = (f32[8,128]{1,0:T(8,128)S(1)}, f32[8,128]{1,0:T(8,128)S(1)}, u32[]{:S(2)}, u32[]{:S(2)}) collective-permute-start(f32[8,128]{1,0:T(8,128)S(1)} %add.46), channel_id=1, source_target_pairs={{0,48},{1,49},{2,50},{3,51},{4,52},{5,53},{6,54},{7,55},{8,56},{9,... | collective-permute-start | bytes 12296 | tf_op jit(solution)/shard_map/ppermute | solution.py:25
  92.4 1.5 %collective-permute-done.28 = f32[8,128]{1,0:T(8,128)S(1)} collective-permute-done((f32[8,128]{1,0:T(8,128)S(1)}, f32[8,128]{1,0:T(8,128)S(1)}, u32[]{:S(2)}, u32[]{:S(2)}) %collective-permute-start.28) | collective-permute-done | bytes 4128 | tf_op jit(solution)/shard_map/ppermute | solution.py:25
  94.0 1.2 %collective-permute-done.26.x_ref = bf16[256,1152]{1,0:T(8,128)(2,1)S(1)} collective-permute-done((bf16[256,1152]{1,0:T(8,128)(2,1)S(1)}, bf16[256,1152]{1,0:T(8,128)(2,1)S(1)}, u32[]{:S(2)}, u32[]{:S(2)}) %collective-permute-start.26) | collective-permute-done | bytes 589856 | tf_op jit(solution)/shard_map/ppermute | solution.py:25
  95.2 1.3 %gather_sums.1 = (f32[128,1152]{1,0:T(8,128)S(1)}, f32[136,1152]{1,0:T(8,128)S(1)}) custom-call(s32[1]{0:T(128)} %bitcast.core_ref.refs_0_, f32[1024,1152]{1,0:T(8,128)S(1)} %base.1.refs_1_.base_ref, bf16[256,1152]{1,0:T(8,128)(2,1)S(1)} %collective-permute-done.22.a_ref, bf16[256,1152]{1,0:T(8,128)(2,1)S(1)} %collective-permute-done.24.b_ref, ...), custom_call_target="tpu_custom_call" | custom-call | tf_op jit(solution)/shard_map/gather_sums/pallas_call | solution.py:276
  96.4 1.5 %collective-permute-start.29 = (f32[136,1152]{1,0:T(8,128)S(1)}, f32[136,1152]{1,0:T(8,128)S(1)}, u32[]{:S(2)}, u32[]{:S(2)}) collective-permute-start(f32[136,1152]{1,0:T(8,128)S(1)} %get-tuple-element.123), channel_id=1, source_target_pairs={{0,8},{1,9},{2,10},{3,11},{4,12},{5,13},{6,14},{7,15},{8,0},{9,1},... | collective-permute-start | bytes 1880072 | tf_op jit(solution)/shard_map/ppermute | solution.py:25
  97.9 1.7 %collective-permute-done.29.refs_4_ = f32[136,1152]{1,0:T(8,128)S(1)} collective-permute-done((f32[136,1152]{1,0:T(8,128)S(1)}, f32[136,1152]{1,0:T(8,128)S(1)}, u32[]{:S(2)}, u32[]{:S(2)}) %collective-permute-start.29) | collective-permute-done | bytes 626720 | tf_op jit(solution)/shard_map/ppermute | solution.py:25
  99.6 1.7 %finish.1 = (f32[1,1]{1,0:T(1,128)}, f32[128,1152]{1,0:T(8,128)}, f32[128,1152]{1,0:T(8,128)}) custom-call(s32[1]{0:T(128)} %bitcast.core_ref.refs_0_, f32[128,1152]{1,0:T(8,128)S(1)} %copy-done.1, f32[128,1152]{1,0:T(8,128)S(1)} %copy-done.3, f32[128,1152]{1,0:T(8,128)S(1)} %get-tuple-element.122.refs_3_, f32[136,1152]{1,0:T(8,128)S(1)} %collective-permute-done.29.refs_4_, ...), custom_call_target="tpu_custom_call" | custom-call | tf_op jit(solution)/shard_map/finish/pallas_call | solution.py:276
  (55 shorter events, 7.4 us)
Async XLA Ops:
  0.6 1.1 %copy-start = (f32[128,1152]{1,0:T(8,128)S(1)}, f32[128,1152]{1,0:T(8,128)}, u32[]{:S(2)}) copy-start(f32[128,1152]{1,0:T(8,128)} %refs_1_.1) | copy-start | bytes 1769476
  1.7 1.1 %copy-start.2 = (f32[128,1152]{1,0:T(8,128)S(1)}, f32[128,1152]{1,0:T(8,128)}, u32[]{:S(2)}) copy-start(f32[128,1152]{1,0:T(8,128)} %refs_2_.1) | copy-start | bytes 1769476
  3.3 2.7 %collective-permute-start = (bf16[128,1152]{1,0:T(8,128)(2,1)S(1)}, bf16[128,1152]{1,0:T(8,128)(2,1)S(1)}, u32[]{:S(2)}, u32[]{:S(2)}) collective-permute-start(bf16[128,1152]{1,0:T(8,128)(2,1)S(1)} %get-tuple-element.67), channel_id=1, source_target_pairs={{0,8},{1,9},{2,10},{3,11},{4,12},{5,13},{6,14},{7,15},{8,0},{9,1},... | collective-permute-start | bytes 884744 | tf_op jit(solution)/shard_map/ppermute | solution.py:25
  6.1 9.4 %collective-permute-start.5 = (bf16[256,1152]{1,0:T(8,128)(2,1)S(1)}, bf16[256,1152]{1,0:T(8,128)(2,1)S(1)}, u32[]{:S(2)}, u32[]{:S(2)}) collective-permute-start(bf16[256,1152]{1,0:T(8,128)(2,1)S(1)} %pack.4.refs_0_), channel_id=1, source_target_pairs={{0,2},{1,3},{2,0},{3,1},{4,6},{5,7},{6,4},{7,5},{8,24},{9,25},{10,... | collective-permute-start | bytes 1769480 | tf_op jit(solution)/shard_map/ppermute | solution.py:25
  7.9 10.2 %collective-permute-start.3 = (bf16[256,1152]{1,0:T(8,128)(2,1)S(1)}, bf16[256,1152]{1,0:T(8,128)(2,1)S(1)}, u32[]{:S(2)}, u32[]{:S(2)}) collective-permute-start(bf16[256,1152]{1,0:T(8,128)(2,1)S(1)} %pack.4.refs_0_), channel_id=1, source_target_pairs={{0,1},{1,0},{2,3},{3,2},{4,5},{5,4},{6,7},{7,6},{8,73},{9,72},{10,... | collective-permute-start | bytes 1769480 | tf_op jit(solution)/shard_map/ppermute | solution.py:25
  10.3 10.0 %collective-permute-start.1 = (bf16[256,1152]{1,0:T(8,128)(2,1)S(1)}, bf16[256,1152]{1,0:T(8,128)(2,1)S(1)}, u32[]{:S(2)}, u32[]{:S(2)}) collective-permute-start(bf16[256,1152]{1,0:T(8,128)(2,1)S(1)} %pack.4.refs_0_), channel_id=1, source_target_pairs={{0,6},{1,7},{2,4},{3,5},{4,2},{5,3},{6,0},{7,1},{8,56},{9,57},{10,... | collective-permute-start | bytes 1769480 | tf_op jit(solution)/shard_map/ppermute | solution.py:25
  20.5 7.4 %collective-permute-start.7 = (bf16[1024,1152]{1,0:T(8,128)(2,1)S(1)}, bf16[1024,1152]{1,0:T(8,128)(2,1)S(1)}, u32[]{:S(2)}, u32[]{:S(2)}) collective-permute-start(bf16[1024,1152]{1,0:T(8,128)(2,1)S(1)} %pack.5.near_ref), channel_id=1, source_target_pairs={{0,8},{1,9},{2,10},{3,11},{4,12},{5,13},{6,14},{7,15},{8,0},{9,1},... | collective-permute-start | bytes 7077896 | tf_op jit(solution)/shard_map/ppermute | solution.py:25
  21.0 10.4 %collective-permute-start.6 = (bf16[256,1152]{1,0:T(8,128)(2,1)S(1)}, bf16[256,1152]{1,0:T(8,128)(2,1)S(1)}, u32[]{:S(2)}, u32[]{:S(2)}) collective-permute-start(bf16[256,1152]{1,0:T(8,128)(2,1)S(1)} %collective-permute-done.5.refs_2_), channel_id=1, source_target_pairs={{0,1},{1,0},{2,3},{3,2},{4,5},{5,4},{6,7},{7,6},{8,73},{9,72},{10,... | collective-permute-start | bytes 1769480 | tf_op jit(solution)/shard_map/ppermute | solution.py:25
  22.8 11.0 %collective-permute-start.4 = (bf16[256,1152]{1,0:T(8,128)(2,1)S(1)}, bf16[256,1152]{1,0:T(8,128)(2,1)S(1)}, u32[]{:S(2)}, u32[]{:S(2)}) collective-permute-start(bf16[256,1152]{1,0:T(8,128)(2,1)S(1)} %collective-permute-done.3.refs_1_), channel_id=1, source_target_pairs={{0,6},{1,7},{2,4},{3,5},{4,2},{5,3},{6,0},{7,1},{8,56},{9,57},{10,... | collective-permute-start | bytes 1769480 | tf_op jit(solution)/shard_map/ppermute | solution.py:25
  26.6 8.7 %collective-permute-start.2 = (bf16[256,1152]{1,0:T(8,128)(2,1)S(1)}, bf16[256,1152]{1,0:T(8,128)(2,1)S(1)}, u32[]{:S(2)}, u32[]{:S(2)}) collective-permute-start(bf16[256,1152]{1,0:T(8,128)(2,1)S(1)} %collective-permute-done.1.refs_3_), channel_id=1, source_target_pairs={{0,2},{1,3},{2,0},{3,1},{4,6},{5,7},{6,4},{7,5},{8,24},{9,25},{10,... | collective-permute-start | bytes 1769480 | tf_op jit(solution)/shard_map/ppermute | solution.py:25
  35.5 3.8 %collective-permute-start.10 = (bf16[768,1152]{1,0:T(8,128)(2,1)S(1)}, bf16[768,1152]{1,0:T(8,128)(2,1)S(1)}, u32[]{:S(2)}, u32[]{:S(2)}) collective-permute-start(bf16[768,1152]{1,0:T(8,128)(2,1)S(1)} %pack.6.far_ref), channel_id=1, source_target_pairs={{0,8},{1,9},{2,10},{3,11},{4,12},{5,13},{6,14},{7,15},{8,0},{9,1},... | collective-permute-start | bytes 5308424 | tf_op jit(solution)/shard_map/ppermute | solution.py:25
  35.6 7.3 %collective-permute-start.9 = (bf16[128,1152]{1,0:T(8,128)(2,1)S(1)}, bf16[128,1152]{1,0:T(8,128)(2,1)S(1)}, u32[]{:S(2)}, u32[]{:S(2)}) collective-permute-start(bf16[128,1152]{1,0:T(8,128)(2,1)S(1)} %half_of.3), channel_id=1, source_target_pairs={{0,6},{1,7},{2,4},{3,5},{4,2},{5,3},{6,0},{7,1},{8,56},{9,57},{10,... | collective-permute-start | bytes 884744 | tf_op jit(solution)/shard_map/ppermute | solution.py:25
  37.8 5.9 %collective-permute-start.8 = (bf16[128,1152]{1,0:T(8,128)(2,1)S(1)}, bf16[128,1152]{1,0:T(8,128)(2,1)S(1)}, u32[]{:S(2)}, u32[]{:S(2)}) collective-permute-start(bf16[128,1152]{1,0:T(8,128)(2,1)S(1)} %half_of.2), channel_id=1, source_target_pairs={{0,2},{1,3},{2,0},{3,1},{4,6},{5,7},{6,4},{7,5},{8,24},{9,25},{10,... | collective-permute-start | bytes 884744 | tf_op jit(solution)/shard_map/ppermute | solution.py:25
  43.7 3.5 %collective-permute-start.11 = (bf16[256,1152]{1,0:T(8,128)(2,1)S(1)}, bf16[256,1152]{1,0:T(8,128)(2,1)S(1)}, u32[]{:S(2)}, u32[]{:S(2)}) collective-permute-start(bf16[256,1152]{1,0:T(8,128)(2,1)S(1)} %pack.7.last_ref), channel_id=1, source_target_pairs={{0,8},{1,9},{2,10},{3,11},{4,12},{5,13},{6,14},{7,15},{8,0},{9,1},... | collective-permute-start | bytes 1769480 | tf_op jit(solution)/shard_map/ppermute | solution.py:25
  51.9 5.4 %collective-permute-start.13 = (f32[8,128]{1,0:T(8,128)S(1)}, f32[8,128]{1,0:T(8,128)S(1)}, u32[]{:S(2)}, u32[]{:S(2)}) collective-permute-start(f32[8,128]{1,0:T(8,128)S(1)} %add_add_fusion), channel_id=1, source_target_pairs={{0,1},{1,0},{2,3},{3,2},{4,5},{5,4},{6,7},{7,6},{8,9},{9,8},{10,11... | collective-permute-start | bytes 12296 | tf_op jit(solution)/shard_map/ppermute | solution.py:25
  53.6 3.7 %collective-permute-start.12 = (bf16[256,1152]{1,0:T(8,128)(2,1)S(1)}, bf16[256,1152]{1,0:T(8,128)(2,1)S(1)}, u32[]{:S(2)}, u32[]{:S(2)}) collective-permute-start(bf16[256,1152]{1,0:T(8,128)(2,1)S(1)} %get-tuple-element.90), channel_id=1, source_target_pairs={{0,8},{1,9},{2,10},{3,11},{4,12},{5,13},{6,14},{7,15},{8,0},{9,1},... | collective-permute-start | bytes 1769480 | tf_op jit(solution)/shard_map/ppermute | solution.py:25
  57.5 8.3 %collective-permute-start.14 = (bf16[768,1152]{1,0:T(8,128)(2,1)S(1)}, bf16[768,1152]{1,0:T(8,128)(2,1)S(1)}, u32[]{:S(2)}, u32[]{:S(2)}) collective-permute-start(bf16[768,1152]{1,0:T(8,128)(2,1)S(1)} %get-tuple-element.106), channel_id=1, source_target_pairs={{0,8},{1,9},{2,10},{3,11},{4,12},{5,13},{6,14},{7,15},{8,0},{9,1},... | collective-permute-start | bytes 5308424 | tf_op jit(solution)/shard_map/ppermute | solution.py:25
  58.2 4.4 %collective-permute-start.17 = (f32[8,128]{1,0:T(8,128)S(1)}, f32[8,128]{1,0:T(8,128)S(1)}, u32[]{:S(2)}, u32[]{:S(2)}) collective-permute-start(f32[8,128]{1,0:T(8,128)S(1)} %add.41), channel_id=1, source_target_pairs={{0,65},{1,64},{2,67},{3,66},{4,69},{5,68},{6,71},{7,70},{8,73},{9,... | collective-permute-start | bytes 12296 | tf_op jit(solution)/shard_map/ppermute | solution.py:25
  59.6 7.0 %collective-permute-start.15 = (bf16[128,1152]{1,0:T(8,128)(2,1)S(1)}, bf16[128,1152]{1,0:T(8,128)(2,1)S(1)}, u32[]{:S(2)}, u32[]{:S(2)}) collective-permute-start(bf16[128,1152]{1,0:T(8,128)(2,1)S(1)} %get-tuple-element.107), channel_id=1, source_target_pairs={{0,2},{1,3},{2,0},{3,1},{4,6},{5,7},{6,4},{7,5},{8,24},{9,25},{10,... | collective-permute-start | bytes 884744 | tf_op jit(solution)/shard_map/ppermute | solution.py:25
  59.6 7.1 %collective-permute-start.16 = (bf16[128,1152]{1,0:T(8,128)(2,1)S(1)}, bf16[128,1152]{1,0:T(8,128)(2,1)S(1)}, u32[]{:S(2)}, u32[]{:S(2)}) collective-permute-start(bf16[128,1152]{1,0:T(8,128)(2,1)S(1)} %get-tuple-element.108), channel_id=1, source_target_pairs={{0,6},{1,7},{2,4},{3,5},{4,2},{5,3},{6,0},{7,1},{8,56},{9,57},{10,... | collective-permute-start | bytes 884744 | tf_op jit(solution)/shard_map/ppermute | solution.py:25
  62.7 3.1 %collective-permute-start.18 = (f32[8,128]{1,0:T(8,128)S(1)}, f32[8,128]{1,0:T(8,128)S(1)}, u32[]{:S(2)}, u32[]{:S(2)}) collective-permute-start(f32[8,128]{1,0:T(8,128)S(1)} %add.43), channel_id=1, source_target_pairs={{0,2},{1,3},{2,0},{3,1},{4,6},{5,7},{6,4},{7,5},{8,10},{9,11},{10,... | collective-permute-start | bytes 12296 | tf_op jit(solution)/shard_map/ppermute | solution.py:25
  67.9 7.0 %collective-permute-start.19 = (bf16[1024,1152]{1,0:T(8,128)(2,1)S(1)}, bf16[1024,1152]{1,0:T(8,128)(2,1)S(1)}, u32[]{:S(2)}, u32[]{:S(2)}) collective-permute-start(bf16[1024,1152]{1,0:T(8,128)(2,1)S(1)} %get-tuple-element.115), channel_id=1, source_target_pairs={{0,8},{1,9},{2,10},{3,11},{4,12},{5,13},{6,14},{7,15},{8,0},{9,1},... | collective-permute-start | bytes 7077896 | tf_op jit(solution)/shard_map/ppermute | solution.py:25
  69.8 10.2 %collective-permute-start.21 = (bf16[256,1152]{1,0:T(8,128)(2,1)S(1)}, bf16[256,1152]{1,0:T(8,128)(2,1)S(1)}, u32[]{:S(2)}, u32[]{:S(2)}) collective-permute-start(bf16[256,1152]{1,0:T(8,128)(2,1)S(1)} %get-tuple-element.118), channel_id=1, source_target_pairs={{0,1},{1,0},{2,3},{3,2},{4,5},{5,4},{6,7},{7,6},{8,73},{9,72},{10,... | collective-permute-start | bytes 1769480 | tf_op jit(solution)/shard_map/ppermute | solution.py:25
  71.2 10.1 %collective-permute-start.23 = (bf16[256,1152]{1,0:T(8,128)(2,1)S(1)}, bf16[256,1152]{1,0:T(8,128)(2,1)S(1)}, u32[]{:S(2)}, u32[]{:S(2)}) collective-permute-start(bf16[256,1152]{1,0:T(8,128)(2,1)S(1)} %second.1), channel_id=1, source_target_pairs={{0,2},{1,3},{2,0},{3,1},{4,6},{5,7},{6,4},{7,5},{8,24},{9,25},{10,... | collective-permute-start | bytes 1769480 | tf_op jit(solution)/shard_map/ppermute | solution.py:25
  71.2 13.1 %collective-permute-start.25 = (bf16[256,1152]{1,0:T(8,128)(2,1)S(1)}, bf16[256,1152]{1,0:T(8,128)(2,1)S(1)}, u32[]{:S(2)}, u32[]{:S(2)}) collective-permute-start(bf16[256,1152]{1,0:T(8,128)(2,1)S(1)} %get-tuple-element.120), channel_id=1, source_target_pairs={{0,6},{1,7},{2,4},{3,5},{4,2},{5,3},{6,0},{7,1},{8,56},{9,57},{10,... | collective-permute-start | bytes 1769480 | tf_op jit(solution)/shard_map/ppermute | solution.py:25
  73.2 4.1 %collective-permute-start.20 = (f32[8,128]{1,0:T(8,128)S(1)}, f32[8,128]{1,0:T(8,128)S(1)}, u32[]{:S(2)}, u32[]{:S(2)}) collective-permute-start(f32[8,128]{1,0:T(8,128)S(1)} %add.44), channel_id=1, source_target_pairs={{0,6},{1,7},{2,4},{3,5},{4,2},{5,3},{6,0},{7,1},{8,14},{9,15},{10,... | collective-permute-start | bytes 12296 | tf_op jit(solution)/shard_map/ppermute | solution.py:25
  80.8 13.1 %collective-permute-start.22 = (bf16[256,1152]{1,0:T(8,128)(2,1)S(1)}, bf16[256,1152]{1,0:T(8,128)(2,1)S(1)}, u32[]{:S(2)}, u32[]{:S(2)}) collective-permute-start(bf16[256,1152]{1,0:T(8,128)(2,1)S(1)} %near.3), channel_id=1, source_target_pairs={{0,2},{1,3},{2,0},{3,1},{4,6},{5,7},{6,4},{7,5},{8,24},{9,25},{10,... | collective-permute-start | bytes 1769480 | tf_op jit(solution)/shard_map/ppermute | solution.py:25
  82.0 12.0 %collective-permute-start.24 = (bf16[256,1152]{1,0:T(8,128)(2,1)S(1)}, bf16[256,1152]{1,0:T(8,128)(2,1)S(1)}, u32[]{:S(2)}, u32[]{:S(2)}) collective-permute-start(bf16[256,1152]{1,0:T(8,128)(2,1)S(1)} %near.4), channel_id=1, source_target_pairs={{0,6},{1,7},{2,4},{3,5},{4,2},{5,3},{6,0},{7,1},{8,56},{9,57},{10,... | collective-permute-start | bytes 1769480 | tf_op jit(solution)/shard_map/ppermute | solution.py:25
  85.1 10.0 %collective-permute-start.26 = (bf16[256,1152]{1,0:T(8,128)(2,1)S(1)}, bf16[256,1152]{1,0:T(8,128)(2,1)S(1)}, u32[]{:S(2)}, u32[]{:S(2)}) collective-permute-start(bf16[256,1152]{1,0:T(8,128)(2,1)S(1)} %near.5), channel_id=1, source_target_pairs={{0,1},{1,0},{2,3},{3,2},{4,5},{5,4},{6,7},{7,6},{8,73},{9,72},{10,... | collective-permute-start | bytes 1769480 | tf_op jit(solution)/shard_map/ppermute | solution.py:25
  86.0 4.0 %collective-permute-start.27 = (f32[8,128]{1,0:T(8,128)S(1)}, f32[8,128]{1,0:T(8,128)S(1)}, u32[]{:S(2)}, u32[]{:S(2)}) collective-permute-start(f32[8,128]{1,0:T(8,128)S(1)} %add.45), channel_id=1, source_target_pairs={{0,16},{1,17},{2,18},{3,19},{4,20},{5,21},{6,22},{7,23},{8,24},{9,... | collective-permute-start | bytes 12296 | tf_op jit(solution)/shard_map/ppermute | solution.py:25
  90.0 4.0 %collective-permute-start.28 = (f32[8,128]{1,0:T(8,128)S(1)}, f32[8,128]{1,0:T(8,128)S(1)}, u32[]{:S(2)}, u32[]{:S(2)}) collective-permute-start(f32[8,128]{1,0:T(8,128)S(1)} %add.46), channel_id=1, source_target_pairs={{0,48},{1,49},{2,50},{3,51},{4,52},{5,53},{6,54},{7,55},{8,56},{9,... | collective-permute-start | bytes 12296 | tf_op jit(solution)/shard_map/ppermute | solution.py:25
  94.0 5.6 %copy-start.1 = (f32[128,1152]{1,0:T(8,128)S(1)}, f32[128,1152]{1,0:T(8,128)}, u32[]{:S(2)}) copy-start(f32[128,1152]{1,0:T(8,128)} %refs_1_.1) | copy-start | bytes 1769476
  94.0 5.6 %copy-start.3 = (f32[128,1152]{1,0:T(8,128)S(1)}, f32[128,1152]{1,0:T(8,128)}, u32[]{:S(2)}) copy-start(f32[128,1152]{1,0:T(8,128)} %refs_2_.1) | copy-start | bytes 1769476
  96.4 3.2 %collective-permute-start.29 = (f32[136,1152]{1,0:T(8,128)S(1)}, f32[136,1152]{1,0:T(8,128)S(1)}, u32[]{:S(2)}, u32[]{:S(2)}) collective-permute-start(f32[136,1152]{1,0:T(8,128)S(1)} %get-tuple-element.123), channel_id=1, source_target_pairs={{0,8},{1,9},{2,10},{3,11},{4,12},{5,13},{6,14},{7,15},{8,0},{9,1},... | collective-permute-start | bytes 1880072 | tf_op jit(solution)/shard_map/ppermute | solution.py:25

commit v7 on v5

--- a/solution.py
+++ b/solution.py
@@ -538,7 +538,7 @@
     (second,) = small_call(
         second_kernel, "second", core, (far_part, rest_received), (low_piece,)
     )
-    from_a, from_b, second, sent, loss = lax.optimization_barrier((from_a, from_b, second, sent, loss))
+    from_a, from_b, sent, loss = lax.optimization_barrier((from_a, from_b, sent, loss))
 
     second_received = move(second, "a")
     x, b = small_call(

time: 102 us -> 102 us (level)
  transfers between devices with their start and end apart: 30 -> 30, of which waited for: 16 -> 17; matrix products, arithmetic and copies ran while one was open for 8% -> 8% of each run, Pallas kernels for 13% -> 13%
where the time goes in v7:
time: 102 us
  starting transfers between devices  38.1 us (37%)
  waiting for transfers between devices  28 us (27%)
  Pallas kernels  23 us (23%)
  matrix products  8.31 us (8%)
  between operations  2.26 us (2%)
  local copies, waits for them, and re-layouts  2.14 us (2%)
    ppermute x30, starting transfers between devices, exchange(): return lax.ppermute(x, AXES, pairs)  38.1 us
    ppermute x30, waiting for transfers between devices, exchange(): return lax.ppermute(x, AXES, pairs)  28 us
    pallas_call x4, Pallas kernels, tile_call(): pl.pallas_call(kernel, out_shape=outs, in_specs=[SMEM] + [VMEM] * (len(sc...  13.7 us
    pallas_call x9, Pallas kernels, small_call(): pl.pallas_call(kernel, out_shape=outs, in_specs=[SMEM] + [VMEM] * len(arr...  8.38 us
    dot_general x6, matrix products, transposed_product(): lax.dot_general(weights, img, (((0,), (0,)), ((), ())), preferred_element...  8.31 us
    unnamed x8, local copies, waits for them, and re-layouts  2.13 us
  transfers between devices with their start and end apart: 30, of which 17 were waited for; matrix products, arithmetic and copies ran while one was open for 8% of the time, Pallas kernels for 13%

profile of v7, /device:TPU:1, one launch (start us, length us, event | category | flops | bytes accessed | tf_op | source)
XLA Modules:
  0.0 101.8 jit_solution(8606516124763927105)
XLA Ops:
  0.6 1.1 %copy-done = f32[128,1152]{1,0:T(8,128)S(1)} copy-done((f32[128,1152]{1,0:T(8,128)S(1)}, f32[128,1152]{1,0:T(8,128)}, u32[]{:S(2)}) %copy-start) | copy-done | bytes 589848
  1.7 1.1 %copy-done.2 = f32[128,1152]{1,0:T(8,128)S(1)} copy-done((f32[128,1152]{1,0:T(8,128)S(1)}, f32[128,1152]{1,0:T(8,128)}, u32[]{:S(2)}) %copy-start.2) | copy-done | bytes 589848
  3.3 1.5 %collective-permute-start = (bf16[128,1152]{1,0:T(8,128)(2,1)S(1)}, bf16[128,1152]{1,0:T(8,128)(2,1)S(1)}, u32[]{:S(2)}, u32[]{:S(2)}) collective-permute-start(bf16[128,1152]{1,0:T(8,128)(2,1)S(1)} %get-tuple-element.68), channel_id=1, source_target_pairs={{0,8},{1,9},{2,10},{3,11},{4,12},{5,13},{6,14},{7,15},{8,0},{9,1},... | collective-permute-start | bytes 884744 | tf_op jit(solution)/shard_map/ppermute | solution.py:25
  4.8 1.2 %collective-permute-done.refs_1_ = bf16[128,1152]{1,0:T(8,128)(2,1)S(1)} collective-permute-done((bf16[128,1152]{1,0:T(8,128)(2,1)S(1)}, bf16[128,1152]{1,0:T(8,128)(2,1)S(1)}, u32[]{:S(2)}, u32[]{:S(2)}) %collective-permute-start) | collective-permute-done | bytes 294944 | tf_op jit(solution)/shard_map/ppermute | solution.py:25
  6.1 1.8 %collective-permute-start.5 = (bf16[256,1152]{1,0:T(8,128)(2,1)S(1)}, bf16[256,1152]{1,0:T(8,128)(2,1)S(1)}, u32[]{:S(2)}, u32[]{:S(2)}) collective-permute-start(bf16[256,1152]{1,0:T(8,128)(2,1)S(1)} %pack.4.refs_0_), channel_id=1, source_target_pairs={{0,2},{1,3},{2,0},{3,1},{4,6},{5,7},{6,4},{7,5},{8,24},{9,25},{10,... | collective-permute-start | bytes 1769480 | tf_op jit(solution)/shard_map/ppermute | solution.py:25
  7.9 2.5 %collective-permute-start.3 = (bf16[256,1152]{1,0:T(8,128)(2,1)S(1)}, bf16[256,1152]{1,0:T(8,128)(2,1)S(1)}, u32[]{:S(2)}, u32[]{:S(2)}) collective-permute-start(bf16[256,1152]{1,0:T(8,128)(2,1)S(1)} %pack.4.refs_0_), channel_id=1, source_target_pairs={{0,1},{1,0},{2,3},{3,2},{4,5},{5,4},{6,7},{7,6},{8,73},{9,72},{10,... | collective-permute-start | bytes 1769480 | tf_op jit(solution)/shard_map/ppermute | solution.py:25
  10.3 2.2 %collective-permute-start.1 = (bf16[256,1152]{1,0:T(8,128)(2,1)S(1)}, bf16[256,1152]{1,0:T(8,128)(2,1)S(1)}, u32[]{:S(2)}, u32[]{:S(2)}) collective-permute-start(bf16[256,1152]{1,0:T(8,128)(2,1)S(1)} %pack.4.refs_0_), channel_id=1, source_target_pairs={{0,6},{1,7},{2,4},{3,5},{4,2},{5,3},{6,0},{7,1},{8,56},{9,57},{10,... | collective-permute-start | bytes 1769480 | tf_op jit(solution)/shard_map/ppermute | solution.py:25
  12.6 2.8 %collective-permute-done.5.refs_2_ = bf16[256,1152]{1,0:T(8,128)(2,1)S(1)} collective-permute-done((bf16[256,1152]{1,0:T(8,128)(2,1)S(1)}, bf16[256,1152]{1,0:T(8,128)(2,1)S(1)}, u32[]{:S(2)}, u32[]{:S(2)}) %collective-permute-start.5) | collective-permute-done | bytes 589856 | tf_op jit(solution)/shard_map/ppermute | solution.py:25
  15.4 2.7 %collective-permute-done.3.refs_1_ = bf16[256,1152]{1,0:T(8,128)(2,1)S(1)} collective-permute-done((bf16[256,1152]{1,0:T(8,128)(2,1)S(1)}, bf16[256,1152]{1,0:T(8,128)(2,1)S(1)}, u32[]{:S(2)}, u32[]{:S(2)}) %collective-permute-start.3) | collective-permute-done | bytes 589856 | tf_op jit(solution)/shard_map/ppermute | solution.py:25
  18.1 2.3 %collective-permute-done.1.refs_3_ = bf16[256,1152]{1,0:T(8,128)(2,1)S(1)} collective-permute-done((bf16[256,1152]{1,0:T(8,128)(2,1)S(1)}, bf16[256,1152]{1,0:T(8,128)(2,1)S(1)}, u32[]{:S(2)}, u32[]{:S(2)}) %collective-permute-start.1) | collective-permute-done | bytes 589856 | tf_op jit(solution)/shard_map/ppermute | solution.py:25
  21.0 1.8 %collective-permute-start.6 = (bf16[256,1152]{1,0:T(8,128)(2,1)S(1)}, bf16[256,1152]{1,0:T(8,128)(2,1)S(1)}, u32[]{:S(2)}, u32[]{:S(2)}) collective-permute-start(bf16[256,1152]{1,0:T(8,128)(2,1)S(1)} %collective-permute-done.5.refs_2_), channel_id=1, source_target_pairs={{0,1},{1,0},{2,3},{3,2},{4,5},{5,4},{6,7},{7,6},{8,73},{9,72},{10,... | collective-permute-start | bytes 1769480 | tf_op jit(solution)/shard_map/ppermute | solution.py:25
  22.8 3.8 %collective-permute-start.4 = (bf16[256,1152]{1,0:T(8,128)(2,1)S(1)}, bf16[256,1152]{1,0:T(8,128)(2,1)S(1)}, u32[]{:S(2)}, u32[]{:S(2)}) collective-permute-start(bf16[256,1152]{1,0:T(8,128)(2,1)S(1)} %collective-permute-done.3.refs_1_), channel_id=1, source_target_pairs={{0,6},{1,7},{2,4},{3,5},{4,2},{5,3},{6,0},{7,1},{8,56},{9,57},{10,... | collective-permute-start | bytes 1769480 | tf_op jit(solution)/shard_map/ppermute | solution.py:25
  27.9 3.5 %tile_near.1 = (bf16[512,1152]{1,0:T(8,128)(2,1)S(1)}, bf16[1024,1152]{1,0:T(8,128)(2,1)S(1)}, bf16[512,1024]{1,0:T(8,128)(2,1)S(1)}, f32[512,1152]{1,0:T(8,128)S(1)}, f32[8,128]{1,0:T(8,128)S(1)}) custom-call(s32[1]{0:T(128)} %bitcast.core_ref.refs_0_, f32[8,128]{1,0:T(8,128)S(1)} %broadcast_in_dim.15.sharp_ref, f32[8,128]{1,0:T(8,128)S(1)} %broadcast_in_dim.17.bias_ref, ...), custom_call_target="tpu_custom_call" | custom-call | flops 2415919104 | bytes 4718592 | tf_op jit(solution)/shard_map/tile_near/pallas_call | solution.py:258
  31.4 2.4 %collective-permute-done.4.refs_0_.refs_2_ = bf16[256,1152]{1,0:T(8,128)(2,1)S(1)} collective-permute-done((bf16[256,1152]{1,0:T(8,128)(2,1)S(1)}, bf16[256,1152]{1,0:T(8,128)(2,1)S(1)}, u32[]{:S(2)}, u32[]{:S(2)}) %collective-permute-start.4) | collective-permute-done | bytes 589856 | tf_op jit(solution)/shard_map/ppermute | solution.py:25
  33.9 1.5 %collective-permute-done.2.refs_0_ = bf16[256,1152]{1,0:T(8,128)(2,1)S(1)} collective-permute-done((bf16[256,1152]{1,0:T(8,128)(2,1)S(1)}, bf16[256,1152]{1,0:T(8,128)(2,1)S(1)}, u32[]{:S(2)}, u32[]{:S(2)}) %collective-permute-start.2) | collective-permute-done | bytes 589856 | tf_op jit(solution)/shard_map/ppermute | solution.py:25
  35.6 2.2 %collective-permute-start.9 = (bf16[128,1152]{1,0:T(8,128)(2,1)S(1)}, bf16[128,1152]{1,0:T(8,128)(2,1)S(1)}, u32[]{:S(2)}, u32[]{:S(2)}) collective-permute-start(bf16[128,1152]{1,0:T(8,128)(2,1)S(1)} %half_of.3), channel_id=1, source_target_pairs={{0,6},{1,7},{2,4},{3,5},{4,2},{5,3},{6,0},{7,1},{8,56},{9,57},{10,... | collective-permute-start | bytes 884744 | tf_op jit(solution)/shard_map/ppermute | solution.py:25
  37.8 1.4 %collective-permute-done.10.received_ref.far_received_ref = bf16[768,1152]{1,0:T(8,128)(2,1)S(1)} collective-permute-done((bf16[768,1152]{1,0:T(8,128)(2,1)S(1)}, bf16[768,1152]{1,0:T(8,128)(2,1)S(1)}, u32[]{:S(2)}, u32[]{:S(2)}) %collective-permute-start.10) | collective-permute-done | bytes 1769504 | tf_op jit(solution)/shard_map/ppermute | solution.py:25
  39.2 3.7 %tile_far.1 = (bf16[768,1152]{1,0:T(8,128)(2,1)S(1)}, bf16[768,1152]{1,0:T(8,128)(2,1)S(1)}, bf16[768,768]{1,0:T(8,128)(2,1)S(1)}, f32[768,1152]{1,0:T(8,128)S(1)}, f32[8,128]{1,0:T(8,128)S(1)}) custom-call(s32[1]{0:T(128)} %bitcast.core_ref.refs_0_, f32[8,128]{1,0:T(8,128)S(1)} %broadcast_in_dim.15.sharp_ref, f32[8,128]{1,0:T(8,128)S(1)} %broadcast_in_dim.17.bias_ref, ...), custom_call_target="tpu_custom_call" | custom-call | flops 2717908992 | bytes 5898240 | tf_op jit(solution)/shard_map/tile_far/pallas_call | solution.py:258
  43.7 1.7 %collective-permute-start.11 = (bf16[256,1152]{1,0:T(8,128)(2,1)S(1)}, bf16[256,1152]{1,0:T(8,128)(2,1)S(1)}, u32[]{:S(2)}, u32[]{:S(2)}) collective-permute-start(bf16[256,1152]{1,0:T(8,128)(2,1)S(1)} %pack.7.last_ref), channel_id=1, source_target_pairs={{0,8},{1,9},{2,10},{3,11},{4,12},{5,13},{6,14},{7,15},{8,0},{9,1},... | collective-permute-start | bytes 1769480 | tf_op jit(solution)/shard_map/ppermute | solution.py:25
  45.4 1.9 %tile_middle.1 = (bf16[768,1024]{1,0:T(8,128)(2,1)S(1)}, f32[256,1152]{1,0:T(8,128)S(1)}, f32[8,128]{1,0:T(8,128)S(1)}) custom-call(s32[1]{0:T(128)} %bitcast.core_ref.refs_0_, f32[8,128]{1,0:T(8,128)S(1)} %broadcast_in_dim.15.sharp_ref, f32[8,128]{1,0:T(8,128)S(1)} %broadcast_in_dim.17.bias_ref, bf16[768,1152]{1,0:T(8,128)(2,1)S(1)} %get-tuple-element.80.img_ref, ...), custom_call_target="tpu_custom_call" | custom-call | flops 1207959552 | bytes 6946816 | tf_op jit(solution)/shard_map/tile_middle/pallas_call | solution.py:258
  47.3 4.6 %tile_last.1 = (bf16[768,256]{1,0:T(8,128)(2,1)S(1)}, f32[768,1152]{1,0:T(8,128)S(1)}, bf16[256,1152]{1,0:T(8,128)(2,1)S(1)}, bf16[256,1024]{1,0:T(8,128)(2,1)S(...) custom-call(s32[1]{0:T(128)} %bitcast.core_ref.refs_0_, ...), custom_call_target="tpu_custom_call" | custom-call | flops 3321888768 | bytes 12976128 | tf_op jit(solution)/shard_map/tile_last/pallas_call | solution.py:258
  52.7 0.9 fusion.5
  54.8 2.5 %fusion.3 = (bf16[768,1152]{1,0:T(8,128)(2,1)S(1)}, f32[768,1152]{1,0:T(8,128)S(1)}) fusion(f32[768,1152]{1,0:T(8,128)S(1)} %get-tuple-element.92.img_ref, pred[]{:T(512)S(6)} %eq.3, f32[768,1152]{1,0:T(8,128)S(1)} %fusion.7, bf16[768,768]{1,0:T(8,128)(2,1)S(1)} %get-tuple-element.93, bf16[768,1152]{1,0:T(8,128)(2,1)S(1)} %get-tuple-element.80.img_ref), kind=kOutput, calls=%fused_computation.9 | convolution fusion | flops 1367801856 | bytes 15335425 | tf_op jit(solution)/shard_map/dot_general | solution.py:423
  58.2 1.3 %collective-permute-start.17 = (f32[8,128]{1,0:T(8,128)S(1)}, f32[8,128]{1,0:T(8,128)S(1)}, u32[]{:S(2)}, u32[]{:S(2)}) collective-permute-start(f32[8,128]{1,0:T(8,128)S(1)} %add.41), channel_id=1, source_target_pairs={{0,65},{1,64},{2,67},{3,66},{4,69},{5,68},{6,71},{7,70},{8,73},{9,... | collective-permute-start | bytes 12296 | tf_op jit(solution)/shard_map/ppermute | solution.py:25
  59.6 2.2 %collective-permute-start.16 = (bf16[128,1152]{1,0:T(8,128)(2,1)S(1)}, bf16[128,1152]{1,0:T(8,128)(2,1)S(1)}, u32[]{:S(2)}, u32[]{:S(2)}) collective-permute-start(bf16[128,1152]{1,0:T(8,128)(2,1)S(1)} %get-tuple-element.109), channel_id=1, source_target_pairs={{0,6},{1,7},{2,4},{3,5},{4,2},{5,3},{6,0},{7,1},{8,56},{9,57},{10,... | collective-permute-start | bytes 884744 | tf_op jit(solution)/shard_map/ppermute | solution.py:25
  61.8 0.9 fusion.8
  62.8 3.0 %fusion.1 = (bf16[1024,1152]{1,0:T(8,128)(2,1)S(1)}, f32[1024,1152]{1,0:T(8,128)S(1)}) fusion(f32[1024,1152]{1,0:T(8,128)S(1)} %fusion.8, bf16[768,1024]{1,0:T(8,128)(2,1)S(1)} %get-tuple-element.105, bf16[768,1152]{1,0:T(8,128)(2,1)S(1)} %get-tuple-element.80.img_ref), kind=kOutput, calls=%fused_computation.5 | convolution fusion | flops 1822556160 | bytes 15138816 | tf_op jit(solution)/shard_map/dot_general | solution.py:423
  65.8 0.9 collective-permute-done.16.from_b_ref
  66.7 1.2 %far.1 = (bf16[256,1152]{1,0:T(8,128)(2,1)S(1)}, bf16[256,1152]{1,0:T(8,128)(2,1)S(1)}) custom-call(s32[1]{0:T(128)} %bitcast.core_ref.refs_0_, f32[768,1152]{1,0:T(8,128)S(1)} %get-tuple-element.132.txt_ref, bf16[768,1152]{1,0:T(8,128)(2,1)S(1)} %collective-permute-done.14.txt_received_ref.img_received_ref.received_ref, ...), custom_call_target="tpu_custom_call" | custom-call | tf_op jit(solution)/shard_map/far/pallas_call | solution.py:276
  67.9 2.0 %collective-permute-start.19 = (bf16[1024,1152]{1,0:T(8,128)(2,1)S(1)}, bf16[1024,1152]{1,0:T(8,128)(2,1)S(1)}, u32[]{:S(2)}, u32[]{:S(2)}) collective-permute-start(bf16[1024,1152]{1,0:T(8,128)(2,1)S(1)} %get-tuple-element.116), channel_id=1, source_target_pairs={{0,8},{1,9},{2,10},{3,11},{4,12},{5,13},{6,14},{7,15},{8,0},{9,1},... | collective-permute-start | bytes 7077896 | tf_op jit(solution)/shard_map/ppermute | solution.py:25
  69.8 1.3 %collective-permute-start.21 = (bf16[256,1152]{1,0:T(8,128)(2,1)S(1)}, bf16[256,1152]{1,0:T(8,128)(2,1)S(1)}, u32[]{:S(2)}, u32[]{:S(2)}) collective-permute-start(bf16[256,1152]{1,0:T(8,128)(2,1)S(1)} %get-tuple-element.121), channel_id=1, source_target_pairs={{0,1},{1,0},{2,3},{3,2},{4,5},{5,4},{6,7},{7,6},{8,73},{9,72},{10,... | collective-permute-start | bytes 1769480 | tf_op jit(solution)/shard_map/ppermute | solution.py:25
  72.1 1.7 %collective-permute-start.25 = (bf16[256,1152]{1,0:T(8,128)(2,1)S(1)}, bf16[256,1152]{1,0:T(8,128)(2,1)S(1)}, u32[]{:S(2)}, u32[]{:S(2)}) collective-permute-start(bf16[256,1152]{1,0:T(8,128)(2,1)S(1)} %get-tuple-element.122), channel_id=1, source_target_pairs={{0,6},{1,7},{2,4},{3,5},{4,2},{5,3},{6,0},{7,1},{8,56},{9,57},{10,... | collective-permute-start | bytes 1769480 | tf_op jit(solution)/shard_map/ppermute | solution.py:25
  74.0 1.0 base.1.refs_1_.base_ref
  75.0 1.6 %collective-permute-start.20 = (f32[8,128]{1,0:T(8,128)S(1)}, f32[8,128]{1,0:T(8,128)S(1)}, u32[]{:S(2)}, u32[]{:S(2)}) collective-permute-start(f32[8,128]{1,0:T(8,128)S(1)} %add.44), channel_id=1, source_target_pairs={{0,6},{1,7},{2,4},{3,5},{4,2},{5,3},{6,0},{7,1},{8,14},{9,15},{10,... | collective-permute-start | bytes 12296 | tf_op jit(solution)/shard_map/ppermute | solution.py:25
  76.6 2.6 %collective-permute-done.20 = f32[8,128]{1,0:T(8,128)S(1)} collective-permute-done((f32[8,128]{1,0:T(8,128)S(1)}, f32[8,128]{1,0:T(8,128)S(1)}, u32[]{:S(2)}, u32[]{:S(2)}) %collective-permute-start.20) | collective-permute-done | bytes 4128 | tf_op jit(solution)/shard_map/ppermute | solution.py:25
  79.2 0.9 collective-permute-done.21.refs_2_
  80.1 0.8 near.3
  81.0 0.8 near.4
  81.8 2.2 %collective-permute-start.24 = (bf16[256,1152]{1,0:T(8,128)(2,1)S(1)}, bf16[256,1152]{1,0:T(8,128)(2,1)S(1)}, u32[]{:S(2)}, u32[]{:S(2)}) collective-permute-start(bf16[256,1152]{1,0:T(8,128)(2,1)S(1)} %near.4), channel_id=1, source_target_pairs={{0,6},{1,7},{2,4},{3,5},{4,2},{5,3},{6,0},{7,1},{8,56},{9,57},{10,... | collective-permute-start | bytes 1769480 | tf_op jit(solution)/shard_map/ppermute | solution.py:25
  84.8 1.4 %collective-permute-start.26 = (bf16[256,1152]{1,0:T(8,128)(2,1)S(1)}, bf16[256,1152]{1,0:T(8,128)(2,1)S(1)}, u32[]{:S(2)}, u32[]{:S(2)}) collective-permute-start(bf16[256,1152]{1,0:T(8,128)(2,1)S(1)} %near.5), channel_id=1, source_target_pairs={{0,1},{1,0},{2,3},{3,2},{4,5},{5,4},{6,7},{7,6},{8,73},{9,72},{10,... | collective-permute-start | bytes 1769480 | tf_op jit(solution)/shard_map/ppermute | solution.py:25
  86.4 3.6 %collective-permute-done.27 = f32[8,128]{1,0:T(8,128)S(1)} collective-permute-done((f32[8,128]{1,0:T(8,128)S(1)}, f32[8,128]{1,0:T(8,128)S(1)}, u32[]{:S(2)}, u32[]{:S(2)}) %collective-permute-start.27) | collective-permute-done | bytes 4128 | tf_op jit(solution)/shard_map/ppermute | solution.py:25
  90.0 2.1 %collective-permute-start.28 = (f32[8,128]{1,0:T(8,128)S(1)}, f32[8,128]{1,0:T(8,128)S(1)}, u32[]{:S(2)}, u32[]{:S(2)}) collective-permute-start(f32[8,128]{1,0:T(8,128)S(1)} %add.46), channel_id=1, source_target_pairs={{0,48},{1,49},{2,50},{3,51},{4,52},{5,53},{6,54},{7,55},{8,56},{9,... | collective-permute-start | bytes 12296 | tf_op jit(solution)/shard_map/ppermute | solution.py:25
  92.1 1.8 %collective-permute-done.28 = f32[8,128]{1,0:T(8,128)S(1)} collective-permute-done((f32[8,128]{1,0:T(8,128)S(1)}, f32[8,128]{1,0:T(8,128)S(1)}, u32[]{:S(2)}, u32[]{:S(2)}) %collective-permute-start.28) | collective-permute-done | bytes 4128 | tf_op jit(solution)/shard_map/ppermute | solution.py:25
  94.0 1.1 %collective-permute-done.26.x_ref = bf16[256,1152]{1,0:T(8,128)(2,1)S(1)} collective-permute-done((bf16[256,1152]{1,0:T(8,128)(2,1)S(1)}, bf16[256,1152]{1,0:T(8,128)(2,1)S(1)}, u32[]{:S(2)}, u32[]{:S(2)}) %collective-permute-start.26) | collective-permute-done | bytes 589856 | tf_op jit(solution)/shard_map/ppermute | solution.py:25
  95.1 1.3 %gather_sums.1 = (f32[128,1152]{1,0:T(8,128)S(1)}, f32[136,1152]{1,0:T(8,128)S(1)}) custom-call(s32[1]{0:T(128)} %bitcast.core_ref.refs_0_, f32[1024,1152]{1,0:T(8,128)S(1)} %base.1.refs_1_.base_ref, bf16[256,1152]{1,0:T(8,128)(2,1)S(1)} %collective-permute-done.22.a_ref, bf16[256,1152]{1,0:T(8,128)(2,1)S(1)} %collective-permute-done.24.b_ref, ...), custom_call_target="tpu_custom_call" | custom-call | tf_op jit(solution)/shard_map/gather_sums/pallas_call | solution.py:276
  96.4 2.1 %collective-permute-start.29 = (f32[136,1152]{1,0:T(8,128)S(1)}, f32[136,1152]{1,0:T(8,128)S(1)}, u32[]{:S(2)}, u32[]{:S(2)}) collective-permute-start(f32[136,1152]{1,0:T(8,128)S(1)} %get-tuple-element.125), channel_id=1, source_target_pairs={{0,8},{1,9},{2,10},{3,11},{4,12},{5,13},{6,14},{7,15},{8,0},{9,1},... | collective-permute-start | bytes 1880072 | tf_op jit(solution)/shard_map/ppermute | solution.py:25
  98.5 1.7 %collective-permute-done.29.refs_4_ = f32[136,1152]{1,0:T(8,128)S(1)} collective-permute-done((f32[136,1152]{1,0:T(8,128)S(1)}, f32[136,1152]{1,0:T(8,128)S(1)}, u32[]{:S(2)}, u32[]{:S(2)}) %collective-permute-start.29) | collective-permute-done | bytes 626720 | tf_op jit(solution)/shard_map/ppermute | solution.py:25
  100.2 1.7 %finish.1 = (f32[1,1]{1,0:T(1,128)}, f32[128,1152]{1,0:T(8,128)}, f32[128,1152]{1,0:T(8,128)}) custom-call(s32[1]{0:T(128)} %bitcast.core_ref.refs_0_, f32[128,1152]{1,0:T(8,128)S(1)} %copy-done.1, f32[128,1152]{1,0:T(8,128)S(1)} %copy-done.3, f32[128,1152]{1,0:T(8,128)S(1)} %get-tuple-element.124.refs_3_, f32[136,1152]{1,0:T(8,128)S(1)} %collective-permute-done.29.refs_4_, ...), custom_call_target="tpu_custom_call" | custom-call | tf_op jit(solution)/shard_map/finish/pallas_call | solution.py:276
  (55 shorter events, 7.6 us)
Async XLA Ops:
  0.6 1.1 %copy-start = (f32[128,1152]{1,0:T(8,128)S(1)}, f32[128,1152]{1,0:T(8,128)}, u32[]{:S(2)}) copy-start(f32[128,1152]{1,0:T(8,128)} %refs_1_.1) | copy-start | bytes 1769476
  1.7 1.1 %copy-start.2 = (f32[128,1152]{1,0:T(8,128)S(1)}, f32[128,1152]{1,0:T(8,128)}, u32[]{:S(2)}) copy-start(f32[128,1152]{1,0:T(8,128)} %refs_2_.1) | copy-start | bytes 1769476
  3.3 2.7 %collective-permute-start = (bf16[128,1152]{1,0:T(8,128)(2,1)S(1)}, bf16[128,1152]{1,0:T(8,128)(2,1)S(1)}, u32[]{:S(2)}, u32[]{:S(2)}) collective-permute-start(bf16[128,1152]{1,0:T(8,128)(2,1)S(1)} %get-tuple-element.68), channel_id=1, source_target_pairs={{0,8},{1,9},{2,10},{3,11},{4,12},{5,13},{6,14},{7,15},{8,0},{9,1},... | collective-permute-start | bytes 884744 | tf_op jit(solution)/shard_map/ppermute | solution.py:25
  6.1 9.4 %collective-permute-start.5 = (bf16[256,1152]{1,0:T(8,128)(2,1)S(1)}, bf16[256,1152]{1,0:T(8,128)(2,1)S(1)}, u32[]{:S(2)}, u32[]{:S(2)}) collective-permute-start(bf16[256,1152]{1,0:T(8,128)(2,1)S(1)} %pack.4.refs_0_), channel_id=1, source_target_pairs={{0,2},{1,3},{2,0},{3,1},{4,6},{5,7},{6,4},{7,5},{8,24},{9,25},{10,... | collective-permute-start | bytes 1769480 | tf_op jit(solution)/shard_map/ppermute | solution.py:25
  7.9 10.2 %collective-permute-start.3 = (bf16[256,1152]{1,0:T(8,128)(2,1)S(1)}, bf16[256,1152]{1,0:T(8,128)(2,1)S(1)}, u32[]{:S(2)}, u32[]{:S(2)}) collective-permute-start(bf16[256,1152]{1,0:T(8,128)(2,1)S(1)} %pack.4.refs_0_), channel_id=1, source_target_pairs={{0,1},{1,0},{2,3},{3,2},{4,5},{5,4},{6,7},{7,6},{8,73},{9,72},{10,... | collective-permute-start | bytes 1769480 | tf_op jit(solution)/shard_map/ppermute | solution.py:25
  10.3 10.0 %collective-permute-start.1 = (bf16[256,1152]{1,0:T(8,128)(2,1)S(1)}, bf16[256,1152]{1,0:T(8,128)(2,1)S(1)}, u32[]{:S(2)}, u32[]{:S(2)}) collective-permute-start(bf16[256,1152]{1,0:T(8,128)(2,1)S(1)} %pack.4.refs_0_), channel_id=1, source_target_pairs={{0,6},{1,7},{2,4},{3,5},{4,2},{5,3},{6,0},{7,1},{8,56},{9,57},{10,... | collective-permute-start | bytes 1769480 | tf_op jit(solution)/shard_map/ppermute | solution.py:25
  20.5 7.4 %collective-permute-start.7 = (bf16[1024,1152]{1,0:T(8,128)(2,1)S(1)}, bf16[1024,1152]{1,0:T(8,128)(2,1)S(1)}, u32[]{:S(2)}, u32[]{:S(2)}) collective-permute-start(bf16[1024,1152]{1,0:T(8,128)(2,1)S(1)} %pack.5.near_ref), channel_id=1, source_target_pairs={{0,8},{1,9},{2,10},{3,11},{4,12},{5,13},{6,14},{7,15},{8,0},{9,1},... | collective-permute-start | bytes 7077896 | tf_op jit(solution)/shard_map/ppermute | solution.py:25
  21.0 10.4 %collective-permute-start.6 = (bf16[256,1152]{1,0:T(8,128)(2,1)S(1)}, bf16[256,1152]{1,0:T(8,128)(2,1)S(1)}, u32[]{:S(2)}, u32[]{:S(2)}) collective-permute-start(bf16[256,1152]{1,0:T(8,128)(2,1)S(1)} %collective-permute-done.5.refs_2_), channel_id=1, source_target_pairs={{0,1},{1,0},{2,3},{3,2},{4,5},{5,4},{6,7},{7,6},{8,73},{9,72},{10,... | collective-permute-start | bytes 1769480 | tf_op jit(solution)/shard_map/ppermute | solution.py:25
  22.8 11.0 %collective-permute-start.4 = (bf16[256,1152]{1,0:T(8,128)(2,1)S(1)}, bf16[256,1152]{1,0:T(8,128)(2,1)S(1)}, u32[]{:S(2)}, u32[]{:S(2)}) collective-permute-start(bf16[256,1152]{1,0:T(8,128)(2,1)S(1)} %collective-permute-done.3.refs_1_), channel_id=1, source_target_pairs={{0,6},{1,7},{2,4},{3,5},{4,2},{5,3},{6,0},{7,1},{8,56},{9,57},{10,... | collective-permute-start | bytes 1769480 | tf_op jit(solution)/shard_map/ppermute | solution.py:25
  26.6 8.7 %collective-permute-start.2 = (bf16[256,1152]{1,0:T(8,128)(2,1)S(1)}, bf16[256,1152]{1,0:T(8,128)(2,1)S(1)}, u32[]{:S(2)}, u32[]{:S(2)}) collective-permute-start(bf16[256,1152]{1,0:T(8,128)(2,1)S(1)} %collective-permute-done.1.refs_3_), channel_id=1, source_target_pairs={{0,2},{1,3},{2,0},{3,1},{4,6},{5,7},{6,4},{7,5},{8,24},{9,25},{10,... | collective-permute-start | bytes 1769480 | tf_op jit(solution)/shard_map/ppermute | solution.py:25
  35.5 3.8 %collective-permute-start.10 = (bf16[768,1152]{1,0:T(8,128)(2,1)S(1)}, bf16[768,1152]{1,0:T(8,128)(2,1)S(1)}, u32[]{:S(2)}, u32[]{:S(2)}) collective-permute-start(bf16[768,1152]{1,0:T(8,128)(2,1)S(1)} %pack.6.far_ref), channel_id=1, source_target_pairs={{0,8},{1,9},{2,10},{3,11},{4,12},{5,13},{6,14},{7,15},{8,0},{9,1},... | collective-permute-start | bytes 5308424 | tf_op jit(solution)/shard_map/ppermute | solution.py:25
  35.6 7.3 %collective-permute-start.9 = (bf16[128,1152]{1,0:T(8,128)(2,1)S(1)}, bf16[128,1152]{1,0:T(8,128)(2,1)S(1)}, u32[]{:S(2)}, u32[]{:S(2)}) collective-permute-start(bf16[128,1152]{1,0:T(8,128)(2,1)S(1)} %half_of.3), channel_id=1, source_target_pairs={{0,6},{1,7},{2,4},{3,5},{4,2},{5,3},{6,0},{7,1},{8,56},{9,57},{10,... | collective-permute-start | bytes 884744 | tf_op jit(solution)/shard_map/ppermute | solution.py:25
  37.8 5.9 %collective-permute-start.8 = (bf16[128,1152]{1,0:T(8,128)(2,1)S(1)}, bf16[128,1152]{1,0:T(8,128)(2,1)S(1)}, u32[]{:S(2)}, u32[]{:S(2)}) collective-permute-start(bf16[128,1152]{1,0:T(8,128)(2,1)S(1)} %half_of.2), channel_id=1, source_target_pairs={{0,2},{1,3},{2,0},{3,1},{4,6},{5,7},{6,4},{7,5},{8,24},{9,25},{10,... | collective-permute-start | bytes 884744 | tf_op jit(solution)/shard_map/ppermute | solution.py:25
  43.7 3.5 %collective-permute-start.11 = (bf16[256,1152]{1,0:T(8,128)(2,1)S(1)}, bf16[256,1152]{1,0:T(8,128)(2,1)S(1)}, u32[]{:S(2)}, u32[]{:S(2)}) collective-permute-start(bf16[256,1152]{1,0:T(8,128)(2,1)S(1)} %pack.7.last_ref), channel_id=1, source_target_pairs={{0,8},{1,9},{2,10},{3,11},{4,12},{5,13},{6,14},{7,15},{8,0},{9,1},... | collective-permute-start | bytes 1769480 | tf_op jit(solution)/shard_map/ppermute | solution.py:25
  51.9 5.4 %collective-permute-start.13 = (f32[8,128]{1,0:T(8,128)S(1)}, f32[8,128]{1,0:T(8,128)S(1)}, u32[]{:S(2)}, u32[]{:S(2)}) collective-permute-start(f32[8,128]{1,0:T(8,128)S(1)} %add_add_fusion), channel_id=1, source_target_pairs={{0,1},{1,0},{2,3},{3,2},{4,5},{5,4},{6,7},{7,6},{8,9},{9,8},{10,11... | collective-permute-start | bytes 12296 | tf_op jit(solution)/shard_map/ppermute | solution.py:25
  53.6 3.7 %collective-permute-start.12 = (bf16[256,1152]{1,0:T(8,128)(2,1)S(1)}, bf16[256,1152]{1,0:T(8,128)(2,1)S(1)}, u32[]{:S(2)}, u32[]{:S(2)}) collective-permute-start(bf16[256,1152]{1,0:T(8,128)(2,1)S(1)} %get-tuple-element.91), channel_id=1, source_target_pairs={{0,8},{1,9},{2,10},{3,11},{4,12},{5,13},{6,14},{7,15},{8,0},{9,1},... | collective-permute-start | bytes 1769480 | tf_op jit(solution)/shard_map/ppermute | solution.py:25
  57.5 9.1 %collective-permute-start.14 = (bf16[768,1152]{1,0:T(8,128)(2,1)S(1)}, bf16[768,1152]{1,0:T(8,128)(2,1)S(1)}, u32[]{:S(2)}, u32[]{:S(2)}) collective-permute-start(bf16[768,1152]{1,0:T(8,128)(2,1)S(1)} %get-tuple-element.107), channel_id=1, source_target_pairs={{0,8},{1,9},{2,10},{3,11},{4,12},{5,13},{6,14},{7,15},{8,0},{9,1},... | collective-permute-start | bytes 5308424 | tf_op jit(solution)/shard_map/ppermute | solution.py:25
  58.2 4.4 %collective-permute-start.17 = (f32[8,128]{1,0:T(8,128)S(1)}, f32[8,128]{1,0:T(8,128)S(1)}, u32[]{:S(2)}, u32[]{:S(2)}) collective-permute-start(f32[8,128]{1,0:T(8,128)S(1)} %add.41), channel_id=1, source_target_pairs={{0,65},{1,64},{2,67},{3,66},{4,69},{5,68},{6,71},{7,70},{8,73},{9,... | collective-permute-start | bytes 12296 | tf_op jit(solution)/shard_map/ppermute | solution.py:25
  59.6 6.2 %collective-permute-start.15 = (bf16[128,1152]{1,0:T(8,128)(2,1)S(1)}, bf16[128,1152]{1,0:T(8,128)(2,1)S(1)}, u32[]{:S(2)}, u32[]{:S(2)}) collective-permute-start(bf16[128,1152]{1,0:T(8,128)(2,1)S(1)} %get-tuple-element.108), channel_id=1, source_target_pairs={{0,2},{1,3},{2,0},{3,1},{4,6},{5,7},{6,4},{7,5},{8,24},{9,25},{10,... | collective-permute-start | bytes 884744 | tf_op jit(solution)/shard_map/ppermute | solution.py:25
  59.6 7.1 %collective-permute-start.16 = (bf16[128,1152]{1,0:T(8,128)(2,1)S(1)}, bf16[128,1152]{1,0:T(8,128)(2,1)S(1)}, u32[]{:S(2)}, u32[]{:S(2)}) collective-permute-start(bf16[128,1152]{1,0:T(8,128)(2,1)S(1)} %get-tuple-element.109), channel_id=1, source_target_pairs={{0,6},{1,7},{2,4},{3,5},{4,2},{5,3},{6,0},{7,1},{8,56},{9,57},{10,... | collective-permute-start | bytes 884744 | tf_op jit(solution)/shard_map/ppermute | solution.py:25
  62.7 3.1 %collective-permute-start.18 = (f32[8,128]{1,0:T(8,128)S(1)}, f32[8,128]{1,0:T(8,128)S(1)}, u32[]{:S(2)}, u32[]{:S(2)}) collective-permute-start(f32[8,128]{1,0:T(8,128)S(1)} %add.43), channel_id=1, source_target_pairs={{0,2},{1,3},{2,0},{3,1},{4,6},{5,7},{6,4},{7,5},{8,10},{9,11},{10,... | collective-permute-start | bytes 12296 | tf_op jit(solution)/shard_map/ppermute | solution.py:25
  67.9 6.1 %collective-permute-start.19 = (bf16[1024,1152]{1,0:T(8,128)(2,1)S(1)}, bf16[1024,1152]{1,0:T(8,128)(2,1)S(1)}, u32[]{:S(2)}, u32[]{:S(2)}) collective-permute-start(bf16[1024,1152]{1,0:T(8,128)(2,1)S(1)} %get-tuple-element.116), channel_id=1, source_target_pairs={{0,8},{1,9},{2,10},{3,11},{4,12},{5,13},{6,14},{7,15},{8,0},{9,1},... | collective-permute-start | bytes 7077896 | tf_op jit(solution)/shard_map/ppermute | solution.py:25
  69.8 10.2 %collective-permute-start.21 = (bf16[256,1152]{1,0:T(8,128)(2,1)S(1)}, bf16[256,1152]{1,0:T(8,128)(2,1)S(1)}, u32[]{:S(2)}, u32[]{:S(2)}) collective-permute-start(bf16[256,1152]{1,0:T(8,128)(2,1)S(1)} %get-tuple-element.121), channel_id=1, source_target_pairs={{0,1},{1,0},{2,3},{3,2},{4,5},{5,4},{6,7},{7,6},{8,73},{9,72},{10,... | collective-permute-start | bytes 1769480 | tf_op jit(solution)/shard_map/ppermute | solution.py:25
  71.9 9.1 %collective-permute-start.23 = (bf16[256,1152]{1,0:T(8,128)(2,1)S(1)}, bf16[256,1152]{1,0:T(8,128)(2,1)S(1)}, u32[]{:S(2)}, u32[]{:S(2)}) collective-permute-start(bf16[256,1152]{1,0:T(8,128)(2,1)S(1)} %second.1), channel_id=1, source_target_pairs={{0,2},{1,3},{2,0},{3,1},{4,6},{5,7},{6,4},{7,5},{8,24},{9,25},{10,... | collective-permute-start | bytes 1769480 | tf_op jit(solution)/shard_map/ppermute | solution.py:25
  72.1 11.9 %collective-permute-start.25 = (bf16[256,1152]{1,0:T(8,128)(2,1)S(1)}, bf16[256,1152]{1,0:T(8,128)(2,1)S(1)}, u32[]{:S(2)}, u32[]{:S(2)}) collective-permute-start(bf16[256,1152]{1,0:T(8,128)(2,1)S(1)} %get-tuple-element.122), channel_id=1, source_target_pairs={{0,6},{1,7},{2,4},{3,5},{4,2},{5,3},{6,0},{7,1},{8,56},{9,57},{10,... | collective-permute-start | bytes 1769480 | tf_op jit(solution)/shard_map/ppermute | solution.py:25
  75.0 4.2 %collective-permute-start.20 = (f32[8,128]{1,0:T(8,128)S(1)}, f32[8,128]{1,0:T(8,128)S(1)}, u32[]{:S(2)}, u32[]{:S(2)}) collective-permute-start(f32[8,128]{1,0:T(8,128)S(1)} %add.44), channel_id=1, source_target_pairs={{0,6},{1,7},{2,4},{3,5},{4,2},{5,3},{6,0},{7,1},{8,14},{9,15},{10,... | collective-permute-start | bytes 12296 | tf_op jit(solution)/shard_map/ppermute | solution.py:25
  80.8 13.1 %collective-permute-start.22 = (bf16[256,1152]{1,0:T(8,128)(2,1)S(1)}, bf16[256,1152]{1,0:T(8,128)(2,1)S(1)}, u32[]{:S(2)}, u32[]{:S(2)}) collective-permute-start(bf16[256,1152]{1,0:T(8,128)(2,1)S(1)} %near.3), channel_id=1, source_target_pairs={{0,2},{1,3},{2,0},{3,1},{4,6},{5,7},{6,4},{7,5},{8,24},{9,25},{10,... | collective-permute-start | bytes 1769480 | tf_op jit(solution)/shard_map/ppermute | solution.py:25
  81.8 12.2 %collective-permute-start.24 = (bf16[256,1152]{1,0:T(8,128)(2,1)S(1)}, bf16[256,1152]{1,0:T(8,128)(2,1)S(1)}, u32[]{:S(2)}, u32[]{:S(2)}) collective-permute-start(bf16[256,1152]{1,0:T(8,128)(2,1)S(1)} %near.4), channel_id=1, source_target_pairs={{0,6},{1,7},{2,4},{3,5},{4,2},{5,3},{6,0},{7,1},{8,56},{9,57},{10,... | collective-permute-start | bytes 1769480 | tf_op jit(solution)/shard_map/ppermute | solution.py:25
  84.8 10.3 %collective-permute-start.26 = (bf16[256,1152]{1,0:T(8,128)(2,1)S(1)}, bf16[256,1152]{1,0:T(8,128)(2,1)S(1)}, u32[]{:S(2)}, u32[]{:S(2)}) collective-permute-start(bf16[256,1152]{1,0:T(8,128)(2,1)S(1)} %near.5), channel_id=1, source_target_pairs={{0,1},{1,0},{2,3},{3,2},{4,5},{5,4},{6,7},{7,6},{8,73},{9,72},{10,... | collective-permute-start | bytes 1769480 | tf_op jit(solution)/shard_map/ppermute | solution.py:25
  86.2 3.8 %collective-permute-start.27 = (f32[8,128]{1,0:T(8,128)S(1)}, f32[8,128]{1,0:T(8,128)S(1)}, u32[]{:S(2)}, u32[]{:S(2)}) collective-permute-start(f32[8,128]{1,0:T(8,128)S(1)} %add.45), channel_id=1, source_target_pairs={{0,16},{1,17},{2,18},{3,19},{4,20},{5,21},{6,22},{7,23},{8,24},{9,... | collective-permute-start | bytes 12296 | tf_op jit(solution)/shard_map/ppermute | solution.py:25
  90.0 4.0 %collective-permute-start.28 = (f32[8,128]{1,0:T(8,128)S(1)}, f32[8,128]{1,0:T(8,128)S(1)}, u32[]{:S(2)}, u32[]{:S(2)}) collective-permute-start(f32[8,128]{1,0:T(8,128)S(1)} %add.46), channel_id=1, source_target_pairs={{0,48},{1,49},{2,50},{3,51},{4,52},{5,53},{6,54},{7,55},{8,56},{9,... | collective-permute-start | bytes 12296 | tf_op jit(solution)/shard_map/ppermute | solution.py:25
  94.0 6.2 %copy-start.1 = (f32[128,1152]{1,0:T(8,128)S(1)}, f32[128,1152]{1,0:T(8,128)}, u32[]{:S(2)}) copy-start(f32[128,1152]{1,0:T(8,128)} %refs_1_.1) | copy-start | bytes 1769476
  94.0 6.2 %copy-start.3 = (f32[128,1152]{1,0:T(8,128)S(1)}, f32[128,1152]{1,0:T(8,128)}, u32[]{:S(2)}) copy-start(f32[128,1152]{1,0:T(8,128)} %refs_2_.1) | copy-start | bytes 1769476
  96.4 3.8 %collective-permute-start.29 = (f32[136,1152]{1,0:T(8,128)S(1)}, f32[136,1152]{1,0:T(8,128)S(1)}, u32[]{:S(2)}, u32[]{:S(2)}) collective-permute-start(f32[136,1152]{1,0:T(8,128)S(1)} %get-tuple-element.125), channel_id=1, source_target_pairs={{0,8},{1,9},{2,10},{3,11},{4,12},{5,13},{6,14},{7,15},{8,0},{9,1},... | collective-permute-start | bytes 1880072 | tf_op jit(solution)/shard_map/ppermute | solution.py:25

commit v8 on v6

--- a/solution.py
+++ b/solution.py
@@ -535,6 +535,7 @@
     sent = encode(near_part, ONE_CHIP)
     loss = loss + swap(loss, 8, 1)
     loss = loss + swap(loss, 0, 2)
+    loss = loss + swap(loss, 0, 6)
     (second,) = small_call(
         second_kernel, "second", core, (far_part, rest_received), (low_piece,)
     )
@@ -554,9 +555,6 @@
     (base,) = small_call(
         base_kernel, "base", core, (near_part, near_received, img_part, rest_received), (array(wide, jnp.float32),)
     )
-    more = swap(loss, 0, 6)
-    base, more = lax.optimization_barrier((base, more))
-    loss = loss + more
 
     def near_slot(k, received):
         (out,) = small_call(

time: 102 us -> 105 us (1.029)
  waiting for transfers between devices: 27 us -> 30.3 us
    ppermute x30, waiting for transfers between devices: 27 us -> 30.3 us  [exchange(): return lax.ppermute(x, AXES, pairs)]
  transfers between devices with their start and end apart: 30 -> 30, of which waited for: 15 -> 16; matrix products, arithmetic and copies ran while one was open for 8% -> 8% of each run, Pallas kernels for 13% -> 13%
where the time goes in v8:
time: 105 us
  starting transfers between devices  38.6 us (37%)
  waiting for transfers between devices  30.3 us (29%)
  Pallas kernels  23 us (22%)
  matrix products  8.3 us (8%)
  between operations  2.26 us (2%)
  local copies, waits for them, and re-layouts  2.14 us (2%)
    ppermute x30, starting transfers between devices, exchange(): return lax.ppermute(x, AXES, pairs)  38.6 us
    ppermute x30, waiting for transfers between devices, exchange(): return lax.ppermute(x, AXES, pairs)  30.3 us
    pallas_call x4, Pallas kernels, tile_call(): pl.pallas_call(kernel, out_shape=outs, in_specs=[SMEM] + [VMEM] * (len(sc...  13.7 us
    pallas_call x9, Pallas kernels, small_call(): pl.pallas_call(kernel, out_shape=outs, in_specs=[SMEM] + [VMEM] * len(arr...  8.42 us
    dot_general x6, matrix products, transposed_product(): lax.dot_general(weights, img, (((0,), (0,)), ((), ())), preferred_element...  8.3 us
    unnamed x8, local copies, waits for them, and re-layouts  2.13 us
  transfers between devices with their start and end apart: 30, of which 16 were waited for; matrix products, arithmetic and copies ran while one was open for 8% of the time, Pallas kernels for 13%

profile of v8, /device:TPU:1, one launch (start us, length us, event | category | flops | bytes accessed | tf_op | source)
XLA Modules:
  0.0 104.7 jit_solution(1980443841406567469)
XLA Ops:
  0.6 1.1 %copy-done = f32[128,1152]{1,0:T(8,128)S(1)} copy-done((f32[128,1152]{1,0:T(8,128)S(1)}, f32[128,1152]{1,0:T(8,128)}, u32[]{:S(2)}) %copy-start) | copy-done | bytes 589848
  1.7 1.1 %copy-done.2 = f32[128,1152]{1,0:T(8,128)S(1)} copy-done((f32[128,1152]{1,0:T(8,128)S(1)}, f32[128,1152]{1,0:T(8,128)}, u32[]{:S(2)}) %copy-start.2) | copy-done | bytes 589848
  3.3 1.5 %collective-permute-start = (bf16[128,1152]{1,0:T(8,128)(2,1)S(1)}, bf16[128,1152]{1,0:T(8,128)(2,1)S(1)}, u32[]{:S(2)}, u32[]{:S(2)}) collective-permute-start(bf16[128,1152]{1,0:T(8,128)(2,1)S(1)} %get-tuple-element.65), channel_id=1, source_target_pairs={{0,8},{1,9},{2,10},{3,11},{4,12},{5,13},{6,14},{7,15},{8,0},{9,1},... | collective-permute-start | bytes 884744 | tf_op jit(solution)/shard_map/ppermute | solution.py:25
  4.8 1.2 %collective-permute-done.refs_1_ = bf16[128,1152]{1,0:T(8,128)(2,1)S(1)} collective-permute-done((bf16[128,1152]{1,0:T(8,128)(2,1)S(1)}, bf16[128,1152]{1,0:T(8,128)(2,1)S(1)}, u32[]{:S(2)}, u32[]{:S(2)}) %collective-permute-start) | collective-permute-done | bytes 294944 | tf_op jit(solution)/shard_map/ppermute | solution.py:25
  6.1 1.8 %collective-permute-start.5 = (bf16[256,1152]{1,0:T(8,128)(2,1)S(1)}, bf16[256,1152]{1,0:T(8,128)(2,1)S(1)}, u32[]{:S(2)}, u32[]{:S(2)}) collective-permute-start(bf16[256,1152]{1,0:T(8,128)(2,1)S(1)} %pack.4.refs_0_), channel_id=1, source_target_pairs={{0,2},{1,3},{2,0},{3,1},{4,6},{5,7},{6,4},{7,5},{8,24},{9,25},{10,... | collective-permute-start | bytes 1769480 | tf_op jit(solution)/shard_map/ppermute | solution.py:25
  7.9 2.5 %collective-permute-start.3 = (bf16[256,1152]{1,0:T(8,128)(2,1)S(1)}, bf16[256,1152]{1,0:T(8,128)(2,1)S(1)}, u32[]{:S(2)}, u32[]{:S(2)}) collective-permute-start(bf16[256,1152]{1,0:T(8,128)(2,1)S(1)} %pack.4.refs_0_), channel_id=1, source_target_pairs={{0,1},{1,0},{2,3},{3,2},{4,5},{5,4},{6,7},{7,6},{8,73},{9,72},{10,... | collective-permute-start | bytes 1769480 | tf_op jit(solution)/shard_map/ppermute | solution.py:25
  10.3 2.2 %collective-permute-start.1 = (bf16[256,1152]{1,0:T(8,128)(2,1)S(1)}, bf16[256,1152]{1,0:T(8,128)(2,1)S(1)}, u32[]{:S(2)}, u32[]{:S(2)}) collective-permute-start(bf16[256,1152]{1,0:T(8,128)(2,1)S(1)} %pack.4.refs_0_), channel_id=1, source_target_pairs={{0,6},{1,7},{2,4},{3,5},{4,2},{5,3},{6,0},{7,1},{8,56},{9,57},{10,... | collective-permute-start | bytes 1769480 | tf_op jit(solution)/shard_map/ppermute | solution.py:25
  12.6 2.8 %collective-permute-done.5.refs_2_ = bf16[256,1152]{1,0:T(8,128)(2,1)S(1)} collective-permute-done((bf16[256,1152]{1,0:T(8,128)(2,1)S(1)}, bf16[256,1152]{1,0:T(8,128)(2,1)S(1)}, u32[]{:S(2)}, u32[]{:S(2)}) %collective-permute-start.5) | collective-permute-done | bytes 589856 | tf_op jit(solution)/shard_map/ppermute | solution.py:25
  15.4 2.7 %collective-permute-done.3.refs_1_ = bf16[256,1152]{1,0:T(8,128)(2,1)S(1)} collective-permute-done((bf16[256,1152]{1,0:T(8,128)(2,1)S(1)}, bf16[256,1152]{1,0:T(8,128)(2,1)S(1)}, u32[]{:S(2)}, u32[]{:S(2)}) %collective-permute-start.3) | collective-permute-done | bytes 589856 | tf_op jit(solution)/shard_map/ppermute | solution.py:25
  18.1 2.3 %collective-permute-done.1.refs_3_ = bf16[256,1152]{1,0:T(8,128)(2,1)S(1)} collective-permute-done((bf16[256,1152]{1,0:T(8,128)(2,1)S(1)}, bf16[256,1152]{1,0:T(8,128)(2,1)S(1)}, u32[]{:S(2)}, u32[]{:S(2)}) %collective-permute-start.1) | collective-permute-done | bytes 589856 | tf_op jit(solution)/shard_map/ppermute | solution.py:25
  21.0 1.8 %collective-permute-start.6 = (bf16[256,1152]{1,0:T(8,128)(2,1)S(1)}, bf16[256,1152]{1,0:T(8,128)(2,1)S(1)}, u32[]{:S(2)}, u32[]{:S(2)}) collective-permute-start(bf16[256,1152]{1,0:T(8,128)(2,1)S(1)} %collective-permute-done.5.refs_2_), channel_id=1, source_target_pairs={{0,1},{1,0},{2,3},{3,2},{4,5},{5,4},{6,7},{7,6},{8,73},{9,72},{10,... | collective-permute-start | bytes 1769480 | tf_op jit(solution)/shard_map/ppermute | solution.py:25
  22.8 3.8 %collective-permute-start.4 = (bf16[256,1152]{1,0:T(8,128)(2,1)S(1)}, bf16[256,1152]{1,0:T(8,128)(2,1)S(1)}, u32[]{:S(2)}, u32[]{:S(2)}) collective-permute-start(bf16[256,1152]{1,0:T(8,128)(2,1)S(1)} %collective-permute-done.3.refs_1_), channel_id=1, source_target_pairs={{0,6},{1,7},{2,4},{3,5},{4,2},{5,3},{6,0},{7,1},{8,56},{9,57},{10,... | collective-permute-start | bytes 1769480 | tf_op jit(solution)/shard_map/ppermute | solution.py:25
  27.9 3.5 %tile_near.1 = (bf16[512,1152]{1,0:T(8,128)(2,1)S(1)}, bf16[1024,1152]{1,0:T(8,128)(2,1)S(1)}, bf16[512,1024]{1,0:T(8,128)(2,1)S(1)}, f32[512,1152]{1,0:T(8,128)S(1)}, f32[8,128]{1,0:T(8,128)S(1)}) custom-call(s32[1]{0:T(128)} %bitcast.core_ref.refs_0_, f32[8,128]{1,0:T(8,128)S(1)} %broadcast_in_dim.15.sharp_ref, f32[8,128]{1,0:T(8,128)S(1)} %broadcast_in_dim.17.bias_ref, ...), custom_call_target="tpu_custom_call" | custom-call | flops 2415919104 | bytes 4718592 | tf_op jit(solution)/shard_map/tile_near/pallas_call | solution.py:258
  31.4 2.4 %collective-permute-done.4.refs_0_.refs_2_ = bf16[256,1152]{1,0:T(8,128)(2,1)S(1)} collective-permute-done((bf16[256,1152]{1,0:T(8,128)(2,1)S(1)}, bf16[256,1152]{1,0:T(8,128)(2,1)S(1)}, u32[]{:S(2)}, u32[]{:S(2)}) %collective-permute-start.4) | collective-permute-done | bytes 589856 | tf_op jit(solution)/shard_map/ppermute | solution.py:25
  33.9 1.5 %collective-permute-done.2.refs_0_ = bf16[256,1152]{1,0:T(8,128)(2,1)S(1)} collective-permute-done((bf16[256,1152]{1,0:T(8,128)(2,1)S(1)}, bf16[256,1152]{1,0:T(8,128)(2,1)S(1)}, u32[]{:S(2)}, u32[]{:S(2)}) %collective-permute-start.2) | collective-permute-done | bytes 589856 | tf_op jit(solution)/shard_map/ppermute | solution.py:25
  35.6 2.2 %collective-permute-start.9 = (bf16[128,1152]{1,0:T(8,128)(2,1)S(1)}, bf16[128,1152]{1,0:T(8,128)(2,1)S(1)}, u32[]{:S(2)}, u32[]{:S(2)}) collective-permute-start(bf16[128,1152]{1,0:T(8,128)(2,1)S(1)} %half_of.3), channel_id=1, source_target_pairs={{0,6},{1,7},{2,4},{3,5},{4,2},{5,3},{6,0},{7,1},{8,56},{9,57},{10,... | collective-permute-start | bytes 884744 | tf_op jit(solution)/shard_map/ppermute | solution.py:25
  37.8 1.4 %collective-permute-done.10.received_ref.far_received_ref = bf16[768,1152]{1,0:T(8,128)(2,1)S(1)} collective-permute-done((bf16[768,1152]{1,0:T(8,128)(2,1)S(1)}, bf16[768,1152]{1,0:T(8,128)(2,1)S(1)}, u32[]{:S(2)}, u32[]{:S(2)}) %collective-permute-start.10) | collective-permute-done | bytes 1769504 | tf_op jit(solution)/shard_map/ppermute | solution.py:25
  39.2 3.7 %tile_far.1 = (bf16[768,1152]{1,0:T(8,128)(2,1)S(1)}, bf16[768,1152]{1,0:T(8,128)(2,1)S(1)}, bf16[768,768]{1,0:T(8,128)(2,1)S(1)}, f32[768,1152]{1,0:T(8,128)S(1)}, f32[8,128]{1,0:T(8,128)S(1)}) custom-call(s32[1]{0:T(128)} %bitcast.core_ref.refs_0_, f32[8,128]{1,0:T(8,128)S(1)} %broadcast_in_dim.15.sharp_ref, f32[8,128]{1,0:T(8,128)S(1)} %broadcast_in_dim.17.bias_ref, ...), custom_call_target="tpu_custom_call" | custom-call | flops 2717908992 | bytes 5898240 | tf_op jit(solution)/shard_map/tile_far/pallas_call | solution.py:258
  42.9 0.8 collective-permute-done.8.refs_0_
  43.7 1.7 %collective-permute-start.11 = (bf16[256,1152]{1,0:T(8,128)(2,1)S(1)}, bf16[256,1152]{1,0:T(8,128)(2,1)S(1)}, u32[]{:S(2)}, u32[]{:S(2)}) collective-permute-start(bf16[256,1152]{1,0:T(8,128)(2,1)S(1)} %pack.7.last_ref), channel_id=1, source_target_pairs={{0,8},{1,9},{2,10},{3,11},{4,12},{5,13},{6,14},{7,15},{8,0},{9,1},... | collective-permute-start | bytes 1769480 | tf_op jit(solution)/shard_map/ppermute | solution.py:25
  45.4 1.9 %tile_middle.1 = (bf16[768,1024]{1,0:T(8,128)(2,1)S(1)}, f32[256,1152]{1,0:T(8,128)S(1)}, f32[8,128]{1,0:T(8,128)S(1)}) custom-call(s32[1]{0:T(128)} %bitcast.core_ref.refs_0_, f32[8,128]{1,0:T(8,128)S(1)} %broadcast_in_dim.15.sharp_ref, f32[8,128]{1,0:T(8,128)S(1)} %broadcast_in_dim.17.bias_ref, bf16[768,1152]{1,0:T(8,128)(2,1)S(1)} %get-tuple-element.77.img_ref, ...), custom_call_target="tpu_custom_call" | custom-call | flops 1207959552 | bytes 6946816 | tf_op jit(solution)/shard_map/tile_middle/pallas_call | solution.py:258
  47.3 4.6 %tile_last.1 = (bf16[768,256]{1,0:T(8,128)(2,1)S(1)}, f32[768,1152]{1,0:T(8,128)S(1)}, bf16[256,1152]{1,0:T(8,128)(2,1)S(1)}, bf16[256,1024]{1,0:T(8,128)(2,1)S(...) custom-call(s32[1]{0:T(128)} %bitcast.core_ref.refs_0_, ...), custom_call_target="tpu_custom_call" | custom-call | flops 3321888768 | bytes 12976128 | tf_op jit(solution)/shard_map/tile_last/pallas_call | solution.py:258
  52.7 0.9 fusion.5
  54.8 2.5 %fusion.3 = (bf16[768,1152]{1,0:T(8,128)(2,1)S(1)}, f32[768,1152]{1,0:T(8,128)S(1)}) fusion(f32[768,1152]{1,0:T(8,128)S(1)} %get-tuple-element.89.img_ref, pred[]{:T(512)S(6)} %eq.3, f32[768,1152]{1,0:T(8,128)S(1)} %fusion.7, bf16[768,768]{1,0:T(8,128)(2,1)S(1)} %get-tuple-element.90, bf16[768,1152]{1,0:T(8,128)(2,1)S(1)} %get-tuple-element.77.img_ref), kind=kOutput, calls=%fused_computation.9 | convolution fusion | flops 1367801856 | bytes 15335425 | tf_op jit(solution)/shard_map/dot_general | solution.py:423
  58.2 1.3 %collective-permute-start.17 = (f32[8,128]{1,0:T(8,128)S(1)}, f32[8,128]{1,0:T(8,128)S(1)}, u32[]{:S(2)}, u32[]{:S(2)}) collective-permute-start(f32[8,128]{1,0:T(8,128)S(1)} %add.41), channel_id=1, source_target_pairs={{0,65},{1,64},{2,67},{3,66},{4,69},{5,68},{6,71},{7,70},{8,73},{9,... | collective-permute-start | bytes 12296 | tf_op jit(solution)/shard_map/ppermute | solution.py:25
  59.6 2.2 %collective-permute-start.16 = (bf16[128,1152]{1,0:T(8,128)(2,1)S(1)}, bf16[128,1152]{1,0:T(8,128)(2,1)S(1)}, u32[]{:S(2)}, u32[]{:S(2)}) collective-permute-start(bf16[128,1152]{1,0:T(8,128)(2,1)S(1)} %get-tuple-element.106), channel_id=1, source_target_pairs={{0,6},{1,7},{2,4},{3,5},{4,2},{5,3},{6,0},{7,1},{8,56},{9,57},{10,... | collective-permute-start | bytes 884744 | tf_op jit(solution)/shard_map/ppermute | solution.py:25
  61.9 0.9 fusion.8
  62.8 2.0 %collective-permute-done.18 = f32[8,128]{1,0:T(8,128)S(1)} collective-permute-done((f32[8,128]{1,0:T(8,128)S(1)}, f32[8,128]{1,0:T(8,128)S(1)}, u32[]{:S(2)}, u32[]{:S(2)}) %collective-permute-start.18) | collective-permute-done | bytes 4128 | tf_op jit(solution)/shard_map/ppermute | solution.py:25
  64.8 1.6 %collective-permute-start.19 = (f32[8,128]{1,0:T(8,128)S(1)}, f32[8,128]{1,0:T(8,128)S(1)}, u32[]{:S(2)}, u32[]{:S(2)}) collective-permute-start(f32[8,128]{1,0:T(8,128)S(1)} %add.44), channel_id=1, source_target_pairs={{0,6},{1,7},{2,4},{3,5},{4,2},{5,3},{6,0},{7,1},{8,14},{9,15},{10,... | collective-permute-start | bytes 12296 | tf_op jit(solution)/shard_map/ppermute | solution.py:25
  66.4 3.0 %fusion.1 = (bf16[1024,1152]{1,0:T(8,128)(2,1)S(1)}, f32[1024,1152]{1,0:T(8,128)S(1)}) fusion(f32[1024,1152]{1,0:T(8,128)S(1)} %fusion.8, bf16[768,1024]{1,0:T(8,128)(2,1)S(1)} %get-tuple-element.102, bf16[768,1152]{1,0:T(8,128)(2,1)S(1)} %get-tuple-element.77.img_ref), kind=kOutput, calls=%fused_computation.5 | convolution fusion | flops 1822556160 | bytes 15138816 | tf_op jit(solution)/shard_map/dot_general | solution.py:423
  70.2 1.2 %far.1 = (bf16[256,1152]{1,0:T(8,128)(2,1)S(1)}, bf16[256,1152]{1,0:T(8,128)(2,1)S(1)}) custom-call(s32[1]{0:T(128)} %bitcast.core_ref.refs_0_, f32[768,1152]{1,0:T(8,128)S(1)} %get-tuple-element.126.txt_ref, bf16[768,1152]{1,0:T(8,128)(2,1)S(1)} %collective-permute-done.14.received_ref.txt_received_ref.img_received_ref, ...), custom_call_target="tpu_custom_call" | custom-call | tf_op jit(solution)/shard_map/far/pallas_call | solution.py:276
  71.4 2.9 %collective-permute-start.20 = (bf16[1024,1152]{1,0:T(8,128)(2,1)S(1)}, bf16[1024,1152]{1,0:T(8,128)(2,1)S(1)}, u32[]{:S(2)}, u32[]{:S(2)}) collective-permute-start(bf16[1024,1152]{1,0:T(8,128)(2,1)S(1)} %get-tuple-element.113), channel_id=1, source_target_pairs={{0,8},{1,9},{2,10},{3,11},{4,12},{5,13},{6,14},{7,15},{8,0},{9,1},... | collective-permute-start | bytes 7077896 | tf_op jit(solution)/shard_map/ppermute | solution.py:25
  74.4 1.3 %collective-permute-start.21 = (bf16[256,1152]{1,0:T(8,128)(2,1)S(1)}, bf16[256,1152]{1,0:T(8,128)(2,1)S(1)}, u32[]{:S(2)}, u32[]{:S(2)}) collective-permute-start(bf16[256,1152]{1,0:T(8,128)(2,1)S(1)} %get-tuple-element.114), channel_id=1, source_target_pairs={{0,1},{1,0},{2,3},{3,2},{4,5},{5,4},{6,7},{7,6},{8,73},{9,72},{10,... | collective-permute-start | bytes 1769480 | tf_op jit(solution)/shard_map/ppermute | solution.py:25
  75.9 2.2 %collective-permute-start.25 = (bf16[256,1152]{1,0:T(8,128)(2,1)S(1)}, bf16[256,1152]{1,0:T(8,128)(2,1)S(1)}, u32[]{:S(2)}, u32[]{:S(2)}) collective-permute-start(bf16[256,1152]{1,0:T(8,128)(2,1)S(1)} %get-tuple-element.116), channel_id=1, source_target_pairs={{0,6},{1,7},{2,4},{3,5},{4,2},{5,3},{6,0},{7,1},{8,56},{9,57},{10,... | collective-permute-start | bytes 1769480 | tf_op jit(solution)/shard_map/ppermute | solution.py:25
  78.5 1.0 base.1.refs_1_.base_ref
  79.6 5.1 %collective-permute-done.21.refs_2_ = bf16[256,1152]{1,0:T(8,128)(2,1)S(1)} collective-permute-done((bf16[256,1152]{1,0:T(8,128)(2,1)S(1)}, bf16[256,1152]{1,0:T(8,128)(2,1)S(1)}, u32[]{:S(2)}, u32[]{:S(2)}) %collective-permute-start.21) | collective-permute-done | bytes 589856 | tf_op jit(solution)/shard_map/ppermute | solution.py:25
  84.6 0.8 near.3
  85.7 0.8 near.4
  86.4 2.3 %collective-permute-start.24 = (bf16[256,1152]{1,0:T(8,128)(2,1)S(1)}, bf16[256,1152]{1,0:T(8,128)(2,1)S(1)}, u32[]{:S(2)}, u32[]{:S(2)}) collective-permute-start(bf16[256,1152]{1,0:T(8,128)(2,1)S(1)} %near.4), channel_id=1, source_target_pairs={{0,6},{1,7},{2,4},{3,5},{4,2},{5,3},{6,0},{7,1},{8,56},{9,57},{10,... | collective-permute-start | bytes 1769480 | tf_op jit(solution)/shard_map/ppermute | solution.py:25
  88.8 0.8 near.5
  89.5 1.4 %collective-permute-start.26 = (bf16[256,1152]{1,0:T(8,128)(2,1)S(1)}, bf16[256,1152]{1,0:T(8,128)(2,1)S(1)}, u32[]{:S(2)}, u32[]{:S(2)}) collective-permute-start(bf16[256,1152]{1,0:T(8,128)(2,1)S(1)} %near.5), channel_id=1, source_target_pairs={{0,1},{1,0},{2,3},{3,2},{4,5},{5,4},{6,7},{7,6},{8,73},{9,72},{10,... | collective-permute-start | bytes 1769480 | tf_op jit(solution)/shard_map/ppermute | solution.py:25
  91.6 2.9 %collective-permute-done.27 = f32[8,128]{1,0:T(8,128)S(1)} collective-permute-done((f32[8,128]{1,0:T(8,128)S(1)}, f32[8,128]{1,0:T(8,128)S(1)}, u32[]{:S(2)}, u32[]{:S(2)}) %collective-permute-start.27) | collective-permute-done | bytes 4128 | tf_op jit(solution)/shard_map/ppermute | solution.py:25
  94.6 2.3 %collective-permute-start.28 = (f32[8,128]{1,0:T(8,128)S(1)}, f32[8,128]{1,0:T(8,128)S(1)}, u32[]{:S(2)}, u32[]{:S(2)}) collective-permute-start(f32[8,128]{1,0:T(8,128)S(1)} %add.46), channel_id=1, source_target_pairs={{0,48},{1,49},{2,50},{3,51},{4,52},{5,53},{6,54},{7,55},{8,56},{9,... | collective-permute-start | bytes 12296 | tf_op jit(solution)/shard_map/ppermute | solution.py:25
  96.9 1.4 %collective-permute-done.28 = f32[8,128]{1,0:T(8,128)S(1)} collective-permute-done((f32[8,128]{1,0:T(8,128)S(1)}, f32[8,128]{1,0:T(8,128)S(1)}, u32[]{:S(2)}, u32[]{:S(2)}) %collective-permute-start.28) | collective-permute-done | bytes 4128 | tf_op jit(solution)/shard_map/ppermute | solution.py:25
  98.3 1.3 %collective-permute-done.26.x_ref = bf16[256,1152]{1,0:T(8,128)(2,1)S(1)} collective-permute-done((bf16[256,1152]{1,0:T(8,128)(2,1)S(1)}, bf16[256,1152]{1,0:T(8,128)(2,1)S(1)}, u32[]{:S(2)}, u32[]{:S(2)}) %collective-permute-start.26) | collective-permute-done | bytes 589856 | tf_op jit(solution)/shard_map/ppermute | solution.py:25
  99.5 1.3 %gather_sums.1 = (f32[128,1152]{1,0:T(8,128)S(1)}, f32[136,1152]{1,0:T(8,128)S(1)}) custom-call(s32[1]{0:T(128)} %bitcast.core_ref.refs_0_, f32[1024,1152]{1,0:T(8,128)S(1)} %base.1.refs_1_.base_ref, bf16[256,1152]{1,0:T(8,128)(2,1)S(1)} %collective-permute-done.22.a_ref, bf16[256,1152]{1,0:T(8,128)(2,1)S(1)} %collective-permute-done.24.b_ref, ...), custom_call_target="tpu_custom_call" | custom-call | tf_op jit(solution)/shard_map/gather_sums/pallas_call | solution.py:276
  100.9 2.0 %collective-permute-done.29.refs_4_ = f32[136,1152]{1,0:T(8,128)S(1)} collective-permute-done((f32[136,1152]{1,0:T(8,128)S(1)}, f32[136,1152]{1,0:T(8,128)S(1)}, u32[]{:S(2)}, u32[]{:S(2)}) %collective-permute-start.29) | collective-permute-done | bytes 626720 | tf_op jit(solution)/shard_map/ppermute | solution.py:25
  103.0 1.7 %finish.1 = (f32[1,1]{1,0:T(1,128)}, f32[128,1152]{1,0:T(8,128)}, f32[128,1152]{1,0:T(8,128)}) custom-call(s32[1]{0:T(128)} %bitcast.core_ref.refs_0_, f32[128,1152]{1,0:T(8,128)S(1)} %copy-done.1, f32[128,1152]{1,0:T(8,128)S(1)} %copy-done.3, f32[128,1152]{1,0:T(8,128)S(1)} %get-tuple-element.118.refs_3_, f32[136,1152]{1,0:T(8,128)S(1)} %collective-permute-done.29.refs_4_, ...), custom_call_target="tpu_custom_call" | custom-call | tf_op jit(solution)/shard_map/finish/pallas_call | solution.py:276
  (55 shorter events, 7.0 us)
Async XLA Ops:
  0.6 1.1 %copy-start = (f32[128,1152]{1,0:T(8,128)S(1)}, f32[128,1152]{1,0:T(8,128)}, u32[]{:S(2)}) copy-start(f32[128,1152]{1,0:T(8,128)} %refs_1_.1) | copy-start | bytes 1769476
  1.7 1.1 %copy-start.2 = (f32[128,1152]{1,0:T(8,128)S(1)}, f32[128,1152]{1,0:T(8,128)}, u32[]{:S(2)}) copy-start(f32[128,1152]{1,0:T(8,128)} %refs_2_.1) | copy-start | bytes 1769476
  3.3 2.7 %collective-permute-start = (bf16[128,1152]{1,0:T(8,128)(2,1)S(1)}, bf16[128,1152]{1,0:T(8,128)(2,1)S(1)}, u32[]{:S(2)}, u32[]{:S(2)}) collective-permute-start(bf16[128,1152]{1,0:T(8,128)(2,1)S(1)} %get-tuple-element.65), channel_id=1, source_target_pairs={{0,8},{1,9},{2,10},{3,11},{4,12},{5,13},{6,14},{7,15},{8,0},{9,1},... | collective-permute-start | bytes 884744 | tf_op jit(solution)/shard_map/ppermute | solution.py:25
  6.1 9.4 %collective-permute-start.5 = (bf16[256,1152]{1,0:T(8,128)(2,1)S(1)}, bf16[256,1152]{1,0:T(8,128)(2,1)S(1)}, u32[]{:S(2)}, u32[]{:S(2)}) collective-permute-start(bf16[256,1152]{1,0:T(8,128)(2,1)S(1)} %pack.4.refs_0_), channel_id=1, source_target_pairs={{0,2},{1,3},{2,0},{3,1},{4,6},{5,7},{6,4},{7,5},{8,24},{9,25},{10,... | collective-permute-start | bytes 1769480 | tf_op jit(solution)/shard_map/ppermute | solution.py:25
  7.9 10.2 %collective-permute-start.3 = (bf16[256,1152]{1,0:T(8,128)(2,1)S(1)}, bf16[256,1152]{1,0:T(8,128)(2,1)S(1)}, u32[]{:S(2)}, u32[]{:S(2)}) collective-permute-start(bf16[256,1152]{1,0:T(8,128)(2,1)S(1)} %pack.4.refs_0_), channel_id=1, source_target_pairs={{0,1},{1,0},{2,3},{3,2},{4,5},{5,4},{6,7},{7,6},{8,73},{9,72},{10,... | collective-permute-start | bytes 1769480 | tf_op jit(solution)/shard_map/ppermute | solution.py:25
  10.3 10.0 %collective-permute-start.1 = (bf16[256,1152]{1,0:T(8,128)(2,1)S(1)}, bf16[256,1152]{1,0:T(8,128)(2,1)S(1)}, u32[]{:S(2)}, u32[]{:S(2)}) collective-permute-start(bf16[256,1152]{1,0:T(8,128)(2,1)S(1)} %pack.4.refs_0_), channel_id=1, source_target_pairs={{0,6},{1,7},{2,4},{3,5},{4,2},{5,3},{6,0},{7,1},{8,56},{9,57},{10,... | collective-permute-start | bytes 1769480 | tf_op jit(solution)/shard_map/ppermute | solution.py:25
  20.5 7.4 %collective-permute-start.7 = (bf16[1024,1152]{1,0:T(8,128)(2,1)S(1)}, bf16[1024,1152]{1,0:T(8,128)(2,1)S(1)}, u32[]{:S(2)}, u32[]{:S(2)}) collective-permute-start(bf16[1024,1152]{1,0:T(8,128)(2,1)S(1)} %pack.5.near_ref), channel_id=1, source_target_pairs={{0,8},{1,9},{2,10},{3,11},{4,12},{5,13},{6,14},{7,15},{8,0},{9,1},... | collective-permute-start | bytes 7077896 | tf_op jit(solution)/shard_map/ppermute | solution.py:25
  21.0 10.4 %collective-permute-start.6 = (bf16[256,1152]{1,0:T(8,128)(2,1)S(1)}, bf16[256,1152]{1,0:T(8,128)(2,1)S(1)}, u32[]{:S(2)}, u32[]{:S(2)}) collective-permute-start(bf16[256,1152]{1,0:T(8,128)(2,1)S(1)} %collective-permute-done.5.refs_2_), channel_id=1, source_target_pairs={{0,1},{1,0},{2,3},{3,2},{4,5},{5,4},{6,7},{7,6},{8,73},{9,72},{10,... | collective-permute-start | bytes 1769480 | tf_op jit(solution)/shard_map/ppermute | solution.py:25
  22.8 11.0 %collective-permute-start.4 = (bf16[256,1152]{1,0:T(8,128)(2,1)S(1)}, bf16[256,1152]{1,0:T(8,128)(2,1)S(1)}, u32[]{:S(2)}, u32[]{:S(2)}) collective-permute-start(bf16[256,1152]{1,0:T(8,128)(2,1)S(1)} %collective-permute-done.3.refs_1_), channel_id=1, source_target_pairs={{0,6},{1,7},{2,4},{3,5},{4,2},{5,3},{6,0},{7,1},{8,56},{9,57},{10,... | collective-permute-start | bytes 1769480 | tf_op jit(solution)/shard_map/ppermute | solution.py:25
  26.6 8.7 %collective-permute-start.2 = (bf16[256,1152]{1,0:T(8,128)(2,1)S(1)}, bf16[256,1152]{1,0:T(8,128)(2,1)S(1)}, u32[]{:S(2)}, u32[]{:S(2)}) collective-permute-start(bf16[256,1152]{1,0:T(8,128)(2,1)S(1)} %collective-permute-done.1.refs_3_), channel_id=1, source_target_pairs={{0,2},{1,3},{2,0},{3,1},{4,6},{5,7},{6,4},{7,5},{8,24},{9,25},{10,... | collective-permute-start | bytes 1769480 | tf_op jit(solution)/shard_map/ppermute | solution.py:25
  35.5 3.8 %collective-permute-start.10 = (bf16[768,1152]{1,0:T(8,128)(2,1)S(1)}, bf16[768,1152]{1,0:T(8,128)(2,1)S(1)}, u32[]{:S(2)}, u32[]{:S(2)}) collective-permute-start(bf16[768,1152]{1,0:T(8,128)(2,1)S(1)} %pack.6.far_ref), channel_id=1, source_target_pairs={{0,8},{1,9},{2,10},{3,11},{4,12},{5,13},{6,14},{7,15},{8,0},{9,1},... | collective-permute-start | bytes 5308424 | tf_op jit(solution)/shard_map/ppermute | solution.py:25
  35.6 7.3 %collective-permute-start.9 = (bf16[128,1152]{1,0:T(8,128)(2,1)S(1)}, bf16[128,1152]{1,0:T(8,128)(2,1)S(1)}, u32[]{:S(2)}, u32[]{:S(2)}) collective-permute-start(bf16[128,1152]{1,0:T(8,128)(2,1)S(1)} %half_of.3), channel_id=1, source_target_pairs={{0,6},{1,7},{2,4},{3,5},{4,2},{5,3},{6,0},{7,1},{8,56},{9,57},{10,... | collective-permute-start | bytes 884744 | tf_op jit(solution)/shard_map/ppermute | solution.py:25
  37.8 5.9 %collective-permute-start.8 = (bf16[128,1152]{1,0:T(8,128)(2,1)S(1)}, bf16[128,1152]{1,0:T(8,128)(2,1)S(1)}, u32[]{:S(2)}, u32[]{:S(2)}) collective-permute-start(bf16[128,1152]{1,0:T(8,128)(2,1)S(1)} %half_of.2), channel_id=1, source_target_pairs={{0,2},{1,3},{2,0},{3,1},{4,6},{5,7},{6,4},{7,5},{8,24},{9,25},{10,... | collective-permute-start | bytes 884744 | tf_op jit(solution)/shard_map/ppermute | solution.py:25
  43.7 3.5 %collective-permute-start.11 = (bf16[256,1152]{1,0:T(8,128)(2,1)S(1)}, bf16[256,1152]{1,0:T(8,128)(2,1)S(1)}, u32[]{:S(2)}, u32[]{:S(2)}) collective-permute-start(bf16[256,1152]{1,0:T(8,128)(2,1)S(1)} %pack.7.last_ref), channel_id=1, source_target_pairs={{0,8},{1,9},{2,10},{3,11},{4,12},{5,13},{6,14},{7,15},{8,0},{9,1},... | collective-permute-start | bytes 1769480 | tf_op jit(solution)/shard_map/ppermute | solution.py:25
  51.9 5.4 %collective-permute-start.13 = (f32[8,128]{1,0:T(8,128)S(1)}, f32[8,128]{1,0:T(8,128)S(1)}, u32[]{:S(2)}, u32[]{:S(2)}) collective-permute-start(f32[8,128]{1,0:T(8,128)S(1)} %add_add_fusion), channel_id=1, source_target_pairs={{0,1},{1,0},{2,3},{3,2},{4,5},{5,4},{6,7},{7,6},{8,9},{9,8},{10,11... | collective-permute-start | bytes 12296 | tf_op jit(solution)/shard_map/ppermute | solution.py:25
  53.6 3.7 %collective-permute-start.12 = (bf16[256,1152]{1,0:T(8,128)(2,1)S(1)}, bf16[256,1152]{1,0:T(8,128)(2,1)S(1)}, u32[]{:S(2)}, u32[]{:S(2)}) collective-permute-start(bf16[256,1152]{1,0:T(8,128)(2,1)S(1)} %get-tuple-element.88), channel_id=1, source_target_pairs={{0,8},{1,9},{2,10},{3,11},{4,12},{5,13},{6,14},{7,15},{8,0},{9,1},... | collective-permute-start | bytes 1769480 | tf_op jit(solution)/shard_map/ppermute | solution.py:25
  57.5 11.9 %collective-permute-start.14 = (bf16[768,1152]{1,0:T(8,128)(2,1)S(1)}, bf16[768,1152]{1,0:T(8,128)(2,1)S(1)}, u32[]{:S(2)}, u32[]{:S(2)}) collective-permute-start(bf16[768,1152]{1,0:T(8,128)(2,1)S(1)} %get-tuple-element.104), channel_id=1, source_target_pairs={{0,8},{1,9},{2,10},{3,11},{4,12},{5,13},{6,14},{7,15},{8,0},{9,1},... | collective-permute-start | bytes 5308424 | tf_op jit(solution)/shard_map/ppermute | solution.py:25
  58.2 3.7 %collective-permute-start.17 = (f32[8,128]{1,0:T(8,128)S(1)}, f32[8,128]{1,0:T(8,128)S(1)}, u32[]{:S(2)}, u32[]{:S(2)}) collective-permute-start(f32[8,128]{1,0:T(8,128)S(1)} %add.41), channel_id=1, source_target_pairs={{0,65},{1,64},{2,67},{3,66},{4,69},{5,68},{6,71},{7,70},{8,73},{9,... | collective-permute-start | bytes 12296 | tf_op jit(solution)/shard_map/ppermute | solution.py:25
  59.6 10.6 %collective-permute-start.15 = (bf16[128,1152]{1,0:T(8,128)(2,1)S(1)}, bf16[128,1152]{1,0:T(8,128)(2,1)S(1)}, u32[]{:S(2)}, u32[]{:S(2)}) collective-permute-start(bf16[128,1152]{1,0:T(8,128)(2,1)S(1)} %get-tuple-element.105), channel_id=1, source_target_pairs={{0,2},{1,3},{2,0},{3,1},{4,6},{5,7},{6,4},{7,5},{8,24},{9,25},{10,... | collective-permute-start | bytes 884744 | tf_op jit(solution)/shard_map/ppermute | solution.py:25
  59.6 10.6 %collective-permute-start.16 = (bf16[128,1152]{1,0:T(8,128)(2,1)S(1)}, bf16[128,1152]{1,0:T(8,128)(2,1)S(1)}, u32[]{:S(2)}, u32[]{:S(2)}) collective-permute-start(bf16[128,1152]{1,0:T(8,128)(2,1)S(1)} %get-tuple-element.106), channel_id=1, source_target_pairs={{0,6},{1,7},{2,4},{3,5},{4,2},{5,3},{6,0},{7,1},{8,56},{9,57},{10,... | collective-permute-start | bytes 884744 | tf_op jit(solution)/shard_map/ppermute | solution.py:25
  61.9 2.9 %collective-permute-start.18 = (f32[8,128]{1,0:T(8,128)S(1)}, f32[8,128]{1,0:T(8,128)S(1)}, u32[]{:S(2)}, u32[]{:S(2)}) collective-permute-start(f32[8,128]{1,0:T(8,128)S(1)} %add.43), channel_id=1, source_target_pairs={{0,2},{1,3},{2,0},{3,1},{4,6},{5,7},{6,4},{7,5},{8,10},{9,11},{10,... | collective-permute-start | bytes 12296 | tf_op jit(solution)/shard_map/ppermute | solution.py:25
  64.8 4.6 %collective-permute-start.19 = (f32[8,128]{1,0:T(8,128)S(1)}, f32[8,128]{1,0:T(8,128)S(1)}, u32[]{:S(2)}, u32[]{:S(2)}) collective-permute-start(f32[8,128]{1,0:T(8,128)S(1)} %add.44), channel_id=1, source_target_pairs={{0,6},{1,7},{2,4},{3,5},{4,2},{5,3},{6,0},{7,1},{8,14},{9,15},{10,... | collective-permute-start | bytes 12296 | tf_op jit(solution)/shard_map/ppermute | solution.py:25
  71.4 7.1 %collective-permute-start.20 = (bf16[1024,1152]{1,0:T(8,128)(2,1)S(1)}, bf16[1024,1152]{1,0:T(8,128)(2,1)S(1)}, u32[]{:S(2)}, u32[]{:S(2)}) collective-permute-start(bf16[1024,1152]{1,0:T(8,128)(2,1)S(1)} %get-tuple-element.113), channel_id=1, source_target_pairs={{0,8},{1,9},{2,10},{3,11},{4,12},{5,13},{6,14},{7,15},{8,0},{9,1},... | collective-permute-start | bytes 7077896 | tf_op jit(solution)/shard_map/ppermute | solution.py:25
  74.4 10.2 %collective-permute-start.21 = (bf16[256,1152]{1,0:T(8,128)(2,1)S(1)}, bf16[256,1152]{1,0:T(8,128)(2,1)S(1)}, u32[]{:S(2)}, u32[]{:S(2)}) collective-permute-start(bf16[256,1152]{1,0:T(8,128)(2,1)S(1)} %get-tuple-element.114), channel_id=1, source_target_pairs={{0,1},{1,0},{2,3},{3,2},{4,5},{5,4},{6,7},{7,6},{8,73},{9,72},{10,... | collective-permute-start | bytes 1769480 | tf_op jit(solution)/shard_map/ppermute | solution.py:25
  75.7 9.9 %collective-permute-start.23 = (bf16[256,1152]{1,0:T(8,128)(2,1)S(1)}, bf16[256,1152]{1,0:T(8,128)(2,1)S(1)}, u32[]{:S(2)}, u32[]{:S(2)}) collective-permute-start(bf16[256,1152]{1,0:T(8,128)(2,1)S(1)} %second.1), channel_id=1, source_target_pairs={{0,2},{1,3},{2,0},{3,1},{4,6},{5,7},{6,4},{7,5},{8,24},{9,25},{10,... | collective-permute-start | bytes 1769480 | tf_op jit(solution)/shard_map/ppermute | solution.py:25
  75.9 12.8 %collective-permute-start.25 = (bf16[256,1152]{1,0:T(8,128)(2,1)S(1)}, bf16[256,1152]{1,0:T(8,128)(2,1)S(1)}, u32[]{:S(2)}, u32[]{:S(2)}) collective-permute-start(bf16[256,1152]{1,0:T(8,128)(2,1)S(1)} %get-tuple-element.116), channel_id=1, source_target_pairs={{0,6},{1,7},{2,4},{3,5},{4,2},{5,3},{6,0},{7,1},{8,56},{9,57},{10,... | collective-permute-start | bytes 1769480 | tf_op jit(solution)/shard_map/ppermute | solution.py:25
  85.4 12.9 %collective-permute-start.22 = (bf16[256,1152]{1,0:T(8,128)(2,1)S(1)}, bf16[256,1152]{1,0:T(8,128)(2,1)S(1)}, u32[]{:S(2)}, u32[]{:S(2)}) collective-permute-start(bf16[256,1152]{1,0:T(8,128)(2,1)S(1)} %near.3), channel_id=1, source_target_pairs={{0,2},{1,3},{2,0},{3,1},{4,6},{5,7},{6,4},{7,5},{8,24},{9,25},{10,... | collective-permute-start | bytes 1769480 | tf_op jit(solution)/shard_map/ppermute | solution.py:25
  86.4 11.8 %collective-permute-start.24 = (bf16[256,1152]{1,0:T(8,128)(2,1)S(1)}, bf16[256,1152]{1,0:T(8,128)(2,1)S(1)}, u32[]{:S(2)}, u32[]{:S(2)}) collective-permute-start(bf16[256,1152]{1,0:T(8,128)(2,1)S(1)} %near.4), channel_id=1, source_target_pairs={{0,6},{1,7},{2,4},{3,5},{4,2},{5,3},{6,0},{7,1},{8,56},{9,57},{10,... | collective-permute-start | bytes 1769480 | tf_op jit(solution)/shard_map/ppermute | solution.py:25
  89.5 10.0 %collective-permute-start.26 = (bf16[256,1152]{1,0:T(8,128)(2,1)S(1)}, bf16[256,1152]{1,0:T(8,128)(2,1)S(1)}, u32[]{:S(2)}, u32[]{:S(2)}) collective-permute-start(bf16[256,1152]{1,0:T(8,128)(2,1)S(1)} %near.5), channel_id=1, source_target_pairs={{0,1},{1,0},{2,3},{3,2},{4,5},{5,4},{6,7},{7,6},{8,73},{9,72},{10,... | collective-permute-start | bytes 1769480 | tf_op jit(solution)/shard_map/ppermute | solution.py:25
  90.9 3.6 %collective-permute-start.27 = (f32[8,128]{1,0:T(8,128)S(1)}, f32[8,128]{1,0:T(8,128)S(1)}, u32[]{:S(2)}, u32[]{:S(2)}) collective-permute-start(f32[8,128]{1,0:T(8,128)S(1)} %add.45), channel_id=1, source_target_pairs={{0,16},{1,17},{2,18},{3,19},{4,20},{5,21},{6,22},{7,23},{8,24},{9,... | collective-permute-start | bytes 12296 | tf_op jit(solution)/shard_map/ppermute | solution.py:25
  94.6 3.7 %collective-permute-start.28 = (f32[8,128]{1,0:T(8,128)S(1)}, f32[8,128]{1,0:T(8,128)S(1)}, u32[]{:S(2)}, u32[]{:S(2)}) collective-permute-start(f32[8,128]{1,0:T(8,128)S(1)} %add.46), channel_id=1, source_target_pairs={{0,48},{1,49},{2,50},{3,51},{4,52},{5,53},{6,54},{7,55},{8,56},{9,... | collective-permute-start | bytes 12296 | tf_op jit(solution)/shard_map/ppermute | solution.py:25
  98.3 4.7 %copy-start.1 = (f32[128,1152]{1,0:T(8,128)S(1)}, f32[128,1152]{1,0:T(8,128)}, u32[]{:S(2)}) copy-start(f32[128,1152]{1,0:T(8,128)} %refs_1_.1) | copy-start | bytes 1769476
  98.3 4.7 %copy-start.3 = (f32[128,1152]{1,0:T(8,128)S(1)}, f32[128,1152]{1,0:T(8,128)}, u32[]{:S(2)}) copy-start(f32[128,1152]{1,0:T(8,128)} %refs_2_.1) | copy-start | bytes 1769476
  100.8 2.1 %collective-permute-start.29 = (f32[136,1152]{1,0:T(8,128)S(1)}, f32[136,1152]{1,0:T(8,128)S(1)}, u32[]{:S(2)}, u32[]{:S(2)}) collective-permute-start(f32[136,1152]{1,0:T(8,128)S(1)} %get-tuple-element.119), channel_id=1, source_target_pairs={{0,8},{1,9},{2,10},{3,11},{4,12},{5,13},{6,14},{7,15},{8,0},{9,1},... | collective-permute-start | bytes 1880072 | tf_op jit(solution)/shard_map/ppermute | solution.py:25

commit v9 on v5

--- a/solution.py
+++ b/solution.py
@@ -286,13 +286,13 @@
 CHUNK = 64
 
 
-def each_chunk(rows, work):
+def each_chunk(rows, work, chunk=CHUNK):
     def step(i, carry):
-        first = pl.multiple_of(i * CHUNK, CHUNK)
-        work(lambda start=0: pl.ds(start + first, CHUNK))
+        first = pl.multiple_of(i * chunk, chunk)
+        work(lambda start=0: pl.ds(start + first, chunk))
         return carry
 
-    lax.fori_loop(0, rows // CHUNK, step, 0)
+    lax.fori_loop(0, rows // chunk, step, 0)
 
 
 def opposite_kernel(core_ref, txt_ref, img_ref, received_ref, a_ref, b_ref):
@@ -380,7 +380,7 @@
         value = base_ref[at(k * pair)] + decode(received_ref[at()], TWO_CHIPS)
         out_ref[at()] = encode(value, FOUR_CHIPS)
 
-    each_chunk(pair, rows)
+    each_chunk(pair, rows, 2 * CHUNK)
 
 
 def gather_sums_kernel(core_ref, base_ref, a_ref, b_ref, x_ref, loss_ref, keep_ref, give_ref):

time: 102 us -> 101 us (level)
  no operation moved by 1% of the time
where the time goes in v9:
time: 101 us
  starting transfers between devices  38.3 us (38%)
  waiting for transfers between devices  27.2 us (27%)
  Pallas kernels  22.9 us (23%)
  matrix products  8.31 us (8%)
  between operations  2.28 us (2%)
  local copies, waits for them, and re-layouts  2.14 us (2%)
    ppermute x30, starting transfers between devices, exchange(): return lax.ppermute(x, AXES, pairs)  38.3 us
    ppermute x30, waiting for transfers between devices, exchange(): return lax.ppermute(x, AXES, pairs)  27.2 us
    pallas_call x4, Pallas kernels, tile_call(): pl.pallas_call(kernel, out_shape=outs, in_specs=[SMEM] + [VMEM] * (len(sc...  13.7 us
    dot_general x6, matrix products, transposed_product(): lax.dot_general(weights, img, (((0,), (0,)), ((), ())), preferred_element...  8.31 us
    pallas_call x9, Pallas kernels, small_call(): pl.pallas_call(kernel, out_shape=outs, in_specs=[SMEM] + [VMEM] * len(arr...  8.29 us
    unnamed x8, local copies, waits for them, and re-layouts  2.13 us
  transfers between devices with their start and end apart: 30, of which 16 were waited for; matrix products, arithmetic and copies ran while one was open for 8% of the time, Pallas kernels for 13%

profile of v9, /device:TPU:1, one launch (start us, length us, event | category | flops | bytes accessed | tf_op | source)
XLA Modules:
  0.0 101.2 jit_solution(14381308240759762044)
XLA Ops:
  0.6 1.1 %copy-done = f32[128,1152]{1,0:T(8,128)S(1)} copy-done((f32[128,1152]{1,0:T(8,128)S(1)}, f32[128,1152]{1,0:T(8,128)}, u32[]{:S(2)}) %copy-start) | copy-done | bytes 589848
  1.7 1.1 %copy-done.2 = f32[128,1152]{1,0:T(8,128)S(1)} copy-done((f32[128,1152]{1,0:T(8,128)S(1)}, f32[128,1152]{1,0:T(8,128)}, u32[]{:S(2)}) %copy-start.2) | copy-done | bytes 589848
  3.3 1.5 %collective-permute-start = (bf16[128,1152]{1,0:T(8,128)(2,1)S(1)}, bf16[128,1152]{1,0:T(8,128)(2,1)S(1)}, u32[]{:S(2)}, u32[]{:S(2)}) collective-permute-start(bf16[128,1152]{1,0:T(8,128)(2,1)S(1)} %get-tuple-element.69), channel_id=1, source_target_pairs={{0,8},{1,9},{2,10},{3,11},{4,12},{5,13},{6,14},{7,15},{8,0},{9,1},... | collective-permute-start | bytes 884744 | tf_op jit(solution)/shard_map/ppermute | solution.py:25
  4.8 1.2 %collective-permute-done.refs_1_ = bf16[128,1152]{1,0:T(8,128)(2,1)S(1)} collective-permute-done((bf16[128,1152]{1,0:T(8,128)(2,1)S(1)}, bf16[128,1152]{1,0:T(8,128)(2,1)S(1)}, u32[]{:S(2)}, u32[]{:S(2)}) %collective-permute-start) | collective-permute-done | bytes 294944 | tf_op jit(solution)/shard_map/ppermute | solution.py:25
  6.1 1.8 %collective-permute-start.5 = (bf16[256,1152]{1,0:T(8,128)(2,1)S(1)}, bf16[256,1152]{1,0:T(8,128)(2,1)S(1)}, u32[]{:S(2)}, u32[]{:S(2)}) collective-permute-start(bf16[256,1152]{1,0:T(8,128)(2,1)S(1)} %pack.4.refs_0_), channel_id=1, source_target_pairs={{0,2},{1,3},{2,0},{3,1},{4,6},{5,7},{6,4},{7,5},{8,24},{9,25},{10,... | collective-permute-start | bytes 1769480 | tf_op jit(solution)/shard_map/ppermute | solution.py:25
  7.9 2.5 %collective-permute-start.3 = (bf16[256,1152]{1,0:T(8,128)(2,1)S(1)}, bf16[256,1152]{1,0:T(8,128)(2,1)S(1)}, u32[]{:S(2)}, u32[]{:S(2)}) collective-permute-start(bf16[256,1152]{1,0:T(8,128)(2,1)S(1)} %pack.4.refs_0_), channel_id=1, source_target_pairs={{0,1},{1,0},{2,3},{3,2},{4,5},{5,4},{6,7},{7,6},{8,73},{9,72},{10,... | collective-permute-start | bytes 1769480 | tf_op jit(solution)/shard_map/ppermute | solution.py:25
  10.3 2.2 %collective-permute-start.1 = (bf16[256,1152]{1,0:T(8,128)(2,1)S(1)}, bf16[256,1152]{1,0:T(8,128)(2,1)S(1)}, u32[]{:S(2)}, u32[]{:S(2)}) collective-permute-start(bf16[256,1152]{1,0:T(8,128)(2,1)S(1)} %pack.4.refs_0_), channel_id=1, source_target_pairs={{0,6},{1,7},{2,4},{3,5},{4,2},{5,3},{6,0},{7,1},{8,56},{9,57},{10,... | collective-permute-start | bytes 1769480 | tf_op jit(solution)/shard_map/ppermute | solution.py:25
  12.6 2.8 %collective-permute-done.5.refs_2_ = bf16[256,1152]{1,0:T(8,128)(2,1)S(1)} collective-permute-done((bf16[256,1152]{1,0:T(8,128)(2,1)S(1)}, bf16[256,1152]{1,0:T(8,128)(2,1)S(1)}, u32[]{:S(2)}, u32[]{:S(2)}) %collective-permute-start.5) | collective-permute-done | bytes 589856 | tf_op jit(solution)/shard_map/ppermute | solution.py:25
  15.4 2.7 %collective-permute-done.3.refs_1_ = bf16[256,1152]{1,0:T(8,128)(2,1)S(1)} collective-permute-done((bf16[256,1152]{1,0:T(8,128)(2,1)S(1)}, bf16[256,1152]{1,0:T(8,128)(2,1)S(1)}, u32[]{:S(2)}, u32[]{:S(2)}) %collective-permute-start.3) | collective-permute-done | bytes 589856 | tf_op jit(solution)/shard_map/ppermute | solution.py:25
  18.1 2.3 %collective-permute-done.1.refs_3_ = bf16[256,1152]{1,0:T(8,128)(2,1)S(1)} collective-permute-done((bf16[256,1152]{1,0:T(8,128)(2,1)S(1)}, bf16[256,1152]{1,0:T(8,128)(2,1)S(1)}, u32[]{:S(2)}, u32[]{:S(2)}) %collective-permute-start.1) | collective-permute-done | bytes 589856 | tf_op jit(solution)/shard_map/ppermute | solution.py:25
  21.0 1.8 %collective-permute-start.6 = (bf16[256,1152]{1,0:T(8,128)(2,1)S(1)}, bf16[256,1152]{1,0:T(8,128)(2,1)S(1)}, u32[]{:S(2)}, u32[]{:S(2)}) collective-permute-start(bf16[256,1152]{1,0:T(8,128)(2,1)S(1)} %collective-permute-done.5.refs_2_), channel_id=1, source_target_pairs={{0,1},{1,0},{2,3},{3,2},{4,5},{5,4},{6,7},{7,6},{8,73},{9,72},{10,... | collective-permute-start | bytes 1769480 | tf_op jit(solution)/shard_map/ppermute | solution.py:25
  22.8 3.8 %collective-permute-start.4 = (bf16[256,1152]{1,0:T(8,128)(2,1)S(1)}, bf16[256,1152]{1,0:T(8,128)(2,1)S(1)}, u32[]{:S(2)}, u32[]{:S(2)}) collective-permute-start(bf16[256,1152]{1,0:T(8,128)(2,1)S(1)} %collective-permute-done.3.refs_1_), channel_id=1, source_target_pairs={{0,6},{1,7},{2,4},{3,5},{4,2},{5,3},{6,0},{7,1},{8,56},{9,57},{10,... | collective-permute-start | bytes 1769480 | tf_op jit(solution)/shard_map/ppermute | solution.py:25
  27.9 3.5 %tile_near.1 = (bf16[512,1152]{1,0:T(8,128)(2,1)S(1)}, bf16[1024,1152]{1,0:T(8,128)(2,1)S(1)}, bf16[512,1024]{1,0:T(8,128)(2,1)S(1)}, f32[512,1152]{1,0:T(8,128)S(1)}, f32[8,128]{1,0:T(8,128)S(1)}) custom-call(s32[1]{0:T(128)} %bitcast.core_ref.refs_0_, f32[8,128]{1,0:T(8,128)S(1)} %broadcast_in_dim.15.sharp_ref, f32[8,128]{1,0:T(8,128)S(1)} %broadcast_in_dim.17.bias_ref, ...), custom_call_target="tpu_custom_call" | custom-call | flops 2415919104 | bytes 4718592 | tf_op jit(solution)/shard_map/tile_near/pallas_call | solution.py:258
  31.4 2.4 %collective-permute-done.4.refs_0_.refs_2_ = bf16[256,1152]{1,0:T(8,128)(2,1)S(1)} collective-permute-done((bf16[256,1152]{1,0:T(8,128)(2,1)S(1)}, bf16[256,1152]{1,0:T(8,128)(2,1)S(1)}, u32[]{:S(2)}, u32[]{:S(2)}) %collective-permute-start.4) | collective-permute-done | bytes 589856 | tf_op jit(solution)/shard_map/ppermute | solution.py:25
  33.9 1.5 %collective-permute-done.2.refs_0_ = bf16[256,1152]{1,0:T(8,128)(2,1)S(1)} collective-permute-done((bf16[256,1152]{1,0:T(8,128)(2,1)S(1)}, bf16[256,1152]{1,0:T(8,128)(2,1)S(1)}, u32[]{:S(2)}, u32[]{:S(2)}) %collective-permute-start.2) | collective-permute-done | bytes 589856 | tf_op jit(solution)/shard_map/ppermute | solution.py:25
  35.6 2.2 %collective-permute-start.9 = (bf16[128,1152]{1,0:T(8,128)(2,1)S(1)}, bf16[128,1152]{1,0:T(8,128)(2,1)S(1)}, u32[]{:S(2)}, u32[]{:S(2)}) collective-permute-start(bf16[128,1152]{1,0:T(8,128)(2,1)S(1)} %half_of.3), channel_id=1, source_target_pairs={{0,6},{1,7},{2,4},{3,5},{4,2},{5,3},{6,0},{7,1},{8,56},{9,57},{10,... | collective-permute-start | bytes 884744 | tf_op jit(solution)/shard_map/ppermute | solution.py:25
  37.8 1.4 %collective-permute-done.10.received_ref.far_received_ref = bf16[768,1152]{1,0:T(8,128)(2,1)S(1)} collective-permute-done((bf16[768,1152]{1,0:T(8,128)(2,1)S(1)}, bf16[768,1152]{1,0:T(8,128)(2,1)S(1)}, u32[]{:S(2)}, u32[]{:S(2)}) %collective-permute-start.10) | collective-permute-done | bytes 1769504 | tf_op jit(solution)/shard_map/ppermute | solution.py:25
  39.2 3.7 %tile_far.1 = (bf16[768,1152]{1,0:T(8,128)(2,1)S(1)}, bf16[768,1152]{1,0:T(8,128)(2,1)S(1)}, bf16[768,768]{1,0:T(8,128)(2,1)S(1)}, f32[768,1152]{1,0:T(8,128)S(1)}, f32[8,128]{1,0:T(8,128)S(1)}) custom-call(s32[1]{0:T(128)} %bitcast.core_ref.refs_0_, f32[8,128]{1,0:T(8,128)S(1)} %broadcast_in_dim.15.sharp_ref, f32[8,128]{1,0:T(8,128)S(1)} %broadcast_in_dim.17.bias_ref, ...), custom_call_target="tpu_custom_call" | custom-call | flops 2717908992 | bytes 5898240 | tf_op jit(solution)/shard_map/tile_far/pallas_call | solution.py:258
  42.9 0.8 collective-permute-done.8.refs_0_
  43.7 1.7 %collective-permute-start.11 = (bf16[256,1152]{1,0:T(8,128)(2,1)S(1)}, bf16[256,1152]{1,0:T(8,128)(2,1)S(1)}, u32[]{:S(2)}, u32[]{:S(2)}) collective-permute-start(bf16[256,1152]{1,0:T(8,128)(2,1)S(1)} %pack.7.last_ref), channel_id=1, source_target_pairs={{0,8},{1,9},{2,10},{3,11},{4,12},{5,13},{6,14},{7,15},{8,0},{9,1},... | collective-permute-start | bytes 1769480 | tf_op jit(solution)/shard_map/ppermute | solution.py:25
  45.4 1.9 %tile_middle.1 = (bf16[768,1024]{1,0:T(8,128)(2,1)S(1)}, f32[256,1152]{1,0:T(8,128)S(1)}, f32[8,128]{1,0:T(8,128)S(1)}) custom-call(s32[1]{0:T(128)} %bitcast.core_ref.refs_0_, f32[8,128]{1,0:T(8,128)S(1)} %broadcast_in_dim.15.sharp_ref, f32[8,128]{1,0:T(8,128)S(1)} %broadcast_in_dim.17.bias_ref, bf16[768,1152]{1,0:T(8,128)(2,1)S(1)} %get-tuple-element.81.img_ref, ...), custom_call_target="tpu_custom_call" | custom-call | flops 1207959552 | bytes 6946816 | tf_op jit(solution)/shard_map/tile_middle/pallas_call | solution.py:258
  47.3 4.6 %tile_last.1 = (bf16[768,256]{1,0:T(8,128)(2,1)S(1)}, f32[768,1152]{1,0:T(8,128)S(1)}, bf16[256,1152]{1,0:T(8,128)(2,1)S(1)}, bf16[256,1024]{1,0:T(8,128)(2,1)S(...) custom-call(s32[1]{0:T(128)} %bitcast.core_ref.refs_0_, ...), custom_call_target="tpu_custom_call" | custom-call | flops 3321888768 | bytes 12976128 | tf_op jit(solution)/shard_map/tile_last/pallas_call | solution.py:258
  52.7 0.9 fusion.5
  54.8 2.5 %fusion.3 = (bf16[768,1152]{1,0:T(8,128)(2,1)S(1)}, f32[768,1152]{1,0:T(8,128)S(1)}) fusion(f32[768,1152]{1,0:T(8,128)S(1)} %get-tuple-element.93.img_ref, pred[]{:T(512)S(6)} %eq.3, f32[768,1152]{1,0:T(8,128)S(1)} %fusion.7, bf16[768,768]{1,0:T(8,128)(2,1)S(1)} %get-tuple-element.94, bf16[768,1152]{1,0:T(8,128)(2,1)S(1)} %get-tuple-element.81.img_ref), kind=kOutput, calls=%fused_computation.9 | convolution fusion | flops 1367801856 | bytes 15335425 | tf_op jit(solution)/shard_map/dot_general | solution.py:423
  58.2 1.3 %collective-permute-start.17 = (f32[8,128]{1,0:T(8,128)S(1)}, f32[8,128]{1,0:T(8,128)S(1)}, u32[]{:S(2)}, u32[]{:S(2)}) collective-permute-start(f32[8,128]{1,0:T(8,128)S(1)} %add.41), channel_id=1, source_target_pairs={{0,65},{1,64},{2,67},{3,66},{4,69},{5,68},{6,71},{7,70},{8,73},{9,... | collective-permute-start | bytes 12296 | tf_op jit(solution)/shard_map/ppermute | solution.py:25
  59.6 2.2 %collective-permute-start.16 = (bf16[128,1152]{1,0:T(8,128)(2,1)S(1)}, bf16[128,1152]{1,0:T(8,128)(2,1)S(1)}, u32[]{:S(2)}, u32[]{:S(2)}) collective-permute-start(bf16[128,1152]{1,0:T(8,128)(2,1)S(1)} %get-tuple-element.110), channel_id=1, source_target_pairs={{0,6},{1,7},{2,4},{3,5},{4,2},{5,3},{6,0},{7,1},{8,56},{9,57},{10,... | collective-permute-start | bytes 884744 | tf_op jit(solution)/shard_map/ppermute | solution.py:25
  61.8 0.9 fusion.8
  62.8 3.0 %fusion.1 = (bf16[1024,1152]{1,0:T(8,128)(2,1)S(1)}, f32[1024,1152]{1,0:T(8,128)S(1)}) fusion(f32[1024,1152]{1,0:T(8,128)S(1)} %fusion.8, bf16[768,1024]{1,0:T(8,128)(2,1)S(1)} %get-tuple-element.106, bf16[768,1152]{1,0:T(8,128)(2,1)S(1)} %get-tuple-element.81.img_ref), kind=kOutput, calls=%fused_computation.5 | convolution fusion | flops 1822556160 | bytes 15138816 | tf_op jit(solution)/shard_map/dot_general | solution.py:423
  66.7 1.2 %far.1 = (bf16[256,1152]{1,0:T(8,128)(2,1)S(1)}, bf16[256,1152]{1,0:T(8,128)(2,1)S(1)}) custom-call(s32[1]{0:T(128)} %bitcast.core_ref.refs_0_, f32[768,1152]{1,0:T(8,128)S(1)} %get-tuple-element.134.txt_ref, bf16[768,1152]{1,0:T(8,128)(2,1)S(1)} %collective-permute-done.14.received_ref.txt_received_ref.img_received_ref, ...), custom_call_target="tpu_custom_call" | custom-call | tf_op jit(solution)/shard_map/far/pallas_call | solution.py:276
  67.9 2.0 %collective-permute-start.19 = (bf16[1024,1152]{1,0:T(8,128)(2,1)S(1)}, bf16[1024,1152]{1,0:T(8,128)(2,1)S(1)}, u32[]{:S(2)}, u32[]{:S(2)}) collective-permute-start(bf16[1024,1152]{1,0:T(8,128)(2,1)S(1)} %get-tuple-element.117), channel_id=1, source_target_pairs={{0,8},{1,9},{2,10},{3,11},{4,12},{5,13},{6,14},{7,15},{8,0},{9,1},... | collective-permute-start | bytes 7077896 | tf_op jit(solution)/shard_map/ppermute | solution.py:25
  69.8 1.3 %collective-permute-start.21 = (bf16[256,1152]{1,0:T(8,128)(2,1)S(1)}, bf16[256,1152]{1,0:T(8,128)(2,1)S(1)}, u32[]{:S(2)}, u32[]{:S(2)}) collective-permute-start(bf16[256,1152]{1,0:T(8,128)(2,1)S(1)} %get-tuple-element.122), channel_id=1, source_target_pairs={{0,1},{1,0},{2,3},{3,2},{4,5},{5,4},{6,7},{7,6},{8,73},{9,72},{10,... | collective-permute-start | bytes 1769480 | tf_op jit(solution)/shard_map/ppermute | solution.py:25
  71.2 2.0 %collective-permute-start.25 = (bf16[256,1152]{1,0:T(8,128)(2,1)S(1)}, bf16[256,1152]{1,0:T(8,128)(2,1)S(1)}, u32[]{:S(2)}, u32[]{:S(2)}) collective-permute-start(bf16[256,1152]{1,0:T(8,128)(2,1)S(1)} %get-tuple-element.124), channel_id=1, source_target_pairs={{0,6},{1,7},{2,4},{3,5},{4,2},{5,3},{6,0},{7,1},{8,56},{9,57},{10,... | collective-permute-start | bytes 1769480 | tf_op jit(solution)/shard_map/ppermute | solution.py:25
  73.2 0.8 collective-permute-done.19.received_ref
  74.0 1.0 base.1.refs_1_.base_ref
  75.0 1.4 %collective-permute-start.20 = (f32[8,128]{1,0:T(8,128)S(1)}, f32[8,128]{1,0:T(8,128)S(1)}, u32[]{:S(2)}, u32[]{:S(2)}) collective-permute-start(f32[8,128]{1,0:T(8,128)S(1)} %add.44), channel_id=1, source_target_pairs={{0,6},{1,7},{2,4},{3,5},{4,2},{5,3},{6,0},{7,1},{8,14},{9,15},{10,... | collective-permute-start | bytes 12296 | tf_op jit(solution)/shard_map/ppermute | solution.py:25
  76.4 2.8 %collective-permute-done.20 = f32[8,128]{1,0:T(8,128)S(1)} collective-permute-done((f32[8,128]{1,0:T(8,128)S(1)}, f32[8,128]{1,0:T(8,128)S(1)}, u32[]{:S(2)}, u32[]{:S(2)}) %collective-permute-start.20) | collective-permute-done | bytes 4128 | tf_op jit(solution)/shard_map/ppermute | solution.py:25
  79.2 0.9 collective-permute-done.21.refs_2_
  82.0 2.3 %collective-permute-start.24 = (bf16[256,1152]{1,0:T(8,128)(2,1)S(1)}, bf16[256,1152]{1,0:T(8,128)(2,1)S(1)}, u32[]{:S(2)}, u32[]{:S(2)}) collective-permute-start(bf16[256,1152]{1,0:T(8,128)(2,1)S(1)} %near.4), channel_id=1, source_target_pairs={{0,6},{1,7},{2,4},{3,5},{4,2},{5,3},{6,0},{7,1},{8,56},{9,57},{10,... | collective-permute-start | bytes 1769480 | tf_op jit(solution)/shard_map/ppermute | solution.py:25
  85.0 0.9 collective-permute-start.26
  85.9 0.8 collective-permute-start.27
  86.7 3.3 %collective-permute-done.27 = f32[8,128]{1,0:T(8,128)S(1)} collective-permute-done((f32[8,128]{1,0:T(8,128)S(1)}, f32[8,128]{1,0:T(8,128)S(1)}, u32[]{:S(2)}, u32[]{:S(2)}) %collective-permute-start.27) | collective-permute-done | bytes 4128 | tf_op jit(solution)/shard_map/ppermute | solution.py:25
  90.0 2.4 %collective-permute-start.28 = (f32[8,128]{1,0:T(8,128)S(1)}, f32[8,128]{1,0:T(8,128)S(1)}, u32[]{:S(2)}, u32[]{:S(2)}) collective-permute-start(f32[8,128]{1,0:T(8,128)S(1)} %add.46), channel_id=1, source_target_pairs={{0,48},{1,49},{2,50},{3,51},{4,52},{5,53},{6,54},{7,55},{8,56},{9,... | collective-permute-start | bytes 12296 | tf_op jit(solution)/shard_map/ppermute | solution.py:25
  92.4 1.5 %collective-permute-done.28 = f32[8,128]{1,0:T(8,128)S(1)} collective-permute-done((f32[8,128]{1,0:T(8,128)S(1)}, f32[8,128]{1,0:T(8,128)S(1)}, u32[]{:S(2)}, u32[]{:S(2)}) %collective-permute-start.28) | collective-permute-done | bytes 4128 | tf_op jit(solution)/shard_map/ppermute | solution.py:25
  94.0 1.1 %collective-permute-done.26.x_ref = bf16[256,1152]{1,0:T(8,128)(2,1)S(1)} collective-permute-done((bf16[256,1152]{1,0:T(8,128)(2,1)S(1)}, bf16[256,1152]{1,0:T(8,128)(2,1)S(1)}, u32[]{:S(2)}, u32[]{:S(2)}) %collective-permute-start.26) | collective-permute-done | bytes 589856 | tf_op jit(solution)/shard_map/ppermute | solution.py:25
  95.1 1.3 %gather_sums.1 = (f32[128,1152]{1,0:T(8,128)S(1)}, f32[136,1152]{1,0:T(8,128)S(1)}) custom-call(s32[1]{0:T(128)} %bitcast.core_ref.refs_0_, f32[1024,1152]{1,0:T(8,128)S(1)} %base.1.refs_1_.base_ref, bf16[256,1152]{1,0:T(8,128)(2,1)S(1)} %collective-permute-done.22.a_ref, bf16[256,1152]{1,0:T(8,128)(2,1)S(1)} %collective-permute-done.24.b_ref, ...), custom_call_target="tpu_custom_call" | custom-call | tf_op jit(solution)/shard_map/gather_sums/pallas_call | solution.py:276
  96.3 1.5 %collective-permute-start.29 = (f32[136,1152]{1,0:T(8,128)S(1)}, f32[136,1152]{1,0:T(8,128)S(1)}, u32[]{:S(2)}, u32[]{:S(2)}) collective-permute-start(f32[136,1152]{1,0:T(8,128)S(1)} %get-tuple-element.127), channel_id=1, source_target_pairs={{0,8},{1,9},{2,10},{3,11},{4,12},{5,13},{6,14},{7,15},{8,0},{9,1},... | collective-permute-start | bytes 1880072 | tf_op jit(solution)/shard_map/ppermute | solution.py:25
  97.8 1.7 %collective-permute-done.29.refs_4_ = f32[136,1152]{1,0:T(8,128)S(1)} collective-permute-done((f32[136,1152]{1,0:T(8,128)S(1)}, f32[136,1152]{1,0:T(8,128)S(1)}, u32[]{:S(2)}, u32[]{:S(2)}) %collective-permute-start.29) | collective-permute-done | bytes 626720 | tf_op jit(solution)/shard_map/ppermute | solution.py:25
  99.5 1.7 %finish.1 = (f32[1,1]{1,0:T(1,128)}, f32[128,1152]{1,0:T(8,128)}, f32[128,1152]{1,0:T(8,128)}) custom-call(s32[1]{0:T(128)} %bitcast.core_ref.refs_0_, f32[128,1152]{1,0:T(8,128)S(1)} %copy-done.1, f32[128,1152]{1,0:T(8,128)S(1)} %copy-done.3, f32[128,1152]{1,0:T(8,128)S(1)} %get-tuple-element.126.refs_3_, f32[136,1152]{1,0:T(8,128)S(1)} %collective-permute-done.29.refs_4_, ...), custom_call_target="tpu_custom_call" | custom-call | tf_op jit(solution)/shard_map/finish/pallas_call | solution.py:276
  (55 shorter events, 8.1 us)
Async XLA Ops:
  0.6 1.1 %copy-start = (f32[128,1152]{1,0:T(8,128)S(1)}, f32[128,1152]{1,0:T(8,128)}, u32[]{:S(2)}) copy-start(f32[128,1152]{1,0:T(8,128)} %refs_1_.1) | copy-start | bytes 1769476
  1.7 1.1 %copy-start.2 = (f32[128,1152]{1,0:T(8,128)S(1)}, f32[128,1152]{1,0:T(8,128)}, u32[]{:S(2)}) copy-start(f32[128,1152]{1,0:T(8,128)} %refs_2_.1) | copy-start | bytes 1769476
  3.3 2.7 %collective-permute-start = (bf16[128,1152]{1,0:T(8,128)(2,1)S(1)}, bf16[128,1152]{1,0:T(8,128)(2,1)S(1)}, u32[]{:S(2)}, u32[]{:S(2)}) collective-permute-start(bf16[128,1152]{1,0:T(8,128)(2,1)S(1)} %get-tuple-element.69), channel_id=1, source_target_pairs={{0,8},{1,9},{2,10},{3,11},{4,12},{5,13},{6,14},{7,15},{8,0},{9,1},... | collective-permute-start | bytes 884744 | tf_op jit(solution)/shard_map/ppermute | solution.py:25
  6.1 9.4 %collective-permute-start.5 = (bf16[256,1152]{1,0:T(8,128)(2,1)S(1)}, bf16[256,1152]{1,0:T(8,128)(2,1)S(1)}, u32[]{:S(2)}, u32[]{:S(2)}) collective-permute-start(bf16[256,1152]{1,0:T(8,128)(2,1)S(1)} %pack.4.refs_0_), channel_id=1, source_target_pairs={{0,2},{1,3},{2,0},{3,1},{4,6},{5,7},{6,4},{7,5},{8,24},{9,25},{10,... | collective-permute-start | bytes 1769480 | tf_op jit(solution)/shard_map/ppermute | solution.py:25
  7.9 10.2 %collective-permute-start.3 = (bf16[256,1152]{1,0:T(8,128)(2,1)S(1)}, bf16[256,1152]{1,0:T(8,128)(2,1)S(1)}, u32[]{:S(2)}, u32[]{:S(2)}) collective-permute-start(bf16[256,1152]{1,0:T(8,128)(2,1)S(1)} %pack.4.refs_0_), channel_id=1, source_target_pairs={{0,1},{1,0},{2,3},{3,2},{4,5},{5,4},{6,7},{7,6},{8,73},{9,72},{10,... | collective-permute-start | bytes 1769480 | tf_op jit(solution)/shard_map/ppermute | solution.py:25
  10.3 10.0 %collective-permute-start.1 = (bf16[256,1152]{1,0:T(8,128)(2,1)S(1)}, bf16[256,1152]{1,0:T(8,128)(2,1)S(1)}, u32[]{:S(2)}, u32[]{:S(2)}) collective-permute-start(bf16[256,1152]{1,0:T(8,128)(2,1)S(1)} %pack.4.refs_0_), channel_id=1, source_target_pairs={{0,6},{1,7},{2,4},{3,5},{4,2},{5,3},{6,0},{7,1},{8,56},{9,57},{10,... | collective-permute-start | bytes 1769480 | tf_op jit(solution)/shard_map/ppermute | solution.py:25
  20.5 7.4 %collective-permute-start.7 = (bf16[1024,1152]{1,0:T(8,128)(2,1)S(1)}, bf16[1024,1152]{1,0:T(8,128)(2,1)S(1)}, u32[]{:S(2)}, u32[]{:S(2)}) collective-permute-start(bf16[1024,1152]{1,0:T(8,128)(2,1)S(1)} %pack.5.near_ref), channel_id=1, source_target_pairs={{0,8},{1,9},{2,10},{3,11},{4,12},{5,13},{6,14},{7,15},{8,0},{9,1},... | collective-permute-start | bytes 7077896 | tf_op jit(solution)/shard_map/ppermute | solution.py:25
  21.0 10.4 %collective-permute-start.6 = (bf16[256,1152]{1,0:T(8,128)(2,1)S(1)}, bf16[256,1152]{1,0:T(8,128)(2,1)S(1)}, u32[]{:S(2)}, u32[]{:S(2)}) collective-permute-start(bf16[256,1152]{1,0:T(8,128)(2,1)S(1)} %collective-permute-done.5.refs_2_), channel_id=1, source_target_pairs={{0,1},{1,0},{2,3},{3,2},{4,5},{5,4},{6,7},{7,6},{8,73},{9,72},{10,... | collective-permute-start | bytes 1769480 | tf_op jit(solution)/shard_map/ppermute | solution.py:25
  22.8 11.0 %collective-permute-start.4 = (bf16[256,1152]{1,0:T(8,128)(2,1)S(1)}, bf16[256,1152]{1,0:T(8,128)(2,1)S(1)}, u32[]{:S(2)}, u32[]{:S(2)}) collective-permute-start(bf16[256,1152]{1,0:T(8,128)(2,1)S(1)} %collective-permute-done.3.refs_1_), channel_id=1, source_target_pairs={{0,6},{1,7},{2,4},{3,5},{4,2},{5,3},{6,0},{7,1},{8,56},{9,57},{10,... | collective-permute-start | bytes 1769480 | tf_op jit(solution)/shard_map/ppermute | solution.py:25
  26.6 8.7 %collective-permute-start.2 = (bf16[256,1152]{1,0:T(8,128)(2,1)S(1)}, bf16[256,1152]{1,0:T(8,128)(2,1)S(1)}, u32[]{:S(2)}, u32[]{:S(2)}) collective-permute-start(bf16[256,1152]{1,0:T(8,128)(2,1)S(1)} %collective-permute-done.1.refs_3_), channel_id=1, source_target_pairs={{0,2},{1,3},{2,0},{3,1},{4,6},{5,7},{6,4},{7,5},{8,24},{9,25},{10,... | collective-permute-start | bytes 1769480 | tf_op jit(solution)/shard_map/ppermute | solution.py:25
  35.5 3.8 %collective-permute-start.10 = (bf16[768,1152]{1,0:T(8,128)(2,1)S(1)}, bf16[768,1152]{1,0:T(8,128)(2,1)S(1)}, u32[]{:S(2)}, u32[]{:S(2)}) collective-permute-start(bf16[768,1152]{1,0:T(8,128)(2,1)S(1)} %pack.6.far_ref), channel_id=1, source_target_pairs={{0,8},{1,9},{2,10},{3,11},{4,12},{5,13},{6,14},{7,15},{8,0},{9,1},... | collective-permute-start | bytes 5308424 | tf_op jit(solution)/shard_map/ppermute | solution.py:25
  35.6 7.3 %collective-permute-start.9 = (bf16[128,1152]{1,0:T(8,128)(2,1)S(1)}, bf16[128,1152]{1,0:T(8,128)(2,1)S(1)}, u32[]{:S(2)}, u32[]{:S(2)}) collective-permute-start(bf16[128,1152]{1,0:T(8,128)(2,1)S(1)} %half_of.3), channel_id=1, source_target_pairs={{0,6},{1,7},{2,4},{3,5},{4,2},{5,3},{6,0},{7,1},{8,56},{9,57},{10,... | collective-permute-start | bytes 884744 | tf_op jit(solution)/shard_map/ppermute | solution.py:25
  37.8 5.9 %collective-permute-start.8 = (bf16[128,1152]{1,0:T(8,128)(2,1)S(1)}, bf16[128,1152]{1,0:T(8,128)(2,1)S(1)}, u32[]{:S(2)}, u32[]{:S(2)}) collective-permute-start(bf16[128,1152]{1,0:T(8,128)(2,1)S(1)} %half_of.2), channel_id=1, source_target_pairs={{0,2},{1,3},{2,0},{3,1},{4,6},{5,7},{6,4},{7,5},{8,24},{9,25},{10,... | collective-permute-start | bytes 884744 | tf_op jit(solution)/shard_map/ppermute | solution.py:25
  43.7 3.5 %collective-permute-start.11 = (bf16[256,1152]{1,0:T(8,128)(2,1)S(1)}, bf16[256,1152]{1,0:T(8,128)(2,1)S(1)}, u32[]{:S(2)}, u32[]{:S(2)}) collective-permute-start(bf16[256,1152]{1,0:T(8,128)(2,1)S(1)} %pack.7.last_ref), channel_id=1, source_target_pairs={{0,8},{1,9},{2,10},{3,11},{4,12},{5,13},{6,14},{7,15},{8,0},{9,1},... | collective-permute-start | bytes 1769480 | tf_op jit(solution)/shard_map/ppermute | solution.py:25
  51.9 5.4 %collective-permute-start.13 = (f32[8,128]{1,0:T(8,128)S(1)}, f32[8,128]{1,0:T(8,128)S(1)}, u32[]{:S(2)}, u32[]{:S(2)}) collective-permute-start(f32[8,128]{1,0:T(8,128)S(1)} %add_add_fusion), channel_id=1, source_target_pairs={{0,1},{1,0},{2,3},{3,2},{4,5},{5,4},{6,7},{7,6},{8,9},{9,8},{10,11... | collective-permute-start | bytes 12296 | tf_op jit(solution)/shard_map/ppermute | solution.py:25
  53.6 3.7 %collective-permute-start.12 = (bf16[256,1152]{1,0:T(8,128)(2,1)S(1)}, bf16[256,1152]{1,0:T(8,128)(2,1)S(1)}, u32[]{:S(2)}, u32[]{:S(2)}) collective-permute-start(bf16[256,1152]{1,0:T(8,128)(2,1)S(1)} %get-tuple-element.92), channel_id=1, source_target_pairs={{0,8},{1,9},{2,10},{3,11},{4,12},{5,13},{6,14},{7,15},{8,0},{9,1},... | collective-permute-start | bytes 1769480 | tf_op jit(solution)/shard_map/ppermute | solution.py:25
  57.5 8.3 %collective-permute-start.14 = (bf16[768,1152]{1,0:T(8,128)(2,1)S(1)}, bf16[768,1152]{1,0:T(8,128)(2,1)S(1)}, u32[]{:S(2)}, u32[]{:S(2)}) collective-permute-start(bf16[768,1152]{1,0:T(8,128)(2,1)S(1)} %get-tuple-element.108), channel_id=1, source_target_pairs={{0,8},{1,9},{2,10},{3,11},{4,12},{5,13},{6,14},{7,15},{8,0},{9,1},... | collective-permute-start | bytes 5308424 | tf_op jit(solution)/shard_map/ppermute | solution.py:25
  58.2 4.4 %collective-permute-start.17 = (f32[8,128]{1,0:T(8,128)S(1)}, f32[8,128]{1,0:T(8,128)S(1)}, u32[]{:S(2)}, u32[]{:S(2)}) collective-permute-start(f32[8,128]{1,0:T(8,128)S(1)} %add.41), channel_id=1, source_target_pairs={{0,65},{1,64},{2,67},{3,66},{4,69},{5,68},{6,71},{7,70},{8,73},{9,... | collective-permute-start | bytes 12296 | tf_op jit(solution)/shard_map/ppermute | solution.py:25
  59.6 7.0 %collective-permute-start.15 = (bf16[128,1152]{1,0:T(8,128)(2,1)S(1)}, bf16[128,1152]{1,0:T(8,128)(2,1)S(1)}, u32[]{:S(2)}, u32[]{:S(2)}) collective-permute-start(bf16[128,1152]{1,0:T(8,128)(2,1)S(1)} %get-tuple-element.109), channel_id=1, source_target_pairs={{0,2},{1,3},{2,0},{3,1},{4,6},{5,7},{6,4},{7,5},{8,24},{9,25},{10,... | collective-permute-start | bytes 884744 | tf_op jit(solution)/shard_map/ppermute | solution.py:25
  59.6 7.1 %collective-permute-start.16 = (bf16[128,1152]{1,0:T(8,128)(2,1)S(1)}, bf16[128,1152]{1,0:T(8,128)(2,1)S(1)}, u32[]{:S(2)}, u32[]{:S(2)}) collective-permute-start(bf16[128,1152]{1,0:T(8,128)(2,1)S(1)} %get-tuple-element.110), channel_id=1, source_target_pairs={{0,6},{1,7},{2,4},{3,5},{4,2},{5,3},{6,0},{7,1},{8,56},{9,57},{10,... | collective-permute-start | bytes 884744 | tf_op jit(solution)/shard_map/ppermute | solution.py:25
  62.7 3.1 %collective-permute-start.18 = (f32[8,128]{1,0:T(8,128)S(1)}, f32[8,128]{1,0:T(8,128)S(1)}, u32[]{:S(2)}, u32[]{:S(2)}) collective-permute-start(f32[8,128]{1,0:T(8,128)S(1)} %add.43), channel_id=1, source_target_pairs={{0,2},{1,3},{2,0},{3,1},{4,6},{5,7},{6,4},{7,5},{8,10},{9,11},{10,... | collective-permute-start | bytes 12296 | tf_op jit(solution)/shard_map/ppermute | solution.py:25
  67.9 6.1 %collective-permute-start.19 = (bf16[1024,1152]{1,0:T(8,128)(2,1)S(1)}, bf16[1024,1152]{1,0:T(8,128)(2,1)S(1)}, u32[]{:S(2)}, u32[]{:S(2)}) collective-permute-start(bf16[1024,1152]{1,0:T(8,128)(2,1)S(1)} %get-tuple-element.117), channel_id=1, source_target_pairs={{0,8},{1,9},{2,10},{3,11},{4,12},{5,13},{6,14},{7,15},{8,0},{9,1},... | collective-permute-start | bytes 7077896 | tf_op jit(solution)/shard_map/ppermute | solution.py:25
  69.8 10.2 %collective-permute-start.21 = (bf16[256,1152]{1,0:T(8,128)(2,1)S(1)}, bf16[256,1152]{1,0:T(8,128)(2,1)S(1)}, u32[]{:S(2)}, u32[]{:S(2)}) collective-permute-start(bf16[256,1152]{1,0:T(8,128)(2,1)S(1)} %get-tuple-element.122), channel_id=1, source_target_pairs={{0,1},{1,0},{2,3},{3,2},{4,5},{5,4},{6,7},{7,6},{8,73},{9,72},{10,... | collective-permute-start | bytes 1769480 | tf_op jit(solution)/shard_map/ppermute | solution.py:25
  71.2 10.0 %collective-permute-start.23 = (bf16[256,1152]{1,0:T(8,128)(2,1)S(1)}, bf16[256,1152]{1,0:T(8,128)(2,1)S(1)}, u32[]{:S(2)}, u32[]{:S(2)}) collective-permute-start(bf16[256,1152]{1,0:T(8,128)(2,1)S(1)} %second.1), channel_id=1, source_target_pairs={{0,2},{1,3},{2,0},{3,1},{4,6},{5,7},{6,4},{7,5},{8,24},{9,25},{10,... | collective-permute-start | bytes 1769480 | tf_op jit(solution)/shard_map/ppermute | solution.py:25
  71.2 13.1 %collective-permute-start.25 = (bf16[256,1152]{1,0:T(8,128)(2,1)S(1)}, bf16[256,1152]{1,0:T(8,128)(2,1)S(1)}, u32[]{:S(2)}, u32[]{:S(2)}) collective-permute-start(bf16[256,1152]{1,0:T(8,128)(2,1)S(1)} %get-tuple-element.124), channel_id=1, source_target_pairs={{0,6},{1,7},{2,4},{3,5},{4,2},{5,3},{6,0},{7,1},{8,56},{9,57},{10,... | collective-permute-start | bytes 1769480 | tf_op jit(solution)/shard_map/ppermute | solution.py:25
  75.0 4.2 %collective-permute-start.20 = (f32[8,128]{1,0:T(8,128)S(1)}, f32[8,128]{1,0:T(8,128)S(1)}, u32[]{:S(2)}, u32[]{:S(2)}) collective-permute-start(f32[8,128]{1,0:T(8,128)S(1)} %add.44), channel_id=1, source_target_pairs={{0,6},{1,7},{2,4},{3,5},{4,2},{5,3},{6,0},{7,1},{8,14},{9,15},{10,... | collective-permute-start | bytes 12296 | tf_op jit(solution)/shard_map/ppermute | solution.py:25
  80.8 13.1 %collective-permute-start.22 = (bf16[256,1152]{1,0:T(8,128)(2,1)S(1)}, bf16[256,1152]{1,0:T(8,128)(2,1)S(1)}, u32[]{:S(2)}, u32[]{:S(2)}) collective-permute-start(bf16[256,1152]{1,0:T(8,128)(2,1)S(1)} %near.3), channel_id=1, source_target_pairs={{0,2},{1,3},{2,0},{3,1},{4,6},{5,7},{6,4},{7,5},{8,24},{9,25},{10,... | collective-permute-start | bytes 1769480 | tf_op jit(solution)/shard_map/ppermute | solution.py:25
  82.0 12.0 %collective-permute-start.24 = (bf16[256,1152]{1,0:T(8,128)(2,1)S(1)}, bf16[256,1152]{1,0:T(8,128)(2,1)S(1)}, u32[]{:S(2)}, u32[]{:S(2)}) collective-permute-start(bf16[256,1152]{1,0:T(8,128)(2,1)S(1)} %near.4), channel_id=1, source_target_pairs={{0,6},{1,7},{2,4},{3,5},{4,2},{5,3},{6,0},{7,1},{8,56},{9,57},{10,... | collective-permute-start | bytes 1769480 | tf_op jit(solution)/shard_map/ppermute | solution.py:25
  85.0 10.0 %collective-permute-start.26 = (bf16[256,1152]{1,0:T(8,128)(2,1)S(1)}, bf16[256,1152]{1,0:T(8,128)(2,1)S(1)}, u32[]{:S(2)}, u32[]{:S(2)}) collective-permute-start(bf16[256,1152]{1,0:T(8,128)(2,1)S(1)} %near.5), channel_id=1, source_target_pairs={{0,1},{1,0},{2,3},{3,2},{4,5},{5,4},{6,7},{7,6},{8,73},{9,72},{10,... | collective-permute-start | bytes 1769480 | tf_op jit(solution)/shard_map/ppermute | solution.py:25
  85.9 4.0 %collective-permute-start.27 = (f32[8,128]{1,0:T(8,128)S(1)}, f32[8,128]{1,0:T(8,128)S(1)}, u32[]{:S(2)}, u32[]{:S(2)}) collective-permute-start(f32[8,128]{1,0:T(8,128)S(1)} %add.45), channel_id=1, source_target_pairs={{0,16},{1,17},{2,18},{3,19},{4,20},{5,21},{6,22},{7,23},{8,24},{9,... | collective-permute-start | bytes 12296 | tf_op jit(solution)/shard_map/ppermute | solution.py:25
  90.0 4.0 %collective-permute-start.28 = (f32[8,128]{1,0:T(8,128)S(1)}, f32[8,128]{1,0:T(8,128)S(1)}, u32[]{:S(2)}, u32[]{:S(2)}) collective-permute-start(f32[8,128]{1,0:T(8,128)S(1)} %add.46), channel_id=1, source_target_pairs={{0,48},{1,49},{2,50},{3,51},{4,52},{5,53},{6,54},{7,55},{8,56},{9,... | collective-permute-start | bytes 12296 | tf_op jit(solution)/shard_map/ppermute | solution.py:25
  93.9 5.6 %copy-start.1 = (f32[128,1152]{1,0:T(8,128)S(1)}, f32[128,1152]{1,0:T(8,128)}, u32[]{:S(2)}) copy-start(f32[128,1152]{1,0:T(8,128)} %refs_1_.1) | copy-start | bytes 1769476
  93.9 5.6 %copy-start.3 = (f32[128,1152]{1,0:T(8,128)S(1)}, f32[128,1152]{1,0:T(8,128)}, u32[]{:S(2)}) copy-start(f32[128,1152]{1,0:T(8,128)} %refs_2_.1) | copy-start | bytes 1769476
  96.3 3.2 %collective-permute-start.29 = (f32[136,1152]{1,0:T(8,128)S(1)}, f32[136,1152]{1,0:T(8,128)S(1)}, u32[]{:S(2)}, u32[]{:S(2)}) collective-permute-start(f32[136,1152]{1,0:T(8,128)S(1)} %get-tuple-element.127), channel_id=1, source_target_pairs={{0,8},{1,9},{2,10},{3,11},{4,12},{5,13},{6,14},{7,15},{8,0},{9,1},... | collective-permute-start | bytes 1880072 | tf_op jit(solution)/shard_map/ppermute | solution.py:25
